TPU v7x, 128 devices: a whole 4x4x4 slice. The times are simulated.
128 devices in a mesh: ctx: 16 (over z, y), ep: 8 (over x, core).
Axes of the slice: x: 4, y: 4, z: 4, core: 2. Of those that a mesh axis runs over, the one named last changes fastest.
Arguments:
- queries: bfloat16 [4096, 8192], P('ctx', 'ep'), may hold values from -0.625 to 0.625
- keys: bfloat16 [4096, 8192], P('ctx', 'ep'), may hold values from -0.625 to 0.625
- values: bfloat16 [4096, 8192], P('ctx', 'ep'), may hold values from -0.625 to 0.625
- out_grad: bfloat16 [4096, 8192], P('ctx', 'ep'), may hold values from -0.625 to 0.625
- log_decay: float32 [64, 4096], P('ep', 'ctx'), may hold values from -1 to 0
- doc_ids: int32 [4096], P('ctx'), may hold values from 0 to 2, never falling along the last dimension, each value on 1 to 2048 neighbouring positions
- moe_input: bfloat16 [4096, 3072], P('ctx', 'ep'), may hold values from -6 to 6
- moe_cotangent: bfloat16 [4096, 3072], P('ctx', 'ep'), may hold values from -6 to 6
- router_weights: float32 [4096, 2], P('ctx'), may hold values from 0.1 to 0.9
- expert_ids: int32 [4096, 2], P('ctx'), may hold values from 0 to 15, all different within a row; in each aligned block of 256 rows (0 to 255, 256 to 511, ...) at most 40 rows name the same one
- w_gate: bfloat16 [16, 3072, 5120], P('ctx', None, 'ep'), may hold values from -0.109375 to 0.109375
- w_up: bfloat16 [16, 3072, 5120], P('ctx', None, 'ep'), may hold values from -0.109375 to 0.109375
- w_down: bfloat16 [16, 5120, 3072], P('ctx', 'ep'), may hold values from -0.078125 to 0.078125
Outputs:
- grad_q: bfloat16 [4096, 8192], P('ctx', 'ep')
- grad_k: bfloat16 [4096, 8192], P('ctx', 'ep')
- grad_v: bfloat16 [4096, 8192], P('ctx', 'ep')
- grad_moe_input: bfloat16 [4096, 3072], P('ctx', 'ep')
Inputs may be any that keep to these rules, and one draw needn't show every extreme that they name: `doc_ids`: document numbers never fall along the sequence; a document holds 1 to 2048 tokens, one exactly that many. `expert_ids`: A token names two different experts. In the rows of one device no expert is named more than 40 times, a bound that some block reaches.
All inputs are finite; a program needn't handle non-finite values.
Results may differ from a plain program's by a relative error of at most 0.0057.
Values may be sent and summed in bfloat16 or wider, within the bound.
No kernel may reach another device: no remote copies, remote signals or barrier semaphores. Data moves between devices by JAX's collectives and lax.ppermute only.
A program may use at most 128 MiB of HBM per device.

v0:
```python
import jax
import jax.numpy as jnp
from jax import lax
from jax.sharding import PartitionSpec as P


def expert_part(x_rows, d_rows, gate_local, up_local, down_local):
    gate_pre = jnp.dot(x_rows, gate_local, preferred_element_type=jnp.float32)
    up_pre = jnp.dot(x_rows, up_local, preferred_element_type=jnp.float32)
    hidden_grad = lax.dot_general(
        d_rows, down_local, (((1,), (1,)), ((), ())), preferred_element_type=jnp.float32
    )
    sigmoid_gate = jax.nn.sigmoid(gate_pre)
    gate_grad = (
        hidden_grad * up_pre * sigmoid_gate * (1.0 + gate_pre * (1.0 - sigmoid_gate))
    ).astype(jnp.bfloat16)
    up_grad = (hidden_grad * gate_pre * sigmoid_gate).astype(jnp.bfloat16)
    first_term = lax.dot_general(
        gate_grad, gate_local, (((1,), (1,)), ((), ())), preferred_element_type=jnp.float32
    )
    second_term = lax.dot_general(
        up_grad, up_local, (((1,), (1,)), ((), ())), preferred_element_type=jnp.float32
    )
    return first_term + second_term


def local(
    queries,
    keys,
    values,
    out_grad,
    log_decay,
    doc_ids,
    moe_input,
    moe_cotangent,
    router_weights,
    expert_ids,
    w_gate,
    w_up,
    w_down,
):
    heads_dev = log_decay.shape[0]
    tok_rows = queries.shape[0]
    head_dim = queries.shape[1] // heads_dev
    query_h = queries.reshape(tok_rows, heads_dev, head_dim)
    key_h = keys.reshape(tok_rows, heads_dev, head_dim)
    value_h = values.reshape(tok_rows, heads_dev, head_dim)
    grad_h = out_grad.reshape(tok_rows, heads_dev, head_dim)
    cum_decay = jnp.cumsum(log_decay, axis=1)
    log_total = cum_decay[:, -1]
    first_doc = doc_ids[0]
    last_doc = doc_ids[-1]
    positions = jnp.arange(tok_rows)
    causal = positions[:, None] >= positions[None, :]
    same_doc = causal & (doc_ids[:, None] == doc_ids[None, :])
    spread = jnp.where(causal[None], cum_decay[:, :, None] - cum_decay[:, None, :], 0.0)
    decay_mask = jnp.where(same_doc[None], jnp.exp(spread), 0.0)
    end_weight = jnp.where(
        doc_ids[None, :] == last_doc, jnp.exp(log_total[:, None] - cum_decay), 0.0
    )
    keys_end = (end_weight.T[:, :, None] * key_h).astype(jnp.bfloat16)
    block_state = jnp.einsum("thd,the->hde", keys_end, value_h, preferred_element_type=jnp.float32)
    zero_state = jnp.zeros_like(block_state)
    first_weight = jnp.where(doc_ids[None, :] == first_doc, jnp.exp(cum_decay), 0.0)
    queries_first = (first_weight.T[:, :, None] * query_h).astype(jnp.bfloat16)
    first_adjoint = jnp.einsum(
        "thd,the->hde", queries_first, grad_h, preferred_element_type=jnp.float32
    )
    states = jnp.stack([block_state, first_adjoint])
    marks = jnp.concatenate(
        [jnp.exp(log_total), jnp.stack([first_doc, last_doc]).astype(jnp.float32)]
    )
    all_states, all_marks = (
        lax.all_gather(states[None], "ctx", axis=0, tiled=True),
        lax.all_gather(marks[None], "ctx", axis=0, tiled=True),
    )
    own_index = lax.axis_index("ctx")
    group_count = all_marks.shape[0]
    block_index = jnp.arange(group_count)
    firsts = all_marks[:, heads_dev]
    lasts = all_marks[:, heads_dev + 1]
    prevs = jnp.concatenate([jnp.full((1,), -1.0, jnp.float32), lasts[:-1]])
    rates = jnp.where((prevs == lasts)[:, None], all_marks[:, :heads_dev], 0.0)
    adjoint_terms = jnp.where((prevs == firsts)[:, None, None, None], all_states[:, 1], 0.0)

    def forward_step(state_sum, carried):
        factor, summand, position = carried
        return (
            jnp.where(position < own_index, factor[:, None, None] * state_sum + summand, state_sum),
            None,
        )

    def backward_step(state_sum, carried):
        factor, summand, position = carried
        return (
            jnp.where(position > own_index, factor[:, None, None] * state_sum + summand, state_sum),
            None,
        )

    incoming, _ = lax.scan(forward_step, zero_state, (rates, all_states[:, 0], block_index))
    adjoint, _ = lax.scan(
        backward_step, zero_state, (rates, adjoint_terms, block_index), reverse=True
    )
    prev_doc = prevs[own_index]
    start_weight = jnp.where(
        doc_ids[None, :].astype(jnp.float32) == prev_doc, jnp.exp(cum_decay), 0.0
    )
    incoming_low = incoming.astype(jnp.bfloat16)
    adjoint_low = adjoint.astype(jnp.bfloat16)
    score_do = jnp.einsum("ihd,jhd->hij", grad_h, value_h, preferred_element_type=jnp.float32)
    score_qk = jnp.einsum("ihd,jhd->hij", query_h, key_h, preferred_element_type=jnp.float32)
    weighted_do = (decay_mask * score_do).astype(jnp.bfloat16)
    weighted_qk = (decay_mask * score_qk).astype(jnp.bfloat16)
    grad_query = jnp.einsum(
        "hij,jhd->ihd", weighted_do, key_h, preferred_element_type=jnp.float32
    ) + start_weight.T[:, :, None] * jnp.einsum(
        "ihe,hde->ihd", grad_h, incoming_low, preferred_element_type=jnp.float32
    )
    grad_key = jnp.einsum(
        "hij,ihd->jhd", weighted_do, query_h, preferred_element_type=jnp.float32
    ) + end_weight.T[:, :, None] * jnp.einsum(
        "jhe,hde->jhd", value_h, adjoint_low, preferred_element_type=jnp.float32
    )
    grad_value = jnp.einsum(
        "hij,ihe->jhe", weighted_qk, grad_h, preferred_element_type=jnp.float32
    ) + end_weight.T[:, :, None] * jnp.einsum(
        "jhd,hde->jhe", key_h, adjoint_low, preferred_element_type=jnp.float32
    )
    grad_q = grad_query.reshape(tok_rows, heads_dev * head_dim).astype(jnp.bfloat16)
    grad_k = grad_key.reshape(tok_rows, heads_dev * head_dim).astype(jnp.bfloat16)
    grad_v = grad_value.reshape(tok_rows, heads_dev * head_dim).astype(jnp.bfloat16)
    moe_rows = moe_input.shape[0]
    expert_count = lax.axis_size("ctx")
    capacity = 5 * moe_rows // (2 * expert_count)
    flat_expert = expert_ids.reshape(-1)
    is_expert = (flat_expert[:, None] == jnp.arange(expert_count)[None, :]).astype(jnp.int32)
    slot_rank = jnp.sum((jnp.cumsum(is_expert, axis=0) - is_expert) * is_expert, axis=1)
    slot_index = flat_expert * capacity + slot_rank
    gate_local = w_gate[0]
    up_local = w_up[0]
    down_local = w_down[0]

    def pack_rows(source_rows):
        buffer = jnp.zeros((expert_count * capacity, source_rows.shape[1]), source_rows.dtype)
        buffer = buffer.at[slot_index].set(jnp.repeat(source_rows, 2, axis=0))
        return buffer.reshape(expert_count, capacity, source_rows.shape[1])

    x_full = lax.all_gather(
        lax.all_to_all(pack_rows(moe_input), "ctx", split_axis=0, concat_axis=0, tiled=True),
        "ep",
        axis=2,
        tiled=True,
    )
    d_full = lax.all_gather(
        lax.all_to_all(pack_rows(moe_cotangent), "ctx", split_axis=0, concat_axis=0, tiled=True),
        "ep",
        axis=2,
        tiled=True,
    )
    full_shape = x_full.shape
    partial_grad = expert_part(
        x_full.reshape(-1, full_shape[2]),
        d_full.reshape(-1, full_shape[2]),
        gate_local,
        up_local,
        down_local,
    ).reshape(full_shape)
    shard_grad = lax.psum_scatter(partial_grad, "ep", scatter_dimension=2, tiled=True)
    returned = lax.all_to_all(shard_grad, "ctx", split_axis=0, concat_axis=0, tiled=True)
    slot_grads = returned.reshape(-1, returned.shape[2])[slot_index].reshape(moe_rows, 2, -1)
    grad_moe_input = jnp.sum(slot_grads * router_weights[:, :, None], axis=1).astype(jnp.bfloat16)
    return (grad_q, grad_k, grad_v, grad_moe_input)


def solution(mesh):
    in_specs = (
        P("ctx", "ep"),
        P("ctx", "ep"),
        P("ctx", "ep"),
        P("ctx", "ep"),
        P("ep", "ctx"),
        P("ctx"),
        P("ctx", "ep"),
        P("ctx", "ep"),
        P("ctx", None),
        P("ctx", None),
        P("ctx", None, "ep"),
        P("ctx", None, "ep"),
        P("ctx", "ep", None),
    )
    out_specs = (P("ctx", "ep"), P("ctx", "ep"), P("ctx", "ep"), P("ctx", "ep"))
    return jax.shard_map(local, mesh=mesh, in_specs=in_specs, out_specs=out_specs, check_vma=False)
```

profile of v0, /device:TPU:0, one launch (start us, length us, event | category | flops | bytes accessed | tf_op | source)
XLA Modules:
  0.0 391.1 jit_solution(16804430476218179430)
XLA Ops:
  13.1 2.5 scatter_custom_fusion.1
  15.6 19.2 %all_to_all.15 = bf16[16,40,384]{2,1,0:T(8,128)(2,1)} all-to-all(bf16[16,40,384]{2,1,0:T(8,128)(2,1)S(1)} %bitcast.184), channel_id=1, replica_groups=mesh['ctx'=16,'ep'=8] {'ctx'}, dimensions={0} | all-to-all | bytes 983040 | tf_op jit(solution)/shard_map/all_to_all | solution.py:149
  35.2 2.5 scatter_custom_fusion
  37.7 13.6 %all_to_all.16 = bf16[16,40,384]{2,1,0:T(8,128)(2,1)} all-to-all(bf16[16,40,384]{2,1,0:T(8,128)(2,1)S(1)} %bitcast.183), channel_id=1, replica_groups=mesh['ctx'=16,'ep'=8] {'ctx'}, dimensions={0} | all-to-all | bytes 983040 | tf_op jit(solution)/shard_map/all_to_all | solution.py:155
  51.6 11.7 %all-gather.8.cloned.1.call-done = bf16[16,40,3072]{2,1,0:T(8,128)(2,1)} async-done(((bf16[16,40,384]{2,1,0:T(8,128)(2,1)}), bf16[16,40,3072]{2,1,0:T(8,128)(2,1)}) %all-gather.8.cloned.1.call-update) | async-done | bytes 3932176 | tf_op jit(solution)/shard_map/all_gather | solution.py:148
  63.4 6.5 %fusion.5 = f32[640,640]{1,0:T(8,128)S(1)} fusion(bf16[640,3072]{1,0:T(8,128)(2,1)} %bitcast.190, bf16[1,3072,640]{2,1,0:T(8,128)(2,1)} %param.27), kind=kOutput, calls=%fused_computation.15 | convolution fusion | flops 2516582400 | bytes 9502720 | tf_op jit(solution)/shard_map/dot_general | solution.py:8
  69.9 26.1 %all-gather.6.cloned.1.call-done = bf16[16,40,3072]{2,1,0:T(8,128)(2,1)} async-done(((bf16[16,40,384]{2,1,0:T(8,128)(2,1)}), bf16[16,40,3072]{2,1,0:T(8,128)(2,1)}) %all-gather.6.cloned.1.call-update) | async-done | bytes 3932176 | tf_op jit(solution)/shard_map/all_gather | solution.py:154
  96.0 6.7 %fusion.10 = f32[640,640]{1,0:T(8,128)S(1)} fusion(bf16[640,3072]{1,0:T(8,128)(2,1)} %bitcast.192, bf16[1,640,3072]{2,1,0:T(8,128)(2,1)} %param.29), kind=kOutput, calls=%fused_computation.20 | convolution fusion | flops 2516582400 | bytes 9502720 | tf_op jit(solution)/shard_map/dot_general | solution.py:10
  102.7 3.4 multiply_convert_fusion.3
  106.1 3.2 fusion.3
  109.4 5.4 %convolution_add_fusion = f32[640,3072]{1,0:T(8,128)} fusion(f32[640,3072]{1,0:T(8,128)S(1)} %fusion.3, bf16[1,3072,640]{2,1,0:T(8,128)(2,1)S(1)} %copy-done.8, f32[640,640]{1,0:T(8,128)S(1)} %fusion.10, f32[640,640]{1,0:T(8,128)S(1)} %fusion.5), kind=kOutput, calls=%fused_computation.12 | convolution fusion | flops 2521006080 | bytes 22937600 | tf_op jit(solution)/shard_map/dot_general | solution.py:21
  119.1 1.4 add_convert_fusion
  120.6 40.8 %all-reduce = f32[160]{0:T(256)S(1)} all-reduce(f32[160]{0:T(256)S(1)} %maximum_dynamic-update-slice_fusion), channel_id=2, replica_groups=mesh['ctx'=16,'ep'=8] {'ctx'}, use_global_device_ids=true, to_apply=%add | all-reduce | flops 160 | bytes 1280
  163.3 1.3 broadcast_compare_fusion.1
  166.8 1.9 multiply_convert_fusion.1
  168.7 3.7 all-to-all-start.2
  172.6 3.0 convolution_bitcast_fusion.4
  175.5 1.5 convolution_bitcast_fusion.5
  177.1 3.2 convolution_bitcast_fusion.3
  180.2 19.0 %all-to-all-done.2 = f32[16,40,384]{2,1,0:T(8,128)S(1)} async-done(((f32[16,40,384]{2,1,0:T(8,128)}), f32[16,40,384]{2,1,0:T(8,128)S(1)}, u32[]{:S(2)}, u32[]{:S(2)}) %all-to-all-start.2) | async-done | bytes 983072 | tf_op jit(solution)/shard_map/all_to_all | solution.py:169
  199.2 2.3 gather_fusion
  201.5 1.6 reshape.235
  203.1 1.7 multiply_reduce_fusion
  204.7 76.2 %all-gather.10.cloned.1.call-done = f32[32,8,128,128]{3,2,1,0:T(8,128)} async-done(((f32[2,8,128,128]{3,2,1,0:T(8,128)}), f32[32,8,128,128]{3,2,1,0:T(8,128)}) %all-gather.10.cloned.1.call-update) | async-done | bytes 16777232 | tf_op jit(solution)/shard_map/all_gather | solution.py:74
  280.9 8.9 %slice_bitcast_fusion.1 = f32[16,8,128,128]{3,2,1,0:T(8,128)} fusion(f32[16,2,8,128,128]{4,3,2,1,0:T(8,128)} %bitcast.167), kind=kLoop, calls=%fused_computation.11 | loop fusion | bytes 16777216 | tf_op jit(solution)/shard_map/squeeze | solution.py:100
  289.8 2.3 copy-done.1
  292.1 4.2 %fusion.2 = f32[16,8,128,128]{3,2,1,0:T(8,128)} fusion(f32[16,2,8,128,128]{4,3,2,1,0:T(8,128)S(1)} %bitcast.168, pred[16]{0:T(512)(128)(4,1)S(1)} %fusion.51), kind=kLoop, calls=%fused_computation.10 | loop fusion | flops 2097152 | bytes 16777232 | tf_op jit(solution)/shard_map/jit(_where)/select_n | solution.py:84
  296.3 39.3 %while.27 = (s32[]{:T(128)}, f32[8,128,128]{2,1,0:T(8,128)S(1)}, s32[16]{0:T(128)S(1)}, s32[]{:T(128)}, f32[16,8]{1,0:T(8,128)S(1)}, /*index=5*/f32[16,8,128,128]{3,2,1,0:T(8,128)}, s32[]{:T(128)}, s32[]{:T(128)}, s32[]{:T(128)}) while((s32[]{:T(128)}, f32[8,128,128]{2,1,0:T(8,128)S(1)}, s32[16]{0:T(128)S(1)}, s32[]{:T(128)}, ...), condition=%wide.region_5.6_spmd.clone, body=%wide.region_4.5_spmd.clone.sunk | while | flops 524293 | bytes 1573105 | solution.py:101
  297.5 1.2 fusion.75
  300.0 1.2 fusion.75
  302.5 1.2 fusion.75
  304.9 1.2 fusion.75
  307.4 1.2 fusion.75
  309.8 1.2 fusion.75
  312.3 1.2 fusion.75
  314.8 1.2 fusion.75
  317.2 1.2 fusion.75
  319.7 1.2 fusion.75
  322.1 1.2 fusion.75
  324.6 1.2 fusion.75
  327.0 1.2 fusion.75
  329.5 1.2 fusion.75
  332.0 1.2 fusion.75
  334.4 1.2 fusion.75
  335.6 2.5 fusion.22
  338.1 2.0 copy.161
  341.4 41.2 %while.26 = (s32[]{:T(128)}, f32[8,128,128]{2,1,0:T(8,128)S(1)}, s32[16]{0:T(128)S(1)}, s32[]{:T(128)}, f32[16,8]{1,0:T(8,128)S(1)}, /*index=5*/f32[16,8,128,128]{3,2,1,0:T(8,128)}, s32[]{:T(128)}, s32[]{:T(128)}) while((s32[]{:T(128)}, f32[8,128,128]{2,1,0:T(8,128)S(1)}, s32[16]{0:T(128)S(1)}, s32[]{:T(128)}, ...), condition=%wide.region_3.4_spmd.clone, body=%wide.region_2.3_spmd.clone.sunk | while | flops 524292 | bytes 1573085 | solution.py:100
  342.8 1.2 fusion.74
  (180 shorter events, 54.1 us)
Async XLA Ops:
  8.0 156.7 %copy-start = (bf16[256,1024]{1,0:T(8,128)(2,1)S(1)}, bf16[256,1024]{1,0:T(8,128)(2,1)}, u32[]{:S(2)}) copy-start(bf16[256,1024]{1,0:T(8,128)(2,1)} %param.19) | copy-start | bytes 1572868
  8.0 26.9 %copy-start.12 = (bf16[256,384]{1,0:T(8,128)(2,1)S(1)}, bf16[256,384]{1,0:T(8,128)(2,1)}, u32[]{:S(2)}) copy-start(bf16[256,384]{1,0:T(8,128)(2,1)} %param.24) | copy-start | bytes 589828
  8.0 55.3 %all-gather.8.cloned.1.call-start = ((), (), s32[]{:S(2)}) async-start(), calls=%async_computation.5 | async-start | bytes 4423680 | tf_op jit(solution)/shard_map/all_gather | solution.py:148
  34.8 61.2 %all-gather.6.cloned.1.call-start = ((), (), s32[]{:S(2)}) async-start(), calls=%async_computation.4 | async-start | bytes 4423680 | tf_op jit(solution)/shard_map/all_gather | solution.py:154
  51.4 117.3 %reduce-scatter.2.cloned.1.call-start = ((), (), s32[]{:S(2)}) async-start(), calls=%async_computation.6 | async-start | bytes 8847360 | tf_op jit(solution)/shard_map/reduce_scatter | solution.py:168
  96.0 6.7 %copy-start.8 = (bf16[1,3072,640]{2,1,0:T(8,128)(2,1)S(1)}, bf16[1,3072,640]{2,1,0:T(8,128)(2,1)}, u32[]{:S(2)}) copy-start(bf16[1,3072,640]{2,1,0:T(8,128)(2,1)} %param.28) | copy-start | bytes 11796484
  96.0 6.7 %copy-start.17 = (bf16[16,40,3072]{2,1,0:T(8,128)(2,1)S(1)}, bf16[16,40,3072]{2,1,0:T(8,128)(2,1)}, u32[]{:S(2)}) copy-start(bf16[16,40,3072]{2,1,0:T(8,128)(2,1)} %all-gather.8.cloned.1.call-done) | copy-start | bytes 11796484
  102.7 3.4 copy-start.16
  114.8 0.7 copy-start.14
  114.8 1.5 copy-start.13
  114.8 3.0 copy-start.18
  114.8 46.6 %copy-start.9 = (bf16[256,1024]{1,0:T(8,128)(2,1)S(1)}, bf16[256,1024]{1,0:T(8,128)(2,1)}, u32[]{:S(2)}) copy-start(bf16[256,1024]{1,0:T(8,128)(2,1)} %param.18) | copy-start | bytes 1572868
  114.8 46.8 %copy-start.10 = (bf16[256,1024]{1,0:T(8,128)(2,1)S(1)}, bf16[256,1024]{1,0:T(8,128)(2,1)}, u32[]{:S(2)}) copy-start(bf16[256,1024]{1,0:T(8,128)(2,1)} %param.20) | copy-start | bytes 1572868
  114.9 47.0 %copy-start.11 = (bf16[256,1024]{1,0:T(8,128)(2,1)S(1)}, bf16[256,1024]{1,0:T(8,128)(2,1)}, u32[]{:S(2)}) copy-start(bf16[256,1024]{1,0:T(8,128)(2,1)} %param.17) | copy-start | bytes 1572868
  114.9 166.0 %all-gather.10.cloned.1.call-start = ((), (), s32[]{:S(2)}) async-start(), calls=%async_computation.7 | async-start | bytes 17825792 | tf_op jit(solution)/shard_map/all_gather | solution.py:74
  161.9 4.8 %copy-start.2 = (bf16[256,1024]{0,1:T(8,128)(2,1)}, bf16[256,1024]{0,1:T(8,128)(2,1)S(1)}, u32[]{:S(2)}) copy-start(bf16[256,1024]{0,1:T(8,128)(2,1)S(1)} %copy.167) | copy-start | bytes 1572868
  162.1 3.9 %copy-start.4 = (bf16[256,1024]{0,1:T(8,128)(2,1)}, bf16[256,1024]{0,1:T(8,128)(2,1)S(1)}, u32[]{:S(2)}) copy-start(bf16[256,1024]{0,1:T(8,128)(2,1)S(1)} %copy.168) | copy-start | bytes 1572868
  166.7 5.6 %copy-start.15 = (f32[256,2]{0,1:T(2,128)S(1)}, f32[256,2]{0,1:T(2,128)}, u32[]{:S(2)}) copy-start(f32[256,2]{0,1:T(2,128)} %param.25) | copy-start | bytes 6148
  168.7 30.5 %all-to-all-start.2 = ((f32[16,40,384]{2,1,0:T(8,128)}), f32[16,40,384]{2,1,0:T(8,128)S(1)}, u32[]{:S(2)}, u32[]{:S(2)}) async-start(f32[16,40,384]{2,1,0:T(8,128)} %reduce-scatter.2.cloned.1.call-done), calls=%async_computation.3 | async-start | bytes 1966080 | tf_op jit(solution)/shard_map/all_to_all | solution.py:169
  172.5 3.0 copy-start.7
  280.9 11.2 %copy-start.1 = (f32[32,8,128,128]{3,2,1,0:T(8,128)S(1)}, f32[32,8,128,128]{3,2,1,0:T(8,128)}, u32[]{:S(2)}) copy-start(f32[32,8,128,128]{3,2,1,0:T(8,128)} %all-gather.10.cloned.1.call-done) | copy-start | bytes 50331652
  335.6 4.5 %copy-start.6 = (f32[256,8,128]{0,2,1:T(8,128)S(1)}, f32[256,8,128]{0,2,1:T(8,128)}, u32[]{:S(2)}) copy-start(f32[256,8,128]{0,2,1:T(8,128)} %convolution_bitcast_fusion.4) | copy-start | bytes 3145732
  341.4 41.3 %copy-start.3 = (bf16[256,1024]{0,1:T(8,128)(2,1)S(1)}, bf16[256,1024]{0,1:T(8,128)(2,1)}, u32[]{:S(2)}) copy-start(bf16[256,1024]{0,1:T(8,128)(2,1)} %copy-done.2) | copy-start | bytes 1572868
  341.4 41.3 %copy-start.5 = (f32[256,8,128]{0,2,1:T(8,128)S(1)}, f32[256,8,128]{0,2,1:T(8,128)}, u32[]{:S(2)}) copy-start(f32[256,8,128]{0,2,1:T(8,128)} %convolution_bitcast_fusion.5) | copy-start | bytes 3145732
Sparse Core Ops, SparseCore 0:
  34.9 28.3 all-gather.7
  65.1 30.8 all-gather.5
  115.0 49.8 reduce-scatter.1
Sparse Core Ops, SparseCore 1:
  166.2 114.7 all-gather.9
where the time goes:
time: 394 us; the launch traced here: 391 us
  waiting for transfers between devices  133 us (34%)
  blocking collectives  73.6 us (19%)
  local copies, waits for them, and re-layouts  51.8 us (13%)
  other arithmetic  51.3 us (13%)
  matrix products  38.5 us (10%)
  loops' own time  22.6 us (6%)
  between operations  16.3 us (4%)
  starting transfers between devices  4 us (1%)
    all_gather x1, waiting for transfers between devices, local(): lax.all_gather(states[None], 'ctx', axis=0, tiled=True)  76.2 us
    unnamed x1, blocking collectives  40.8 us
    all_gather x1, waiting for transfers between devices, local(): lax.all_gather(lax.all_to_all(pack_rows(moe_cotangent), 'ctx', split_axis...  26.1 us
    dynamic_slice x32, local copies, waits for them, and re-layouts, local(): lax.scan(forward_step, zero_state, (rates, all_states[:, 0], block_index))  20 us
    all_to_all x1, blocking collectives, local(): lax.all_to_all(pack_rows(moe_input), 'ctx', split_axis=0, concat_axis=0,...  19.2 us
    all_to_all x1, waiting for transfers between devices, local(): lax.all_to_all(shard_grad, 'ctx', split_axis=0, concat_axis=0, tiled=True)  19 us
    select_n x16, other arithmetic, backward_step(): jnp.where(position > own_index, factor[:, None, None] * state_sum + summa...  18.8 us
    select_n x16, other arithmetic, forward_step(): jnp.where(position < own_index, factor[:, None, None] * state_sum + summa...  18.8 us
  transfers between devices with their start and end apart: 5, of which 4 were waited for; matrix products, arithmetic and copies ran while one was open for 9% of the time, Pallas kernels for 0%

commit v1 on v0

v1 whole, which is shorter than its diff:
```python
import jax
import jax.numpy as jnp
from jax import lax
from jax.experimental import pallas as pl
from jax.experimental.pallas import tpu as pltpu
from jax.sharding import Mesh, PartitionSpec as P

BF = jnp.bfloat16
F32 = jnp.float32
I32 = jnp.int32
TOK = 256
HEADS = 8
HD = 128
HALF = HD // 2
CTX = 16
CAP = 40
ROWS = CTX * CAP
FEAT = 384
HID = 640
MARKS = 16
RINGX = 4
RIGHT = [(i, (i + 1) % RINGX) for i in range(RINGX)]
LEFT = [(i, (i - 1) % RINGX) for i in range(RINGX)]
SWAP = [(0, 1), (1, 0)]
MIB = 1 << 20

NT = (((1,), (1,)), ((), ()))
TN = (((0,), (0,)), ((), ()))


def vmem():
    return pl.BlockSpec(memory_space=pltpu.VMEM)


def anywhere():
    return pl.BlockSpec(memory_space=pl.ANY)


def call(kernel, outs, ins, scratch=(), flops=0, size=0, limit=32):
    return pl.pallas_call(
        kernel,
        out_shape=outs,
        in_specs=ins,
        out_specs=jax.tree.map(lambda _: vmem(), outs),
        scratch_shapes=scratch,
        compiler_params=pltpu.CompilerParams(vmem_limit_bytes=limit * MIB),
        cost_estimate=pl.CostEstimate(flops=flops, bytes_accessed=size, transcendentals=0),
    )


def mm(a, b, dims=(((1,), (0,)), ((), ()))):
    return lax.dot_general(a, b, dims, preferred_element_type=F32)


def onehot(slot):
    row = lax.broadcasted_iota(I32, (ROWS, TOK), 0)
    return row == slot


def pack_kernel(ids_ref, x_ref, d_ref, rows_ref, slots_ref):
    ids = ids_ref[...]
    expert = lax.broadcasted_iota(I32, (CTX, TOK), 0)
    first, second = ids[0:1] == expert, ids[1:2] == expert
    hits = jnp.where(first | second, 1.0, 0.0).astype(BF)
    before = lax.broadcasted_iota(I32, (TOK, TOK), 0) < lax.broadcasted_iota(I32, (TOK, TOK), 1)
    rank = mm(hits, jnp.where(before, 1.0, 0.0).astype(BF))
    slot0 = ids[0:1] * CAP + jnp.sum(jnp.where(first, rank, 0.0), axis=0, keepdims=True).astype(I32)
    slot1 = ids[1:2] * CAP + jnp.sum(jnp.where(second, rank, 0.0), axis=0, keepdims=True).astype(I32)
    slots_ref[0:1, :] = slot0
    slots_ref[1:2, :] = slot1
    pick = jnp.where(onehot(slot0) | onehot(slot1), 1.0, 0.0).astype(BF)
    rows_ref[:, :FEAT] = mm(pick, x_ref[...]).astype(BF)
    rows_ref[:, FEAT:] = mm(pick, d_ref[...]).astype(BF)


def combine_kernel(rows_ref, slots_ref, weights_ref, out_ref):
    rows = rows_ref[...]
    columns = jnp.concatenate([weights_ref[...], jnp.zeros((6, TOK), F32)], axis=0).T
    total = jnp.zeros((TOK, FEAT), F32)
    for k in range(2):
        pick = jnp.where(onehot(slots_ref[k : k + 1, :]), 1.0, 0.0).astype(BF)
        total += columns[:, k : k + 1] * mm(pick, rows, TN)
    out_ref[...] = total.astype(BF)


def state_kernel(q_ref, k_ref, v_ref, g_ref, decay_ref, doc_ref, out_ref, row_ref, col_ref):
    upto = lax.broadcasted_iota(I32, (TOK, TOK), 0) <= lax.broadcasted_iota(I32, (TOK, TOK), 1)
    cum = lax.dot_general(
        decay_ref[...],
        jnp.where(upto, 1.0, 0.0),
        (((1,), (0,)), ((), ())),
        precision=lax.Precision.HIGHEST,
        preferred_element_type=F32,
    )
    doc = jnp.broadcast_to(doc_ref[...].astype(F32), (HEADS, TOK))
    both = jnp.concatenate([cum, doc], axis=0)
    row_ref[...] = both
    turned = both.T
    cum_c, doc_c = turned[:, :HEADS], turned[:, HEADS:]
    total, first, last = cum_c[TOK - 1 :], doc_c[0:1], doc_c[TOK - 1 :]
    end_w = jnp.where(doc_c == last, jnp.exp(total - cum_c), 0.0)
    first_w = jnp.where(doc_c == first, jnp.exp(cum_c), 0.0)
    col_ref[:, 0:8] = cum_c
    col_ref[:, 8:16] = doc_c
    col_ref[:, 16:24] = first_w
    col_ref[:, 24:32] = end_w
    line = lax.broadcasted_iota(I32, (MARKS, HD), 0)
    for h in range(HEADS):
        cols = slice(h * HD, (h + 1) * HD)
        keys_end = (end_w[:, h : h + 1] * k_ref[:, cols].astype(F32)).astype(BF)
        queries_first = (first_w[:, h : h + 1] * q_ref[:, cols].astype(F32)).astype(BF)
        state = mm(keys_end, v_ref[:, cols], TN).astype(BF)
        adjoint = mm(queries_first, g_ref[:, cols], TN).astype(BF)
        sum_h = jnp.broadcast_to(total[:, h : h + 1], (MARKS, HD))
        high = sum_h.astype(BF).astype(F32)
        mid = (sum_h - high).astype(BF).astype(F32)
        low = sum_h - high - mid
        marks = jnp.where(line == 0, high, jnp.where(line == 1, mid, jnp.where(line == 2, low, 0.0)))
        marks = jnp.where(line == 3, first[:, h : h + 1], jnp.where(line == 4, last[:, h : h + 1], marks))
        for part in range(2):
            lines = slice(part * HALF, (part + 1) * HALF)
            out_ref[2 * h + part, 0:HALF, :] = state[lines]
            out_ref[2 * h + part, HALF:HD, :] = adjoint[lines]
            out_ref[2 * h + part, HD:, :] = marks.astype(BF)


def scan_kernel(in_ref, out_ref):
    rates, live = [], []
    prev = jnp.full((1, HD), -1.0, F32)
    for b in range(CTX):
        marks = in_ref[b, HD:, :].astype(F32)
        first, last = marks[3:4], marks[4:5]
        rates.append(jnp.where(prev == last, jnp.exp(marks[0:1] + marks[1:2] + marks[2:3]), 0.0))
        live.append(prev == first)
        prev = last
    total = jnp.zeros((HALF, HD), F32)
    for b in range(CTX):
        out_ref[b, 0:HALF, :] = jnp.where(live[b], total, 0.0).astype(BF)
        total = rates[b] * total + in_ref[b, 0:HALF, :].astype(F32)
    total = jnp.zeros((HALF, HD), F32)
    for b in reversed(range(CTX)):
        out_ref[b, HALF:, :] = total.astype(BF)
        total = rates[b] * total + jnp.where(live[b], in_ref[b, HALF:HD, :].astype(F32), 0.0)


def attention_kernel(q_ref, k_ref, v_ref, g_ref, row_ref, col_ref, carried_ref, gq_ref, gk_ref, gv_ref):
    seen = lax.broadcasted_iota(I32, (TOK, TOK), 0) >= lax.broadcasted_iota(I32, (TOK, TOK), 1)
    same = seen & (col_ref[:, 8:9] == row_ref[8:9, :])
    for h in range(HEADS):
        cols = slice(h * HD, (h + 1) * HD)
        q, k, v, g = q_ref[:, cols], k_ref[:, cols], v_ref[:, cols], g_ref[:, cols]
        spread = jnp.where(same, col_ref[:, h : h + 1] - row_ref[h : h + 1, :], -1e30)
        decay = jnp.exp(spread)
        weighted_do = (decay * mm(g, v, NT)).astype(BF)
        weighted_qk = (decay * mm(q, k, NT)).astype(BF)
        incoming = jnp.concatenate([carried_ref[2 * h, 0:HALF, :], carried_ref[2 * h + 1, 0:HALF, :]], axis=0)
        adjoint = jnp.concatenate([carried_ref[2 * h, HALF:, :], carried_ref[2 * h + 1, HALF:, :]], axis=0)
        start = col_ref[:, 16 + h : 17 + h]
        end = col_ref[:, 24 + h : 25 + h]
        gq_ref[:, cols] = (mm(weighted_do, k) + start * mm(g, incoming, NT)).astype(BF)
        gk_ref[:, cols] = (mm(weighted_do, q, TN) + end * mm(v, adjoint, NT)).astype(BF)
        gv_ref[:, cols] = (mm(weighted_qk, g, TN) + end * mm(k, adjoint)).astype(BF)


def feature_block(place, offset, sibling):
    core = place[1]
    core = 1 - core if sibling else core
    return pl.multiple_of((((place[0] + offset) % RINGX) * 2 + core) * FEAT, FEAT)


def first_layer(place, offsets, chunks, weights, xs, ds, gate_w, up_w, down_w, sems):
    groups = ([], [], [])
    n = 0
    for i, (offset, sibling) in enumerate(offsets):
        block = feature_block(place, offset, sibling)
        side = pl.ds(i * FEAT, FEAT)
        x_src, d_src = chunks[i]
        moves = (
            (0, x_src, xs.at[:, side]),
            (0, weights[0].at[0, pl.ds(block, FEAT), :], gate_w.at[side, :]),
            (1, weights[1].at[0, pl.ds(block, FEAT), :], up_w.at[side, :]),
            (2, d_src, ds.at[:, side]),
            (2, weights[2].at[0, :, pl.ds(block, FEAT)], down_w.at[:, side]),
        )
        for group, src, dst in moves:
            groups[group].append(pltpu.make_async_copy(src, dst, sems.at[n]))
            n += 1
    for group in groups:
        for copy in group:
            copy.start()
    return groups


A_OFFSETS = ((0, False), (0, True), (-1, False), (1, False), (-1, True), (1, True))


def expert_a_kernel(place, a0, a1, a2, a3, a4, a5, wg, wu, wd, gate_ref, up_ref, hid_ref, xs, ds, gate_w, up_w, down_w, sems):
    chunks = [(a.at[:, pl.ds(0, FEAT)], a.at[:, pl.ds(FEAT, FEAT)]) for a in (a0, a1, a2, a3, a4, a5)]
    groups = first_layer(place, A_OFFSETS, chunks, (wg, wu, wd), xs, ds, gate_w, up_w, down_w, sems)
    for copy in groups[0]:
        copy.wait()
    gate_ref[...] = mm(xs[...], gate_w[...])
    for copy in groups[1]:
        copy.wait()
    up_ref[...] = mm(xs[...], up_w[...])
    for copy in groups[2]:
        copy.wait()
    hid_ref[...] = mm(ds[...], down_w[...], NT)


def out_weights(place, sibling, wg, wu, cat, sems, at):
    copies = []
    for i, offset in enumerate(OUT_OFFSETS):
        block = feature_block(place, offset, sibling)
        side = pl.ds(i * FEAT, FEAT)
        copies.append(pltpu.make_async_copy(wg.at[0, pl.ds(block, FEAT), :], cat.at[side, pl.ds(0, HID)], sems.at[at + 2 * i]))
        copies.append(pltpu.make_async_copy(wu.at[0, pl.ds(block, FEAT), :], cat.at[side, pl.ds(HID, HID)], sems.at[at + 2 * i + 1]))
    for copy in copies:
        copy.start()
    return copies


B_OFFSETS = ((2, False), (2, True))
OUT_OFFSETS = (2, 1, -1, 0)


def expert_b_kernel(place, gate_ref, up_ref, hid_ref, x0, d0, x1, d1, wg, wu, wd, mid_ref, out_ref, xs, ds, gate_w, up_w, down_w, cat, sems):
    chunks = [(x0, d0), (x1, d1)]
    groups = first_layer(place, B_OFFSETS, chunks, (wg, wu, wd), xs, ds, gate_w, up_w, down_w, sems)
    late = out_weights(place, True, wg, wu, cat, sems, 10)
    for group in groups:
        for copy in group:
            copy.wait()
    gate = gate_ref[...] + mm(xs[...], gate_w[...])
    up = up_ref[...] + mm(xs[...], up_w[...])
    hid = hid_ref[...] + mm(ds[...], down_w[...], NT)
    s = 1.0 / (1.0 + jnp.exp(-gate))
    mid_ref[:, :HID] = (hid * up * s * (1.0 + gate * (1.0 - s))).astype(BF)
    mid_ref[:, HID:] = (hid * gate * s).astype(BF)
    for copy in late:
        copy.wait()
    for i in range(RINGX):
        out_ref[i] = mm(mid_ref[...], cat[i * FEAT : (i + 1) * FEAT, :], NT).astype(BF)


def expert_c_kernel(place, mid_ref, wg, wu, out_ref, cat, sems):
    for copy in out_weights(place, False, wg, wu, cat, sems, 0):
        copy.wait()
    for i in range(RINGX):
        out_ref[i] = mm(mid_ref[...], cat[i * FEAT : (i + 1) * FEAT, :], NT)


def local(
    queries, keys, values, out_grad, log_decay, doc_ids, moe_input, moe_cotangent, router_weights, expert_ids, w_gate, w_up, w_down
):
    S = jax.ShapeDtypeStruct
    place = jnp.stack([lax.axis_index("x"), lax.axis_index("core")]).astype(I32)
    smem = pl.BlockSpec(memory_space=pltpu.SMEM)

    def ring(value, way):
        return lax.ppermute(value, "x", way)

    def swap(value):
        return lax.ppermute(value, "core", SWAP)

    rows, slots = call(
        pack_kernel,
        (S((ROWS, 2 * FEAT), BF), S((2, TOK), I32)),
        [vmem()] * 3,
        flops=2 * ROWS * TOK * 2 * FEAT,
        size=2 * MIB,
    )(expert_ids.T, moe_input, moe_cotangent)
    own = lax.all_to_all(rows.reshape(CTX, CAP, 2 * FEAT), "ctx", 0, 0, tiled=True).reshape(ROWS, 2 * FEAT)
    from_left, from_right = ring(own, RIGHT), ring(own, LEFT)
    x_opp, d_opp = ring(from_left[:, :FEAT], RIGHT), ring(from_right[:, FEAT:], LEFT)
    own_s, left_s, right_s = swap(own), swap(from_left), swap(from_right)
    x_opp_s, d_opp_s = swap(x_opp), swap(d_opp)

    message, lines, columns = call(
        state_kernel,
        (S((CTX, HD + MARKS, HD), BF), S((2 * HEADS, TOK), F32), S((TOK, 4 * HEADS), F32)),
        [vmem()] * 6,
        flops=4 * HEADS * TOK * HD * HD,
        size=3 * MIB,
    )(queries, keys, values, out_grad, log_decay, doc_ids.reshape(1, TOK))
    message = lax.all_to_all(message, "ctx", 0, 0, tiled=True)
    carried = call(scan_kernel, S((CTX, HD, HD), BF), [vmem()], flops=MIB, size=MIB)(message)
    carried = lax.all_to_all(carried, "ctx", 0, 0, tiled=True)
    grads = call(
        attention_kernel,
        (S((TOK, HEADS * HD), BF),) * 3,
        [vmem()] * 7,
        flops=16 * HEADS * TOK * TOK * HD,
        size=4 * MIB,
    )(queries, keys, values, out_grad, lines, columns, carried)

    square = S((ROWS, HID), F32)
    n = len(A_OFFSETS)
    gate, up, hid = call(
        expert_a_kernel,
        (square,) * 3,
        [smem] + [anywhere()] * 9,
        [
            pltpu.VMEM((ROWS, n * FEAT), BF),
            pltpu.VMEM((ROWS, n * FEAT), BF),
            pltpu.VMEM((n * FEAT, HID), BF),
            pltpu.VMEM((n * FEAT, HID), BF),
            pltpu.VMEM((HID, n * FEAT), BF),
            pltpu.SemaphoreType.DMA((5 * n,)),
        ],
        flops=6 * ROWS * HID * n * FEAT,
        size=18 * MIB,
    )(place, own, own_s, from_left, from_right, left_s, right_s, w_gate, w_up, w_down)
    n = len(B_OFFSETS)
    mid, away = call(
        expert_b_kernel,
        (S((ROWS, 2 * HID), BF), S((RINGX, ROWS, FEAT), BF)),
        [smem] + [vmem()] * 3 + [anywhere()] * 7,
        [
            pltpu.VMEM((ROWS, n * FEAT), BF),
            pltpu.VMEM((ROWS, n * FEAT), BF),
            pltpu.VMEM((n * FEAT, HID), BF),
            pltpu.VMEM((n * FEAT, HID), BF),
            pltpu.VMEM((HID, n * FEAT), BF),
            pltpu.VMEM((RINGX * FEAT, 2 * HID), BF),
            pltpu.SemaphoreType.DMA((5 * n + 8,)),
        ],
        flops=10 * ROWS * HID * RINGX * FEAT,
        size=14 * MIB,
        limit=48,
    )(place, gate, up, hid, x_opp, d_opp, x_opp_s, d_opp_s, w_gate, w_up, w_down)
    away = swap(away)
    mine = call(
        expert_c_kernel,
        S((RINGX, ROWS, FEAT), F32),
        [smem, vmem()] + [anywhere()] * 2,
        [pltpu.VMEM((RINGX * FEAT, 2 * HID), BF), pltpu.SemaphoreType.DMA((8,))],
        flops=4 * ROWS * HID * RINGX * FEAT,
        size=8 * MIB,
    )(place, mid, w_gate, w_up)

    chip = mine + away.astype(F32)
    cut = ROWS // 2
    via_right = ring(chip[0, :cut].astype(BF), RIGHT).astype(F32)
    via_left = ring(chip[0, cut:].astype(BF), LEFT).astype(F32)
    to_right = jnp.concatenate([chip[1, :cut] + via_right, chip[1, cut:]], axis=0).astype(BF)
    to_left = jnp.concatenate([chip[2, :cut], chip[2, cut:] + via_left], axis=0).astype(BF)
    summed = chip[3] + ring(to_right, RIGHT).astype(F32) + ring(to_left, LEFT).astype(F32)
    back = lax.all_to_all(summed.astype(BF).reshape(CTX, CAP, FEAT), "ctx", 0, 0, tiled=True)
    grad_moe = call(
        combine_kernel,
        S((TOK, FEAT), BF),
        [vmem()] * 3,
        flops=4 * ROWS * TOK * FEAT,
        size=MIB,
    )(back.reshape(ROWS, FEAT), slots, router_weights.T)
    return (*grads, grad_moe)


def solution(mesh):
    fine = Mesh(mesh.devices.reshape(CTX, RINGX, 2), ("ctx", "x", "core"))
    ep = ("x", "core")
    row = P("ctx", ep)
    in_specs = (row, row, row, row, P(ep, "ctx"), P("ctx"), row, row, P("ctx", None), P("ctx", None))
    in_specs += (P("ctx", None, ep), P("ctx", None, ep), P("ctx", ep, None))
    return jax.shard_map(local, mesh=fine, in_specs=in_specs, out_specs=(row,) * 4, check_vma=False)
```

time: 394 us -> 172 us (0.44)
  waiting for transfers between devices: 133 us -> 51.5 us
  blocking collectives: 73.6 us -> 24.4 us
  other arithmetic: 51.3 us -> 7.92 us
  Pallas kernels: 0 us -> 41 us
  matrix products: 38.5 us -> 0 us
  local copies, waits for them, and re-layouts: 51.8 us -> 20.1 us
  loops' own time: 22.6 us -> 0 us
  starting transfers between devices: 4 us -> 25 us
  between operations: 16.3 us -> 0.87 us
    all_gather x3 -> x0, waiting for transfers between devices: 114 us -> none  [the longest x1 76.2 us: local(): lax.all_gather(states[None], 'ctx', axis=0, tiled=True)]
    select_n x35 -> x0, other arithmetic: 41.8 us -> none  [the longest x16 18.8 us: backward_step(): jnp.where(position > own_index, factor[:, None, None] * state_sum + summa...]
    pallas_call x0 -> x8, Pallas kernels: none -> 41 us  [the longest x1 14.2 us: local(): call(expert_a_kernel, (square,) * 3, [smem] + [anywhere()] * 9, [pltpu.VM...]
    unnamed x1 -> x0, blocking collectives: 40.8 us -> none
    dot_general x14 -> x0, matrix products: 38.5 us -> none  [the longest x1 6.68 us: expert_part(): lax.dot_general(d_rows, down_local, (((1,), (1,)), ((), ())), preferred_e...]
    ppermute x0 -> x14, waiting for transfers between devices: none -> 31.7 us  [the longest x8 31.7 us: ring(): return lax.ppermute(value, 'x', way)]
    another operation x2 -> x0, loops' own time: 22.6 us -> none  [the longest x1 11.6 us: local(): lax.scan(forward_step, zero_state, (rates, all_states[:, 0], block_index))]
    dynamic_slice x33 -> x0, local copies, waits for them, and re-layouts: 20.6 us -> none  [the longest x32 20 us: local(): lax.scan(forward_step, zero_state, (rates, all_states[:, 0], block_index))]
  transfers between devices with their start and end apart: 5 -> 17, of which waited for: 4 -> 6; matrix products, arithmetic and copies ran while one was open for 9% -> 4% of each run, Pallas kernels for 0% -> 15%
where the time goes in v1:
time: 172 us; the launch traced here: 171 us
  waiting for transfers between devices  51.5 us (30%)
  Pallas kernels  41 us (24%)
  starting transfers between devices  25 us (15%)
  blocking collectives  24.4 us (14%)
  local copies, waits for them, and re-layouts  20.1 us (12%)
  other arithmetic  7.92 us (5%)
    ppermute x8, waiting for transfers between devices, ring(): return lax.ppermute(value, 'x', way)  31.7 us
    all_to_all x1, blocking collectives, local(): lax.all_to_all(rows.reshape(CTX, CAP, 2 * FEAT), 'ctx', 0, 0, tiled=True)  24.4 us
    unnamed x46, local copies, waits for them, and re-layouts  17.5 us
    pallas_call x1, Pallas kernels, local(): call(expert_a_kernel, (square,) * 3, [smem] + [anywhere()] * 9, [pltpu.VM...  14.2 us
    ppermute x8, starting transfers between devices, ring(): return lax.ppermute(value, 'x', way)  12.9 us
    pallas_call x1, Pallas kernels, local(): call(expert_b_kernel, (S((ROWS, 2 * HID), BF), S((RINGX, ROWS, FEAT), BF)...  12.6 us
    all_to_all x1, waiting for transfers between devices, local(): carried = lax.all_to_all(carried, 'ctx', 0, 0, tiled=True)  8 us
    all_to_all x1, waiting for transfers between devices, local(): lax.all_to_all(summed.astype(BF).reshape(CTX, CAP, FEAT), 'ctx', 0, 0, ti...  6.07 us
  transfers between devices with their start and end apart: 17, of which 6 were waited for; matrix products, arithmetic and copies ran while one was open for 4% of the time, Pallas kernels for 15%

profile of v1, /device:TPU:0, one launch (start us, length us, event | category | flops | bytes accessed | tf_op | source)
XLA Modules:
  0.0 170.7 jit_solution(1439942657703755495)
XLA Ops:
  0.6 0.9 copy-done.15
  1.6 0.9 copy-done.16
  2.5 0.7 copy-done.17
  3.8 24.4 %all_to_all.20 = bf16[16,40,768]{2,1,0:T(8,128)(2,1)S(1)} all-to-all(bf16[16,40,768]{2,1,0:T(8,128)(2,1)S(1)} %bitcast.41), channel_id=1, replica_groups=mesh['ctx'=16,'x'=4,'core'=2] {'ctx'}, dimensions={0} | all-to-all | bytes 1966080 | tf_op jit(solution)/shard_map/all_to_all | solution.py:273
  28.2 1.5 collective-permute-start.1
  29.7 1.8 %collective-permute-start.2 = (bf16[640,768]{1,0:T(8,128)(2,1)S(1)}, bf16[640,768]{1,0:T(8,128)(2,1)S(1)}, u32[]{:S(2)}, u32[]{:S(2)}) collective-permute-start(bf16[640,768]{1,0:T(8,128)(2,1)S(1)} %bitcast.38), channel_id=1, source_target_pairs={{0,6},{2,0},{4,2},{6,4},{1,7},{3,1},{5,3},{7,5},{8,14},{10,8},{12,... | collective-permute-start | bytes 2949128 | tf_op jit(solution)/shard_map/ppermute | solution.py:261
  31.5 20.3 %collective-permute-done.1.a2 = bf16[640,768]{1,0:T(8,128)(2,1)S(1)} collective-permute-done((bf16[640,768]{1,0:T(8,128)(2,1)S(1)}, bf16[640,768]{1,0:T(8,128)(2,1)S(1)}, u32[]{:S(2)}, u32[]{:S(2)}) %collective-permute-start.1) | collective-permute-done | bytes 983072 | tf_op jit(solution)/shard_map/ppermute | solution.py:261
  52.3 0.8 slice.40
  53.1 1.0 collective-permute-start.5
  54.1 0.8 slice.41
  54.9 2.3 %collective-permute-start.6 = (bf16[640,384]{1,0:T(8,128)(2,1)}, bf16[640,384]{1,0:T(8,128)(2,1)}, u32[]{:S(2)}, u32[]{:S(2)}) collective-permute-start(bf16[640,384]{1,0:T(8,128)(2,1)} %slice.41), channel_id=1, source_target_pairs={{0,6},{2,0},{4,2},{6,4},{1,7},{3,1},{5,3},{7,5},{8,14},{10,8},{12,... | collective-permute-start | bytes 1474568 | tf_op jit(solution)/shard_map/ppermute | solution.py:261
  57.3 10.4 %collective-permute-done.5.x0 = bf16[640,384]{1,0:T(8,128)(2,1)S(1)} collective-permute-done((bf16[640,384]{1,0:T(8,128)(2,1)}, bf16[640,384]{1,0:T(8,128)(2,1)S(1)}, u32[]{:S(2)}, u32[]{:S(2)}) %collective-permute-start.5) | collective-permute-done | bytes 491552 | tf_op jit(solution)/shard_map/ppermute | solution.py:261
  67.7 0.9 collective-permute-done.6.d0
  68.6 2.1 %copy-done = bf16[1,3072,640]{2,1,0:T(8,128)(2,1)S(1)} copy-done((bf16[1,3072,640]{2,1,0:T(8,128)(2,1)S(1)}, bf16[1,3072,640]{2,1,0:T(8,128)(2,1)}, u32[]{:S(2)}) %copy-start) | copy-done | bytes 3932184
  70.7 2.1 %copy-done.2 = bf16[1,3072,640]{2,1,0:T(8,128)(2,1)S(1)} copy-done((bf16[1,3072,640]{2,1,0:T(8,128)(2,1)S(1)}, bf16[1,3072,640]{2,1,0:T(8,128)(2,1)}, u32[]{:S(2)}) %copy-start.2) | copy-done | bytes 3932184
  72.9 2.1 %copy-done.10 = bf16[1,640,3072]{2,1,0:T(8,128)(2,1)S(1)} copy-done((bf16[1,640,3072]{2,1,0:T(8,128)(2,1)S(1)}, bf16[1,640,3072]{2,1,0:T(8,128)(2,1)}, u32[]{:S(2)}) %copy-start.10) | copy-done | bytes 3932184
  75.0 14.2 %shard_map.160 = (f32[640,640]{1,0:T(8,128)S(1)}, f32[640,640]{1,0:T(8,128)S(1)}, f32[640,640]{1,0:T(8,128)S(1)}) custom-call(s32[2]{0:T(128)S(1)} %pad_add_fusion.place, bf16[640,768]{1,0:T(8,128)(2,1)S(1)} %bitcast.40, bf16[640,768]{1,0:T(8,128)(2,1)} %collective-permute-done.a1, bf16[640,768]{1,0:T(8,128)(2,1)S(1)} %collective-permute-done.1.a2, ...), custom_call_target="tpu_custom_call" | custom-call | flops 5662310400 | bytes 18874368 | tf_op jit(solution)/shard_map/pallas_call | solution.py:299
  89.2 1.2 copy-done.19
  90.4 1.2 copy-done.21
  91.6 1.2 copy-done.22
  92.8 0.8 copy-done.11
  93.6 0.8 copy-done.13
  94.3 1.0 copy-done.12
  95.4 1.0 copy-done.14
  96.4 1.4 copy-done.20
  97.8 12.6 %shard_map.161 = (bf16[640,1280]{1,0:T(8,128)(2,1)S(1)}, bf16[4,640,384]{2,1,0:T(8,128)(2,1)}) custom-call(s32[2]{0:T(128)S(1)} %pad_add_fusion.place, f32[640,640]{1,0:T(8,128)S(1)} %copy-done.20, f32[640,640]{1,0:T(8,128)} %copy-done.21, f32[640,640]{1,0:T(8,128)} %copy-done.22, bf16[640,384]{1,0:T(8,128)(2,1)S(1)} %collective-permute-done.5.x0, ...), custom_call_target="tpu_custom_call" | custom-call | flops 6291456000 | bytes 14680064 | tf_op jit(solution)/shard_map/pallas_call | solution.py:315
  110.5 0.8 collective-permute-start.9
  111.3 4.6 %shard_map.162 = f32[4,640,384]{2,1,0:T(8,128)S(1)} custom-call(s32[2]{0:T(128)S(1)} %pad_add_fusion.place, bf16[640,1280]{1,0:T(8,128)(2,1)S(1)} %get-tuple-element.27.mid_ref, bf16[1,3072,640]{2,1,0:T(8,128)(2,1)S(1)} %copy-done.1, bf16[1,3072,640]{2,1,0:T(8,128)(2,1)S(1)} %copy-done.3), custom_call_target="tpu_custom_call" | custom-call | flops 2516582400 | bytes 8388608 | tf_op jit(solution)/shard_map/pallas_call | solution.py:333
  115.9 2.5 %fusion.7 = (bf16[4,640,384]{2,1,0:T(8,128)(2,1)S(1)}, f32[4,640,384]{2,1,0:T(8,128)}) fusion(f32[4,640,384]{2,1,0:T(8,128)S(1)} %shard_map.162, bf16[4,640,384]{2,1,0:T(8,128)(2,1)S(1)} %collective-permute-done.9), kind=kLoop, calls=%fused_computation.18 | loop fusion | flops 2949120 | bytes 11796480 | tf_op jit(solution)/shard_map/convert.9
  118.4 0.9 slice_bitcast_fusion.6
  119.2 1.2 collective-permute-start.10
  120.5 2.0 %collective-permute-start.12 = (bf16[320,384]{1,0:T(8,128)(2,1)}, bf16[320,384]{1,0:T(8,128)(2,1)}, u32[]{:S(2)}, u32[]{:S(2)}) collective-permute-start(bf16[320,384]{1,0:T(8,128)(2,1)} %get-tuple-element.35), channel_id=1, source_target_pairs={{0,6},{2,0},{4,2},{6,4},{1,7},{3,1},{5,3},{7,5},{8,14},{10,8},{12,... | collective-permute-start | bytes 737288 | tf_op jit(solution)/shard_map/ppermute | solution.py:261
  122.5 2.7 %shard_map.156 = (bf16[16,144,128]{2,1,0:T(8,128)(2,1)}, f32[16,256]{1,0:T(8,128)S(1)}, f32[256,32]{1,0:T(8,128)S(1)}) custom-call(bf16[256,1024]{1,0:T(8,128)(2,1)S(1)} %copy-done.4, bf16[256,1024]{1,0:T(8,128)(2,1)S(1)} %copy-done.5, bf16[256,1024]{1,0:T(8,128)(2,1)S(1)} %copy-done.6, bf16[256,1024]{1,0:T(8,128)(2,1)S(1)} %copy-done.7, ...), custom_call_target="tpu_custom_call" | custom-call | flops 134217728 | bytes 3145728 | tf_op jit(solution)/shard_map/pallas_call | solution.py:279
  125.3 3.6 %all-to-all-start = ((bf16[16,144,128]{2,1,0:T(8,128)(2,1)}), bf16[16,144,128]{2,1,0:T(8,128)(2,1)S(1)}, u32[]{:S(2)}, u32[]{:S(2)}) async-start(bf16[16,144,128]{2,1,0:T(8,128)(2,1)} %get-tuple-element.19), calls=%async_computation | async-start | bytes 1179648 | tf_op jit(solution)/shard_map/all_to_all | solution.py:286
  128.9 1.4 fusion.6
  130.3 0.8 pad_maximum_fusion
  131.1 1.2 collective-permute-start.11
  132.3 0.8 pad_maximum_fusion.1
  133.1 2.0 %collective-permute-start.13 = (bf16[640,384]{1,0:T(8,128)(2,1)}, bf16[640,384]{1,0:T(8,128)(2,1)S(1)}, u32[]{:S(2)}, u32[]{:S(2)}) collective-permute-start(bf16[640,384]{1,0:T(8,128)(2,1)} %pad_maximum_fusion.1), channel_id=1, source_target_pairs={{0,6},{2,0},{4,2},{6,4},{1,7},{3,1},{5,3},{7,5},{8,14},{10,8},{12,... | collective-permute-start | bytes 1474568 | tf_op jit(solution)/shard_map/ppermute | solution.py:261
  135.2 5.8 %all-to-all-done.in_ref = bf16[16,144,128]{2,1,0:T(8,128)(2,1)S(1)} async-done(((bf16[16,144,128]{2,1,0:T(8,128)(2,1)}), bf16[16,144,128]{2,1,0:T(8,128)(2,1)S(1)}, u32[]{:S(2)}, u32[]{:S(2)}) %all-to-all-start) | async-done | bytes 589856 | tf_op jit(solution)/shard_map/all_to_all | solution.py:286
  141.0 1.0 shard_map.157
  141.9 3.6 %all-to-all-start.1 = ((bf16[16,128,128]{2,1,0:T(8,128)(2,1)}), bf16[16,128,128]{2,1,0:T(8,128)(2,1)S(1)}, u32[]{:S(2)}, u32[]{:S(2)}) async-start(bf16[16,128,128]{2,1,0:T(8,128)(2,1)} %shard_map.157), calls=%async_computation.1 | async-start | bytes 1048576 | tf_op jit(solution)/shard_map/all_to_all | solution.py:288
  145.6 2.3 %fusion.2 = bf16[640,384]{1,0:T(8,128)(2,1)} fusion(f32[4,640,384]{2,1,0:T(8,128)} %get-tuple-element.31, bf16[640,384]{1,0:T(8,128)(2,1)S(1)} %collective-permute-done.13, bf16[640,384]{1,0:T(8,128)(2,1)} %collective-permute-done.11), kind=kLoop, calls=%fused_computation.4 | loop fusion | flops 1228800 | bytes 2457600 | tf_op jit(solution)/shard_map/convert_element_type | solution.py:349
  147.9 8.0 %all-to-all-done.1.carried_ref = bf16[16,128,128]{2,1,0:T(8,128)(2,1)S(1)} async-done(((bf16[16,128,128]{2,1,0:T(8,128)(2,1)}), bf16[16,128,128]{2,1,0:T(8,128)(2,1)S(1)}, u32[]{:S(2)}, u32[]{:S(2)}) %all-to-all-start.1) | async-done | bytes 524320 | tf_op jit(solution)/shard_map/all_to_all | solution.py:288
  155.9 3.6 %all-to-all-start.3 = ((bf16[16,40,384]{2,1,0:T(8,128)(2,1)}), bf16[16,40,384]{2,1,0:T(8,128)(2,1)S(1)}, u32[]{:S(2)}, u32[]{:S(2)}) async-start(bf16[16,40,384]{2,1,0:T(8,128)(2,1)} %bitcast.46), calls=%async_computation.3 | async-start | bytes 983040 | tf_op jit(solution)/shard_map/all_to_all | solution.py:349
  159.5 3.9 %shard_map.158 = (bf16[256,1024]{1,0:T(8,128)(2,1)}, bf16[256,1024]{1,0:T(8,128)(2,1)}, bf16[256,1024]{1,0:T(8,128)(2,1)}) custom-call(bf16[256,1024]{1,0:T(8,128)(2,1)S(1)} %copy-done.4, bf16[256,1024]{1,0:T(8,128)(2,1)S(1)} %copy-done.5, bf16[256,1024]{1,0:T(8,128)(2,1)S(1)} %copy-done.6, bf16[256,1024]{1,0:T(8,128)(2,1)S(1)} %copy-done.7, ...), custom_call_target="tpu_custom_call" | custom-call | flops 1073741824 | bytes 4194304 | tf_op jit(solution)/shard_map/pallas_call | solution.py:289
  163.3 6.1 %all-to-all-done.3 = bf16[16,40,384]{2,1,0:T(8,128)(2,1)S(1)} async-done(((bf16[16,40,384]{2,1,0:T(8,128)(2,1)}), bf16[16,40,384]{2,1,0:T(8,128)(2,1)S(1)}, u32[]{:S(2)}, u32[]{:S(2)}) %all-to-all-start.3) | async-done | bytes 491552 | tf_op jit(solution)/shard_map/all_to_all | solution.py:349
  169.4 1.3 shard_map.163
  (50 shorter events, 1.4 us)
Async XLA Ops:
  0.6 0.9 copy-start.15
  1.6 0.9 copy-start.16
  2.5 0.7 copy-start.17
  28.2 23.6 %collective-permute-start.1 = (bf16[640,768]{1,0:T(8,128)(2,1)S(1)}, bf16[640,768]{1,0:T(8,128)(2,1)S(1)}, u32[]{:S(2)}, u32[]{:S(2)}) collective-permute-start(bf16[640,768]{1,0:T(8,128)(2,1)S(1)} %bitcast.37), channel_id=1, source_target_pairs={{0,2},{2,4},{4,6},{6,0},{1,3},{3,5},{5,7},{7,1},{8,10},{10,12},{12... | collective-permute-start | bytes 2949128 | tf_op jit(solution)/shard_map/ppermute | solution.py:261
  29.7 22.1 %collective-permute-start.2 = (bf16[640,768]{1,0:T(8,128)(2,1)S(1)}, bf16[640,768]{1,0:T(8,128)(2,1)S(1)}, u32[]{:S(2)}, u32[]{:S(2)}) collective-permute-start(bf16[640,768]{1,0:T(8,128)(2,1)S(1)} %bitcast.38), channel_id=1, source_target_pairs={{0,6},{2,0},{4,2},{6,4},{1,7},{3,1},{5,3},{7,5},{8,14},{10,8},{12,... | collective-permute-start | bytes 2949128 | tf_op jit(solution)/shard_map/ppermute | solution.py:261
  31.5 37.1 %collective-permute-start = (bf16[640,768]{1,0:T(8,128)(2,1)S(1)}, bf16[640,768]{1,0:T(8,128)(2,1)}, u32[]{:S(2)}, u32[]{:S(2)}) collective-permute-start(bf16[640,768]{1,0:T(8,128)(2,1)S(1)} %bitcast.39), channel_id=1, source_target_pairs={{0,1},{1,0},{2,3},{3,2},{4,5},{5,4},{6,7},{7,6},{8,9},{9,8},{10,11... | collective-permute-start | bytes 2949128 | tf_op jit(solution)/shard_map/ppermute | solution.py:264
  51.8 16.8 %collective-permute-start.3 = (bf16[640,768]{1,0:T(8,128)(2,1)S(1)}, bf16[640,768]{1,0:T(8,128)(2,1)}, u32[]{:S(2)}, u32[]{:S(2)}) collective-permute-start(bf16[640,768]{1,0:T(8,128)(2,1)S(1)} %collective-permute-done.1.a2), channel_id=1, source_target_pairs={{0,1},{1,0},{2,3},{3,2},{4,5},{5,4},{6,7},{7,6},{8,9},{9,8},{10,11... | collective-permute-start | bytes 2949128 | tf_op jit(solution)/shard_map/ppermute | solution.py:264
  51.8 16.8 %collective-permute-start.4 = (bf16[640,768]{1,0:T(8,128)(2,1)S(1)}, bf16[640,768]{1,0:T(8,128)(2,1)}, u32[]{:S(2)}, u32[]{:S(2)}) collective-permute-start(bf16[640,768]{1,0:T(8,128)(2,1)S(1)} %collective-permute-done.2.a3), channel_id=1, source_target_pairs={{0,1},{1,0},{2,3},{3,2},{4,5},{5,4},{6,7},{7,6},{8,9},{9,8},{10,11... | collective-permute-start | bytes 2949128 | tf_op jit(solution)/shard_map/ppermute | solution.py:264
  53.1 14.6 %collective-permute-start.5 = (bf16[640,384]{1,0:T(8,128)(2,1)}, bf16[640,384]{1,0:T(8,128)(2,1)S(1)}, u32[]{:S(2)}, u32[]{:S(2)}) collective-permute-start(bf16[640,384]{1,0:T(8,128)(2,1)} %slice.40), channel_id=1, source_target_pairs={{0,2},{2,4},{4,6},{6,0},{1,3},{3,5},{5,7},{7,1},{8,10},{10,12},{12... | collective-permute-start | bytes 1474568 | tf_op jit(solution)/shard_map/ppermute | solution.py:261
  54.9 13.7 %collective-permute-start.6 = (bf16[640,384]{1,0:T(8,128)(2,1)}, bf16[640,384]{1,0:T(8,128)(2,1)}, u32[]{:S(2)}, u32[]{:S(2)}) collective-permute-start(bf16[640,384]{1,0:T(8,128)(2,1)} %slice.41), channel_id=1, source_target_pairs={{0,6},{2,0},{4,2},{6,4},{1,7},{3,1},{5,3},{7,5},{8,14},{10,8},{12,... | collective-permute-start | bytes 1474568 | tf_op jit(solution)/shard_map/ppermute | solution.py:261
  67.7 25.1 %collective-permute-start.7 = (bf16[640,384]{1,0:T(8,128)(2,1)S(1)}, bf16[640,384]{1,0:T(8,128)(2,1)S(1)}, u32[]{:S(2)}, u32[]{:S(2)}) collective-permute-start(bf16[640,384]{1,0:T(8,128)(2,1)S(1)} %collective-permute-done.5.x0), channel_id=1, source_target_pairs={{0,1},{1,0},{2,3},{3,2},{4,5},{5,4},{6,7},{7,6},{8,9},{9,8},{10,11... | collective-permute-start | bytes 1474568 | tf_op jit(solution)/shard_map/ppermute | solution.py:264
  68.6 25.0 %collective-permute-start.8 = (bf16[640,384]{1,0:T(8,128)(2,1)}, bf16[640,384]{1,0:T(8,128)(2,1)S(1)}, u32[]{:S(2)}, u32[]{:S(2)}) collective-permute-start(bf16[640,384]{1,0:T(8,128)(2,1)} %collective-permute-done.6.d0), channel_id=1, source_target_pairs={{0,1},{1,0},{2,3},{3,2},{4,5},{5,4},{6,7},{7,6},{8,9},{9,8},{10,11... | collective-permute-start | bytes 1474568 | tf_op jit(solution)/shard_map/ppermute | solution.py:264
  68.6 2.1 %copy-start = (bf16[1,3072,640]{2,1,0:T(8,128)(2,1)S(1)}, bf16[1,3072,640]{2,1,0:T(8,128)(2,1)}, u32[]{:S(2)}) copy-start(bf16[1,3072,640]{2,1,0:T(8,128)(2,1)} %wg.5) | copy-start | bytes 11796484
  70.7 2.1 %copy-start.2 = (bf16[1,3072,640]{2,1,0:T(8,128)(2,1)S(1)}, bf16[1,3072,640]{2,1,0:T(8,128)(2,1)}, u32[]{:S(2)}) copy-start(bf16[1,3072,640]{2,1,0:T(8,128)(2,1)} %wu.5) | copy-start | bytes 11796484
  72.9 2.1 %copy-start.10 = (bf16[1,640,3072]{2,1,0:T(8,128)(2,1)S(1)}, bf16[1,640,3072]{2,1,0:T(8,128)(2,1)}, u32[]{:S(2)}) copy-start(bf16[1,640,3072]{2,1,0:T(8,128)(2,1)} %wd.3) | copy-start | bytes 11796484
  89.2 1.2 copy-start.19
  90.4 1.2 copy-start.21
  91.6 1.2 copy-start.22
  92.8 0.8 copy-start.11
  93.6 0.8 copy-start.13
  94.3 1.0 copy-start.12
  95.4 1.0 copy-start.14
  96.4 1.4 copy-start.20
  97.8 13.4 %copy-start.1 = (bf16[1,3072,640]{2,1,0:T(8,128)(2,1)S(1)}, bf16[1,3072,640]{2,1,0:T(8,128)(2,1)}, u32[]{:S(2)}) copy-start(bf16[1,3072,640]{2,1,0:T(8,128)(2,1)} %wg.5) | copy-start | bytes 11796484
  97.8 13.4 %copy-start.3 = (bf16[1,3072,640]{2,1,0:T(8,128)(2,1)S(1)}, bf16[1,3072,640]{2,1,0:T(8,128)(2,1)}, u32[]{:S(2)}) copy-start(bf16[1,3072,640]{2,1,0:T(8,128)(2,1)} %wu.5) | copy-start | bytes 11796484
  110.5 5.4 %collective-permute-start.9 = (bf16[4,640,384]{2,1,0:T(8,128)(2,1)}, bf16[4,640,384]{2,1,0:T(8,128)(2,1)S(1)}, u32[]{:S(2)}, u32[]{:S(2)}) collective-permute-start(bf16[4,640,384]{2,1,0:T(8,128)(2,1)} %get-tuple-element.28), channel_id=1, source_target_pairs={{0,1},{1,0},{2,3},{3,2},{4,5},{5,4},{6,7},{7,6},{8,9},{9,8},{10,11... | collective-permute-start | bytes 5898248 | tf_op jit(solution)/shard_map/ppermute | solution.py:264
  115.8 6.6 %copy-start.4 = (bf16[256,1024]{1,0:T(8,128)(2,1)S(1)}, bf16[256,1024]{1,0:T(8,128)(2,1)}, u32[]{:S(2)}) copy-start(bf16[256,1024]{1,0:T(8,128)(2,1)} %q_ref.3) | copy-start | bytes 1572868
  115.9 6.6 %copy-start.5 = (bf16[256,1024]{1,0:T(8,128)(2,1)S(1)}, bf16[256,1024]{1,0:T(8,128)(2,1)}, u32[]{:S(2)}) copy-start(bf16[256,1024]{1,0:T(8,128)(2,1)} %k_ref.3) | copy-start | bytes 1572868
  115.9 6.6 %copy-start.6 = (bf16[256,1024]{1,0:T(8,128)(2,1)S(1)}, bf16[256,1024]{1,0:T(8,128)(2,1)}, u32[]{:S(2)}) copy-start(bf16[256,1024]{1,0:T(8,128)(2,1)} %v_ref.3) | copy-start | bytes 1572868
  115.9 6.6 %copy-start.7 = (bf16[256,1024]{1,0:T(8,128)(2,1)S(1)}, bf16[256,1024]{1,0:T(8,128)(2,1)}, u32[]{:S(2)}) copy-start(bf16[256,1024]{1,0:T(8,128)(2,1)} %g_ref.3) | copy-start | bytes 1572868
  115.9 6.6 %copy-start.8 = (f32[8,256]{1,0:T(8,128)S(1)}, f32[8,256]{1,0:T(8,128)}, u32[]{:S(2)}) copy-start(f32[8,256]{1,0:T(8,128)} %decay_ref.1) | copy-start | bytes 24580
  115.9 6.6 %copy-start.9 = (s32[256]{0:T(256)S(1)}, s32[256]{0:T(256)}, u32[]{:S(2)}) copy-start(s32[256]{0:T(256)} %param.18) | copy-start | bytes 3076
  119.2 9.6 %collective-permute-start.10 = (bf16[320,384]{1,0:T(8,128)(2,1)}, bf16[320,384]{1,0:T(8,128)(2,1)}, u32[]{:S(2)}, u32[]{:S(2)}) collective-permute-start(bf16[320,384]{1,0:T(8,128)(2,1)} %get-tuple-element.34), channel_id=1, source_target_pairs={{0,2},{2,4},{4,6},{6,0},{1,3},{3,5},{5,7},{7,1},{8,10},{10,12},{12... | collective-permute-start | bytes 737288 | tf_op jit(solution)/shard_map/ppermute | solution.py:261
  120.5 8.4 %collective-permute-start.12 = (bf16[320,384]{1,0:T(8,128)(2,1)}, bf16[320,384]{1,0:T(8,128)(2,1)}, u32[]{:S(2)}, u32[]{:S(2)}) collective-permute-start(bf16[320,384]{1,0:T(8,128)(2,1)} %get-tuple-element.35), channel_id=1, source_target_pairs={{0,6},{2,0},{4,2},{6,4},{1,7},{3,1},{5,3},{7,5},{8,14},{10,8},{12,... | collective-permute-start | bytes 737288 | tf_op jit(solution)/shard_map/ppermute | solution.py:261
  125.3 15.7 %all-to-all-start = ((bf16[16,144,128]{2,1,0:T(8,128)(2,1)}), bf16[16,144,128]{2,1,0:T(8,128)(2,1)S(1)}, u32[]{:S(2)}, u32[]{:S(2)}) async-start(bf16[16,144,128]{2,1,0:T(8,128)(2,1)} %get-tuple-element.19), calls=%async_computation | async-start | bytes 1179648 | tf_op jit(solution)/shard_map/all_to_all | solution.py:286
  131.1 14.4 %collective-permute-start.11 = (bf16[640,384]{1,0:T(8,128)(2,1)}, bf16[640,384]{1,0:T(8,128)(2,1)}, u32[]{:S(2)}, u32[]{:S(2)}) collective-permute-start(bf16[640,384]{1,0:T(8,128)(2,1)} %pad_maximum_fusion), channel_id=1, source_target_pairs={{0,2},{2,4},{4,6},{6,0},{1,3},{3,5},{5,7},{7,1},{8,10},{10,12},{12... | collective-permute-start | bytes 1474568 | tf_op jit(solution)/shard_map/ppermute | solution.py:261
  133.1 12.4 %collective-permute-start.13 = (bf16[640,384]{1,0:T(8,128)(2,1)}, bf16[640,384]{1,0:T(8,128)(2,1)S(1)}, u32[]{:S(2)}, u32[]{:S(2)}) collective-permute-start(bf16[640,384]{1,0:T(8,128)(2,1)} %pad_maximum_fusion.1), channel_id=1, source_target_pairs={{0,6},{2,0},{4,2},{6,4},{1,7},{3,1},{5,3},{7,5},{8,14},{10,8},{12,... | collective-permute-start | bytes 1474568 | tf_op jit(solution)/shard_map/ppermute | solution.py:261
  141.9 13.9 %all-to-all-start.1 = ((bf16[16,128,128]{2,1,0:T(8,128)(2,1)}), bf16[16,128,128]{2,1,0:T(8,128)(2,1)S(1)}, u32[]{:S(2)}, u32[]{:S(2)}) async-start(bf16[16,128,128]{2,1,0:T(8,128)(2,1)} %shard_map.157), calls=%async_computation.1 | async-start | bytes 1048576 | tf_op jit(solution)/shard_map/all_to_all | solution.py:288
  145.5 23.9 %copy-start.18 = (f32[256,2]{0,1:T(2,128)S(1)}, f32[256,2]{0,1:T(2,128)}, u32[]{:S(2)}) copy-start(f32[256,2]{0,1:T(2,128)} %param.21) | copy-start | bytes 6148
  155.9 13.5 %all-to-all-start.3 = ((bf16[16,40,384]{2,1,0:T(8,128)(2,1)}), bf16[16,40,384]{2,1,0:T(8,128)(2,1)S(1)}, u32[]{:S(2)}, u32[]{:S(2)}) async-start(bf16[16,40,384]{2,1,0:T(8,128)(2,1)} %bitcast.46), calls=%async_computation.3 | async-start | bytes 983040 | tf_op jit(solution)/shard_map/all_to_all | solution.py:349

commit v2 on v1

--- a/solution.py
+++ b/solution.py
@@ -36,6 +36,10 @@
     return pl.BlockSpec(memory_space=pl.ANY)
 
 
+def hbm():
+    return pl.BlockSpec(memory_space=pltpu.HBM)
+
+
 def call(kernel, outs, ins, scratch=(), flops=0, size=0, limit=32):
     return pl.pallas_call(
         kernel,
@@ -57,7 +61,14 @@
     return row == slot
 
 
-def pack_kernel(ids_ref, x_ref, d_ref, rows_ref, slots_ref):
+def pack_kernel(ids_hbm, x_hbm, d_hbm, rows_ref, slots_ref, ids_ref, x_ref, d_ref, sems):
+    copies = [
+        pltpu.make_async_copy(src, dst, sems.at[i])
+        for i, (src, dst) in enumerate(((ids_hbm, ids_ref), (x_hbm, x_ref), (d_hbm, d_ref)))
+    ]
+    for copy in copies:
+        copy.start()
+    copies[0].wait()
     ids = ids_ref[...]
     expert = lax.broadcasted_iota(I32, (CTX, TOK), 0)
     first, second = ids[0:1] == expert, ids[1:2] == expert
@@ -69,6 +80,8 @@
     slots_ref[0:1, :] = slot0
     slots_ref[1:2, :] = slot1
     pick = jnp.where(onehot(slot0) | onehot(slot1), 1.0, 0.0).astype(BF)
+    copies[1].wait()
+    copies[2].wait()
     rows_ref[:, :FEAT] = mm(pick, x_ref[...]).astype(BF)
     rows_ref[:, FEAT:] = mm(pick, d_ref[...]).astype(BF)
 
@@ -83,7 +96,7 @@
     out_ref[...] = total.astype(BF)
 
 
-def state_kernel(q_ref, k_ref, v_ref, g_ref, decay_ref, doc_ref, out_ref, row_ref, col_ref):
+def state_kernel(q_ref, k_ref, v_ref, g_ref, decay_ref, doc_ref, token, out_ref, row_ref, col_ref):
     upto = lax.broadcasted_iota(I32, (TOK, TOK), 0) <= lax.broadcasted_iota(I32, (TOK, TOK), 1)
     cum = lax.dot_general(
         decay_ref[...],
@@ -168,86 +181,63 @@
     return pl.multiple_of((((place[0] + offset) % RINGX) * 2 + core) * FEAT, FEAT)
 
 
-def first_layer(place, offsets, chunks, weights, xs, ds, gate_w, up_w, down_w, sems):
-    groups = ([], [], [])
-    n = 0
-    for i, (offset, sibling) in enumerate(offsets):
+ORDER = ((0, 0), (0, 1), (-1, 0), (1, 0), (-1, 1), (1, 1), (2, 0), (2, 1))
+EARLY = 6
+OUT_ORDER = (2, 1, -1, 0)
+
+
+def weights_kernel(place, wg, wu, wd, token, cat, down, sems):
+    copies = []
+    for i, (offset, sibling) in enumerate(ORDER):
         block = feature_block(place, offset, sibling)
         side = pl.ds(i * FEAT, FEAT)
-        x_src, d_src = chunks[i]
-        moves = (
-            (0, x_src, xs.at[:, side]),
-            (0, weights[0].at[0, pl.ds(block, FEAT), :], gate_w.at[side, :]),
-            (1, weights[1].at[0, pl.ds(block, FEAT), :], up_w.at[side, :]),
-            (2, d_src, ds.at[:, side]),
-            (2, weights[2].at[0, :, pl.ds(block, FEAT)], down_w.at[:, side]),
-        )
-        for group, src, dst in moves:
-            groups[group].append(pltpu.make_async_copy(src, dst, sems.at[n]))
-            n += 1
-    for group in groups:
-        for copy in group:
-            copy.start()
-    return groups
-
-
-A_OFFSETS = ((0, False), (0, True), (-1, False), (1, False), (-1, True), (1, True))
-
-
-def expert_a_kernel(place, a0, a1, a2, a3, a4, a5, wg, wu, wd, gate_ref, up_ref, hid_ref, xs, ds, gate_w, up_w, down_w, sems):
-    chunks = [(a.at[:, pl.ds(0, FEAT)], a.at[:, pl.ds(FEAT, FEAT)]) for a in (a0, a1, a2, a3, a4, a5)]
-    groups = first_layer(place, A_OFFSETS, chunks, (wg, wu, wd), xs, ds, gate_w, up_w, down_w, sems)
-    for copy in groups[0]:
-        copy.wait()
-    gate_ref[...] = mm(xs[...], gate_w[...])
-    for copy in groups[1]:
-        copy.wait()
-    up_ref[...] = mm(xs[...], up_w[...])
-    for copy in groups[2]:
-        copy.wait()
-    hid_ref[...] = mm(ds[...], down_w[...], NT)
-
-
-def out_weights(place, sibling, wg, wu, cat, sems, at):
-    copies = []
-    for i, offset in enumerate(OUT_OFFSETS):
-        block = feature_block(place, offset, sibling)
-        side = pl.ds(i * FEAT, FEAT)
-        copies.append(pltpu.make_async_copy(wg.at[0, pl.ds(block, FEAT), :], cat.at[side, pl.ds(0, HID)], sems.at[at + 2 * i]))
-        copies.append(pltpu.make_async_copy(wu.at[0, pl.ds(block, FEAT), :], cat.at[side, pl.ds(HID, HID)], sems.at[at + 2 * i + 1]))
+        for j, (src, dst) in enumerate(
+            (
+                (wg.at[0, pl.ds(block, FEAT), :], cat.at[side, pl.ds(0, HID)]),
+                (wu.at[0, pl.ds(block, FEAT), :], cat.at[side, pl.ds(HID, HID)]),
+                (wd.at[0, :, pl.ds(block, FEAT)], down.at[:, side]),
+            )
+        ):
+            copies.append(pltpu.make_async_copy(src, dst, sems.at[3 * i + j]))
     for copy in copies:
         copy.start()
-    return copies
-
-
-B_OFFSETS = ((2, False), (2, True))
-OUT_OFFSETS = (2, 1, -1, 0)
-
-
-def expert_b_kernel(place, gate_ref, up_ref, hid_ref, x0, d0, x1, d1, wg, wu, wd, mid_ref, out_ref, xs, ds, gate_w, up_w, down_w, cat, sems):
-    chunks = [(x0, d0), (x1, d1)]
-    groups = first_layer(place, B_OFFSETS, chunks, (wg, wu, wd), xs, ds, gate_w, up_w, down_w, sems)
-    late = out_weights(place, True, wg, wu, cat, sems, 10)
-    for group in groups:
-        for copy in group:
-            copy.wait()
-    gate = gate_ref[...] + mm(xs[...], gate_w[...])
-    up = up_ref[...] + mm(xs[...], up_w[...])
-    hid = hid_ref[...] + mm(ds[...], down_w[...], NT)
+    for copy in copies:
+        copy.wait()
+
+
+def expert_x_kernel(a0, a1, a2, a3, a4, a5, cat, token, out_ref, xs):
+    for i, a in enumerate((a0, a1, a2, a3, a4, a5)):
+        xs[:, i * FEAT : (i + 1) * FEAT] = a[:, :FEAT]
+    out_ref[...] = mm(xs[...], cat[: EARLY * FEAT, :])
+
+
+def expert_d_kernel(a0, a1, a2, a3, a4, a5, down, out_ref, ds):
+    for i, a in enumerate((a0, a1, a2, a3, a4, a5)):
+        ds[:, i * FEAT : (i + 1) * FEAT] = a[:, FEAT:]
+    out_ref[...] = mm(ds[...], down[:, : EARLY * FEAT], NT)
+
+
+def expert_mid_kernel(gu_ref, hid_ref, x0, d0, x1, d1, cat, down, mid_ref, o0, o1, o2, o3):
+    late = slice(EARLY * FEAT, None)
+    xs = jnp.concatenate([x0[...], x1[...]], axis=1)
+    ds = jnp.concatenate([d0[...], d1[...]], axis=1)
+    pre = gu_ref[...] + mm(xs, cat[late, :])
+    hid = hid_ref[...] + mm(ds, down[:, late], NT)
+    gate, up = pre[:, :HID], pre[:, HID:]
     s = 1.0 / (1.0 + jnp.exp(-gate))
     mid_ref[:, :HID] = (hid * up * s * (1.0 + gate * (1.0 - s))).astype(BF)
     mid_ref[:, HID:] = (hid * gate * s).astype(BF)
-    for copy in late:
-        copy.wait()
-    for i in range(RINGX):
-        out_ref[i] = mm(mid_ref[...], cat[i * FEAT : (i + 1) * FEAT, :], NT).astype(BF)
-
-
-def expert_c_kernel(place, mid_ref, wg, wu, out_ref, cat, sems):
-    for copy in out_weights(place, False, wg, wu, cat, sems, 0):
-        copy.wait()
-    for i in range(RINGX):
-        out_ref[i] = mm(mid_ref[...], cat[i * FEAT : (i + 1) * FEAT, :], NT)
+    out_blocks(mid_ref, cat, 1, (o0, o1, o2, o3))
+
+
+def out_blocks(mid_ref, cat, sibling, outs):
+    for offset, out in zip(OUT_ORDER, outs):
+        at = ORDER.index((offset, sibling)) * FEAT
+        out[...] = mm(mid_ref[...], cat[at : at + FEAT, :], NT).astype(out.dtype)
+
+
+def expert_out_kernel(mid_ref, cat, o0, o1, o2, o3):
+    out_blocks(mid_ref, cat, 0, (o0, o1, o2, o3))
 
 
 def local(
@@ -266,9 +256,11 @@
     rows, slots = call(
         pack_kernel,
         (S((ROWS, 2 * FEAT), BF), S((2, TOK), I32)),
-        [vmem()] * 3,
+        [hbm()] * 3,
+        [pltpu.VMEM((2, TOK), I32)] + [pltpu.VMEM((TOK, FEAT), BF)] * 2 + [pltpu.SemaphoreType.DMA((3,))],
         flops=2 * ROWS * TOK * 2 * FEAT,
         size=2 * MIB,
+        limit=6,
     )(expert_ids.T, moe_input, moe_cotangent)
     own = lax.all_to_all(rows.reshape(CTX, CAP, 2 * FEAT), "ctx", 0, 0, tiled=True).reshape(ROWS, 2 * FEAT)
     from_left, from_right = ring(own, RIGHT), ring(own, LEFT)
@@ -276,76 +268,82 @@
     own_s, left_s, right_s = swap(own), swap(from_left), swap(from_right)
     x_opp_s, d_opp_s = swap(x_opp), swap(d_opp)
 
+    cat, down = call(
+        weights_kernel,
+        (S((RINGX * 2 * FEAT, 2 * HID), BF), S((HID, RINGX * 2 * FEAT), BF)),
+        [smem] + [hbm()] * 3 + [anywhere()],
+        [pltpu.SemaphoreType.DMA((3 * len(ORDER),))],
+        size=24 * MIB,
+        limit=14,
+    )(place, w_gate, w_up, w_down, own)
+
     message, lines, columns = call(
         state_kernel,
         (S((CTX, HD + MARKS, HD), BF), S((2 * HEADS, TOK), F32), S((TOK, 4 * HEADS), F32)),
-        [vmem()] * 6,
+        [vmem()] * 6 + [anywhere()],
         flops=4 * HEADS * TOK * HD * HD,
         size=3 * MIB,
-    )(queries, keys, values, out_grad, log_decay, doc_ids.reshape(1, TOK))
+        limit=8,
+    )(queries, keys, values, out_grad, log_decay, doc_ids.reshape(1, TOK), own)
     message = lax.all_to_all(message, "ctx", 0, 0, tiled=True)
-    carried = call(scan_kernel, S((CTX, HD, HD), BF), [vmem()], flops=MIB, size=MIB)(message)
-    carried = lax.all_to_all(carried, "ctx", 0, 0, tiled=True)
+    scanned = call(scan_kernel, S((CTX, HD, HD), BF), [vmem()], flops=MIB, size=MIB, limit=4)(message)
+    carried = lax.all_to_all(scanned, "ctx", 0, 0, tiled=True)
     grads = call(
         attention_kernel,
         (S((TOK, HEADS * HD), BF),) * 3,
         [vmem()] * 7,
         flops=16 * HEADS * TOK * TOK * HD,
         size=4 * MIB,
+        limit=12,
     )(queries, keys, values, out_grad, lines, columns, carried)
 
-    square = S((ROWS, HID), F32)
-    n = len(A_OFFSETS)
-    gate, up, hid = call(
-        expert_a_kernel,
-        (square,) * 3,
-        [smem] + [anywhere()] * 9,
-        [
-            pltpu.VMEM((ROWS, n * FEAT), BF),
-            pltpu.VMEM((ROWS, n * FEAT), BF),
-            pltpu.VMEM((n * FEAT, HID), BF),
-            pltpu.VMEM((n * FEAT, HID), BF),
-            pltpu.VMEM((HID, n * FEAT), BF),
-            pltpu.SemaphoreType.DMA((5 * n,)),
-        ],
-        flops=6 * ROWS * HID * n * FEAT,
+    n = EARLY * FEAT
+    early = (own, own_s, from_left, from_right, left_s, right_s)
+    pre = call(
+        expert_x_kernel,
+        S((ROWS, 2 * HID), F32),
+        [vmem()] * 7 + [anywhere()],
+        [pltpu.VMEM((ROWS, n), BF)],
+        flops=4 * ROWS * HID * n,
         size=18 * MIB,
-    )(place, own, own_s, from_left, from_right, left_s, right_s, w_gate, w_up, w_down)
-    n = len(B_OFFSETS)
-    mid, away = call(
-        expert_b_kernel,
-        (S((ROWS, 2 * HID), BF), S((RINGX, ROWS, FEAT), BF)),
-        [smem] + [vmem()] * 3 + [anywhere()] * 7,
-        [
-            pltpu.VMEM((ROWS, n * FEAT), BF),
-            pltpu.VMEM((ROWS, n * FEAT), BF),
-            pltpu.VMEM((n * FEAT, HID), BF),
-            pltpu.VMEM((n * FEAT, HID), BF),
-            pltpu.VMEM((HID, n * FEAT), BF),
-            pltpu.VMEM((RINGX * FEAT, 2 * HID), BF),
-            pltpu.SemaphoreType.DMA((5 * n + 8,)),
-        ],
+        limit=26,
+    )(*early, cat, scanned)
+    hid = call(
+        expert_d_kernel,
+        S((ROWS, HID), F32),
+        [vmem()] * 7,
+        [pltpu.VMEM((ROWS, n), BF)],
+        flops=2 * ROWS * HID * n,
+        size=14 * MIB,
+        limit=20,
+    )(*early, down)
+    block = S((ROWS, FEAT), BF)
+    mid, *away = call(
+        expert_mid_kernel,
+        (S((ROWS, 2 * HID), BF),) + (block,) * RINGX,
+        [vmem()] * 8,
         flops=10 * ROWS * HID * RINGX * FEAT,
         size=14 * MIB,
-        limit=48,
-    )(place, gate, up, hid, x_opp, d_opp, x_opp_s, d_opp_s, w_gate, w_up, w_down)
-    away = swap(away)
+        limit=32,
+    )(pre, hid, x_opp, d_opp, x_opp_s, d_opp_s, cat, down)
+    away = [swap(a) for a in away]
     mine = call(
-        expert_c_kernel,
-        S((RINGX, ROWS, FEAT), F32),
-        [smem, vmem()] + [anywhere()] * 2,
-        [pltpu.VMEM((RINGX * FEAT, 2 * HID), BF), pltpu.SemaphoreType.DMA((8,))],
+        expert_out_kernel,
+        (S((ROWS, FEAT), F32),) * RINGX,
+        [vmem()] * 2,
         flops=4 * ROWS * HID * RINGX * FEAT,
         size=8 * MIB,
-    )(place, mid, w_gate, w_up)
-
-    chip = mine + away.astype(F32)
+        limit=18,
+    )(mid, cat)
+
     cut = ROWS // 2
-    via_right = ring(chip[0, :cut].astype(BF), RIGHT).astype(F32)
-    via_left = ring(chip[0, cut:].astype(BF), LEFT).astype(F32)
-    to_right = jnp.concatenate([chip[1, :cut] + via_right, chip[1, cut:]], axis=0).astype(BF)
-    to_left = jnp.concatenate([chip[2, :cut], chip[2, cut:] + via_left], axis=0).astype(BF)
-    summed = chip[3] + ring(to_right, RIGHT).astype(F32) + ring(to_left, LEFT).astype(F32)
+    opp, right, left, here = [(m, a.astype(F32)) for m, a in zip(mine, away)]
+    via_right = ring((opp[0][:cut] + opp[1][:cut]).astype(BF), RIGHT).astype(F32)
+    via_left = ring((opp[0][cut:] + opp[1][cut:]).astype(BF), LEFT).astype(F32)
+    none = jnp.zeros((cut, FEAT), F32)
+    to_right = (right[0] + right[1] + jnp.concatenate([via_right, none], axis=0)).astype(BF)
+    to_left = (left[0] + left[1] + jnp.concatenate([none, via_left], axis=0)).astype(BF)
+    summed = here[0] + here[1] + ring(to_right, RIGHT).astype(F32) + ring(to_left, LEFT).astype(F32)
     back = lax.all_to_all(summed.astype(BF).reshape(CTX, CAP, FEAT), "ctx", 0, 0, tiled=True)
     grad_moe = call(
         combine_kernel,
@@ -353,6 +351,7 @@
         [vmem()] * 3,
         flops=4 * ROWS * TOK * FEAT,
         size=MIB,
+        limit=8,
     )(back.reshape(ROWS, FEAT), slots, router_weights.T)
     return (*grads, grad_moe)
 

time: 172 us -> 162 us (0.942)
  waiting for transfers between devices: 51.5 us -> 39.3 us
  local copies, waits for them, and re-layouts: 20.1 us -> 26.9 us
  Pallas kernels: 41 us -> 34.8 us
  starting transfers between devices: 25 us -> 30 us
  other arithmetic: 7.92 us -> 4.41 us
    unnamed x46 -> x48, local copies, waits for them, and re-layouts: 17.5 us -> 25.3 us
    pallas_call x5 -> x7, Pallas kernels: 33 us -> 27 us  [the longest x1 7.67 us: local(): call(expert_mid_kernel, (S((ROWS, 2 * HID), BF),) + (block,) * RINGX, [vm...]
    all_to_all x1, waiting for transfers between devices: 5.79 us -> 0.01 us  [local(): message = lax.all_to_all(message, 'ctx', 0, 0, tiled=True)]
    another operation x2 -> x0, other arithmetic: 3.86 us -> none
    all_to_all x1, starting transfers between devices: 3.57 us -> 7.1 us  [local(): carried = lax.all_to_all(scanned, 'ctx', 0, 0, tiled=True)]
    all_to_all x1, waiting for transfers between devices: 8 us -> 5.27 us  [local(): carried = lax.all_to_all(scanned, 'ctx', 0, 0, tiled=True)]
    ppermute x8, waiting for transfers between devices: 31.7 us -> 28.9 us  [ring(): return lax.ppermute(value, 'x', way)]
    convert_element_type x0 -> x4, other arithmetic: none -> 1.99 us  [the longest x1 0.91 us: local(): (right[0] + right[1] + jnp.concatenate([via_right, none], axis=0)).astype...]
  transfers between devices with their start and end apart: 17 -> 20, of which waited for: 6 -> 6; matrix products, arithmetic and copies ran while one was open for 4% -> 4% of each run, Pallas kernels for 15% -> 15%
where the time goes in v2:
time: 162 us; the launch traced here: 161 us
  waiting for transfers between devices  39.3 us (24%)
  Pallas kernels  34.8 us (21%)
  starting transfers between devices  30 us (19%)
  local copies, waits for them, and re-layouts  26.9 us (17%)
  blocking collectives  24.4 us (15%)
  other arithmetic  4.41 us (3%)
    ppermute x8, waiting for transfers between devices, ring(): return lax.ppermute(value, 'x', way)  28.9 us
    unnamed x48, local copies, waits for them, and re-layouts  25.3 us
    all_to_all x1, blocking collectives, local(): lax.all_to_all(rows.reshape(CTX, CAP, 2 * FEAT), 'ctx', 0, 0, tiled=True)  24.4 us
    ppermute x8, starting transfers between devices, ring(): return lax.ppermute(value, 'x', way)  12.8 us
    pallas_call x1, Pallas kernels, local(): call(expert_mid_kernel, (S((ROWS, 2 * HID), BF),) + (block,) * RINGX, [vm...  7.67 us
    all_to_all x1, starting transfers between devices, local(): carried = lax.all_to_all(scanned, 'ctx', 0, 0, tiled=True)  7.1 us
    pallas_call x1, Pallas kernels, local(): call(expert_x_kernel, S((ROWS, 2 * HID), F32), [vmem()] * 7 + [anywhere()...  5.78 us
    all_to_all x1, waiting for transfers between devices, local(): carried = lax.all_to_all(scanned, 'ctx', 0, 0, tiled=True)  5.27 us
  transfers between devices with their start and end apart: 20, of which 6 were waited for; matrix products, arithmetic and copies ran while one was open for 4% of the time, Pallas kernels for 15%

profile of v2, /device:TPU:0, one launch (start us, length us, event | category | flops | bytes accessed | tf_op | source)
XLA Modules:
  0.0 160.7 jit_solution(18425981409077479281)
XLA Ops:
  0.6 0.9 copy-done.18
  1.6 0.9 copy-done.19
  2.5 0.7 copy-done.22
  3.2 1.3 shard_map.156
  4.5 24.4 %all_to_all.20 = bf16[16,40,768]{2,1,0:T(8,128)(2,1)S(1)} all-to-all(bf16[16,40,768]{2,1,0:T(8,128)(2,1)S(1)} %bitcast.16), channel_id=1, replica_groups=mesh['ctx'=16,'x'=4,'core'=2] {'ctx'}, dimensions={0} | all-to-all | bytes 1966080 | tf_op jit(solution)/shard_map/all_to_all | solution.py:265
  28.9 1.5 collective-permute-start.1
  30.4 1.7 %collective-permute-start.2 = (bf16[640,768]{1,0:T(8,128)(2,1)S(1)}, bf16[640,768]{1,0:T(8,128)(2,1)S(1)}, u32[]{:S(2)}, u32[]{:S(2)}) collective-permute-start(bf16[640,768]{1,0:T(8,128)(2,1)S(1)} %bitcast.10), channel_id=1, source_target_pairs={{0,6},{2,0},{4,2},{6,4},{1,7},{3,1},{5,3},{7,5},{8,14},{10,8},{12,... | collective-permute-start | bytes 2949128 | tf_op jit(solution)/shard_map/ppermute | solution.py:251
  32.1 20.3 %collective-permute-done.1.a2 = bf16[640,768]{1,0:T(8,128)(2,1)S(1)} collective-permute-done((bf16[640,768]{1,0:T(8,128)(2,1)S(1)}, bf16[640,768]{1,0:T(8,128)(2,1)S(1)}, u32[]{:S(2)}, u32[]{:S(2)}) %collective-permute-start.1) | collective-permute-done | bytes 983072 | tf_op jit(solution)/shard_map/ppermute | solution.py:251
  53.0 1.0 copy-done.8
  54.0 1.0 copy-done.10
  55.1 1.0 copy-done.12
  56.1 1.0 copy-done.14
  57.2 0.7 copy-done.16
  57.8 0.7 copy-done.17
  58.5 2.7 %shard_map.157 = (bf16[16,144,128]{2,1,0:T(8,128)(2,1)}, f32[16,256]{1,0:T(8,128)S(1)}, f32[256,32]{1,0:T(8,128)S(1)}) custom-call(bf16[256,1024]{1,0:T(8,128)(2,1)S(1)} %copy-done.8, bf16[256,1024]{1,0:T(8,128)(2,1)S(1)} %copy-done.10, bf16[256,1024]{1,0:T(8,128)(2,1)S(1)} %copy-done.12, bf16[256,1024]{1,0:T(8,128)(2,1)S(1)} %copy-done.14, ...), custom_call_target="tpu_custom_call" | custom-call | flops 134217728 | bytes 3145728 | tf_op jit(solution)/shard_map/pallas_call | solution.py:280
  61.2 0.7 copy-done.20
  61.9 4.2 %all-to-all-start.1 = ((bf16[16,144,128]{2,1,0:T(8,128)(2,1)}), bf16[16,144,128]{2,1,0:T(8,128)(2,1)}, u32[]{:S(2)}, u32[]{:S(2)}) async-start(bf16[16,144,128]{2,1,0:T(8,128)(2,1)} %get-tuple-element.26), calls=%async_computation.1 | async-start | bytes 1179648 | tf_op jit(solution)/shard_map/all_to_all | solution.py:288
  66.2 0.8 slice.24
  67.0 1.0 collective-permute-start.5
  68.0 0.8 slice.25
  68.8 2.3 %collective-permute-start.6 = (bf16[640,384]{1,0:T(8,128)(2,1)}, bf16[640,384]{1,0:T(8,128)(2,1)}, u32[]{:S(2)}, u32[]{:S(2)}) collective-permute-start(bf16[640,384]{1,0:T(8,128)(2,1)} %slice.25), channel_id=1, source_target_pairs={{0,6},{2,0},{4,2},{6,4},{1,7},{3,1},{5,3},{7,5},{8,14},{10,8},{12,... | collective-permute-start | bytes 1474568 | tf_op jit(solution)/shard_map/ppermute | solution.py:251
  71.1 2.1 %copy-done.2 = bf16[1,3072,640]{2,1,0:T(8,128)(2,1)S(1)} copy-done((bf16[1,3072,640]{2,1,0:T(8,128)(2,1)S(1)}, bf16[1,3072,640]{2,1,0:T(8,128)(2,1)}, u32[]{:S(2)}) %copy-start.2) | copy-done | bytes 3932184
  73.2 2.1 %copy-done.3 = bf16[1,3072,640]{2,1,0:T(8,128)(2,1)S(1)} copy-done((bf16[1,3072,640]{2,1,0:T(8,128)(2,1)S(1)}, bf16[1,3072,640]{2,1,0:T(8,128)(2,1)}, u32[]{:S(2)}) %copy-start.3) | copy-done | bytes 3932184
  75.4 2.1 %copy-done.4 = bf16[1,640,3072]{2,1,0:T(8,128)(2,1)S(1)} copy-done((bf16[1,640,3072]{2,1,0:T(8,128)(2,1)S(1)}, bf16[1,640,3072]{2,1,0:T(8,128)(2,1)}, u32[]{:S(2)}) %copy-start.4) | copy-done | bytes 3932184
  77.5 2.2 %shard_map.160 = (bf16[3072,1280]{1,0:T(8,128)(2,1)S(1)}, bf16[640,3072]{1,0:T(8,128)(2,1)S(1)}) custom-call(s32[2]{0:T(128)S(1)} %pad_add_fusion.place, bf16[1,3072,640]{2,1,0:T(8,128)(2,1)S(1)} %copy-done.2, bf16[1,3072,640]{2,1,0:T(8,128)(2,1)S(1)} %copy-done.3, bf16[1,640,3072]{2,1,0:T(8,128)(2,1)S(1)} %copy-done.4, bf16[640,768]{1,0:T(8,128)(2,1)S(1)} %bitcast.13), custom_call_target="tpu_custom_call" | custom-call | bytes 25165824 | tf_op jit(solution)/shard_map/pallas_call | solution.py:271
  79.7 3.1 %copy-done = bf16[3072,1280]{1,0:T(8,128)(2,1)} copy-done((bf16[3072,1280]{1,0:T(8,128)(2,1)}, bf16[3072,1280]{1,0:T(8,128)(2,1)S(1)}, u32[]{:S(2)}) %copy-start) | copy-done | bytes 7864344
  82.7 1.9 %copy-done.5 = bf16[640,3072]{1,0:T(8,128)(2,1)} copy-done((bf16[640,3072]{1,0:T(8,128)(2,1)}, bf16[640,3072]{1,0:T(8,128)(2,1)S(1)}, u32[]{:S(2)}) %copy-start.5) | copy-done | bytes 3932184
  84.6 2.0 %shard_map.158.token = bf16[16,128,128]{2,1,0:T(8,128)(2,1)} custom-call(bf16[16,144,128]{2,1,0:T(8,128)(2,1)} %all-to-all-done.1.in_ref), custom_call_target="tpu_custom_call" | custom-call | flops 1048576 | bytes 1048576 | tf_op jit(solution)/shard_map/pallas_call | solution.py:289
  87.2 2.1 %copy-done.6 = bf16[640,3072]{1,0:T(8,128)(2,1)S(1)} copy-done((bf16[640,3072]{1,0:T(8,128)(2,1)S(1)}, bf16[640,3072]{1,0:T(8,128)(2,1)}, u32[]{:S(2)}) %copy-start.6) | copy-done | bytes 3932184
  89.3 4.4 %shard_map.162.hid_ref = f32[640,640]{1,0:T(8,128)S(1)} custom-call(bf16[640,768]{1,0:T(8,128)(2,1)S(1)} %bitcast.14, bf16[640,768]{1,0:T(8,128)(2,1)} %collective-permute-done.a1, bf16[640,768]{1,0:T(8,128)(2,1)S(1)} %collective-permute-done.1.a2, bf16[640,768]{1,0:T(8,128)(2,1)S(1)} %collective-permute-done.2.a3, ...), custom_call_target="tpu_custom_call" | custom-call | flops 1887436800 | bytes 14680064 | tf_op jit(solution)/shard_map/pallas_call | solution.py:311
  93.8 5.8 %shard_map.161.gu_ref = f32[640,1280]{1,0:T(8,128)S(1)} custom-call(bf16[640,768]{1,0:T(8,128)(2,1)S(1)} %bitcast.15, bf16[640,768]{1,0:T(8,128)(2,1)} %collective-permute-done.a1, bf16[640,768]{1,0:T(8,128)(2,1)S(1)} %collective-permute-done.1.a2, bf16[640,768]{1,0:T(8,128)(2,1)S(1)} %collective-permute-done.2.a3, ...), custom_call_target="tpu_custom_call" | custom-call | flops 3774873600 | bytes 18874368 | tf_op jit(solution)/shard_map/pallas_call | solution.py:302
  99.6 2.1 %copy-done.7 = bf16[640,3072]{1,0:T(8,128)(2,1)S(1)} copy-done((bf16[640,3072]{1,0:T(8,128)(2,1)S(1)}, bf16[640,3072]{1,0:T(8,128)(2,1)}, u32[]{:S(2)}) %copy-start.7) | copy-done | bytes 3932184
  101.7 7.7 %shard_map.163 = (bf16[640,1280]{1,0:T(8,128)(2,1)S(1)}, bf16[640,384]{1,0:T(8,128)(2,1)S(1)}, bf16[640,384]{1,0:T(8,128)(2,1)S(1)}, bf16[640,384]{1,0:T(8,128)(2,1)S(1)}, bf16[640,384]{1,0:T(8,128)(2,1)}) custom-call(f32[640,1280]{1,0:T(8,128)S(1)} %shard_map.161.gu_ref, f32[640,640]{1,0:T(8,128)S(1)} %shard_map.162.hid_ref, ...), custom_call_target="tpu_custom_call" | custom-call | flops 6291456000 | bytes 14680064 | tf_op jit(solution)/shard_map/pallas_call | solution.py:321
  109.9 3.5 %shard_map.164 = (f32[640,384]{1,0:T(8,128)S(1)}, f32[640,384]{1,0:T(8,128)S(1)}, f32[640,384]{1,0:T(8,128)S(1)}, f32[640,384]{1,0:T(8,128)S(1)}) custom-call(bf16[640,1280]{1,0:T(8,128)(2,1)S(1)} %get-tuple-element.32.mid_ref, bf16[3072,1280]{1,0:T(8,128)(2,1)S(1)} %copy-done.1), custom_call_target="tpu_custom_call" | custom-call | flops 2516582400 | bytes 8388608 | tf_op jit(solution)/shard_map/pallas_call | solution.py:330
  114.5 2.9 %collective-permute-start.15 = (bf16[320,384]{1,0:T(8,128)(2,1)S(1)}, bf16[320,384]{1,0:T(8,128)(2,1)S(1)}, u32[]{:S(2)}, u32[]{:S(2)}) collective-permute-start(bf16[320,384]{1,0:T(8,128)(2,1)S(1)} %get-tuple-element.43), channel_id=1, source_target_pairs={{0,6},{2,0},{4,2},{6,4},{1,7},{3,1},{5,3},{7,5},{8,14},{10,8},{12,... | collective-permute-start | bytes 737288 | tf_op jit(solution)/shard_map/ppermute | solution.py:251
  117.4 5.6 %collective-permute-done.12 = bf16[320,384]{1,0:T(8,128)(2,1)S(1)} collective-permute-done((bf16[320,384]{1,0:T(8,128)(2,1)S(1)}, bf16[320,384]{1,0:T(8,128)(2,1)S(1)}, u32[]{:S(2)}, u32[]{:S(2)}) %collective-permute-start.12) | collective-permute-done | bytes 245792 | tf_op jit(solution)/shard_map/ppermute | solution.py:251
  123.0 0.9 add_convert_fusion.2
  124.1 0.9 add_convert_fusion.1
  125.0 3.2 %collective-permute-start.16 = (bf16[640,384]{1,0:T(8,128)(2,1)}, bf16[640,384]{1,0:T(8,128)(2,1)}, u32[]{:S(2)}, u32[]{:S(2)}) collective-permute-start(bf16[640,384]{1,0:T(8,128)(2,1)} %add_convert_fusion.1), channel_id=1, source_target_pairs={{0,6},{2,0},{4,2},{6,4},{1,7},{3,1},{5,3},{7,5},{8,14},{10,8},{12,... | collective-permute-start | bytes 1474568 | tf_op jit(solution)/shard_map/ppermute | solution.py:251
  128.2 7.1 %all-to-all-start.2 = ((bf16[16,128,128]{2,1,0:T(8,128)(2,1)}), bf16[16,128,128]{2,1,0:T(8,128)(2,1)S(1)}, u32[]{:S(2)}, u32[]{:S(2)}) async-start(bf16[16,128,128]{2,1,0:T(8,128)(2,1)} %shard_map.158.token), calls=%async_computation.2 | async-start | bytes 1048576 | tf_op jit(solution)/shard_map/all_to_all | solution.py:290
  135.3 2.9 %collective-permute-done.13 = bf16[640,384]{1,0:T(8,128)(2,1)} collective-permute-done((bf16[640,384]{1,0:T(8,128)(2,1)}, bf16[640,384]{1,0:T(8,128)(2,1)}, u32[]{:S(2)}, u32[]{:S(2)}) %collective-permute-start.13) | collective-permute-done | bytes 491552 | tf_op jit(solution)/shard_map/ppermute | solution.py:251
  138.3 2.3 %add_convert_fusion = bf16[640,384]{1,0:T(8,128)(2,1)} fusion(bf16[640,384]{1,0:T(8,128)(2,1)} %collective-permute-done.16, bf16[640,384]{1,0:T(8,128)(2,1)} %collective-permute-done.13, f32[640,384]{1,0:T(8,128)S(1)} %get-tuple-element.33, bf16[640,384]{1,0:T(8,128)(2,1)} %collective-permute-done.9), kind=kLoop, calls=%fused_computation | loop fusion | flops 1720320 | bytes 2949120 | tf_op jit(solution)/shard_map/convert_element_type | solution.py:347
  140.6 5.3 %all-to-all-done.2.carried_ref = bf16[16,128,128]{2,1,0:T(8,128)(2,1)S(1)} async-done(((bf16[16,128,128]{2,1,0:T(8,128)(2,1)}), bf16[16,128,128]{2,1,0:T(8,128)(2,1)S(1)}, u32[]{:S(2)}, u32[]{:S(2)}) %all-to-all-start.2) | async-done | bytes 524320 | tf_op jit(solution)/shard_map/all_to_all | solution.py:290
  145.9 3.6 %all-to-all-start.3 = ((bf16[16,40,384]{2,1,0:T(8,128)(2,1)}), bf16[16,40,384]{2,1,0:T(8,128)(2,1)S(1)}, u32[]{:S(2)}, u32[]{:S(2)}) async-start(bf16[16,40,384]{2,1,0:T(8,128)(2,1)} %bitcast.21), calls=%async_computation.3 | async-start | bytes 983040 | tf_op jit(solution)/shard_map/all_to_all | solution.py:347
  149.5 1.0 copy-done.15
  150.6 3.8 %shard_map.159 = (bf16[256,1024]{1,0:T(8,128)(2,1)}, bf16[256,1024]{1,0:T(8,128)(2,1)}, bf16[256,1024]{1,0:T(8,128)(2,1)}) custom-call(bf16[256,1024]{1,0:T(8,128)(2,1)S(1)} %copy-done.9, bf16[256,1024]{1,0:T(8,128)(2,1)S(1)} %copy-done.11, bf16[256,1024]{1,0:T(8,128)(2,1)S(1)} %copy-done.13, bf16[256,1024]{1,0:T(8,128)(2,1)S(1)} %copy-done.15, ...), custom_call_target="tpu_custom_call" | custom-call | flops 1073741824 | bytes 4194304 | tf_op jit(solution)/shard_map/pallas_call | solution.py:291
  154.4 5.1 %all-to-all-done.3 = bf16[16,40,384]{2,1,0:T(8,128)(2,1)S(1)} async-done(((bf16[16,40,384]{2,1,0:T(8,128)(2,1)}), bf16[16,40,384]{2,1,0:T(8,128)(2,1)S(1)}, u32[]{:S(2)}, u32[]{:S(2)}) %all-to-all-start.3) | async-done | bytes 491552 | tf_op jit(solution)/shard_map/all_to_all | solution.py:347
  159.4 1.3 shard_map.165
  (59 shorter events, 3.0 us)
Async XLA Ops:
  0.6 0.9 copy-start.18
  1.6 0.9 copy-start.19
  2.5 0.7 copy-start.22
  28.9 23.6 %collective-permute-start.1 = (bf16[640,768]{1,0:T(8,128)(2,1)S(1)}, bf16[640,768]{1,0:T(8,128)(2,1)S(1)}, u32[]{:S(2)}, u32[]{:S(2)}) collective-permute-start(bf16[640,768]{1,0:T(8,128)(2,1)S(1)} %bitcast.9), channel_id=1, source_target_pairs={{0,2},{2,4},{4,6},{6,0},{1,3},{3,5},{5,7},{7,1},{8,10},{10,12},{12... | collective-permute-start | bytes 2949128 | tf_op jit(solution)/shard_map/ppermute | solution.py:251
  30.4 22.1 %collective-permute-start.2 = (bf16[640,768]{1,0:T(8,128)(2,1)S(1)}, bf16[640,768]{1,0:T(8,128)(2,1)S(1)}, u32[]{:S(2)}, u32[]{:S(2)}) collective-permute-start(bf16[640,768]{1,0:T(8,128)(2,1)S(1)} %bitcast.10), channel_id=1, source_target_pairs={{0,6},{2,0},{4,2},{6,4},{1,7},{3,1},{5,3},{7,5},{8,14},{10,8},{12,... | collective-permute-start | bytes 2949128 | tf_op jit(solution)/shard_map/ppermute | solution.py:251
  32.1 55.0 %collective-permute-start = (bf16[640,768]{1,0:T(8,128)(2,1)S(1)}, bf16[640,768]{1,0:T(8,128)(2,1)}, u32[]{:S(2)}, u32[]{:S(2)}) collective-permute-start(bf16[640,768]{1,0:T(8,128)(2,1)S(1)} %bitcast.11), channel_id=1, source_target_pairs={{0,1},{1,0},{2,3},{3,2},{4,5},{5,4},{6,7},{7,6},{8,9},{9,8},{10,11... | collective-permute-start | bytes 2949128 | tf_op jit(solution)/shard_map/ppermute | solution.py:254
  52.5 34.7 %collective-permute-start.3 = (bf16[640,768]{1,0:T(8,128)(2,1)S(1)}, bf16[640,768]{1,0:T(8,128)(2,1)}, u32[]{:S(2)}, u32[]{:S(2)}) collective-permute-start(bf16[640,768]{1,0:T(8,128)(2,1)S(1)} %collective-permute-done.1.a2), channel_id=1, source_target_pairs={{0,1},{1,0},{2,3},{3,2},{4,5},{5,4},{6,7},{7,6},{8,9},{9,8},{10,11... | collective-permute-start | bytes 2949128 | tf_op jit(solution)/shard_map/ppermute | solution.py:254
  52.5 34.7 %collective-permute-start.4 = (bf16[640,768]{1,0:T(8,128)(2,1)S(1)}, bf16[640,768]{1,0:T(8,128)(2,1)}, u32[]{:S(2)}, u32[]{:S(2)}) collective-permute-start(bf16[640,768]{1,0:T(8,128)(2,1)S(1)} %collective-permute-done.2.a3), channel_id=1, source_target_pairs={{0,1},{1,0},{2,3},{3,2},{4,5},{5,4},{6,7},{7,6},{8,9},{9,8},{10,11... | collective-permute-start | bytes 2949128 | tf_op jit(solution)/shard_map/ppermute | solution.py:254
  53.0 1.0 copy-start.8
  54.0 1.0 copy-start.10
  55.1 1.0 copy-start.12
  56.1 1.0 copy-start.14
  57.1 0.7 copy-start.16
  57.8 0.7 copy-start.17
  61.2 0.7 copy-start.20
  61.9 22.7 %all-to-all-start.1 = ((bf16[16,144,128]{2,1,0:T(8,128)(2,1)}), bf16[16,144,128]{2,1,0:T(8,128)(2,1)}, u32[]{:S(2)}, u32[]{:S(2)}) async-start(bf16[16,144,128]{2,1,0:T(8,128)(2,1)} %get-tuple-element.26), calls=%async_computation.1 | async-start | bytes 1179648 | tf_op jit(solution)/shard_map/all_to_all | solution.py:288
  67.0 19.7 %collective-permute-start.5 = (bf16[640,384]{1,0:T(8,128)(2,1)}, bf16[640,384]{1,0:T(8,128)(2,1)S(1)}, u32[]{:S(2)}, u32[]{:S(2)}) collective-permute-start(bf16[640,384]{1,0:T(8,128)(2,1)} %slice.24), channel_id=1, source_target_pairs={{0,2},{2,4},{4,6},{6,0},{1,3},{3,5},{5,7},{7,1},{8,10},{10,12},{12... | collective-permute-start | bytes 1474568 | tf_op jit(solution)/shard_map/ppermute | solution.py:251
  68.8 17.9 %collective-permute-start.6 = (bf16[640,384]{1,0:T(8,128)(2,1)}, bf16[640,384]{1,0:T(8,128)(2,1)}, u32[]{:S(2)}, u32[]{:S(2)}) collective-permute-start(bf16[640,384]{1,0:T(8,128)(2,1)} %slice.25), channel_id=1, source_target_pairs={{0,6},{2,0},{4,2},{6,4},{1,7},{3,1},{5,3},{7,5},{8,14},{10,8},{12,... | collective-permute-start | bytes 1474568 | tf_op jit(solution)/shard_map/ppermute | solution.py:251
  71.1 2.1 %copy-start.2 = (bf16[1,3072,640]{2,1,0:T(8,128)(2,1)S(1)}, bf16[1,3072,640]{2,1,0:T(8,128)(2,1)}, u32[]{:S(2)}) copy-start(bf16[1,3072,640]{2,1,0:T(8,128)(2,1)} %wg.1) | copy-start | bytes 11796484
  73.2 2.1 %copy-start.3 = (bf16[1,3072,640]{2,1,0:T(8,128)(2,1)S(1)}, bf16[1,3072,640]{2,1,0:T(8,128)(2,1)}, u32[]{:S(2)}) copy-start(bf16[1,3072,640]{2,1,0:T(8,128)(2,1)} %wu.1) | copy-start | bytes 11796484
  75.4 2.1 %copy-start.4 = (bf16[1,640,3072]{2,1,0:T(8,128)(2,1)S(1)}, bf16[1,640,3072]{2,1,0:T(8,128)(2,1)}, u32[]{:S(2)}) copy-start(bf16[1,640,3072]{2,1,0:T(8,128)(2,1)} %wd.1) | copy-start | bytes 11796484
  79.7 3.1 %copy-start = (bf16[3072,1280]{1,0:T(8,128)(2,1)}, bf16[3072,1280]{1,0:T(8,128)(2,1)S(1)}, u32[]{:S(2)}) copy-start(bf16[3072,1280]{1,0:T(8,128)(2,1)S(1)} %get-tuple-element.30.cat) | copy-start | bytes 23592964
  82.7 1.9 %copy-start.5 = (bf16[640,3072]{1,0:T(8,128)(2,1)}, bf16[640,3072]{1,0:T(8,128)(2,1)S(1)}, u32[]{:S(2)}) copy-start(bf16[640,3072]{1,0:T(8,128)(2,1)S(1)} %get-tuple-element.31.down) | copy-start | bytes 11796484
  86.7 12.9 %collective-permute-start.7 = (bf16[640,384]{1,0:T(8,128)(2,1)S(1)}, bf16[640,384]{1,0:T(8,128)(2,1)S(1)}, u32[]{:S(2)}, u32[]{:S(2)}) collective-permute-start(bf16[640,384]{1,0:T(8,128)(2,1)S(1)} %collective-permute-done.5.x0), channel_id=1, source_target_pairs={{0,1},{1,0},{2,3},{3,2},{4,5},{5,4},{6,7},{7,6},{8,9},{9,8},{10,11... | collective-permute-start | bytes 1474568 | tf_op jit(solution)/shard_map/ppermute | solution.py:254
  86.7 12.9 %collective-permute-start.8 = (bf16[640,384]{1,0:T(8,128)(2,1)}, bf16[640,384]{1,0:T(8,128)(2,1)S(1)}, u32[]{:S(2)}, u32[]{:S(2)}) collective-permute-start(bf16[640,384]{1,0:T(8,128)(2,1)} %collective-permute-done.6.d0), channel_id=1, source_target_pairs={{0,1},{1,0},{2,3},{3,2},{4,5},{5,4},{6,7},{7,6},{8,9},{9,8},{10,11... | collective-permute-start | bytes 1474568 | tf_op jit(solution)/shard_map/ppermute | solution.py:254
  87.2 2.1 %copy-start.6 = (bf16[640,3072]{1,0:T(8,128)(2,1)S(1)}, bf16[640,3072]{1,0:T(8,128)(2,1)}, u32[]{:S(2)}) copy-start(bf16[640,3072]{1,0:T(8,128)(2,1)} %copy-done.5) | copy-start | bytes 11796484
  89.3 4.4 %copy-start.1 = (bf16[3072,1280]{1,0:T(8,128)(2,1)S(1)}, bf16[3072,1280]{1,0:T(8,128)(2,1)}, u32[]{:S(2)}) copy-start(bf16[3072,1280]{1,0:T(8,128)(2,1)} %copy-done) | copy-start | bytes 23592964
  99.6 2.1 %copy-start.7 = (bf16[640,3072]{1,0:T(8,128)(2,1)S(1)}, bf16[640,3072]{1,0:T(8,128)(2,1)}, u32[]{:S(2)}) copy-start(bf16[640,3072]{1,0:T(8,128)(2,1)} %copy-done.5) | copy-start | bytes 11796484
  109.3 4.1 %collective-permute-start.11 = (bf16[640,384]{1,0:T(8,128)(2,1)S(1)}, bf16[640,384]{1,0:T(8,128)(2,1)S(1)}, u32[]{:S(2)}, u32[]{:S(2)}) collective-permute-start(bf16[640,384]{1,0:T(8,128)(2,1)S(1)} %get-tuple-element.38), channel_id=1, source_target_pairs={{0,1},{1,0},{2,3},{3,2},{4,5},{5,4},{6,7},{7,6},{8,9},{9,8},{10,11... | collective-permute-start | bytes 1474568 | tf_op jit(solution)/shard_map/ppermute | solution.py:254
  109.6 7.8 %collective-permute-start.10 = (bf16[640,384]{1,0:T(8,128)(2,1)S(1)}, bf16[640,384]{1,0:T(8,128)(2,1)S(1)}, u32[]{:S(2)}, u32[]{:S(2)}) collective-permute-start(bf16[640,384]{1,0:T(8,128)(2,1)S(1)} %get-tuple-element.36), channel_id=1, source_target_pairs={{0,1},{1,0},{2,3},{3,2},{4,5},{5,4},{6,7},{7,6},{8,9},{9,8},{10,11... | collective-permute-start | bytes 1474568 | tf_op jit(solution)/shard_map/ppermute | solution.py:254
  113.6 9.4 %collective-permute-start.12 = (bf16[320,384]{1,0:T(8,128)(2,1)S(1)}, bf16[320,384]{1,0:T(8,128)(2,1)S(1)}, u32[]{:S(2)}, u32[]{:S(2)}) collective-permute-start(bf16[320,384]{1,0:T(8,128)(2,1)S(1)} %get-tuple-element.42), channel_id=1, source_target_pairs={{0,2},{2,4},{4,6},{6,0},{1,3},{3,5},{5,7},{7,1},{8,10},{10,12},{12... | collective-permute-start | bytes 737288 | tf_op jit(solution)/shard_map/ppermute | solution.py:251
  113.7 10.3 %collective-permute-start.14 = (bf16[640,384]{1,0:T(8,128)(2,1)S(1)}, bf16[640,384]{1,0:T(8,128)(2,1)S(1)}, u32[]{:S(2)}, u32[]{:S(2)}) collective-permute-start(bf16[640,384]{1,0:T(8,128)(2,1)S(1)} %get-tuple-element.40), channel_id=1, source_target_pairs={{0,1},{1,0},{2,3},{3,2},{4,5},{5,4},{6,7},{7,6},{8,9},{9,8},{10,11... | collective-permute-start | bytes 1474568 | tf_op jit(solution)/shard_map/ppermute | solution.py:254
  114.3 21.0 %collective-permute-start.9 = (bf16[640,384]{1,0:T(8,128)(2,1)}, bf16[640,384]{1,0:T(8,128)(2,1)}, u32[]{:S(2)}, u32[]{:S(2)}) collective-permute-start(bf16[640,384]{1,0:T(8,128)(2,1)} %get-tuple-element.34), channel_id=1, source_target_pairs={{0,1},{1,0},{2,3},{3,2},{4,5},{5,4},{6,7},{7,6},{8,9},{9,8},{10,11... | collective-permute-start | bytes 1474568 | tf_op jit(solution)/shard_map/ppermute | solution.py:254
  114.5 9.5 %collective-permute-start.15 = (bf16[320,384]{1,0:T(8,128)(2,1)S(1)}, bf16[320,384]{1,0:T(8,128)(2,1)S(1)}, u32[]{:S(2)}, u32[]{:S(2)}) collective-permute-start(bf16[320,384]{1,0:T(8,128)(2,1)S(1)} %get-tuple-element.43), channel_id=1, source_target_pairs={{0,6},{2,0},{4,2},{6,4},{1,7},{3,1},{5,3},{7,5},{8,14},{10,8},{12,... | collective-permute-start | bytes 737288 | tf_op jit(solution)/shard_map/ppermute | solution.py:251
  123.9 25.6 %copy-start.9 = (bf16[256,1024]{1,0:T(8,128)(2,1)S(1)}, bf16[256,1024]{1,0:T(8,128)(2,1)}, u32[]{:S(2)}) copy-start(bf16[256,1024]{1,0:T(8,128)(2,1)} %q_ref.3) | copy-start | bytes 1572868
  123.9 25.6 %copy-start.11 = (bf16[256,1024]{1,0:T(8,128)(2,1)S(1)}, bf16[256,1024]{1,0:T(8,128)(2,1)}, u32[]{:S(2)}) copy-start(bf16[256,1024]{1,0:T(8,128)(2,1)} %k_ref.3) | copy-start | bytes 1572868
  123.9 25.6 %copy-start.13 = (bf16[256,1024]{1,0:T(8,128)(2,1)S(1)}, bf16[256,1024]{1,0:T(8,128)(2,1)}, u32[]{:S(2)}) copy-start(bf16[256,1024]{1,0:T(8,128)(2,1)} %v_ref.3) | copy-start | bytes 1572868
  123.9 25.6 %copy-start.21 = (f32[256,32]{1,0:T(8,128)S(1)}, f32[256,32]{1,0:T(8,128)}, u32[]{:S(2)}) copy-start(f32[256,32]{1,0:T(8,128)} %copy-done.20) | copy-start | bytes 98308
  123.9 14.2 %collective-permute-start.13 = (bf16[640,384]{1,0:T(8,128)(2,1)}, bf16[640,384]{1,0:T(8,128)(2,1)}, u32[]{:S(2)}, u32[]{:S(2)}) collective-permute-start(bf16[640,384]{1,0:T(8,128)(2,1)} %add_convert_fusion.2), channel_id=1, source_target_pairs={{0,2},{2,4},{4,6},{6,0},{1,3},{3,5},{5,7},{7,1},{8,10},{10,12},{12... | collective-permute-start | bytes 1474568 | tf_op jit(solution)/shard_map/ppermute | solution.py:251
  125.0 13.4 %collective-permute-start.16 = (bf16[640,384]{1,0:T(8,128)(2,1)}, bf16[640,384]{1,0:T(8,128)(2,1)}, u32[]{:S(2)}, u32[]{:S(2)}) collective-permute-start(bf16[640,384]{1,0:T(8,128)(2,1)} %add_convert_fusion.1), channel_id=1, source_target_pairs={{0,6},{2,0},{4,2},{6,4},{1,7},{3,1},{5,3},{7,5},{8,14},{10,8},{12,... | collective-permute-start | bytes 1474568 | tf_op jit(solution)/shard_map/ppermute | solution.py:251
  128.2 17.8 %all-to-all-start.2 = ((bf16[16,128,128]{2,1,0:T(8,128)(2,1)}), bf16[16,128,128]{2,1,0:T(8,128)(2,1)S(1)}, u32[]{:S(2)}, u32[]{:S(2)}) async-start(bf16[16,128,128]{2,1,0:T(8,128)(2,1)} %shard_map.158.token), calls=%async_computation.2 | async-start | bytes 1048576 | tf_op jit(solution)/shard_map/all_to_all | solution.py:290
  138.3 21.1 %copy-start.23 = (f32[256,2]{0,1:T(2,128)S(1)}, f32[256,2]{0,1:T(2,128)}, u32[]{:S(2)}) copy-start(f32[256,2]{0,1:T(2,128)} %param.21) | copy-start | bytes 6148
  145.9 13.5 %all-to-all-start.3 = ((bf16[16,40,384]{2,1,0:T(8,128)(2,1)}), bf16[16,40,384]{2,1,0:T(8,128)(2,1)S(1)}, u32[]{:S(2)}, u32[]{:S(2)}) async-start(bf16[16,40,384]{2,1,0:T(8,128)(2,1)} %bitcast.21), calls=%async_computation.3 | async-start | bytes 983040 | tf_op jit(solution)/shard_map/all_to_all | solution.py:347
  149.5 1.0 copy-start.15

commit v3 on v2

v3 whole, which is shorter than its diff:
```python
import jax
import jax.numpy as jnp
from jax import lax
from jax.experimental import pallas as pl
from jax.experimental.pallas import tpu as pltpu
from jax.sharding import Mesh, PartitionSpec as P

BF = jnp.bfloat16
F32 = jnp.float32
I32 = jnp.int32
TOK = 256
HEADS = 8
HD = 128
HALF = HD // 2
CTX = 16
CAP = 40
PARTS = (24, 16)
BASES = (0, 24)
FEAT = 384
HID = 640
MARKS = 16
RINGX = 4
RIGHT = [(i, (i + 1) % RINGX) for i in range(RINGX)]
LEFT = [(i, (i - 1) % RINGX) for i in range(RINGX)]
SWAP = [(0, 1), (1, 0)]
MIB = 1 << 20

NT = (((1,), (1,)), ((), ()))
TN = (((0,), (0,)), ((), ()))


def vmem():
    return pl.BlockSpec(memory_space=pltpu.VMEM)


def anywhere():
    return pl.BlockSpec(memory_space=pl.ANY)


def in_hbm(value):
    return pltpu.with_memory_space_constraint(value, pltpu.HBM)


def call(kernel, outs, ins, scratch=(), flops=0, size=0, limit=32):
    return pl.pallas_call(
        kernel,
        out_shape=outs,
        in_specs=ins,
        out_specs=jax.tree.map(lambda o: vmem() if isinstance(o, jax.ShapeDtypeStruct) else anywhere(), outs),
        scratch_shapes=scratch,
        compiler_params=pltpu.CompilerParams(vmem_limit_bytes=limit * MIB),
        cost_estimate=pl.CostEstimate(flops=flops, bytes_accessed=size, transcendentals=0),
    )


def fetch(pairs, sems):
    copies = [pltpu.make_async_copy(src, dst, sems.at[i]) for i, (src, dst) in enumerate(pairs)]
    for copy in copies:
        copy.start()
    return copies


def mm(a, b, dims=(((1,), (0,)), ((), ()))):
    return lax.dot_general(a, b, dims, preferred_element_type=F32)


def onehot(slot, rows):
    return lax.broadcasted_iota(I32, (rows, TOK), 0) == slot


def part_slots(ids):
    expert = lax.broadcasted_iota(I32, (CTX, TOK), 0)
    named = [ids[k : k + 1] == expert for k in range(2)]
    hits = jnp.where(named[0] | named[1], 1.0, 0.0).astype(BF)
    before = lax.broadcasted_iota(I32, (TOK, TOK), 0) < lax.broadcasted_iota(I32, (TOK, TOK), 1)
    rank = mm(hits, jnp.where(before, 1.0, 0.0).astype(BF))
    places = [jnp.sum(jnp.where(m, rank, 0.0), axis=0, keepdims=True).astype(I32) for m in named]
    found = []
    for cap, base in zip(PARTS, BASES):
        at = [place - base for place in places]
        found.append([jnp.where((at[k] >= 0) & (at[k] < cap), ids[k : k + 1] * cap + at[k], -1) for k in range(2)])
    return found


def pack_kernel(ids_hbm, x_hbm, d_hbm, rows0_ref, rows1_ref, ids_ref, x_ref, d_ref, sems):
    copies = fetch(((ids_hbm, ids_ref), (x_hbm, x_ref), (d_hbm, d_ref)), sems)
    copies[0].wait()
    picks = []
    for cap, slots in zip(PARTS, part_slots(ids_ref[...])):
        picks.append(jnp.where(onehot(slots[0], CTX * cap) | onehot(slots[1], CTX * cap), 1.0, 0.0).astype(BF))
    copies[1].wait()
    copies[2].wait()
    for pick, out in zip(picks, (rows0_ref, rows1_ref)):
        out[:, :FEAT] = mm(pick, x_ref[...]).astype(BF)
        out[:, FEAT:] = mm(pick, d_ref[...]).astype(BF)


def combine_kernel(rows0_ref, rows1_ref, ids_hbm, weights_hbm, out_ref, ids_ref, weights_ref, sems):
    for copy in fetch(((ids_hbm, ids_ref), (weights_hbm, weights_ref)), sems):
        copy.wait()
    slots = part_slots(ids_ref[...])
    columns = jnp.concatenate([weights_ref[...], jnp.zeros((6, TOK), F32)], axis=0).T
    total = jnp.zeros((TOK, FEAT), F32)
    for k in range(2):
        for p, rows_ref in enumerate((rows0_ref, rows1_ref)):
            pick = jnp.where(onehot(slots[p][k], CTX * PARTS[p]), 1.0, 0.0).astype(BF)
            total += columns[:, k : k + 1] * mm(pick, rows_ref[...], TN)
    out_ref[...] = total.astype(BF)


def sums_of_decay(decay, doc):
    upto = lax.broadcasted_iota(I32, (TOK, TOK), 0) <= lax.broadcasted_iota(I32, (TOK, TOK), 1)
    cum = lax.dot_general(
        decay,
        jnp.where(upto, 1.0, 0.0),
        (((1,), (0,)), ((), ())),
        precision=lax.Precision.HIGHEST,
        preferred_element_type=F32,
    )
    both = jnp.concatenate([cum, jnp.broadcast_to(doc.astype(F32), (HEADS, TOK))], axis=0)
    return both, both.T


def weights_of(turned):
    cum, doc = turned[:, :HEADS], turned[:, HEADS:]
    first_w = jnp.where(doc == doc[0:1], jnp.exp(cum), 0.0)
    end_w = jnp.where(doc == doc[TOK - 1 :], jnp.exp(cum[TOK - 1 :] - cum), 0.0)
    return cum, doc, first_w, end_w


def state_kernel(*refs):
    sources, out_ref, (decay_ref, doc_ref, q_ref, k_ref, v_ref, g_ref), sems = refs[:6], refs[7], refs[8:14], refs[14]
    copies = fetch(tuple(zip(sources, refs[8:14])), sems)
    copies[0].wait()
    copies[1].wait()
    _, turned = sums_of_decay(decay_ref[...], doc_ref[...])
    cum_c, doc_c, first_w, end_w = weights_of(turned)
    total, first, last = cum_c[TOK - 1 :], doc_c[0:1], doc_c[TOK - 1 :]
    line = lax.broadcasted_iota(I32, (MARKS, HD), 0)
    for copy in copies[2:]:
        copy.wait()
    for h in range(HEADS):
        cols = slice(h * HD, (h + 1) * HD)
        keys_end = (end_w[:, h : h + 1] * k_ref[:, cols].astype(F32)).astype(BF)
        queries_first = (first_w[:, h : h + 1] * q_ref[:, cols].astype(F32)).astype(BF)
        state = mm(keys_end, v_ref[:, cols], TN).astype(BF)
        adjoint = mm(queries_first, g_ref[:, cols], TN).astype(BF)
        sum_h = jnp.broadcast_to(total[:, h : h + 1], (MARKS, HD))
        high = sum_h.astype(BF).astype(F32)
        mid = (sum_h - high).astype(BF).astype(F32)
        low = sum_h - high - mid
        marks = jnp.where(line == 0, high, jnp.where(line == 1, mid, jnp.where(line == 2, low, 0.0)))
        marks = jnp.where(line == 3, first[:, h : h + 1], jnp.where(line == 4, last[:, h : h + 1], marks))
        for part in range(2):
            lines = slice(part * HALF, (part + 1) * HALF)
            out_ref[2 * h + part, 0:HALF, :] = state[lines]
            out_ref[2 * h + part, HALF:HD, :] = adjoint[lines]
            out_ref[2 * h + part, HD:, :] = marks.astype(BF)


def scan_kernel(in_ref, out_ref):
    rates, live = [], []
    prev = jnp.full((1, HD), -1.0, F32)
    for b in range(CTX):
        marks = in_ref[b, HD:, :].astype(F32)
        first, last = marks[3:4], marks[4:5]
        rates.append(jnp.where(prev == last, jnp.exp(marks[0:1] + marks[1:2] + marks[2:3]), 0.0))
        live.append(prev == first)
        prev = last
    total = jnp.zeros((HALF, HD), F32)
    for b in range(CTX):
        out_ref[b, 0:HALF, :] = jnp.where(live[b], total, 0.0).astype(BF)
        total = rates[b] * total + in_ref[b, 0:HALF, :].astype(F32)
    total = jnp.zeros((HALF, HD), F32)
    for b in reversed(range(CTX)):
        out_ref[b, HALF:, :] = total.astype(BF)
        total = rates[b] * total + jnp.where(live[b], in_ref[b, HALF:HD, :].astype(F32), 0.0)


def attention_kernel(*refs):
    sources, carried_ref, (gq_ref, gk_ref, gv_ref), (decay_ref, doc_ref, q_ref, k_ref, v_ref, g_ref), sems = (
        refs[:6], refs[6], refs[7:10], refs[10:16], refs[16]
    )
    copies = fetch(tuple(zip(sources, refs[10:16])), sems)
    copies[0].wait()
    copies[1].wait()
    row, turned = sums_of_decay(decay_ref[...], doc_ref[...])
    cum_c, doc_c, first_w, end_w = weights_of(turned)
    seen = lax.broadcasted_iota(I32, (TOK, TOK), 0) >= lax.broadcasted_iota(I32, (TOK, TOK), 1)
    same = seen & (doc_c[:, 0:1] == row[HEADS : HEADS + 1])
    for copy in copies[2:]:
        copy.wait()
    for h in range(HEADS):
        cols = slice(h * HD, (h + 1) * HD)
        q, k, v, g = q_ref[:, cols], k_ref[:, cols], v_ref[:, cols], g_ref[:, cols]
        spread = jnp.where(same, cum_c[:, h : h + 1] - row[h : h + 1], -1e30)
        decay = jnp.exp(spread)
        weighted_do = (decay * mm(g, v, NT)).astype(BF)
        weighted_qk = (decay * mm(q, k, NT)).astype(BF)
        incoming = jnp.concatenate([carried_ref[2 * h, 0:HALF, :], carried_ref[2 * h + 1, 0:HALF, :]], axis=0)
        adjoint = jnp.concatenate([carried_ref[2 * h, HALF:, :], carried_ref[2 * h + 1, HALF:, :]], axis=0)
        start = first_w[:, h : h + 1]
        end = end_w[:, h : h + 1]
        gq_ref[:, cols] = (mm(weighted_do, k) + start * mm(g, incoming, NT)).astype(BF)
        gk_ref[:, cols] = (mm(weighted_do, q, TN) + end * mm(v, adjoint, NT)).astype(BF)
        gv_ref[:, cols] = (mm(weighted_qk, g, TN) + end * mm(k, adjoint)).astype(BF)


def feature_block(place, offset, sibling):
    core = place[1]
    core = 1 - core if sibling else core
    return pl.multiple_of((((place[0] + offset) % RINGX) * 2 + core) * FEAT, FEAT)


ORDER = ((0, 0), (0, 1), (-1, 0), (-1, 1), (1, 0), (1, 1), (2, 0), (2, 1))
ALL = len(ORDER) * FEAT
OUT_ORDER = (2, -1, 1, 0)


def expert_kernel(place, *refs):
    chunks, (wg, wu, wd) = refs[:8], refs[8:11]
    (away_hbm, mine_hbm), (xs, ds, gate_w, up_w, down_w, gate_mid, up_mid, away, mine, sems, out_sems) = refs[-13:-11], refs[-11:]
    stages = ([], [], [])
    for i, (offset, sibling) in enumerate(ORDER):
        block = feature_block(place, offset, sibling)
        side = pl.ds(i * FEAT, FEAT)
        stages[0].append((wd.at[0, :, pl.ds(block, FEAT)], down_w.at[:, side]))
        stages[0].append((chunks[i].at[:, pl.ds(FEAT, FEAT)], ds.at[:, side]))
        stages[1].append((wg.at[0, pl.ds(block, FEAT), :], gate_w.at[side, :]))
        stages[1].append((chunks[i].at[:, pl.ds(0, FEAT)], xs.at[:, side]))
        stages[2].append((wu.at[0, pl.ds(block, FEAT), :], up_w.at[side, :]))
    copies = fetch(stages[0] + stages[1] + stages[2], sems)

    def ready(n):
        for _ in range(n):
            copies.pop(0).wait()

    ready(len(stages[0]))
    hid = mm(ds[...], down_w[...], NT)
    ready(len(stages[1]))
    gate = mm(xs[...], gate_w[...])
    ready(len(stages[2]))
    up = mm(xs[...], up_w[...])
    s = 1.0 / (1.0 + jnp.exp(-gate))
    gate_mid[...] = (hid * up * s * (1.0 + gate * (1.0 - s))).astype(BF)
    up_mid[...] = (hid * gate * s).astype(BF)
    leaving = []
    for sibling, buffer, out in ((1, away, away_hbm), (0, mine, mine_hbm)):
        for i, offset in enumerate(OUT_ORDER):
            at = slice(ORDER.index((offset, sibling)) * FEAT, (ORDER.index((offset, sibling)) + 1) * FEAT)
            buffer[i] = (mm(gate_mid[...], gate_w[at, :], NT) + mm(up_mid[...], up_w[at, :], NT)).astype(out.dtype)
            leaving.append(pltpu.make_async_copy(buffer.at[i], out.at[i], out_sems.at[len(leaving)]))
            leaving[-1].start()
    for copy in leaving:
        copy.wait()


def add_kernel(mine_hbm, away, *refs):
    outs, (mine, sems) = refs[-6:-2], refs[-2:]
    copies = fetch([(mine_hbm.at[i], mine.at[i]) for i in range(RINGX)], sems)
    for i, out in enumerate(outs):
        copies[i].wait()
        out[...] = (mine[i] + away[i].astype(F32)).astype(out.dtype)


def local(
    queries, keys, values, out_grad, log_decay, doc_ids, moe_input, moe_cotangent, router_weights, expert_ids, w_gate, w_up, w_down
):
    S = jax.ShapeDtypeStruct
    place = jnp.stack([lax.axis_index("x"), lax.axis_index("core")]).astype(I32)
    smem = pl.BlockSpec(memory_space=pltpu.SMEM)

    def ring(value, way):
        return lax.ppermute(value, "x", way)

    def swap(value):
        return lax.ppermute(value, "core", SWAP)

    ids = in_hbm(expert_ids.T)
    rows = call(
        pack_kernel,
        tuple(S((CTX * cap, 2 * FEAT), BF) for cap in PARTS),
        [anywhere()] * 3,
        [pltpu.VMEM((2, TOK), I32)] + [pltpu.VMEM((TOK, FEAT), BF)] * 2 + [pltpu.SemaphoreType.DMA((3,))],
        flops=2 * CTX * CAP * TOK * 2 * FEAT,
        size=2 * MIB,
        limit=6,
    )(ids, in_hbm(moe_input), in_hbm(moe_cotangent))
    own = [
        lax.all_to_all(r.reshape(CTX, cap, 2 * FEAT), "ctx", 0, 0, tiled=True).reshape(CTX * cap, 2 * FEAT)
        for r, cap in zip(rows, PARTS)
    ]
    chunks = []
    for p in range(2):
        from_left, from_right = ring(own[p], RIGHT), ring(own[p], LEFT)
        far = ring(from_left, RIGHT) if p == 0 else ring(from_right, LEFT)
        chunks.append([c for a in (own[p], from_left, from_right, far) for c in (a, swap(a))])
    branch = [in_hbm(a) for a in (log_decay, doc_ids.reshape(1, TOK), queries, keys, values, out_grad)]
    held = [pltpu.VMEM((HEADS, TOK), F32), pltpu.VMEM((1, TOK), I32)] + [pltpu.VMEM((TOK, HEADS * HD), BF)] * 4
    held += [pltpu.SemaphoreType.DMA((6,))]
    message = call(
        state_kernel,
        S((CTX, HD + MARKS, HD), BF),
        [anywhere()] * 7,
        held,
        flops=4 * HEADS * TOK * HD * HD,
        size=3 * MIB,
        limit=8,
    )(*branch, own[0])
    arrived = lax.all_to_all(message, "ctx", 0, 0, tiled=True)
    scanned = call(scan_kernel, S((CTX, HD, HD), BF), [vmem()], flops=MIB, size=MIB, limit=4)(arrived)
    carried = lax.all_to_all(scanned, "ctx", 0, 0, tiled=True)
    grads = call(
        attention_kernel,
        (S((TOK, HEADS * HD), BF),) * 3,
        [anywhere()] * 6 + [vmem()],
        held,
        flops=16 * HEADS * TOK * TOK * HD,
        size=4 * MIB,
        limit=12,
    )(*branch, carried)

    weights = [in_hbm(w) for w in (w_gate, w_up, w_down)]
    back, before, between = [], [message, chunks[1][2], chunks[1][6]], []
    for p, cap in enumerate(PARTS):
        r = CTX * cap
        block, wide = S((r, FEAT), BF), S((r, FEAT), F32)
        away, mine = call(
            expert_kernel,
            (pltpu.HBM((RINGX, r, FEAT), BF), pltpu.HBM((RINGX, r, FEAT), F32)),
            [smem] + [anywhere()] * (11 + len(before)),
            [pltpu.VMEM((r, ALL), BF)] * 2
            + [pltpu.VMEM((ALL, HID), BF)] * 2
            + [pltpu.VMEM((HID, ALL), BF)]
            + [pltpu.VMEM((r, HID), BF)] * 2
            + [pltpu.VMEM((RINGX, r, FEAT), BF), pltpu.VMEM((RINGX, r, FEAT), F32)]
            + [pltpu.SemaphoreType.DMA((5 * len(ORDER),)), pltpu.SemaphoreType.DMA((2 * RINGX,))],
            flops=10 * r * HID * ALL,
            size=20 * MIB,
            limit=40,
        )(place, *[in_hbm(c) for c in chunks[p]], *weights, *before)
        away = swap(away)
        sides = (block, wide) if p == 0 else (wide, block)
        far, left, right, here = call(
            add_kernel,
            (block, *sides, wide),
            [anywhere(), vmem()] + [anywhere()] * len(between),
            [pltpu.VMEM((RINGX, r, FEAT), F32), pltpu.SemaphoreType.DMA((RINGX,))],
            flops=r * FEAT * 4,
            size=4 * MIB,
            limit=10,
        )(in_hbm(mine), away, *between)
        before = [far, scanned]
        if p == 0:
            right = (right + ring(far, RIGHT).astype(F32)).astype(BF)
        else:
            left = (left + ring(far, LEFT).astype(F32)).astype(BF)
        summed = (here + ring(right, RIGHT).astype(F32) + ring(left, LEFT).astype(F32)).astype(BF)
        between = [summed]
        got = lax.all_to_all(summed.reshape(CTX, cap, FEAT), "ctx", 0, 0, tiled=True)
        back.append(got.reshape(r, FEAT))
    grad_moe = call(
        combine_kernel,
        S((TOK, FEAT), BF),
        [vmem()] * 2 + [anywhere()] * 2,
        [pltpu.VMEM((2, TOK), I32), pltpu.VMEM((2, TOK), F32), pltpu.SemaphoreType.DMA((2,))],
        flops=4 * CTX * CAP * TOK * FEAT,
        size=MIB,
        limit=8,
    )(*back, ids, in_hbm(router_weights.T))
    return (*grads, grad_moe)


def solution(mesh):
    fine = Mesh(mesh.devices.reshape(CTX, RINGX, 2), ("ctx", "x", "core"))
    ep = ("x", "core")
    row = P("ctx", ep)
    in_specs = (row, row, row, row, P(ep, "ctx"), P("ctx"), row, row, P("ctx", None), P("ctx", None))
    in_specs += (P("ctx", None, ep), P("ctx", None, ep), P("ctx", ep, None))
    return jax.shard_map(local, mesh=fine, in_specs=in_specs, out_specs=(row,) * 4, check_vma=False)
```

time: 162 us -> 177 us (1.093)
  waiting for transfers between devices: 39.3 us -> 70.9 us
  local copies, waits for them, and re-layouts: 26.9 us -> 0.73 us
  Pallas kernels: 34.8 us -> 47.5 us
  starting transfers between devices: 30 us -> 34.2 us
  blocking collectives: 24.4 us -> 20.2 us
  other arithmetic: 4.41 us -> 1.76 us
    unnamed x48 -> x16, local copies, waits for them, and re-layouts: 25.3 us -> 0.73 us
    all_to_all x2 -> x4, waiting for transfers between devices: 5.07 us -> 22.5 us  [the longest x1 11.8 us: local(): arrived = lax.all_to_all(message, 'ctx', 0, 0, tiled=True)]
    pallas_call x9 -> x8, Pallas kernels: 32.8 us -> 46.5 us  [the longest x2 29.6 us: local(): call(expert_kernel, (pltpu.HBM((RINGX, r, FEAT), BF), pltpu.HBM((RINGX, r...]
    ppermute x8 -> x12, waiting for transfers between devices: 28.9 us -> 41.2 us  [ring(): return lax.ppermute(value, 'x', way)]
    all_to_all x2 -> x4, starting transfers between devices: 7.82 us -> 14.7 us  [the longest x2 7.32 us: local(): lax.all_to_all(summed.reshape(CTX, cap, FEAT), 'ctx', 0, 0, tiled=True)]
    all_to_all x1, blocking collectives: 24.4 us -> 20.2 us  [local(): lax.all_to_all(r.reshape(CTX, cap, 2 * FEAT), 'ctx', 0, 0, tiled=True)]
    all_to_all x1, starting transfers between devices: 7.1 us -> 3.57 us  [local(): carried = lax.all_to_all(scanned, 'ctx', 0, 0, tiled=True)]
    convert_element_type x5 -> x4, other arithmetic: 4.33 us -> 1.69 us  [the longest x2 1.57 us: local(): (here + ring(right, RIGHT).astype(F32) + ring(left, LEFT).astype(F32)).as...]
  transfers between devices with their start and end apart: 20 -> 27, of which waited for: 6 -> 12; matrix products, arithmetic and copies ran while one was open for 4% -> 1% of each run, Pallas kernels for 15% -> 14%
where the time goes in v3:
time: 177 us; the launch traced here: 176 us
  waiting for transfers between devices  70.9 us (40%)
  Pallas kernels  47.5 us (27%)
  starting transfers between devices  34.2 us (19%)
  blocking collectives  20.2 us (11%)
    ppermute x12, waiting for transfers between devices, ring(): return lax.ppermute(value, 'x', way)  41.2 us
    pallas_call x2, Pallas kernels, local(): call(expert_kernel, (pltpu.HBM((RINGX, r, FEAT), BF), pltpu.HBM((RINGX, r...  29.6 us
    all_to_all x1, blocking collectives, local(): lax.all_to_all(r.reshape(CTX, cap, 2 * FEAT), 'ctx', 0, 0, tiled=True)  20.2 us
    ppermute x12, starting transfers between devices, ring(): return lax.ppermute(value, 'x', way)  14.2 us
    all_to_all x1, waiting for transfers between devices, local(): arrived = lax.all_to_all(message, 'ctx', 0, 0, tiled=True)  11.8 us
    all_to_all x2, waiting for transfers between devices, local(): lax.all_to_all(summed.reshape(CTX, cap, FEAT), 'ctx', 0, 0, tiled=True)  10.7 us
    all_to_all x2, starting transfers between devices, local(): lax.all_to_all(summed.reshape(CTX, cap, FEAT), 'ctx', 0, 0, tiled=True)  7.32 us
    all_to_all x1, waiting for transfers between devices, local(): carried = lax.all_to_all(scanned, 'ctx', 0, 0, tiled=True)  7.11 us
  transfers between devices with their start and end apart: 27, of which 12 were waited for; matrix products, arithmetic and copies ran while one was open for 1% of the time, Pallas kernels for 14%

profile of v3, /device:TPU:0, one launch (start us, length us, event | category | flops | bytes accessed | tf_op | source)
XLA Modules:
  0.0 176.4 jit_solution(11356061426109951877)
XLA Ops:
  0.6 2.3 %shard_map.156 = (bf16[384,768]{1,0:T(8,128)(2,1)S(1)}, bf16[256,768]{1,0:T(8,128)(2,1)}) custom-call(s32[2,256]{1,0:T(2,128)} %bitcast.27, bf16[256,384]{1,0:T(8,128)(2,1)} %x_hbm.1, bf16[256,384]{1,0:T(8,128)(2,1)} %d_hbm.1), custom_call_target="tpu_custom_call" | custom-call | flops 251658240 | bytes 2097152 | tf_op jit(solution)/shard_map/pallas_call | solution.py:280
  3.0 20.2 %all_to_all.30 = bf16[16,24,768]{2,1,0:T(8,128)(2,1)S(1)} all-to-all(bf16[16,24,768]{2,1,0:T(8,128)(2,1)S(1)} %bitcast.18), channel_id=1, replica_groups=mesh['ctx'=16,'x'=4,'core'=2] {'ctx'}, dimensions={0} | all-to-all | bytes 1179648 | tf_op jit(solution)/shard_map/all_to_all | solution.py:290
  23.2 1.5 collective-permute-start.1
  24.7 3.6 %all-to-all-start.3 = ((bf16[16,16,768]{2,1,0:T(8,128)(2,1)}), bf16[16,16,768]{2,1,0:T(8,128)(2,1)S(1)}, u32[]{:S(2)}, u32[]{:S(2)}) async-start(bf16[16,16,768]{2,1,0:T(8,128)(2,1)} %bitcast.6), calls=%async_computation.3 | async-start | bytes 786432 | tf_op jit(solution)/shard_map/all_to_all | solution.py:290
  28.2 1.8 %collective-permute-start.3 = (bf16[384,768]{1,0:T(8,128)(2,1)S(1)}, bf16[384,768]{1,0:T(8,128)(2,1)S(1)}, u32[]{:S(2)}, u32[]{:S(2)}) collective-permute-start(bf16[384,768]{1,0:T(8,128)(2,1)S(1)} %bitcast.14), channel_id=1, source_target_pairs={{0,6},{2,0},{4,2},{6,4},{1,7},{3,1},{5,3},{7,5},{8,14},{10,8},{12,... | collective-permute-start | bytes 1769480 | tf_op jit(solution)/shard_map/ppermute | solution.py:274
  30.1 8.1 %collective-permute-done.1.refs_2_ = bf16[384,768]{1,0:T(8,128)(2,1)S(1)} collective-permute-done((bf16[384,768]{1,0:T(8,128)(2,1)S(1)}, bf16[384,768]{1,0:T(8,128)(2,1)S(1)}, u32[]{:S(2)}, u32[]{:S(2)}) %collective-permute-start.1) | collective-permute-done | bytes 589856 | tf_op jit(solution)/shard_map/ppermute | solution.py:274
  38.2 0.3 collective-permute-start.5
  38.5 3.0 %collective-permute-start.8 = (bf16[256,768]{1,0:T(8,128)(2,1)S(1)}, bf16[256,768]{1,0:T(8,128)(2,1)}, u32[]{:S(2)}, u32[]{:S(2)}) collective-permute-start(bf16[256,768]{1,0:T(8,128)(2,1)S(1)} %bitcast.21), channel_id=1, source_target_pairs={{0,6},{2,0},{4,2},{6,4},{1,7},{3,1},{5,3},{7,5},{8,14},{10,8},{12,... | collective-permute-start | bytes 1179656 | tf_op jit(solution)/shard_map/ppermute | solution.py:274
  41.4 8.9 %collective-permute-done.8.refs_4_ = bf16[256,768]{1,0:T(8,128)(2,1)} collective-permute-done((bf16[256,768]{1,0:T(8,128)(2,1)S(1)}, bf16[256,768]{1,0:T(8,128)(2,1)}, u32[]{:S(2)}, u32[]{:S(2)}) %collective-permute-start.8) | collective-permute-done | bytes 393248 | tf_op jit(solution)/shard_map/ppermute | solution.py:274
  50.4 0.5 collective-permute-start.4
  50.9 4.8 %collective-permute-done.5.refs_6_ = bf16[384,768]{1,0:T(8,128)(2,1)S(1)} collective-permute-done((bf16[384,768]{1,0:T(8,128)(2,1)S(1)}, bf16[384,768]{1,0:T(8,128)(2,1)S(1)}, u32[]{:S(2)}, u32[]{:S(2)}) %collective-permute-start.5) | collective-permute-done | bytes 589856 | tf_op jit(solution)/shard_map/ppermute | solution.py:274
  55.7 5.0 %collective-permute-done.7.refs_12_.refs_2_ = bf16[256,768]{1,0:T(8,128)(2,1)S(1)} collective-permute-done((bf16[256,768]{1,0:T(8,128)(2,1)S(1)}, bf16[256,768]{1,0:T(8,128)(2,1)S(1)}, u32[]{:S(2)}, u32[]{:S(2)}) %collective-permute-start.7) | collective-permute-done | bytes 393248 | tf_op jit(solution)/shard_map/ppermute | solution.py:274
  60.7 0.3 collective-permute-start.9
  61.0 0.1 pad_add_fusion.place
  61.1 3.9 %shard_map.157.refs_11_ = bf16[16,144,128]{2,1,0:T(8,128)(2,1)} custom-call(f32[8,256]{1,0:T(8,128)} %refs_0_.3, s32[1,256]{1,0:T(1,128)} %bitcast.25, bf16[256,1024]{1,0:T(8,128)(2,1)} %refs_2_.3, bf16[256,1024]{1,0:T(8,128)(2,1)} %refs_3_.3, bf16[256,1024]{1,0:T(8,128)(2,1)} %refs_4_.3, bf16[256,1024]{1,0:T(8,128)(2,1)} %refs_5_.3, ...), custom_call_target="tpu_custom_call" | custom-call | flops 134217728 | bytes 3145728 | tf_op jit(solution)/shard_map/pallas_call | solution.py:301
  65.1 3.6 %collective-permute-done.9.refs_13_.refs_6_ = bf16[256,768]{1,0:T(8,128)(2,1)S(1)} collective-permute-done((bf16[256,768]{1,0:T(8,128)(2,1)}, bf16[256,768]{1,0:T(8,128)(2,1)S(1)}, u32[]{:S(2)}, u32[]{:S(2)}) %collective-permute-start.9) | collective-permute-done | bytes 393248 | tf_op jit(solution)/shard_map/ppermute | solution.py:274
  68.7 17.1 %shard_map.160 = (bf16[4,384,384]{2,1,0:T(8,128)(2,1)}, f32[4,384,384]{2,1,0:T(8,128)}) custom-call(s32[2]{0:T(128)S(1)} %pad_add_fusion.place, bf16[384,768]{1,0:T(8,128)(2,1)} %bitcast.17, bf16[384,768]{1,0:T(8,128)(2,1)} %collective-permute-done.refs_1_, bf16[384,768]{1,0:T(8,128)(2,1)} %copy-done.4, bf16[384,768]{1,0:T(8,128)(2,1)} %collective-permute-done.2.refs_3_, ...), custom_call_target="tpu_custom_call" | custom-call | flops 7549747200 | bytes 20971520 | tf_op jit(solution)/shard_map/pallas_call | solution.py:328
  85.8 0.1 collective-permute-start.10
  85.9 3.8 %all-to-all-start.1 = ((bf16[16,144,128]{2,1,0:T(8,128)(2,1)}), bf16[16,144,128]{2,1,0:T(8,128)(2,1)S(1)}, u32[]{:S(2)}, u32[]{:S(2)}) async-start(bf16[16,144,128]{2,1,0:T(8,128)(2,1)} %shard_map.157.refs_11_), calls=%async_computation.1 | async-start | bytes 1179648 | tf_op jit(solution)/shard_map/all_to_all | solution.py:310
  89.7 0.4 collective-permute-start.14
  90.1 0.2 collective-permute-start.15
  90.3 0.3 collective-permute-start.16
  90.6 0.2 collective-permute-start.17
  90.8 11.8 %all-to-all-done.1.in_ref = bf16[16,144,128]{2,1,0:T(8,128)(2,1)S(1)} async-done(((bf16[16,144,128]{2,1,0:T(8,128)(2,1)}), bf16[16,144,128]{2,1,0:T(8,128)(2,1)S(1)}, u32[]{:S(2)}, u32[]{:S(2)}) %all-to-all-start.1) | async-done | bytes 589856 | tf_op jit(solution)/shard_map/all_to_all | solution.py:310
  102.6 1.0 shard_map.158.refs_12_
  103.6 1.7 shard_map.161
  105.4 0.7 copy-done.7
  106.1 12.5 %shard_map.162 = (bf16[4,256,384]{2,1,0:T(8,128)(2,1)}, f32[4,256,384]{2,1,0:T(8,128)}) custom-call(s32[2]{0:T(128)S(1)} %pad_add_fusion.place, bf16[256,768]{1,0:T(8,128)(2,1)} %bitcast.24, bf16[256,768]{1,0:T(8,128)(2,1)} %copy-done.7, bf16[256,768]{1,0:T(8,128)(2,1)} %copy-done.1, bf16[256,768]{1,0:T(8,128)(2,1)} %collective-permute-done.15.refs_3_, ...), custom_call_target="tpu_custom_call" | custom-call | flops 5033164800 | bytes 20971520 | tf_op jit(solution)/shard_map/pallas_call | solution.py:328
  118.7 0.1 collective-permute-start.18
  118.8 3.3 %collective-permute-start.13 = (bf16[384,384]{1,0:T(8,128)(2,1)S(1)}, bf16[384,384]{1,0:T(8,128)(2,1)S(1)}, u32[]{:S(2)}, u32[]{:S(2)}) collective-permute-start(bf16[384,384]{1,0:T(8,128)(2,1)S(1)} %get-tuple-element.31), channel_id=1, source_target_pairs={{0,6},{2,0},{4,2},{6,4},{1,7},{3,1},{5,3},{7,5},{8,14},{10,8},{12,... | collective-permute-start | bytes 884744 | tf_op jit(solution)/shard_map/ppermute | solution.py:274
  122.2 0.1 collective-permute-start.12
  122.2 6.7 %collective-permute-done.13 = bf16[384,384]{1,0:T(8,128)(2,1)S(1)} collective-permute-done((bf16[384,384]{1,0:T(8,128)(2,1)S(1)}, bf16[384,384]{1,0:T(8,128)(2,1)S(1)}, u32[]{:S(2)}, u32[]{:S(2)}) %collective-permute-start.13) | collective-permute-done | bytes 294944 | tf_op jit(solution)/shard_map/ppermute | solution.py:274
  129.0 3.6 %collective-permute-done.12 = bf16[384,384]{1,0:T(8,128)(2,1)S(1)} collective-permute-done((bf16[384,384]{1,0:T(8,128)(2,1)S(1)}, bf16[384,384]{1,0:T(8,128)(2,1)S(1)}, u32[]{:S(2)}, u32[]{:S(2)}) %collective-permute-start.12) | collective-permute-done | bytes 294944 | tf_op jit(solution)/shard_map/ppermute | solution.py:274
  132.5 0.8 add_convert_fusion.refs_0_
  133.4 1.4 shard_map.163
  134.8 0.2 collective-permute-start.20
  135.0 3.6 %all-to-all-start.2 = ((bf16[16,128,128]{2,1,0:T(8,128)(2,1)}), bf16[16,128,128]{2,1,0:T(8,128)(2,1)S(1)}, u32[]{:S(2)}, u32[]{:S(2)}) async-start(bf16[16,128,128]{2,1,0:T(8,128)(2,1)} %shard_map.158.refs_12_), calls=%async_computation.2 | async-start | bytes 1048576 | tf_op jit(solution)/shard_map/all_to_all | solution.py:312
  138.6 2.0 %collective-permute-start.19 = (bf16[256,384]{1,0:T(8,128)(2,1)S(1)}, bf16[256,384]{1,0:T(8,128)(2,1)S(1)}, u32[]{:S(2)}, u32[]{:S(2)}) collective-permute-start(bf16[256,384]{1,0:T(8,128)(2,1)S(1)} %get-tuple-element.35), channel_id=1, source_target_pairs={{0,2},{2,4},{4,6},{6,0},{1,3},{3,5},{5,7},{7,1},{8,10},{10,12},{12... | collective-permute-start | bytes 589832 | tf_op jit(solution)/shard_map/ppermute | solution.py:274
  140.5 0.5 collective-permute-done.20
  141.0 1.7 collective-permute-start.21
  142.8 7.1 %all-to-all-done.2.refs_6_ = bf16[16,128,128]{2,1,0:T(8,128)(2,1)S(1)} async-done(((bf16[16,128,128]{2,1,0:T(8,128)(2,1)}), bf16[16,128,128]{2,1,0:T(8,128)(2,1)S(1)}, u32[]{:S(2)}, u32[]{:S(2)}) %all-to-all-start.2) | async-done | bytes 524320 | tf_op jit(solution)/shard_map/all_to_all | solution.py:312
  149.9 3.5 %all-to-all-start.4 = ((bf16[16,24,384]{2,1,0:T(8,128)(2,1)}), bf16[16,24,384]{2,1,0:T(8,128)(2,1)S(1)}, u32[]{:S(2)}, u32[]{:S(2)}) async-start(bf16[16,24,384]{2,1,0:T(8,128)(2,1)} %bitcast.8), calls=%async_computation.4 | async-start | bytes 589824 | tf_op jit(solution)/shard_map/all_to_all | solution.py:360
  153.4 0.7 add_convert_fusion.2
  154.2 8.1 %all-to-all-done.4 = bf16[16,24,384]{2,1,0:T(8,128)(2,1)S(1)} async-done(((bf16[16,24,384]{2,1,0:T(8,128)(2,1)}), bf16[16,24,384]{2,1,0:T(8,128)(2,1)S(1)}, u32[]{:S(2)}, u32[]{:S(2)}) %all-to-all-start.4) | async-done | bytes 294944 | tf_op jit(solution)/shard_map/all_to_all | solution.py:360
  162.3 3.8 %all-to-all-start.5 = ((bf16[16,16,384]{2,1,0:T(8,128)(2,1)}), bf16[16,16,384]{2,1,0:T(8,128)(2,1)S(1)}, u32[]{:S(2)}, u32[]{:S(2)}) async-start(bf16[16,16,384]{2,1,0:T(8,128)(2,1)} %bitcast.10), calls=%async_computation.5 | async-start | bytes 393216 | tf_op jit(solution)/shard_map/all_to_all | solution.py:360
  166.0 5.4 %shard_map.159 = (bf16[256,1024]{1,0:T(8,128)(2,1)}, bf16[256,1024]{1,0:T(8,128)(2,1)}, bf16[256,1024]{1,0:T(8,128)(2,1)}) custom-call(f32[8,256]{1,0:T(8,128)} %refs_0_.3, s32[1,256]{1,0:T(1,128)} %bitcast.26, bf16[256,1024]{1,0:T(8,128)(2,1)} %refs_2_.3, bf16[256,1024]{1,0:T(8,128)(2,1)} %refs_3_.3, bf16[256,1024]{1,0:T(8,128)(2,1)} %refs_4_.3, ...), custom_call_target="tpu_custom_call" | custom-call | flops 1073741824 | bytes 4194304 | tf_op jit(solution)/shard_map/pallas_call | solution.py:313
  171.5 2.6 %all-to-all-done.5 = bf16[16,16,384]{2,1,0:T(8,128)(2,1)S(1)} async-done(((bf16[16,16,384]{2,1,0:T(8,128)(2,1)}), bf16[16,16,384]{2,1,0:T(8,128)(2,1)S(1)}, u32[]{:S(2)}, u32[]{:S(2)}) %all-to-all-start.5) | async-done | bytes 196640 | tf_op jit(solution)/shard_map/all_to_all | solution.py:360
  174.1 2.1 %shard_map.164 = bf16[256,384]{1,0:T(8,128)(2,1)} custom-call(bf16[384,384]{1,0:T(8,128)(2,1)S(1)} %bitcast.19, bf16[256,384]{1,0:T(8,128)(2,1)S(1)} %bitcast.20, s32[2,256]{1,0:T(2,128)} %bitcast.28, f32[2,256]{1,0:T(2,128)} %bitcast.29), custom_call_target="tpu_custom_call" | custom-call | flops 251658240 | bytes 1048576 | tf_op jit(solution)/shard_map/pallas_call | solution.py:362
  (37 shorter events, 0.3 us)
Async XLA Ops:
  23.2 45.5 %copy-start = (bf16[16,24,768]{2,1,0:T(8,128)(2,1)}, bf16[16,24,768]{2,1,0:T(8,128)(2,1)S(1)}, u32[]{:S(2)}) copy-start(bf16[16,24,768]{2,1,0:T(8,128)(2,1)S(1)} %all_to_all.30) | copy-start | bytes 1769476
  23.2 15.0 %collective-permute-start.1 = (bf16[384,768]{1,0:T(8,128)(2,1)S(1)}, bf16[384,768]{1,0:T(8,128)(2,1)S(1)}, u32[]{:S(2)}, u32[]{:S(2)}) collective-permute-start(bf16[384,768]{1,0:T(8,128)(2,1)S(1)} %bitcast.13), channel_id=1, source_target_pairs={{0,2},{2,4},{4,6},{6,0},{1,3},{3,5},{5,7},{7,1},{8,10},{10,12},{12... | collective-permute-start | bytes 1769480 | tf_op jit(solution)/shard_map/ppermute | solution.py:274
  24.7 13.8 %all-to-all-start.3 = ((bf16[16,16,768]{2,1,0:T(8,128)(2,1)}), bf16[16,16,768]{2,1,0:T(8,128)(2,1)S(1)}, u32[]{:S(2)}, u32[]{:S(2)}) async-start(bf16[16,16,768]{2,1,0:T(8,128)(2,1)} %bitcast.6), calls=%async_computation.3 | async-start | bytes 786432 | tf_op jit(solution)/shard_map/all_to_all | solution.py:290
  28.2 22.1 %collective-permute-start.3 = (bf16[384,768]{1,0:T(8,128)(2,1)S(1)}, bf16[384,768]{1,0:T(8,128)(2,1)S(1)}, u32[]{:S(2)}, u32[]{:S(2)}) collective-permute-start(bf16[384,768]{1,0:T(8,128)(2,1)S(1)} %bitcast.14), channel_id=1, source_target_pairs={{0,6},{2,0},{4,2},{6,4},{1,7},{3,1},{5,3},{7,5},{8,14},{10,8},{12,... | collective-permute-start | bytes 1769480 | tf_op jit(solution)/shard_map/ppermute | solution.py:274
  38.2 30.5 %copy-start.4 = (bf16[384,768]{1,0:T(8,128)(2,1)}, bf16[384,768]{1,0:T(8,128)(2,1)S(1)}, u32[]{:S(2)}) copy-start(bf16[384,768]{1,0:T(8,128)(2,1)S(1)} %collective-permute-done.1.refs_2_) | copy-start | bytes 1769476
  38.2 17.5 %collective-permute-start.5 = (bf16[384,768]{1,0:T(8,128)(2,1)S(1)}, bf16[384,768]{1,0:T(8,128)(2,1)S(1)}, u32[]{:S(2)}, u32[]{:S(2)}) collective-permute-start(bf16[384,768]{1,0:T(8,128)(2,1)S(1)} %collective-permute-done.1.refs_2_), channel_id=1, source_target_pairs={{0,2},{2,4},{4,6},{6,0},{1,3},{3,5},{5,7},{7,1},{8,10},{10,12},{12... | collective-permute-start | bytes 1769480 | tf_op jit(solution)/shard_map/ppermute | solution.py:274
  38.5 51.2 %copy-start.3 = (bf16[16,16,768]{2,1,0:T(8,128)(2,1)}, bf16[16,16,768]{2,1,0:T(8,128)(2,1)S(1)}, u32[]{:S(2)}) copy-start(bf16[16,16,768]{2,1,0:T(8,128)(2,1)S(1)} %all-to-all-done.3) | copy-start | bytes 1179652
  38.5 11.9 %collective-permute-start.8 = (bf16[256,768]{1,0:T(8,128)(2,1)S(1)}, bf16[256,768]{1,0:T(8,128)(2,1)}, u32[]{:S(2)}, u32[]{:S(2)}) collective-permute-start(bf16[256,768]{1,0:T(8,128)(2,1)S(1)} %bitcast.21), channel_id=1, source_target_pairs={{0,6},{2,0},{4,2},{6,4},{1,7},{3,1},{5,3},{7,5},{8,14},{10,8},{12,... | collective-permute-start | bytes 1179656 | tf_op jit(solution)/shard_map/ppermute | solution.py:274
  41.4 19.3 %collective-permute-start.7 = (bf16[256,768]{1,0:T(8,128)(2,1)S(1)}, bf16[256,768]{1,0:T(8,128)(2,1)S(1)}, u32[]{:S(2)}, u32[]{:S(2)}) collective-permute-start(bf16[256,768]{1,0:T(8,128)(2,1)S(1)} %bitcast.22), channel_id=1, source_target_pairs={{0,2},{2,4},{4,6},{6,0},{1,3},{3,5},{5,7},{7,1},{8,10},{10,12},{12... | collective-permute-start | bytes 1179656 | tf_op jit(solution)/shard_map/ppermute | solution.py:274
  41.4 23.6 %collective-permute-start = (bf16[384,768]{1,0:T(8,128)(2,1)S(1)}, bf16[384,768]{1,0:T(8,128)(2,1)}, u32[]{:S(2)}, u32[]{:S(2)}) collective-permute-start(bf16[384,768]{1,0:T(8,128)(2,1)S(1)} %bitcast.15), channel_id=1, source_target_pairs={{0,1},{1,0},{2,3},{3,2},{4,5},{5,4},{6,7},{7,6},{8,9},{9,8},{10,11... | collective-permute-start | bytes 1769480 | tf_op jit(solution)/shard_map/ppermute | solution.py:277
  50.3 18.3 %collective-permute-start.2 = (bf16[384,768]{1,0:T(8,128)(2,1)S(1)}, bf16[384,768]{1,0:T(8,128)(2,1)}, u32[]{:S(2)}, u32[]{:S(2)}) collective-permute-start(bf16[384,768]{1,0:T(8,128)(2,1)S(1)} %collective-permute-done.1.refs_2_), channel_id=1, source_target_pairs={{0,1},{1,0},{2,3},{3,2},{4,5},{5,4},{6,7},{7,6},{8,9},{9,8},{10,11... | collective-permute-start | bytes 1769480 | tf_op jit(solution)/shard_map/ppermute | solution.py:277
  50.3 18.4 %copy-start.5 = (bf16[384,768]{1,0:T(8,128)(2,1)}, bf16[384,768]{1,0:T(8,128)(2,1)S(1)}, u32[]{:S(2)}) copy-start(bf16[384,768]{1,0:T(8,128)(2,1)S(1)} %collective-permute-done.3.refs_4_) | copy-start | bytes 1769476
  50.4 18.3 %collective-permute-start.4 = (bf16[384,768]{1,0:T(8,128)(2,1)S(1)}, bf16[384,768]{1,0:T(8,128)(2,1)}, u32[]{:S(2)}, u32[]{:S(2)}) collective-permute-start(bf16[384,768]{1,0:T(8,128)(2,1)S(1)} %collective-permute-done.3.refs_4_), channel_id=1, source_target_pairs={{0,1},{1,0},{2,3},{3,2},{4,5},{5,4},{6,7},{7,6},{8,9},{9,8},{10,11... | collective-permute-start | bytes 1769480 | tf_op jit(solution)/shard_map/ppermute | solution.py:277
  55.7 13.1 %copy-start.6 = (bf16[384,768]{1,0:T(8,128)(2,1)}, bf16[384,768]{1,0:T(8,128)(2,1)S(1)}, u32[]{:S(2)}) copy-start(bf16[384,768]{1,0:T(8,128)(2,1)S(1)} %collective-permute-done.5.refs_6_) | copy-start | bytes 1769476
  55.7 13.0 %collective-permute-start.6 = (bf16[384,768]{1,0:T(8,128)(2,1)S(1)}, bf16[384,768]{1,0:T(8,128)(2,1)}, u32[]{:S(2)}, u32[]{:S(2)}) collective-permute-start(bf16[384,768]{1,0:T(8,128)(2,1)S(1)} %collective-permute-done.5.refs_6_), channel_id=1, source_target_pairs={{0,1},{1,0},{2,3},{3,2},{4,5},{5,4},{6,7},{7,6},{8,9},{9,8},{10,11... | collective-permute-start | bytes 1769480 | tf_op jit(solution)/shard_map/ppermute | solution.py:277
  60.7 29.4 %copy-start.1 = (bf16[256,768]{1,0:T(8,128)(2,1)}, bf16[256,768]{1,0:T(8,128)(2,1)S(1)}, u32[]{:S(2)}) copy-start(bf16[256,768]{1,0:T(8,128)(2,1)S(1)} %collective-permute-done.7.refs_12_.refs_2_) | copy-start | bytes 1179652
  60.7 8.0 %collective-permute-start.9 = (bf16[256,768]{1,0:T(8,128)(2,1)}, bf16[256,768]{1,0:T(8,128)(2,1)S(1)}, u32[]{:S(2)}, u32[]{:S(2)}) collective-permute-start(bf16[256,768]{1,0:T(8,128)(2,1)} %collective-permute-done.8.refs_4_), channel_id=1, source_target_pairs={{0,6},{2,0},{4,2},{6,4},{1,7},{3,1},{5,3},{7,5},{8,14},{10,8},{12,... | collective-permute-start | bytes 1179656 | tf_op jit(solution)/shard_map/ppermute | solution.py:274
  68.7 21.9 %copy-start.2 = (bf16[256,768]{1,0:T(8,128)(2,1)}, bf16[256,768]{1,0:T(8,128)(2,1)S(1)}, u32[]{:S(2)}) copy-start(bf16[256,768]{1,0:T(8,128)(2,1)S(1)} %collective-permute-done.9.refs_13_.refs_6_) | copy-start | bytes 1179652
  85.8 17.8 %collective-permute-start.10 = (bf16[4,384,384]{2,1,0:T(8,128)(2,1)}, bf16[4,384,384]{2,1,0:T(8,128)(2,1)S(1)}, u32[]{:S(2)}, u32[]{:S(2)}) collective-permute-start(bf16[4,384,384]{2,1,0:T(8,128)(2,1)} %get-tuple-element.27), channel_id=1, source_target_pairs={{0,1},{1,0},{2,3},{3,2},{4,5},{5,4},{6,7},{7,6},{8,9},{9,8},{10,11... | collective-permute-start | bytes 3538952 | tf_op jit(solution)/shard_map/ppermute | solution.py:277
  85.9 16.7 %all-to-all-start.1 = ((bf16[16,144,128]{2,1,0:T(8,128)(2,1)}), bf16[16,144,128]{2,1,0:T(8,128)(2,1)S(1)}, u32[]{:S(2)}, u32[]{:S(2)}) async-start(bf16[16,144,128]{2,1,0:T(8,128)(2,1)} %shard_map.157.refs_11_), calls=%async_computation.1 | async-start | bytes 1179648 | tf_op jit(solution)/shard_map/all_to_all | solution.py:310
  89.7 15.7 %collective-permute-start.14 = (bf16[256,768]{1,0:T(8,128)(2,1)S(1)}, bf16[256,768]{1,0:T(8,128)(2,1)S(1)}, u32[]{:S(2)}, u32[]{:S(2)}) collective-permute-start(bf16[256,768]{1,0:T(8,128)(2,1)S(1)} %bitcast.23), channel_id=1, source_target_pairs={{0,1},{1,0},{2,3},{3,2},{4,5},{5,4},{6,7},{7,6},{8,9},{9,8},{10,11... | collective-permute-start | bytes 1179656 | tf_op jit(solution)/shard_map/ppermute | solution.py:277
  90.1 15.3 %collective-permute-start.15 = (bf16[256,768]{1,0:T(8,128)(2,1)S(1)}, bf16[256,768]{1,0:T(8,128)(2,1)}, u32[]{:S(2)}, u32[]{:S(2)}) collective-permute-start(bf16[256,768]{1,0:T(8,128)(2,1)S(1)} %collective-permute-done.7.refs_12_.refs_2_), channel_id=1, source_target_pairs={{0,1},{1,0},{2,3},{3,2},{4,5},{5,4},{6,7},{7,6},{8,9},{9,8},{10,11... | collective-permute-start | bytes 1179656 | tf_op jit(solution)/shard_map/ppermute | solution.py:277
  90.3 15.1 %collective-permute-start.16 = (bf16[256,768]{1,0:T(8,128)(2,1)}, bf16[256,768]{1,0:T(8,128)(2,1)}, u32[]{:S(2)}, u32[]{:S(2)}) collective-permute-start(bf16[256,768]{1,0:T(8,128)(2,1)} %collective-permute-done.8.refs_4_), channel_id=1, source_target_pairs={{0,1},{1,0},{2,3},{3,2},{4,5},{5,4},{6,7},{7,6},{8,9},{9,8},{10,11... | collective-permute-start | bytes 1179656 | tf_op jit(solution)/shard_map/ppermute | solution.py:277
  90.6 14.8 %collective-permute-start.17 = (bf16[256,768]{1,0:T(8,128)(2,1)S(1)}, bf16[256,768]{1,0:T(8,128)(2,1)}, u32[]{:S(2)}, u32[]{:S(2)}) collective-permute-start(bf16[256,768]{1,0:T(8,128)(2,1)S(1)} %collective-permute-done.9.refs_13_.refs_6_), channel_id=1, source_target_pairs={{0,1},{1,0},{2,3},{3,2},{4,5},{5,4},{6,7},{7,6},{8,9},{9,8},{10,11... | collective-permute-start | bytes 1179656 | tf_op jit(solution)/shard_map/ppermute | solution.py:277
  105.3 16.8 %collective-permute-start.11 = (bf16[384,384]{1,0:T(8,128)(2,1)S(1)}, bf16[384,384]{1,0:T(8,128)(2,1)S(1)}, u32[]{:S(2)}, u32[]{:S(2)}) collective-permute-start(bf16[384,384]{1,0:T(8,128)(2,1)S(1)} %get-tuple-element.30.refs_11_), channel_id=1, source_target_pairs={{0,2},{2,4},{4,6},{6,0},{1,3},{3,5},{5,7},{7,1},{8,10},{10,12},{12... | collective-permute-start | bytes 884744 | tf_op jit(solution)/shard_map/ppermute | solution.py:274
  105.4 0.7 copy-start.7
  118.7 14.7 %collective-permute-start.18 = (bf16[4,256,384]{2,1,0:T(8,128)(2,1)}, bf16[4,256,384]{2,1,0:T(8,128)(2,1)S(1)}, u32[]{:S(2)}, u32[]{:S(2)}) collective-permute-start(bf16[4,256,384]{2,1,0:T(8,128)(2,1)} %get-tuple-element.33), channel_id=1, source_target_pairs={{0,1},{1,0},{2,3},{3,2},{4,5},{5,4},{6,7},{7,6},{8,9},{9,8},{10,11... | collective-permute-start | bytes 2359304 | tf_op jit(solution)/shard_map/ppermute | solution.py:277
  118.8 10.2 %collective-permute-start.13 = (bf16[384,384]{1,0:T(8,128)(2,1)S(1)}, bf16[384,384]{1,0:T(8,128)(2,1)S(1)}, u32[]{:S(2)}, u32[]{:S(2)}) collective-permute-start(bf16[384,384]{1,0:T(8,128)(2,1)S(1)} %get-tuple-element.31), channel_id=1, source_target_pairs={{0,6},{2,0},{4,2},{6,4},{1,7},{3,1},{5,3},{7,5},{8,14},{10,8},{12,... | collective-permute-start | bytes 884744 | tf_op jit(solution)/shard_map/ppermute | solution.py:274
  122.2 10.4 %collective-permute-start.12 = (bf16[384,384]{1,0:T(8,128)(2,1)S(1)}, bf16[384,384]{1,0:T(8,128)(2,1)S(1)}, u32[]{:S(2)}, u32[]{:S(2)}) collective-permute-start(bf16[384,384]{1,0:T(8,128)(2,1)S(1)} %add_convert_fusion.1), channel_id=1, source_target_pairs={{0,2},{2,4},{4,6},{6,0},{1,3},{3,5},{5,7},{7,1},{8,10},{10,12},{12... | collective-permute-start | bytes 884744 | tf_op jit(solution)/shard_map/ppermute | solution.py:274
  134.8 6.2 %collective-permute-start.20 = (bf16[256,384]{1,0:T(8,128)(2,1)S(1)}, bf16[256,384]{1,0:T(8,128)(2,1)S(1)}, u32[]{:S(2)}, u32[]{:S(2)}) collective-permute-start(bf16[256,384]{1,0:T(8,128)(2,1)S(1)} %get-tuple-element.37), channel_id=1, source_target_pairs={{0,6},{2,0},{4,2},{6,4},{1,7},{3,1},{5,3},{7,5},{8,14},{10,8},{12,... | collective-permute-start | bytes 589832 | tf_op jit(solution)/shard_map/ppermute | solution.py:274
  135.0 14.9 %all-to-all-start.2 = ((bf16[16,128,128]{2,1,0:T(8,128)(2,1)}), bf16[16,128,128]{2,1,0:T(8,128)(2,1)S(1)}, u32[]{:S(2)}, u32[]{:S(2)}) async-start(bf16[16,128,128]{2,1,0:T(8,128)(2,1)} %shard_map.158.refs_12_), calls=%async_computation.2 | async-start | bytes 1048576 | tf_op jit(solution)/shard_map/all_to_all | solution.py:312
  138.6 14.9 %collective-permute-start.19 = (bf16[256,384]{1,0:T(8,128)(2,1)S(1)}, bf16[256,384]{1,0:T(8,128)(2,1)S(1)}, u32[]{:S(2)}, u32[]{:S(2)}) collective-permute-start(bf16[256,384]{1,0:T(8,128)(2,1)S(1)} %get-tuple-element.35), channel_id=1, source_target_pairs={{0,2},{2,4},{4,6},{6,0},{1,3},{3,5},{5,7},{7,1},{8,10},{10,12},{12... | collective-permute-start | bytes 589832 | tf_op jit(solution)/shard_map/ppermute | solution.py:274
  141.0 12.4 %collective-permute-start.21 = (bf16[256,384]{1,0:T(8,128)(2,1)S(1)}, bf16[256,384]{1,0:T(8,128)(2,1)S(1)}, u32[]{:S(2)}, u32[]{:S(2)}) collective-permute-start(bf16[256,384]{1,0:T(8,128)(2,1)S(1)} %add_convert_fusion.3), channel_id=1, source_target_pairs={{0,6},{2,0},{4,2},{6,4},{1,7},{3,1},{5,3},{7,5},{8,14},{10,8},{12,... | collective-permute-start | bytes 589832 | tf_op jit(solution)/shard_map/ppermute | solution.py:274
  149.9 12.4 %all-to-all-start.4 = ((bf16[16,24,384]{2,1,0:T(8,128)(2,1)}), bf16[16,24,384]{2,1,0:T(8,128)(2,1)S(1)}, u32[]{:S(2)}, u32[]{:S(2)}) async-start(bf16[16,24,384]{2,1,0:T(8,128)(2,1)} %bitcast.8), calls=%async_computation.4 | async-start | bytes 589824 | tf_op jit(solution)/shard_map/all_to_all | solution.py:360
  162.3 11.8 %all-to-all-start.5 = ((bf16[16,16,384]{2,1,0:T(8,128)(2,1)}), bf16[16,16,384]{2,1,0:T(8,128)(2,1)S(1)}, u32[]{:S(2)}, u32[]{:S(2)}) async-start(bf16[16,16,384]{2,1,0:T(8,128)(2,1)} %bitcast.10), calls=%async_computation.5 | async-start | bytes 393216 | tf_op jit(solution)/shard_map/all_to_all | solution.py:360

commit v4 on v3

--- a/solution.py
+++ b/solution.py
@@ -14,8 +14,8 @@
 HALF = HD // 2
 CTX = 16
 CAP = 40
-PARTS = (24, 16)
-BASES = (0, 24)
+ROWS = CTX * CAP
+CUT = ROWS // 2
 FEAT = 384
 HID = 640
 MARKS = 16
@@ -64,47 +64,39 @@
     return lax.dot_general(a, b, dims, preferred_element_type=F32)
 
 
-def onehot(slot, rows):
-    return lax.broadcasted_iota(I32, (rows, TOK), 0) == slot
-
-
-def part_slots(ids):
+def onehot(slot):
+    return lax.broadcasted_iota(I32, (ROWS, TOK), 0) == slot
+
+
+def slots_of(ids):
     expert = lax.broadcasted_iota(I32, (CTX, TOK), 0)
     named = [ids[k : k + 1] == expert for k in range(2)]
     hits = jnp.where(named[0] | named[1], 1.0, 0.0).astype(BF)
     before = lax.broadcasted_iota(I32, (TOK, TOK), 0) < lax.broadcasted_iota(I32, (TOK, TOK), 1)
     rank = mm(hits, jnp.where(before, 1.0, 0.0).astype(BF))
     places = [jnp.sum(jnp.where(m, rank, 0.0), axis=0, keepdims=True).astype(I32) for m in named]
-    found = []
-    for cap, base in zip(PARTS, BASES):
-        at = [place - base for place in places]
-        found.append([jnp.where((at[k] >= 0) & (at[k] < cap), ids[k : k + 1] * cap + at[k], -1) for k in range(2)])
-    return found
-
-
-def pack_kernel(ids_hbm, x_hbm, d_hbm, rows0_ref, rows1_ref, ids_ref, x_ref, d_ref, sems):
+    return [ids[k : k + 1] * CAP + places[k] for k in range(2)]
+
+
+def pack_kernel(ids_hbm, x_hbm, d_hbm, rows_ref, ids_ref, x_ref, d_ref, sems):
     copies = fetch(((ids_hbm, ids_ref), (x_hbm, x_ref), (d_hbm, d_ref)), sems)
     copies[0].wait()
-    picks = []
-    for cap, slots in zip(PARTS, part_slots(ids_ref[...])):
-        picks.append(jnp.where(onehot(slots[0], CTX * cap) | onehot(slots[1], CTX * cap), 1.0, 0.0).astype(BF))
+    slots = slots_of(ids_ref[...])
+    pick = jnp.where(onehot(slots[0]) | onehot(slots[1]), 1.0, 0.0).astype(BF)
     copies[1].wait()
+    rows_ref[:, :FEAT] = mm(pick, x_ref[...]).astype(BF)
     copies[2].wait()
-    for pick, out in zip(picks, (rows0_ref, rows1_ref)):
-        out[:, :FEAT] = mm(pick, x_ref[...]).astype(BF)
-        out[:, FEAT:] = mm(pick, d_ref[...]).astype(BF)
-
-
-def combine_kernel(rows0_ref, rows1_ref, ids_hbm, weights_hbm, out_ref, ids_ref, weights_ref, sems):
+    rows_ref[:, FEAT:] = mm(pick, d_ref[...]).astype(BF)
+
+
+def combine_kernel(rows_ref, ids_hbm, weights_hbm, out_ref, ids_ref, weights_ref, sems):
     for copy in fetch(((ids_hbm, ids_ref), (weights_hbm, weights_ref)), sems):
         copy.wait()
-    slots = part_slots(ids_ref[...])
     columns = jnp.concatenate([weights_ref[...], jnp.zeros((6, TOK), F32)], axis=0).T
     total = jnp.zeros((TOK, FEAT), F32)
-    for k in range(2):
-        for p, rows_ref in enumerate((rows0_ref, rows1_ref)):
-            pick = jnp.where(onehot(slots[p][k], CTX * PARTS[p]), 1.0, 0.0).astype(BF)
-            total += columns[:, k : k + 1] * mm(pick, rows_ref[...], TN)
+    for k, slot in enumerate(slots_of(ids_ref[...])):
+        pick = jnp.where(onehot(slot), 1.0, 0.0).astype(BF)
+        total += columns[:, k : k + 1] * mm(pick, rows_ref[...], TN)
     out_ref[...] = total.astype(BF)
 
 
@@ -214,53 +206,82 @@
 
 ORDER = ((0, 0), (0, 1), (-1, 0), (-1, 1), (1, 0), (1, 1), (2, 0), (2, 1))
 ALL = len(ORDER) * FEAT
+EARLY = 6
 OUT_ORDER = (2, -1, 1, 0)
 
 
-def expert_kernel(place, *refs):
-    chunks, (wg, wu, wd) = refs[:8], refs[8:11]
-    (away_hbm, mine_hbm), (xs, ds, gate_w, up_w, down_w, gate_mid, up_mid, away, mine, sems, out_sems) = refs[-13:-11], refs[-11:]
-    stages = ([], [], [])
+def forward_kernel(from_left, from_right, token, x_ref, d_ref, sems):
+    pairs = ((from_left.at[:, pl.ds(0, FEAT)], x_ref), (from_right.at[:, pl.ds(FEAT, FEAT)], d_ref))
+    for copy in fetch(pairs, sems):
+        copy.wait()
+
+
+def expert_early_kernel(place, *refs):
+    chunks, (wg, wu, wd) = refs[:EARLY], refs[EARLY : EARLY + 3]
+    (pre, hid, cat, down_late), (xs, ds, down_w, sems) = refs[-8:-4], refs[-4:]
+    stages = ([], [], [], [])
     for i, (offset, sibling) in enumerate(ORDER):
         block = feature_block(place, offset, sibling)
         side = pl.ds(i * FEAT, FEAT)
-        stages[0].append((wd.at[0, :, pl.ds(block, FEAT)], down_w.at[:, side]))
-        stages[0].append((chunks[i].at[:, pl.ds(FEAT, FEAT)], ds.at[:, side]))
-        stages[1].append((wg.at[0, pl.ds(block, FEAT), :], gate_w.at[side, :]))
-        stages[1].append((chunks[i].at[:, pl.ds(0, FEAT)], xs.at[:, side]))
-        stages[2].append((wu.at[0, pl.ds(block, FEAT), :], up_w.at[side, :]))
-    copies = fetch(stages[0] + stages[1] + stages[2], sems)
+        late = i >= EARLY
+        if not late:
+            stages[0].append((wd.at[0, :, pl.ds(block, FEAT)], down_w.at[:, side]))
+            stages[0].append((chunks[i].at[:, pl.ds(FEAT, FEAT)], ds.at[:, side]))
+            stages[1].append((chunks[i].at[:, pl.ds(0, FEAT)], xs.at[:, side]))
+        else:
+            stages[3].append((wd.at[0, :, pl.ds(block, FEAT)], down_late.at[:, pl.ds((i - EARLY) * FEAT, FEAT)]))
+        stages[3 if late else 1].append((wg.at[0, pl.ds(block, FEAT), :], cat.at[side, pl.ds(0, HID)]))
+        stages[3 if late else 2].append((wu.at[0, pl.ds(block, FEAT), :], cat.at[side, pl.ds(HID, HID)]))
+    copies = fetch(stages[0] + stages[1] + stages[2] + stages[3], sems)
 
     def ready(n):
         for _ in range(n):
             copies.pop(0).wait()
 
     ready(len(stages[0]))
-    hid = mm(ds[...], down_w[...], NT)
+    hid[...] = mm(ds[...], down_w[...], NT)
     ready(len(stages[1]))
-    gate = mm(xs[...], gate_w[...])
+    pre[:, :HID] = mm(xs[...], cat[: EARLY * FEAT, :HID])
     ready(len(stages[2]))
-    up = mm(xs[...], up_w[...])
+    pre[:, HID:] = mm(xs[...], cat[: EARLY * FEAT, HID:])
+    ready(len(stages[3]))
+
+
+def out_block(mid_ref, cat, offset, sibling):
+    at = ORDER.index((offset, sibling)) * FEAT
+    return mm(mid_ref[...], cat[at : at + FEAT, :], NT)
+
+
+def expert_mid_kernel(pre, hid_ref, x0, d0, x1, d1, cat, down_late, mid_ref, far_ref, rest_ref):
+    late = slice(EARLY * FEAT, None)
+    hid = hid_ref[...] + mm(jnp.concatenate([d0[...], d1[...]], axis=1), down_late[...], NT)
+    both = pre[...] + mm(jnp.concatenate([x0[...], x1[...]], axis=1), cat[late, :])
+    gate, up = both[:, :HID], both[:, HID:]
     s = 1.0 / (1.0 + jnp.exp(-gate))
-    gate_mid[...] = (hid * up * s * (1.0 + gate * (1.0 - s))).astype(BF)
-    up_mid[...] = (hid * gate * s).astype(BF)
-    leaving = []
-    for sibling, buffer, out in ((1, away, away_hbm), (0, mine, mine_hbm)):
-        for i, offset in enumerate(OUT_ORDER):
-            at = slice(ORDER.index((offset, sibling)) * FEAT, (ORDER.index((offset, sibling)) + 1) * FEAT)
-            buffer[i] = (mm(gate_mid[...], gate_w[at, :], NT) + mm(up_mid[...], up_w[at, :], NT)).astype(out.dtype)
-            leaving.append(pltpu.make_async_copy(buffer.at[i], out.at[i], out_sems.at[len(leaving)]))
-            leaving[-1].start()
-    for copy in leaving:
-        copy.wait()
-
-
-def add_kernel(mine_hbm, away, *refs):
-    outs, (mine, sems) = refs[-6:-2], refs[-2:]
-    copies = fetch([(mine_hbm.at[i], mine.at[i]) for i in range(RINGX)], sems)
-    for i, out in enumerate(outs):
-        copies[i].wait()
-        out[...] = (mine[i] + away[i].astype(F32)).astype(out.dtype)
+    mid_ref[:, :HID] = (hid * up * s * (1.0 + gate * (1.0 - s))).astype(BF)
+    mid_ref[:, HID:] = (hid * gate * s).astype(BF)
+    far_ref[...] = out_block(mid_ref, cat, OUT_ORDER[0], 1).astype(BF)
+    for i, offset in enumerate(OUT_ORDER[1:]):
+        rest_ref[i] = out_block(mid_ref, cat, offset, 1).astype(BF)
+
+
+def expert_out_kernel(mid_ref, cat, far_ref, rest_ref):
+    far_ref[...] = out_block(mid_ref, cat, OUT_ORDER[0], 0)
+    for i, offset in enumerate(OUT_ORDER[1:]):
+        rest_ref[i] = out_block(mid_ref, cat, offset, 0)
+
+
+def far_kernel(mine, away, right_ref, left_ref):
+    right_ref[...] = (mine[:CUT] + away[:CUT].astype(F32)).astype(BF)
+    left_ref[...] = (mine[CUT:] + away[CUT:].astype(F32)).astype(BF)
+
+
+def near_kernel(mine, away, via_right, via_left, left_ref, right_ref, here_ref):
+    left_ref[:CUT] = (mine[0, :CUT] + away[0, :CUT].astype(F32)).astype(BF)
+    left_ref[CUT:] = (mine[0, CUT:] + away[0, CUT:].astype(F32) + via_left[...].astype(F32)).astype(BF)
+    right_ref[:CUT] = (mine[1, :CUT] + away[1, :CUT].astype(F32) + via_right[...].astype(F32)).astype(BF)
+    right_ref[CUT:] = (mine[1, CUT:] + away[1, CUT:].astype(F32)).astype(BF)
+    here_ref[...] = mine[2] + away[2].astype(F32)
 
 
 def local(
@@ -269,6 +290,7 @@
     S = jax.ShapeDtypeStruct
     place = jnp.stack([lax.axis_index("x"), lax.axis_index("core")]).astype(I32)
     smem = pl.BlockSpec(memory_space=pltpu.SMEM)
+    block = S((ROWS, FEAT), BF)
 
     def ring(value, way):
         return lax.ppermute(value, "x", way)
@@ -279,22 +301,16 @@
     ids = in_hbm(expert_ids.T)
     rows = call(
         pack_kernel,
-        tuple(S((CTX * cap, 2 * FEAT), BF) for cap in PARTS),
+        S((ROWS, 2 * FEAT), BF),
         [anywhere()] * 3,
         [pltpu.VMEM((2, TOK), I32)] + [pltpu.VMEM((TOK, FEAT), BF)] * 2 + [pltpu.SemaphoreType.DMA((3,))],
-        flops=2 * CTX * CAP * TOK * 2 * FEAT,
+        flops=2 * ROWS * TOK * 2 * FEAT,
         size=2 * MIB,
         limit=6,
     )(ids, in_hbm(moe_input), in_hbm(moe_cotangent))
-    own = [
-        lax.all_to_all(r.reshape(CTX, cap, 2 * FEAT), "ctx", 0, 0, tiled=True).reshape(CTX * cap, 2 * FEAT)
-        for r, cap in zip(rows, PARTS)
-    ]
-    chunks = []
-    for p in range(2):
-        from_left, from_right = ring(own[p], RIGHT), ring(own[p], LEFT)
-        far = ring(from_left, RIGHT) if p == 0 else ring(from_right, LEFT)
-        chunks.append([c for a in (own[p], from_left, from_right, far) for c in (a, swap(a))])
+    own = lax.all_to_all(rows.reshape(CTX, CAP, 2 * FEAT), "ctx", 0, 0, tiled=True).reshape(ROWS, 2 * FEAT)
+    from_left, from_right = ring(own, RIGHT), ring(own, LEFT)
+
     branch = [in_hbm(a) for a in (log_decay, doc_ids.reshape(1, TOK), queries, keys, values, out_grad)]
     held = [pltpu.VMEM((HEADS, TOK), F32), pltpu.VMEM((1, TOK), I32)] + [pltpu.VMEM((TOK, HEADS * HD), BF)] * 4
     held += [pltpu.SemaphoreType.DMA((6,))]
@@ -306,8 +322,20 @@
         flops=4 * HEADS * TOK * HD * HD,
         size=3 * MIB,
         limit=8,
-    )(*branch, own[0])
+    )(*branch, own)
     arrived = lax.all_to_all(message, "ctx", 0, 0, tiled=True)
+
+    x_far, d_far = call(
+        forward_kernel,
+        (block, block),
+        [anywhere()] * 3,
+        [pltpu.SemaphoreType.DMA((2,))],
+        size=2 * MIB,
+        limit=4,
+    )(from_left, from_right, arrived)
+    x_far, d_far = ring(x_far, RIGHT), ring(d_far, LEFT)
+    early = [c for a in (own, from_left, from_right) for c in (a, swap(a))]
+
     scanned = call(scan_kernel, S((CTX, HD, HD), BF), [vmem()], flops=MIB, size=MIB, limit=4)(arrived)
     carried = lax.all_to_all(scanned, "ctx", 0, 0, tiled=True)
     grads = call(
@@ -320,54 +348,52 @@
         limit=12,
     )(*branch, carried)
 
-    weights = [in_hbm(w) for w in (w_gate, w_up, w_down)]
-    back, before, between = [], [message, chunks[1][2], chunks[1][6]], []
-    for p, cap in enumerate(PARTS):
-        r = CTX * cap
-        block, wide = S((r, FEAT), BF), S((r, FEAT), F32)
-        away, mine = call(
-            expert_kernel,
-            (pltpu.HBM((RINGX, r, FEAT), BF), pltpu.HBM((RINGX, r, FEAT), F32)),
-            [smem] + [anywhere()] * (11 + len(before)),
-            [pltpu.VMEM((r, ALL), BF)] * 2
-            + [pltpu.VMEM((ALL, HID), BF)] * 2
-            + [pltpu.VMEM((HID, ALL), BF)]
-            + [pltpu.VMEM((r, HID), BF)] * 2
-            + [pltpu.VMEM((RINGX, r, FEAT), BF), pltpu.VMEM((RINGX, r, FEAT), F32)]
-            + [pltpu.SemaphoreType.DMA((5 * len(ORDER),)), pltpu.SemaphoreType.DMA((2 * RINGX,))],
-            flops=10 * r * HID * ALL,
-            size=20 * MIB,
-            limit=40,
-        )(place, *[in_hbm(c) for c in chunks[p]], *weights, *before)
-        away = swap(away)
-        sides = (block, wide) if p == 0 else (wide, block)
-        far, left, right, here = call(
-            add_kernel,
-            (block, *sides, wide),
-            [anywhere(), vmem()] + [anywhere()] * len(between),
-            [pltpu.VMEM((RINGX, r, FEAT), F32), pltpu.SemaphoreType.DMA((RINGX,))],
-            flops=r * FEAT * 4,
-            size=4 * MIB,
-            limit=10,
-        )(in_hbm(mine), away, *between)
-        before = [far, scanned]
-        if p == 0:
-            right = (right + ring(far, RIGHT).astype(F32)).astype(BF)
-        else:
-            left = (left + ring(far, LEFT).astype(F32)).astype(BF)
-        summed = (here + ring(right, RIGHT).astype(F32) + ring(left, LEFT).astype(F32)).astype(BF)
-        between = [summed]
-        got = lax.all_to_all(summed.reshape(CTX, cap, FEAT), "ctx", 0, 0, tiled=True)
-        back.append(got.reshape(r, FEAT))
+    n = EARLY * FEAT
+    pre, hid, cat, down_late = call(
+        expert_early_kernel,
+        (S((ROWS, 2 * HID), F32), S((ROWS, HID), F32), S((ALL, 2 * HID), BF), S((HID, ALL - n), BF)),
+        [smem] + [anywhere()] * (EARLY + 4),
+        [pltpu.VMEM((ROWS, n), BF)] * 2 + [pltpu.VMEM((HID, n), BF), pltpu.SemaphoreType.DMA((36,))],
+        flops=6 * ROWS * HID * n,
+        size=24 * MIB,
+        limit=28,
+    )(place, *early, *[in_hbm(w) for w in (w_gate, w_up, w_down)], scanned)
+    x_far, d_far, pre = lax.optimization_barrier((x_far, d_far, pre))
+    mid, away_far, away_rest = call(
+        expert_mid_kernel,
+        (S((ROWS, 2 * HID), BF), block, S((RINGX - 1, ROWS, FEAT), BF)),
+        [vmem()] * 8,
+        flops=10 * ROWS * HID * RINGX * FEAT,
+        size=14 * MIB,
+        limit=32,
+    )(pre, hid, x_far, d_far, swap(x_far), swap(d_far), cat, down_late)
+    away_far, away_rest = swap(away_far), swap(away_rest)
+    mine_far, mine_rest = call(
+        expert_out_kernel,
+        (S((ROWS, FEAT), F32), S((RINGX - 1, ROWS, FEAT), F32)),
+        [vmem()] * 2,
+        flops=4 * ROWS * HID * RINGX * FEAT,
+        size=8 * MIB,
+        limit=18,
+    )(mid, cat)
+
+    half = S((CUT, FEAT), BF)
+    to_right, to_left = call(far_kernel, (half, half), [vmem()] * 2, size=2 * MIB, flops=MIB, limit=8)(mine_far, away_far)
+    via_right, via_left = ring(to_right, RIGHT), ring(to_left, LEFT)
+    to_left, to_right, here = call(
+        near_kernel, (block, block, S((ROWS, FEAT), F32)), [vmem()] * 4, size=5 * MIB, flops=MIB, limit=16
+    )(mine_rest, away_rest, via_right, via_left)
+    summed = (here + ring(to_right, RIGHT).astype(F32) + ring(to_left, LEFT).astype(F32)).astype(BF)
+    back = lax.all_to_all(summed.reshape(CTX, CAP, FEAT), "ctx", 0, 0, tiled=True)
     grad_moe = call(
         combine_kernel,
         S((TOK, FEAT), BF),
-        [vmem()] * 2 + [anywhere()] * 2,
+        [vmem()] + [anywhere()] * 2,
         [pltpu.VMEM((2, TOK), I32), pltpu.VMEM((2, TOK), F32), pltpu.SemaphoreType.DMA((2,))],
-        flops=4 * CTX * CAP * TOK * FEAT,
+        flops=4 * ROWS * TOK * FEAT,
         size=MIB,
         limit=8,
-    )(*back, ids, in_hbm(router_weights.T))
+    )(back.reshape(ROWS, FEAT), ids, in_hbm(router_weights.T))
     return (*grads, grad_moe)
 
 

time: 177 us -> 144 us (0.81)
  waiting for transfers between devices: 70.9 us -> 55 us
  Pallas kernels: 47.5 us -> 36.3 us
  starting transfers between devices: 34.2 us -> 25.8 us
  blocking collectives: 20.2 us -> 24.4 us
    pallas_call x6 -> x8, Pallas kernels: 37.2 us -> 26 us  [the longest x1 12.1 us: local(): call(expert_early_kernel, (S((ROWS, 2 * HID), F32), S((ROWS, HID), F32),...]
    ppermute x12 -> x8, waiting for transfers between devices: 41.2 us -> 33.1 us  [ring(): return lax.ppermute(value, 'x', way)]
    all_to_all x3 -> x1, starting transfers between devices: 10.9 us -> 3.79 us  [local(): lax.all_to_all(summed.reshape(CTX, CAP, FEAT), 'ctx', 0, 0, tiled=True)]
    all_to_all x3 -> x1, waiting for transfers between devices: 10.7 us -> 4.3 us  [local(): lax.all_to_all(summed.reshape(CTX, CAP, FEAT), 'ctx', 0, 0, tiled=True)]
    all_to_all x1, blocking collectives: 20.2 us -> 24.4 us  [local(): lax.all_to_all(rows.reshape(CTX, CAP, 2 * FEAT), 'ctx', 0, 0, tiled=True)]
    all_to_all x1, waiting for transfers between devices: 7.11 us -> 2.96 us  [local(): carried = lax.all_to_all(scanned, 'ctx', 0, 0, tiled=True)]
    ppermute x10 -> x7, waiting for transfers between devices: 0.03 us -> 2.07 us  [swap(): return lax.ppermute(value, 'core', SWAP)]
    ppermute x12 -> x8, starting transfers between devices: 14.2 us -> 13.2 us  [ring(): return lax.ppermute(value, 'x', way)]
  transfers between devices with their start and end apart: 27 -> 18, of which waited for: 12 -> 8; matrix products, arithmetic and copies ran while one was open for 1% -> 1% of each run, Pallas kernels for 14% -> 18%
where the time goes in v4:
time: 144 us; the launch traced here: 143 us
  waiting for transfers between devices  55 us (38%)
  Pallas kernels  36.3 us (25%)
  starting transfers between devices  25.8 us (18%)
  blocking collectives  24.4 us (17%)
    ppermute x8, waiting for transfers between devices, ring(): return lax.ppermute(value, 'x', way)  33.1 us
    all_to_all x1, blocking collectives, local(): lax.all_to_all(rows.reshape(CTX, CAP, 2 * FEAT), 'ctx', 0, 0, tiled=True)  24.4 us
    ppermute x8, starting transfers between devices, ring(): return lax.ppermute(value, 'x', way)  13.2 us
    all_to_all x1, waiting for transfers between devices, local(): arrived = lax.all_to_all(message, 'ctx', 0, 0, tiled=True)  12.6 us
    pallas_call x1, Pallas kernels, local(): call(expert_early_kernel, (S((ROWS, 2 * HID), F32), S((ROWS, HID), F32),...  12.1 us
    pallas_call x1, Pallas kernels, local(): call(expert_mid_kernel, (S((ROWS, 2 * HID), BF), block, S((RINGX - 1, ROW...  5.99 us
    pallas_call x1, Pallas kernels, local(): call(attention_kernel, (S((TOK, HEADS * HD), BF),) * 3, [anywhere()] * 6...  5.4 us
    all_to_all x1, waiting for transfers between devices, local(): lax.all_to_all(summed.reshape(CTX, CAP, FEAT), 'ctx', 0, 0, tiled=True)  4.3 us
  transfers between devices with their start and end apart: 18, of which 8 were waited for; matrix products, arithmetic and copies ran while one was open for 1% of the time, Pallas kernels for 18%

profile of v4, /device:TPU:0, one launch (start us, length us, event | category | flops | bytes accessed | tf_op | source)
XLA Modules:
  0.0 143.5 jit_solution(15281579039415474323)
XLA Ops:
  0.6 1.7 %shard_map.156 = bf16[640,768]{1,0:T(8,128)(2,1)S(1)} custom-call(s32[2,256]{1,0:T(2,128)} %bitcast.16, bf16[256,384]{1,0:T(8,128)(2,1)} %x_hbm.1, bf16[256,384]{1,0:T(8,128)(2,1)} %d_hbm.1), custom_call_target="tpu_custom_call" | custom-call | flops 251658240 | bytes 2097152 | tf_op jit(solution)/shard_map/pallas_call | solution.py:302
  2.3 24.4 %all_to_all.20 = bf16[16,40,768]{2,1,0:T(8,128)(2,1)S(1)} all-to-all(bf16[16,40,768]{2,1,0:T(8,128)(2,1)S(1)} %bitcast.9), channel_id=1, replica_groups=mesh['ctx'=16,'x'=4,'core'=2] {'ctx'}, dimensions={0} | all-to-all | bytes 1966080 | tf_op jit(solution)/shard_map/all_to_all | solution.py:311
  26.7 1.5 %collective-permute-start = (bf16[640,768]{1,0:T(8,128)(2,1)S(1)}, bf16[640,768]{1,0:T(8,128)(2,1)S(1)}, u32[]{:S(2)}, u32[]{:S(2)}) collective-permute-start(bf16[640,768]{1,0:T(8,128)(2,1)S(1)} %bitcast.10), channel_id=1, source_target_pairs={{0,2},{2,4},{4,6},{6,0},{1,3},{3,5},{5,7},{7,1},{8,10},{10,12},{12... | collective-permute-start | bytes 2949128 | tf_op jit(solution)/shard_map/ppermute | solution.py:296
  28.2 1.7 %collective-permute-start.1 = (bf16[640,768]{1,0:T(8,128)(2,1)S(1)}, bf16[640,768]{1,0:T(8,128)(2,1)S(1)}, u32[]{:S(2)}, u32[]{:S(2)}) collective-permute-start(bf16[640,768]{1,0:T(8,128)(2,1)S(1)} %bitcast.11), channel_id=1, source_target_pairs={{0,6},{2,0},{4,2},{6,4},{1,7},{3,1},{5,3},{7,5},{8,14},{10,8},{12,... | collective-permute-start | bytes 2949128 | tf_op jit(solution)/shard_map/ppermute | solution.py:296
  30.0 0.0 collective-permute-start.4
  30.0 20.3 %collective-permute-done.from_left.refs_2_ = bf16[640,768]{1,0:T(8,128)(2,1)S(1)} collective-permute-done((bf16[640,768]{1,0:T(8,128)(2,1)S(1)}, bf16[640,768]{1,0:T(8,128)(2,1)S(1)}, u32[]{:S(2)}, u32[]{:S(2)}) %collective-permute-start) | collective-permute-done | bytes 983072 | tf_op jit(solution)/shard_map/ppermute | solution.py:296
  50.3 0.0 collective-permute-start.5
  50.3 0.0 collective-permute-done.1.from_right.refs_4_
  50.3 0.5 collective-permute-start.6
  50.8 3.9 %shard_map.157 = bf16[16,144,128]{2,1,0:T(8,128)(2,1)} custom-call(f32[8,256]{1,0:T(8,128)} %refs_0_.3, s32[1,256]{1,0:T(1,128)} %bitcast.18, bf16[256,1024]{1,0:T(8,128)(2,1)} %refs_2_.3, bf16[256,1024]{1,0:T(8,128)(2,1)} %refs_3_.3, bf16[256,1024]{1,0:T(8,128)(2,1)} %refs_4_.3, bf16[256,1024]{1,0:T(8,128)(2,1)} %refs_5_.3, bf16[640,768]{1,0:T(8,128)(2,1)S(1)} %bitcast.13), custom_call_target="tpu_custom_call" | custom-call | flops 134217728 | bytes 3145728 | tf_op jit(solution)/shard_map/pallas_call | solution.py:317
  54.7 3.6 %all-to-all-start.1 = ((bf16[16,144,128]{2,1,0:T(8,128)(2,1)}), bf16[16,144,128]{2,1,0:T(8,128)(2,1)S(1)}, u32[]{:S(2)}, u32[]{:S(2)}) async-start(bf16[16,144,128]{2,1,0:T(8,128)(2,1)} %shard_map.157), calls=%async_computation.1 | async-start | bytes 1179648 | tf_op jit(solution)/shard_map/all_to_all | solution.py:326
  58.3 0.1 pad_add_fusion.place
  58.4 12.6 %all-to-all-done.1.in_ref.token = bf16[16,144,128]{2,1,0:T(8,128)(2,1)S(1)} async-done(((bf16[16,144,128]{2,1,0:T(8,128)(2,1)}), bf16[16,144,128]{2,1,0:T(8,128)(2,1)S(1)}, u32[]{:S(2)}, u32[]{:S(2)}) %all-to-all-start.1) | async-done | bytes 589856 | tf_op jit(solution)/shard_map/all_to_all | solution.py:326
  71.0 1.0 shard_map.158.refs_9_
  72.0 0.1 shard_map.160
  72.1 1.6 %collective-permute-start.2 = (bf16[640,384]{1,0:T(8,128)(2,1)S(1)}, bf16[640,384]{1,0:T(8,128)(2,1)S(1)}, u32[]{:S(2)}, u32[]{:S(2)}) collective-permute-start(bf16[640,384]{1,0:T(8,128)(2,1)S(1)} %get-tuple-element.29), channel_id=1, source_target_pairs={{0,2},{2,4},{4,6},{6,0},{1,3},{3,5},{5,7},{7,1},{8,10},{10,12},{12... | collective-permute-start | bytes 1474568 | tf_op jit(solution)/shard_map/ppermute | solution.py:296
  73.6 1.8 %collective-permute-start.3 = (bf16[640,384]{1,0:T(8,128)(2,1)S(1)}, bf16[640,384]{1,0:T(8,128)(2,1)S(1)}, u32[]{:S(2)}, u32[]{:S(2)}) collective-permute-start(bf16[640,384]{1,0:T(8,128)(2,1)S(1)} %get-tuple-element.30), channel_id=1, source_target_pairs={{0,6},{2,0},{4,2},{6,4},{1,7},{3,1},{5,3},{7,5},{8,14},{10,8},{12,... | collective-permute-start | bytes 1474568 | tf_op jit(solution)/shard_map/ppermute | solution.py:296
  75.4 0.0 collective-permute-done.4.refs_1_
  75.4 0.0 collective-permute-done.5.refs_3_
  75.4 0.0 collective-permute-done.6.refs_5_
  75.4 12.1 %shard_map.161 = (f32[640,1280]{1,0:T(8,128)S(1)}, f32[640,640]{1,0:T(8,128)S(1)}, bf16[3072,1280]{1,0:T(8,128)(2,1)S(1)}, bf16[640,768]{1,0:T(8,128)(2,1)S(1)}) custom-call(s32[2]{0:T(128)S(1)} %pad_add_fusion.place, bf16[640,768]{1,0:T(8,128)(2,1)S(1)} %bitcast.14, bf16[640,768]{1,0:T(8,128)(2,1)} %collective-permute-done.4.refs_1_, ...), custom_call_target="tpu_custom_call" | custom-call | flops 5662310400 | bytes 25165824 | tf_op jit(solution)/shard_map/pallas_call | solution.py:352
  87.5 0.0 collective-permute-done.3.d0
  87.5 0.1 collective-permute-start.7
  87.6 0.5 collective-permute-start.8
  88.1 1.4 collective-permute-done.7.x1
  89.4 0.7 collective-permute-done.8.d1
  90.1 6.0 %shard_map.162 = (bf16[640,1280]{1,0:T(8,128)(2,1)S(1)}, bf16[640,384]{1,0:T(8,128)(2,1)S(1)}, bf16[3,640,384]{2,1,0:T(8,128)(2,1)S(1)}) custom-call(f32[640,1280]{1,0:T(8,128)S(1)} %get-tuple-element.32.pre, f32[640,640]{1,0:T(8,128)S(1)} %get-tuple-element.33.hid_ref, bf16[640,384]{1,0:T(8,128)(2,1)S(1)} %collective-permute-done.2.x0, ...), custom_call_target="tpu_custom_call" | custom-call | flops 6291456000 | bytes 14680064 | tf_op jit(solution)/shard_map/pallas_call | solution.py:362
  96.1 0.2 collective-permute-start.9
  96.3 0.4 collective-permute-start.10
  96.7 3.5 %shard_map.163 = (f32[640,384]{1,0:T(8,128)S(1)}, f32[3,640,384]{2,1,0:T(8,128)S(1)}) custom-call(bf16[640,1280]{1,0:T(8,128)(2,1)S(1)} %get-tuple-element.38.mid_ref, bf16[3072,1280]{1,0:T(8,128)(2,1)S(1)} %get-tuple-element.36.cat), custom_call_target="tpu_custom_call" | custom-call | flops 2516582400 | bytes 8388608 | tf_op jit(solution)/shard_map/pallas_call | solution.py:371
  100.3 0.1 shard_map.164
  100.4 0.3 collective-permute-start.11
  100.7 3.0 %collective-permute-start.12 = (bf16[320,384]{1,0:T(8,128)(2,1)S(1)}, bf16[320,384]{1,0:T(8,128)(2,1)S(1)}, u32[]{:S(2)}, u32[]{:S(2)}) collective-permute-start(bf16[320,384]{1,0:T(8,128)(2,1)S(1)} %get-tuple-element.44), channel_id=1, source_target_pairs={{0,6},{2,0},{4,2},{6,4},{1,7},{3,1},{5,3},{7,5},{8,14},{10,8},{12,... | collective-permute-start | bytes 737288 | tf_op jit(solution)/shard_map/ppermute | solution.py:296
  103.7 6.0 %collective-permute-done.11.via_right = bf16[320,384]{1,0:T(8,128)(2,1)S(1)} collective-permute-done((bf16[320,384]{1,0:T(8,128)(2,1)S(1)}, bf16[320,384]{1,0:T(8,128)(2,1)S(1)}, u32[]{:S(2)}, u32[]{:S(2)}) %collective-permute-start.11) | collective-permute-done | bytes 245792 | tf_op jit(solution)/shard_map/ppermute | solution.py:296
  109.7 0.0 collective-permute-done.12.via_left
  109.7 0.0 collective-permute-done.9.away
  109.7 0.3 shard_map.165
  110.0 0.1 collective-permute-start.13
  110.1 3.2 %collective-permute-start.14 = (bf16[640,384]{1,0:T(8,128)(2,1)S(1)}, bf16[640,384]{1,0:T(8,128)(2,1)S(1)}, u32[]{:S(2)}, u32[]{:S(2)}) collective-permute-start(bf16[640,384]{1,0:T(8,128)(2,1)S(1)} %get-tuple-element.47), channel_id=1, source_target_pairs={{0,6},{2,0},{4,2},{6,4},{1,7},{3,1},{5,3},{7,5},{8,14},{10,8},{12,... | collective-permute-start | bytes 1474568 | tf_op jit(solution)/shard_map/ppermute | solution.py:296
  113.3 3.6 %all-to-all-start.2 = ((bf16[16,128,128]{2,1,0:T(8,128)(2,1)}), bf16[16,128,128]{2,1,0:T(8,128)(2,1)S(1)}, u32[]{:S(2)}, u32[]{:S(2)}) async-start(bf16[16,128,128]{2,1,0:T(8,128)(2,1)} %shard_map.158.refs_9_), calls=%async_computation.2 | async-start | bytes 1048576 | tf_op jit(solution)/shard_map/all_to_all | solution.py:340
  116.9 6.8 %collective-permute-done.13 = bf16[640,384]{1,0:T(8,128)(2,1)S(1)} collective-permute-done((bf16[640,384]{1,0:T(8,128)(2,1)S(1)}, bf16[640,384]{1,0:T(8,128)(2,1)S(1)}, u32[]{:S(2)}, u32[]{:S(2)}) %collective-permute-start.13) | collective-permute-done | bytes 491552 | tf_op jit(solution)/shard_map/ppermute | solution.py:296
  123.7 0.0 collective-permute-done.14
  123.7 0.9 add_convert_fusion
  124.6 3.0 %all-to-all-done.2.refs_6_ = bf16[16,128,128]{2,1,0:T(8,128)(2,1)S(1)} async-done(((bf16[16,128,128]{2,1,0:T(8,128)(2,1)}), bf16[16,128,128]{2,1,0:T(8,128)(2,1)S(1)}, u32[]{:S(2)}, u32[]{:S(2)}) %all-to-all-start.2) | async-done | bytes 524320 | tf_op jit(solution)/shard_map/all_to_all | solution.py:340
  127.6 3.8 %all-to-all-start.3 = ((bf16[16,40,384]{2,1,0:T(8,128)(2,1)}), bf16[16,40,384]{2,1,0:T(8,128)(2,1)S(1)}, u32[]{:S(2)}, u32[]{:S(2)}) async-start(bf16[16,40,384]{2,1,0:T(8,128)(2,1)} %bitcast.6), calls=%async_computation.3 | async-start | bytes 983040 | tf_op jit(solution)/shard_map/all_to_all | solution.py:387
  131.4 5.4 %shard_map.159 = (bf16[256,1024]{1,0:T(8,128)(2,1)}, bf16[256,1024]{1,0:T(8,128)(2,1)}, bf16[256,1024]{1,0:T(8,128)(2,1)}) custom-call(f32[8,256]{1,0:T(8,128)} %refs_0_.3, s32[1,256]{1,0:T(1,128)} %bitcast.19, bf16[256,1024]{1,0:T(8,128)(2,1)} %refs_2_.3, bf16[256,1024]{1,0:T(8,128)(2,1)} %refs_3_.3, bf16[256,1024]{1,0:T(8,128)(2,1)} %refs_4_.3, ...), custom_call_target="tpu_custom_call" | custom-call | flops 1073741824 | bytes 4194304 | tf_op jit(solution)/shard_map/pallas_call | solution.py:341
  136.8 4.3 %all-to-all-done.3 = bf16[16,40,384]{2,1,0:T(8,128)(2,1)S(1)} async-done(((bf16[16,40,384]{2,1,0:T(8,128)(2,1)}), bf16[16,40,384]{2,1,0:T(8,128)(2,1)S(1)}, u32[]{:S(2)}, u32[]{:S(2)}) %all-to-all-start.3) | async-done | bytes 491552 | tf_op jit(solution)/shard_map/all_to_all | solution.py:387
  141.1 2.2 %shard_map.166 = bf16[256,384]{1,0:T(8,128)(2,1)} custom-call(bf16[640,384]{1,0:T(8,128)(2,1)S(1)} %bitcast.15, s32[2,256]{1,0:T(2,128)} %bitcast.17, f32[2,256]{1,0:T(2,128)} %bitcast.20), custom_call_target="tpu_custom_call" | custom-call | flops 251658240 | bytes 1048576 | tf_op jit(solution)/shard_map/pallas_call | solution.py:388
  (2 shorter events, 0.0 us)
Async XLA Ops:
  26.7 23.6 %collective-permute-start = (bf16[640,768]{1,0:T(8,128)(2,1)S(1)}, bf16[640,768]{1,0:T(8,128)(2,1)S(1)}, u32[]{:S(2)}, u32[]{:S(2)}) collective-permute-start(bf16[640,768]{1,0:T(8,128)(2,1)S(1)} %bitcast.10), channel_id=1, source_target_pairs={{0,2},{2,4},{4,6},{6,0},{1,3},{3,5},{5,7},{7,1},{8,10},{10,12},{12... | collective-permute-start | bytes 2949128 | tf_op jit(solution)/shard_map/ppermute | solution.py:296
  28.2 22.1 %collective-permute-start.1 = (bf16[640,768]{1,0:T(8,128)(2,1)S(1)}, bf16[640,768]{1,0:T(8,128)(2,1)S(1)}, u32[]{:S(2)}, u32[]{:S(2)}) collective-permute-start(bf16[640,768]{1,0:T(8,128)(2,1)S(1)} %bitcast.11), channel_id=1, source_target_pairs={{0,6},{2,0},{4,2},{6,4},{1,7},{3,1},{5,3},{7,5},{8,14},{10,8},{12,... | collective-permute-start | bytes 2949128 | tf_op jit(solution)/shard_map/ppermute | solution.py:296
  30.0 45.4 %collective-permute-start.4 = (bf16[640,768]{1,0:T(8,128)(2,1)S(1)}, bf16[640,768]{1,0:T(8,128)(2,1)}, u32[]{:S(2)}, u32[]{:S(2)}) collective-permute-start(bf16[640,768]{1,0:T(8,128)(2,1)S(1)} %bitcast.12), channel_id=1, source_target_pairs={{0,1},{1,0},{2,3},{3,2},{4,5},{5,4},{6,7},{7,6},{8,9},{9,8},{10,11... | collective-permute-start | bytes 2949128 | tf_op jit(solution)/shard_map/ppermute | solution.py:299
  50.3 25.1 %collective-permute-start.5 = (bf16[640,768]{1,0:T(8,128)(2,1)S(1)}, bf16[640,768]{1,0:T(8,128)(2,1)}, u32[]{:S(2)}, u32[]{:S(2)}) collective-permute-start(bf16[640,768]{1,0:T(8,128)(2,1)S(1)} %collective-permute-done.from_left.refs_2_), channel_id=1, source_target_pairs={{0,1},{1,0},{2,3},{3,2},{4,5},{5,4},{6,7},{7,6},{8,9},{9,8},{10,11... | collective-permute-start | bytes 2949128 | tf_op jit(solution)/shard_map/ppermute | solution.py:299
  50.3 25.1 %collective-permute-start.6 = (bf16[640,768]{1,0:T(8,128)(2,1)S(1)}, bf16[640,768]{1,0:T(8,128)(2,1)}, u32[]{:S(2)}, u32[]{:S(2)}) collective-permute-start(bf16[640,768]{1,0:T(8,128)(2,1)S(1)} %collective-permute-done.1.from_right.refs_4_), channel_id=1, source_target_pairs={{0,1},{1,0},{2,3},{3,2},{4,5},{5,4},{6,7},{7,6},{8,9},{9,8},{10,11... | collective-permute-start | bytes 2949128 | tf_op jit(solution)/shard_map/ppermute | solution.py:299
  54.7 16.2 %all-to-all-start.1 = ((bf16[16,144,128]{2,1,0:T(8,128)(2,1)}), bf16[16,144,128]{2,1,0:T(8,128)(2,1)S(1)}, u32[]{:S(2)}, u32[]{:S(2)}) async-start(bf16[16,144,128]{2,1,0:T(8,128)(2,1)} %shard_map.157), calls=%async_computation.1 | async-start | bytes 1179648 | tf_op jit(solution)/shard_map/all_to_all | solution.py:326
  72.1 15.4 %collective-permute-start.2 = (bf16[640,384]{1,0:T(8,128)(2,1)S(1)}, bf16[640,384]{1,0:T(8,128)(2,1)S(1)}, u32[]{:S(2)}, u32[]{:S(2)}) collective-permute-start(bf16[640,384]{1,0:T(8,128)(2,1)S(1)} %get-tuple-element.29), channel_id=1, source_target_pairs={{0,2},{2,4},{4,6},{6,0},{1,3},{3,5},{5,7},{7,1},{8,10},{10,12},{12... | collective-permute-start | bytes 1474568 | tf_op jit(solution)/shard_map/ppermute | solution.py:296
  73.6 13.8 %collective-permute-start.3 = (bf16[640,384]{1,0:T(8,128)(2,1)S(1)}, bf16[640,384]{1,0:T(8,128)(2,1)S(1)}, u32[]{:S(2)}, u32[]{:S(2)}) collective-permute-start(bf16[640,384]{1,0:T(8,128)(2,1)S(1)} %get-tuple-element.30), channel_id=1, source_target_pairs={{0,6},{2,0},{4,2},{6,4},{1,7},{3,1},{5,3},{7,5},{8,14},{10,8},{12,... | collective-permute-start | bytes 1474568 | tf_op jit(solution)/shard_map/ppermute | solution.py:296
  87.5 1.9 %collective-permute-start.7 = (bf16[640,384]{1,0:T(8,128)(2,1)S(1)}, bf16[640,384]{1,0:T(8,128)(2,1)S(1)}, u32[]{:S(2)}, u32[]{:S(2)}) collective-permute-start(bf16[640,384]{1,0:T(8,128)(2,1)S(1)} %collective-permute-done.2.x0), channel_id=1, source_target_pairs={{0,1},{1,0},{2,3},{3,2},{4,5},{5,4},{6,7},{7,6},{8,9},{9,8},{10,11... | collective-permute-start | bytes 1474568 | tf_op jit(solution)/shard_map/ppermute | solution.py:299
  87.6 2.6 %collective-permute-start.8 = (bf16[640,384]{1,0:T(8,128)(2,1)S(1)}, bf16[640,384]{1,0:T(8,128)(2,1)S(1)}, u32[]{:S(2)}, u32[]{:S(2)}) collective-permute-start(bf16[640,384]{1,0:T(8,128)(2,1)S(1)} %collective-permute-done.3.d0), channel_id=1, source_target_pairs={{0,1},{1,0},{2,3},{3,2},{4,5},{5,4},{6,7},{7,6},{8,9},{9,8},{10,11... | collective-permute-start | bytes 1474568 | tf_op jit(solution)/shard_map/ppermute | solution.py:299
  96.1 13.5 %collective-permute-start.9 = (bf16[3,640,384]{2,1,0:T(8,128)(2,1)S(1)}, bf16[3,640,384]{2,1,0:T(8,128)(2,1)S(1)}, u32[]{:S(2)}, u32[]{:S(2)}) collective-permute-start(bf16[3,640,384]{2,1,0:T(8,128)(2,1)S(1)} %get-tuple-element.40), channel_id=1, source_target_pairs={{0,1},{1,0},{2,3},{3,2},{4,5},{5,4},{6,7},{7,6},{8,9},{9,8},{10,11... | collective-permute-start | bytes 4423688 | tf_op jit(solution)/shard_map/ppermute | solution.py:299
  96.3 3.9 %collective-permute-start.10 = (bf16[640,384]{1,0:T(8,128)(2,1)S(1)}, bf16[640,384]{1,0:T(8,128)(2,1)S(1)}, u32[]{:S(2)}, u32[]{:S(2)}) collective-permute-start(bf16[640,384]{1,0:T(8,128)(2,1)S(1)} %get-tuple-element.42), channel_id=1, source_target_pairs={{0,1},{1,0},{2,3},{3,2},{4,5},{5,4},{6,7},{7,6},{8,9},{9,8},{10,11... | collective-permute-start | bytes 1474568 | tf_op jit(solution)/shard_map/ppermute | solution.py:299
  100.4 9.3 %collective-permute-start.11 = (bf16[320,384]{1,0:T(8,128)(2,1)S(1)}, bf16[320,384]{1,0:T(8,128)(2,1)S(1)}, u32[]{:S(2)}, u32[]{:S(2)}) collective-permute-start(bf16[320,384]{1,0:T(8,128)(2,1)S(1)} %get-tuple-element.43), channel_id=1, source_target_pairs={{0,2},{2,4},{4,6},{6,0},{1,3},{3,5},{5,7},{7,1},{8,10},{10,12},{12... | collective-permute-start | bytes 737288 | tf_op jit(solution)/shard_map/ppermute | solution.py:296
  100.7 8.9 %collective-permute-start.12 = (bf16[320,384]{1,0:T(8,128)(2,1)S(1)}, bf16[320,384]{1,0:T(8,128)(2,1)S(1)}, u32[]{:S(2)}, u32[]{:S(2)}) collective-permute-start(bf16[320,384]{1,0:T(8,128)(2,1)S(1)} %get-tuple-element.44), channel_id=1, source_target_pairs={{0,6},{2,0},{4,2},{6,4},{1,7},{3,1},{5,3},{7,5},{8,14},{10,8},{12,... | collective-permute-start | bytes 737288 | tf_op jit(solution)/shard_map/ppermute | solution.py:296
  110.0 13.7 %collective-permute-start.13 = (bf16[640,384]{1,0:T(8,128)(2,1)S(1)}, bf16[640,384]{1,0:T(8,128)(2,1)S(1)}, u32[]{:S(2)}, u32[]{:S(2)}) collective-permute-start(bf16[640,384]{1,0:T(8,128)(2,1)S(1)} %get-tuple-element.46), channel_id=1, source_target_pairs={{0,2},{2,4},{4,6},{6,0},{1,3},{3,5},{5,7},{7,1},{8,10},{10,12},{12... | collective-permute-start | bytes 1474568 | tf_op jit(solution)/shard_map/ppermute | solution.py:296
  110.1 13.6 %collective-permute-start.14 = (bf16[640,384]{1,0:T(8,128)(2,1)S(1)}, bf16[640,384]{1,0:T(8,128)(2,1)S(1)}, u32[]{:S(2)}, u32[]{:S(2)}) collective-permute-start(bf16[640,384]{1,0:T(8,128)(2,1)S(1)} %get-tuple-element.47), channel_id=1, source_target_pairs={{0,6},{2,0},{4,2},{6,4},{1,7},{3,1},{5,3},{7,5},{8,14},{10,8},{12,... | collective-permute-start | bytes 1474568 | tf_op jit(solution)/shard_map/ppermute | solution.py:296
  113.3 14.3 %all-to-all-start.2 = ((bf16[16,128,128]{2,1,0:T(8,128)(2,1)}), bf16[16,128,128]{2,1,0:T(8,128)(2,1)S(1)}, u32[]{:S(2)}, u32[]{:S(2)}) async-start(bf16[16,128,128]{2,1,0:T(8,128)(2,1)} %shard_map.158.refs_9_), calls=%async_computation.2 | async-start | bytes 1048576 | tf_op jit(solution)/shard_map/all_to_all | solution.py:340
  127.6 13.5 %all-to-all-start.3 = ((bf16[16,40,384]{2,1,0:T(8,128)(2,1)}), bf16[16,40,384]{2,1,0:T(8,128)(2,1)S(1)}, u32[]{:S(2)}, u32[]{:S(2)}) async-start(bf16[16,40,384]{2,1,0:T(8,128)(2,1)} %bitcast.6), calls=%async_computation.3 | async-start | bytes 983040 | tf_op jit(solution)/shard_map/all_to_all | solution.py:387

commit v5 on v4

--- a/solution.py
+++ b/solution.py
@@ -78,24 +78,28 @@
     return [ids[k : k + 1] * CAP + places[k] for k in range(2)]
 
 
-def pack_kernel(ids_hbm, x_hbm, d_hbm, rows_ref, ids_ref, x_ref, d_ref, sems):
+def pack_kernel(ids_hbm, x_hbm, d_hbm, rows_ref, slots_hbm, ids_ref, x_ref, d_ref, slots_ref, sems):
     copies = fetch(((ids_hbm, ids_ref), (x_hbm, x_ref), (d_hbm, d_ref)), sems)
     copies[0].wait()
     slots = slots_of(ids_ref[...])
+    slots_ref[0:1, :], slots_ref[1:2, :] = slots
+    leaving = pltpu.make_async_copy(slots_ref, slots_hbm, sems.at[3])
+    leaving.start()
     pick = jnp.where(onehot(slots[0]) | onehot(slots[1]), 1.0, 0.0).astype(BF)
     copies[1].wait()
     rows_ref[:, :FEAT] = mm(pick, x_ref[...]).astype(BF)
     copies[2].wait()
     rows_ref[:, FEAT:] = mm(pick, d_ref[...]).astype(BF)
-
-
-def combine_kernel(rows_ref, ids_hbm, weights_hbm, out_ref, ids_ref, weights_ref, sems):
-    for copy in fetch(((ids_hbm, ids_ref), (weights_hbm, weights_ref)), sems):
+    leaving.wait()
+
+
+def combine_kernel(rows_ref, slots_hbm, weights_hbm, out_ref, slots_ref, weights_ref, sems):
+    for copy in fetch(((slots_hbm, slots_ref), (weights_hbm, weights_ref)), sems):
         copy.wait()
     columns = jnp.concatenate([weights_ref[...], jnp.zeros((6, TOK), F32)], axis=0).T
     total = jnp.zeros((TOK, FEAT), F32)
-    for k, slot in enumerate(slots_of(ids_ref[...])):
-        pick = jnp.where(onehot(slot), 1.0, 0.0).astype(BF)
+    for k in range(2):
+        pick = jnp.where(onehot(slots_ref[k : k + 1, :]), 1.0, 0.0).astype(BF)
         total += columns[:, k : k + 1] * mm(pick, rows_ref[...], TN)
     out_ref[...] = total.astype(BF)
 
@@ -210,7 +214,7 @@
 OUT_ORDER = (2, -1, 1, 0)
 
 
-def forward_kernel(from_left, from_right, token, x_ref, d_ref, sems):
+def forward_kernel(from_left, from_right, x_ref, d_ref, sems):
     pairs = ((from_left.at[:, pl.ds(0, FEAT)], x_ref), (from_right.at[:, pl.ds(FEAT, FEAT)], d_ref))
     for copy in fetch(pairs, sems):
         copy.wait()
@@ -252,7 +256,7 @@
     return mm(mid_ref[...], cat[at : at + FEAT, :], NT)
 
 
-def expert_mid_kernel(pre, hid_ref, x0, d0, x1, d1, cat, down_late, mid_ref, far_ref, rest_ref):
+def expert_mid_kernel(pre, hid_ref, x0, d0, x1, d1, cat, down_late, mid_ref, far_ref):
     late = slice(EARLY * FEAT, None)
     hid = hid_ref[...] + mm(jnp.concatenate([d0[...], d1[...]], axis=1), down_late[...], NT)
     both = pre[...] + mm(jnp.concatenate([x0[...], x1[...]], axis=1), cat[late, :])
@@ -261,12 +265,15 @@
     mid_ref[:, :HID] = (hid * up * s * (1.0 + gate * (1.0 - s))).astype(BF)
     mid_ref[:, HID:] = (hid * gate * s).astype(BF)
     far_ref[...] = out_block(mid_ref, cat, OUT_ORDER[0], 1).astype(BF)
+
+
+def expert_out_kernel(mid_ref, cat, far_ref, rest_ref):
+    far_ref[...] = out_block(mid_ref, cat, OUT_ORDER[0], 0)
     for i, offset in enumerate(OUT_ORDER[1:]):
         rest_ref[i] = out_block(mid_ref, cat, offset, 1).astype(BF)
 
 
-def expert_out_kernel(mid_ref, cat, far_ref, rest_ref):
-    far_ref[...] = out_block(mid_ref, cat, OUT_ORDER[0], 0)
+def expert_rest_kernel(mid_ref, cat, rest_ref):
     for i, offset in enumerate(OUT_ORDER[1:]):
         rest_ref[i] = out_block(mid_ref, cat, offset, 0)
 
@@ -298,16 +305,15 @@
     def swap(value):
         return lax.ppermute(value, "core", SWAP)
 
-    ids = in_hbm(expert_ids.T)
-    rows = call(
+    rows, slots = call(
         pack_kernel,
-        S((ROWS, 2 * FEAT), BF),
+        (S((ROWS, 2 * FEAT), BF), pltpu.HBM((2, TOK), I32)),
         [anywhere()] * 3,
-        [pltpu.VMEM((2, TOK), I32)] + [pltpu.VMEM((TOK, FEAT), BF)] * 2 + [pltpu.SemaphoreType.DMA((3,))],
+        [pltpu.VMEM((2, TOK), I32)] + [pltpu.VMEM((TOK, FEAT), BF)] * 2 + [pltpu.VMEM((2, TOK), I32), pltpu.SemaphoreType.DMA((4,))],
         flops=2 * ROWS * TOK * 2 * FEAT,
         size=2 * MIB,
         limit=6,
-    )(ids, in_hbm(moe_input), in_hbm(moe_cotangent))
+    )(in_hbm(expert_ids.T), in_hbm(moe_input), in_hbm(moe_cotangent))
     own = lax.all_to_all(rows.reshape(CTX, CAP, 2 * FEAT), "ctx", 0, 0, tiled=True).reshape(ROWS, 2 * FEAT)
     from_left, from_right = ring(own, RIGHT), ring(own, LEFT)
 
@@ -324,15 +330,16 @@
         limit=8,
     )(*branch, own)
     arrived = lax.all_to_all(message, "ctx", 0, 0, tiled=True)
+    from_left, from_right, arrived = lax.optimization_barrier((from_left, from_right, arrived))
 
     x_far, d_far = call(
         forward_kernel,
         (block, block),
-        [anywhere()] * 3,
+        [anywhere()] * 2,
         [pltpu.SemaphoreType.DMA((2,))],
         size=2 * MIB,
         limit=4,
-    )(from_left, from_right, arrived)
+    )(from_left, from_right)
     x_far, d_far = ring(x_far, RIGHT), ring(d_far, LEFT)
     early = [c for a in (own, from_left, from_right) for c in (a, swap(a))]
 
@@ -359,18 +366,19 @@
         limit=28,
     )(place, *early, *[in_hbm(w) for w in (w_gate, w_up, w_down)], scanned)
     x_far, d_far, pre = lax.optimization_barrier((x_far, d_far, pre))
-    mid, away_far, away_rest = call(
+    rest = (RINGX - 1, ROWS, FEAT)
+    mid, away_far = call(
         expert_mid_kernel,
-        (S((ROWS, 2 * HID), BF), block, S((RINGX - 1, ROWS, FEAT), BF)),
+        (S((ROWS, 2 * HID), BF), block),
         [vmem()] * 8,
-        flops=10 * ROWS * HID * RINGX * FEAT,
-        size=14 * MIB,
+        flops=8 * ROWS * HID * 2 * FEAT,
+        size=12 * MIB,
         limit=32,
     )(pre, hid, x_far, d_far, swap(x_far), swap(d_far), cat, down_late)
-    away_far, away_rest = swap(away_far), swap(away_rest)
-    mine_far, mine_rest = call(
+    away_far = swap(away_far)
+    mine_far, away_rest = call(
         expert_out_kernel,
-        (S((ROWS, FEAT), F32), S((RINGX - 1, ROWS, FEAT), F32)),
+        (S((ROWS, FEAT), F32), S(rest, BF)),
         [vmem()] * 2,
         flops=4 * ROWS * HID * RINGX * FEAT,
         size=8 * MIB,
@@ -379,6 +387,16 @@
 
     half = S((CUT, FEAT), BF)
     to_right, to_left = call(far_kernel, (half, half), [vmem()] * 2, size=2 * MIB, flops=MIB, limit=8)(mine_far, away_far)
+    mid, away_rest, to_right, to_left = lax.optimization_barrier((mid, away_rest, to_right, to_left))
+    away_rest = swap(away_rest)
+    mine_rest = call(
+        expert_rest_kernel,
+        S(rest, F32),
+        [vmem()] * 2,
+        flops=3 * ROWS * HID * RINGX * FEAT,
+        size=8 * MIB,
+        limit=18,
+    )(mid, cat)
     via_right, via_left = ring(to_right, RIGHT), ring(to_left, LEFT)
     to_left, to_right, here = call(
         near_kernel, (block, block, S((ROWS, FEAT), F32)), [vmem()] * 4, size=5 * MIB, flops=MIB, limit=16
@@ -393,7 +411,7 @@
         flops=4 * ROWS * TOK * FEAT,
         size=MIB,
         limit=8,
-    )(back.reshape(ROWS, FEAT), ids, in_hbm(router_weights.T))
+    )(back.reshape(ROWS, FEAT), in_hbm(slots), in_hbm(router_weights.T))
     return (*grads, grad_moe)
 
 

time: 144 us -> 121 us (0.84)
  waiting for transfers between devices: 55 us -> 32.1 us
    ppermute x8, waiting for transfers between devices: 33.1 us -> 12.1 us  [ring(): return lax.ppermute(value, 'x', way)]
    all_to_all x1, waiting for transfers between devices: 12.6 us -> 10.7 us  [local(): arrived = lax.all_to_all(message, 'ctx', 0, 0, tiled=True)]
    pallas_call x4 -> x5, Pallas kernels: 11.4 us -> 11.6 us  [the longest x1 3.55 us: local(): call(expert_mid_kernel, (S((ROWS, 2 * HID), BF), block), [vmem()] * 8, fl...]
  transfers between devices with their start and end apart: 18 -> 18, of which waited for: 8 -> 8; matrix products, arithmetic and copies ran while one was open for 1% -> 1% of each run, Pallas kernels for 18% -> 24%
where the time goes in v5:
time: 121 us
  Pallas kernels  36.4 us (30%)
  waiting for transfers between devices  32.1 us (27%)
  starting transfers between devices  25.9 us (21%)
  blocking collectives  24.4 us (20%)
    all_to_all x1, blocking collectives, local(): lax.all_to_all(rows.reshape(CTX, CAP, 2 * FEAT), 'ctx', 0, 0, tiled=True)  24.4 us
    ppermute x8, starting transfers between devices, ring(): return lax.ppermute(value, 'x', way)  13.1 us
    ppermute x8, waiting for transfers between devices, ring(): return lax.ppermute(value, 'x', way)  12.1 us
    pallas_call x1, Pallas kernels, local(): call(expert_early_kernel, (S((ROWS, 2 * HID), F32), S((ROWS, HID), F32),...  12.1 us
    all_to_all x1, waiting for transfers between devices, local(): arrived = lax.all_to_all(message, 'ctx', 0, 0, tiled=True)  10.7 us
    pallas_call x1, Pallas kernels, local(): call(attention_kernel, (S((TOK, HEADS * HD), BF),) * 3, [anywhere()] * 6...  5.41 us
    all_to_all x1, waiting for transfers between devices, local(): lax.all_to_all(summed.reshape(CTX, CAP, FEAT), 'ctx', 0, 0, tiled=True)  4.29 us
    pallas_call x1, Pallas kernels, local(): call(state_kernel, S((CTX, HD + MARKS, HD), BF), [anywhere()] * 7, held,...  3.93 us
  transfers between devices with their start and end apart: 18, of which 8 were waited for; matrix products, arithmetic and copies ran while one was open for 1% of the time, Pallas kernels for 24%

profile of v5, /device:TPU:0, one launch (start us, length us, event | category | flops | bytes accessed | tf_op | source)
XLA Modules:
  0.0 120.8 jit_solution(13343512692735044046)
XLA Ops:
  0.6 1.7 %shard_map.156 = (bf16[640,768]{1,0:T(8,128)(2,1)S(1)}, s32[2,256]{1,0:T(2,128)}) custom-call(s32[2,256]{1,0:T(2,128)} %bitcast.18, bf16[256,384]{1,0:T(8,128)(2,1)} %x_hbm.1, bf16[256,384]{1,0:T(8,128)(2,1)} %d_hbm.1), custom_call_target="tpu_custom_call" | custom-call | flops 251658240 | bytes 2097152 | tf_op jit(solution)/shard_map/pallas_call | solution.py:308
  2.4 24.4 %all_to_all.20 = bf16[16,40,768]{2,1,0:T(8,128)(2,1)S(1)} all-to-all(bf16[16,40,768]{2,1,0:T(8,128)(2,1)S(1)} %bitcast.14), channel_id=1, replica_groups=mesh['ctx'=16,'x'=4,'core'=2] {'ctx'}, dimensions={0} | all-to-all | bytes 1966080 | tf_op jit(solution)/shard_map/all_to_all | solution.py:317
  26.7 1.5 %collective-permute-start = (bf16[640,768]{1,0:T(8,128)(2,1)S(1)}, bf16[640,768]{1,0:T(8,128)(2,1)S(1)}, u32[]{:S(2)}, u32[]{:S(2)}) collective-permute-start(bf16[640,768]{1,0:T(8,128)(2,1)S(1)} %bitcast.9), channel_id=1, source_target_pairs={{0,2},{2,4},{4,6},{6,0},{1,3},{3,5},{5,7},{7,1},{8,10},{10,12},{12... | collective-permute-start | bytes 2949128 | tf_op jit(solution)/shard_map/ppermute | solution.py:303
  28.2 1.7 %collective-permute-start.1 = (bf16[640,768]{1,0:T(8,128)(2,1)S(1)}, bf16[640,768]{1,0:T(8,128)(2,1)S(1)}, u32[]{:S(2)}, u32[]{:S(2)}) collective-permute-start(bf16[640,768]{1,0:T(8,128)(2,1)S(1)} %bitcast.10), channel_id=1, source_target_pairs={{0,6},{2,0},{4,2},{6,4},{1,7},{3,1},{5,3},{7,5},{8,14},{10,8},{12,... | collective-permute-start | bytes 2949128 | tf_op jit(solution)/shard_map/ppermute | solution.py:303
  30.0 3.9 %shard_map.157 = bf16[16,144,128]{2,1,0:T(8,128)(2,1)} custom-call(f32[8,256]{1,0:T(8,128)} %refs_0_.3, s32[1,256]{1,0:T(1,128)} %bitcast.16, bf16[256,1024]{1,0:T(8,128)(2,1)} %refs_2_.3, bf16[256,1024]{1,0:T(8,128)(2,1)} %refs_3_.3, bf16[256,1024]{1,0:T(8,128)(2,1)} %refs_4_.3, bf16[256,1024]{1,0:T(8,128)(2,1)} %refs_5_.3, bf16[640,768]{1,0:T(8,128)(2,1)S(1)} %bitcast.11), custom_call_target="tpu_custom_call" | custom-call | flops 134217728 | bytes 3145728 | tf_op jit(solution)/shard_map/pallas_call | solution.py:323
  33.9 3.6 %all-to-all-start.1 = ((bf16[16,144,128]{2,1,0:T(8,128)(2,1)}), bf16[16,144,128]{2,1,0:T(8,128)(2,1)S(1)}, u32[]{:S(2)}, u32[]{:S(2)}) async-start(bf16[16,144,128]{2,1,0:T(8,128)(2,1)} %shard_map.157), calls=%async_computation.1 | async-start | bytes 1179648 | tf_op jit(solution)/shard_map/all_to_all | solution.py:332
  37.5 0.1 collective-permute-start.4
  37.6 10.7 %all-to-all-done.1.in_ref = bf16[16,144,128]{2,1,0:T(8,128)(2,1)S(1)} async-done(((bf16[16,144,128]{2,1,0:T(8,128)(2,1)}), bf16[16,144,128]{2,1,0:T(8,128)(2,1)S(1)}, u32[]{:S(2)}, u32[]{:S(2)}) %all-to-all-start.1) | async-done | bytes 589856 | tf_op jit(solution)/shard_map/all_to_all | solution.py:332
  48.3 2.0 %collective-permute-done.from_left.refs_2_ = bf16[640,768]{1,0:T(8,128)(2,1)S(1)} collective-permute-done((bf16[640,768]{1,0:T(8,128)(2,1)S(1)}, bf16[640,768]{1,0:T(8,128)(2,1)S(1)}, u32[]{:S(2)}, u32[]{:S(2)}) %collective-permute-start) | collective-permute-done | bytes 983072 | tf_op jit(solution)/shard_map/ppermute | solution.py:303
  50.3 0.0 collective-permute-done.1.from_right.refs_4_
  50.3 0.0 collective-permute-start.5
  50.3 0.5 collective-permute-start.6
  50.8 0.1 pad_add_fusion.place
  50.9 0.1 shard_map.160
  51.0 1.6 %collective-permute-start.2 = (bf16[640,384]{1,0:T(8,128)(2,1)S(1)}, bf16[640,384]{1,0:T(8,128)(2,1)S(1)}, u32[]{:S(2)}, u32[]{:S(2)}) collective-permute-start(bf16[640,384]{1,0:T(8,128)(2,1)S(1)} %get-tuple-element.41), channel_id=1, source_target_pairs={{0,2},{2,4},{4,6},{6,0},{1,3},{3,5},{5,7},{7,1},{8,10},{10,12},{12... | collective-permute-start | bytes 1474568 | tf_op jit(solution)/shard_map/ppermute | solution.py:303
  52.6 1.7 %collective-permute-start.3 = (bf16[640,384]{1,0:T(8,128)(2,1)S(1)}, bf16[640,384]{1,0:T(8,128)(2,1)S(1)}, u32[]{:S(2)}, u32[]{:S(2)}) collective-permute-start(bf16[640,384]{1,0:T(8,128)(2,1)S(1)} %get-tuple-element.42), channel_id=1, source_target_pairs={{0,6},{2,0},{4,2},{6,4},{1,7},{3,1},{5,3},{7,5},{8,14},{10,8},{12,... | collective-permute-start | bytes 1474568 | tf_op jit(solution)/shard_map/ppermute | solution.py:303
  54.3 1.0 shard_map.158.refs_9_
  55.3 0.0 collective-permute-done.4.refs_1_
  55.3 0.0 collective-permute-done.6.refs_5_
  55.3 12.1 %shard_map.161 = (f32[640,1280]{1,0:T(8,128)S(1)}, f32[640,640]{1,0:T(8,128)S(1)}, bf16[3072,1280]{1,0:T(8,128)(2,1)S(1)}, bf16[640,768]{1,0:T(8,128)(2,1)S(1)}) custom-call(s32[2]{0:T(128)S(1)} %pad_add_fusion.place, bf16[640,768]{1,0:T(8,128)(2,1)S(1)} %bitcast.13, bf16[640,768]{1,0:T(8,128)(2,1)} %collective-permute-done.4.refs_1_, ...), custom_call_target="tpu_custom_call" | custom-call | flops 5662310400 | bytes 25165824 | tf_op jit(solution)/shard_map/pallas_call | solution.py:359
  67.4 0.0 collective-permute-done.2.x0
  67.4 0.0 collective-permute-done.3.d0
  67.4 0.1 collective-permute-start.7
  67.5 0.5 collective-permute-start.8
  68.0 1.4 %collective-permute-done.7.x1 = bf16[640,384]{1,0:T(8,128)(2,1)S(1)} collective-permute-done((bf16[640,384]{1,0:T(8,128)(2,1)S(1)}, bf16[640,384]{1,0:T(8,128)(2,1)S(1)}, u32[]{:S(2)}, u32[]{:S(2)}) %collective-permute-start.7) | collective-permute-done | bytes 491552 | tf_op jit(solution)/shard_map/ppermute | solution.py:306
  69.3 0.7 collective-permute-done.8.d1
  70.0 3.6 %shard_map.162 = (bf16[640,1280]{1,0:T(8,128)(2,1)S(1)}, bf16[640,384]{1,0:T(8,128)(2,1)S(1)}) custom-call(f32[640,1280]{1,0:T(8,128)S(1)} %get-tuple-element.44.pre, f32[640,640]{1,0:T(8,128)S(1)} %get-tuple-element.45.hid_ref, bf16[640,384]{1,0:T(8,128)(2,1)S(1)} %collective-permute-done.2.x0, bf16[640,384]{1,0:T(8,128)(2,1)S(1)} %collective-permute-done.3.d0, ...), custom_call_target="tpu_custom_call" | custom-call | flops 2516582400 | bytes 12582912 | tf_op jit(solution)/shard_map/pallas_call | solution.py:370
  73.6 0.2 collective-permute-start.9
  73.8 3.5 %shard_map.163 = (f32[640,384]{1,0:T(8,128)S(1)}, bf16[3,640,384]{2,1,0:T(8,128)(2,1)S(1)}) custom-call(bf16[640,1280]{1,0:T(8,128)(2,1)S(1)} %get-tuple-element.56.mid_ref, bf16[3072,1280]{1,0:T(8,128)(2,1)S(1)} %get-tuple-element.48.cat), custom_call_target="tpu_custom_call" | custom-call | flops 2516582400 | bytes 8388608 | tf_op jit(solution)/shard_map/pallas_call | solution.py:379
  77.4 0.0 collective-permute-done.9.away
  77.4 0.1 shard_map.164
  77.5 0.4 collective-permute-start.10
  77.9 0.6 collective-permute-start.11
  78.5 2.7 %collective-permute-start.12 = (bf16[320,384]{1,0:T(8,128)(2,1)S(1)}, bf16[320,384]{1,0:T(8,128)(2,1)S(1)}, u32[]{:S(2)}, u32[]{:S(2)}) collective-permute-start(bf16[320,384]{1,0:T(8,128)(2,1)S(1)} %get-tuple-element.59), channel_id=1, source_target_pairs={{0,6},{2,0},{4,2},{6,4},{1,7},{3,1},{5,3},{7,5},{8,14},{10,8},{12,... | collective-permute-start | bytes 737288 | tf_op jit(solution)/shard_map/ppermute | solution.py:303
  81.2 2.7 %shard_map.165.mine = f32[3,640,384]{2,1,0:T(8,128)S(1)} custom-call(bf16[640,1280]{1,0:T(8,128)(2,1)S(1)} %get-tuple-element.56.mid_ref, bf16[3072,1280]{1,0:T(8,128)(2,1)S(1)} %get-tuple-element.48.cat), custom_call_target="tpu_custom_call" | custom-call | flops 1887436800 | bytes 8388608 | tf_op jit(solution)/shard_map/pallas_call | solution.py:392
  83.9 3.3 %collective-permute-done.11.via_right = bf16[320,384]{1,0:T(8,128)(2,1)S(1)} collective-permute-done((bf16[320,384]{1,0:T(8,128)(2,1)S(1)}, bf16[320,384]{1,0:T(8,128)(2,1)S(1)}, u32[]{:S(2)}, u32[]{:S(2)}) %collective-permute-start.11) | collective-permute-done | bytes 245792 | tf_op jit(solution)/shard_map/ppermute | solution.py:303
  87.2 0.3 shard_map.166
  87.5 0.3 collective-permute-start.13
  87.8 3.0 %collective-permute-start.14 = (bf16[640,384]{1,0:T(8,128)(2,1)S(1)}, bf16[640,384]{1,0:T(8,128)(2,1)S(1)}, u32[]{:S(2)}, u32[]{:S(2)}) collective-permute-start(bf16[640,384]{1,0:T(8,128)(2,1)S(1)} %get-tuple-element.62), channel_id=1, source_target_pairs={{0,6},{2,0},{4,2},{6,4},{1,7},{3,1},{5,3},{7,5},{8,14},{10,8},{12,... | collective-permute-start | bytes 1474568 | tf_op jit(solution)/shard_map/ppermute | solution.py:303
  90.8 3.6 %all-to-all-start.2 = ((bf16[16,128,128]{2,1,0:T(8,128)(2,1)}), bf16[16,128,128]{2,1,0:T(8,128)(2,1)S(1)}, u32[]{:S(2)}, u32[]{:S(2)}) async-start(bf16[16,128,128]{2,1,0:T(8,128)(2,1)} %shard_map.158.refs_9_), calls=%async_computation.2 | async-start | bytes 1048576 | tf_op jit(solution)/shard_map/all_to_all | solution.py:347
  94.4 6.8 %collective-permute-done.13 = bf16[640,384]{1,0:T(8,128)(2,1)S(1)} collective-permute-done((bf16[640,384]{1,0:T(8,128)(2,1)S(1)}, bf16[640,384]{1,0:T(8,128)(2,1)S(1)}, u32[]{:S(2)}, u32[]{:S(2)}) %collective-permute-start.13) | collective-permute-done | bytes 491552 | tf_op jit(solution)/shard_map/ppermute | solution.py:303
  101.2 0.0 collective-permute-done.14
  101.2 0.9 add_convert_fusion
  102.1 3.0 %all-to-all-done.2.refs_6_ = bf16[16,128,128]{2,1,0:T(8,128)(2,1)S(1)} async-done(((bf16[16,128,128]{2,1,0:T(8,128)(2,1)}), bf16[16,128,128]{2,1,0:T(8,128)(2,1)S(1)}, u32[]{:S(2)}, u32[]{:S(2)}) %all-to-all-start.2) | async-done | bytes 524320 | tf_op jit(solution)/shard_map/all_to_all | solution.py:347
  105.1 3.8 %all-to-all-start.3 = ((bf16[16,40,384]{2,1,0:T(8,128)(2,1)}), bf16[16,40,384]{2,1,0:T(8,128)(2,1)S(1)}, u32[]{:S(2)}, u32[]{:S(2)}) async-start(bf16[16,40,384]{2,1,0:T(8,128)(2,1)} %bitcast.6), calls=%async_computation.3 | async-start | bytes 983040 | tf_op jit(solution)/shard_map/all_to_all | solution.py:405
  108.9 5.4 %shard_map.159 = (bf16[256,1024]{1,0:T(8,128)(2,1)}, bf16[256,1024]{1,0:T(8,128)(2,1)}, bf16[256,1024]{1,0:T(8,128)(2,1)}) custom-call(f32[8,256]{1,0:T(8,128)} %refs_0_.3, s32[1,256]{1,0:T(1,128)} %bitcast.17, bf16[256,1024]{1,0:T(8,128)(2,1)} %refs_2_.3, bf16[256,1024]{1,0:T(8,128)(2,1)} %refs_3_.3, bf16[256,1024]{1,0:T(8,128)(2,1)} %refs_4_.3, ...), custom_call_target="tpu_custom_call" | custom-call | flops 1073741824 | bytes 4194304 | tf_op jit(solution)/shard_map/pallas_call | solution.py:348
  114.3 4.3 %all-to-all-done.3 = bf16[16,40,384]{2,1,0:T(8,128)(2,1)S(1)} async-done(((bf16[16,40,384]{2,1,0:T(8,128)(2,1)}), bf16[16,40,384]{2,1,0:T(8,128)(2,1)S(1)}, u32[]{:S(2)}, u32[]{:S(2)}) %all-to-all-start.3) | async-done | bytes 491552 | tf_op jit(solution)/shard_map/all_to_all | solution.py:405
  118.6 2.0 %shard_map.167 = bf16[256,384]{1,0:T(8,128)(2,1)} custom-call(bf16[640,384]{1,0:T(8,128)(2,1)S(1)} %bitcast.15, s32[2,256]{1,0:T(2,128)} %get-tuple-element.63.slots_hbm, f32[2,256]{1,0:T(2,128)} %bitcast.19), custom_call_target="tpu_custom_call" | custom-call | flops 251658240 | bytes 1048576 | tf_op jit(solution)/shard_map/pallas_call | solution.py:406
  (3 shorter events, 0.0 us)
Async XLA Ops:
  26.7 23.6 %collective-permute-start = (bf16[640,768]{1,0:T(8,128)(2,1)S(1)}, bf16[640,768]{1,0:T(8,128)(2,1)S(1)}, u32[]{:S(2)}, u32[]{:S(2)}) collective-permute-start(bf16[640,768]{1,0:T(8,128)(2,1)S(1)} %bitcast.9), channel_id=1, source_target_pairs={{0,2},{2,4},{4,6},{6,0},{1,3},{3,5},{5,7},{7,1},{8,10},{10,12},{12... | collective-permute-start | bytes 2949128 | tf_op jit(solution)/shard_map/ppermute | solution.py:303
  28.2 22.1 %collective-permute-start.1 = (bf16[640,768]{1,0:T(8,128)(2,1)S(1)}, bf16[640,768]{1,0:T(8,128)(2,1)S(1)}, u32[]{:S(2)}, u32[]{:S(2)}) collective-permute-start(bf16[640,768]{1,0:T(8,128)(2,1)S(1)} %bitcast.10), channel_id=1, source_target_pairs={{0,6},{2,0},{4,2},{6,4},{1,7},{3,1},{5,3},{7,5},{8,14},{10,8},{12,... | collective-permute-start | bytes 2949128 | tf_op jit(solution)/shard_map/ppermute | solution.py:303
  33.9 14.4 %all-to-all-start.1 = ((bf16[16,144,128]{2,1,0:T(8,128)(2,1)}), bf16[16,144,128]{2,1,0:T(8,128)(2,1)S(1)}, u32[]{:S(2)}, u32[]{:S(2)}) async-start(bf16[16,144,128]{2,1,0:T(8,128)(2,1)} %shard_map.157), calls=%async_computation.1 | async-start | bytes 1179648 | tf_op jit(solution)/shard_map/all_to_all | solution.py:332
  37.5 17.8 %collective-permute-start.4 = (bf16[640,768]{1,0:T(8,128)(2,1)S(1)}, bf16[640,768]{1,0:T(8,128)(2,1)}, u32[]{:S(2)}, u32[]{:S(2)}) collective-permute-start(bf16[640,768]{1,0:T(8,128)(2,1)S(1)} %bitcast.12), channel_id=1, source_target_pairs={{0,1},{1,0},{2,3},{3,2},{4,5},{5,4},{6,7},{7,6},{8,9},{9,8},{10,11... | collective-permute-start | bytes 2949128 | tf_op jit(solution)/shard_map/ppermute | solution.py:306
  50.3 5.0 %collective-permute-start.5 = (bf16[640,768]{1,0:T(8,128)(2,1)S(1)}, bf16[640,768]{1,0:T(8,128)(2,1)}, u32[]{:S(2)}, u32[]{:S(2)}) collective-permute-start(bf16[640,768]{1,0:T(8,128)(2,1)S(1)} %collective-permute-done.from_left.refs_2_), channel_id=1, source_target_pairs={{0,1},{1,0},{2,3},{3,2},{4,5},{5,4},{6,7},{7,6},{8,9},{9,8},{10,11... | collective-permute-start | bytes 2949128 | tf_op jit(solution)/shard_map/ppermute | solution.py:306
  50.3 5.0 %collective-permute-start.6 = (bf16[640,768]{1,0:T(8,128)(2,1)S(1)}, bf16[640,768]{1,0:T(8,128)(2,1)}, u32[]{:S(2)}, u32[]{:S(2)}) collective-permute-start(bf16[640,768]{1,0:T(8,128)(2,1)S(1)} %collective-permute-done.1.from_right.refs_4_), channel_id=1, source_target_pairs={{0,1},{1,0},{2,3},{3,2},{4,5},{5,4},{6,7},{7,6},{8,9},{9,8},{10,11... | collective-permute-start | bytes 2949128 | tf_op jit(solution)/shard_map/ppermute | solution.py:306
  51.0 16.4 %collective-permute-start.2 = (bf16[640,384]{1,0:T(8,128)(2,1)S(1)}, bf16[640,384]{1,0:T(8,128)(2,1)S(1)}, u32[]{:S(2)}, u32[]{:S(2)}) collective-permute-start(bf16[640,384]{1,0:T(8,128)(2,1)S(1)} %get-tuple-element.41), channel_id=1, source_target_pairs={{0,2},{2,4},{4,6},{6,0},{1,3},{3,5},{5,7},{7,1},{8,10},{10,12},{12... | collective-permute-start | bytes 1474568 | tf_op jit(solution)/shard_map/ppermute | solution.py:303
  52.6 14.8 %collective-permute-start.3 = (bf16[640,384]{1,0:T(8,128)(2,1)S(1)}, bf16[640,384]{1,0:T(8,128)(2,1)S(1)}, u32[]{:S(2)}, u32[]{:S(2)}) collective-permute-start(bf16[640,384]{1,0:T(8,128)(2,1)S(1)} %get-tuple-element.42), channel_id=1, source_target_pairs={{0,6},{2,0},{4,2},{6,4},{1,7},{3,1},{5,3},{7,5},{8,14},{10,8},{12,... | collective-permute-start | bytes 1474568 | tf_op jit(solution)/shard_map/ppermute | solution.py:303
  67.4 1.9 %collective-permute-start.7 = (bf16[640,384]{1,0:T(8,128)(2,1)S(1)}, bf16[640,384]{1,0:T(8,128)(2,1)S(1)}, u32[]{:S(2)}, u32[]{:S(2)}) collective-permute-start(bf16[640,384]{1,0:T(8,128)(2,1)S(1)} %collective-permute-done.2.x0), channel_id=1, source_target_pairs={{0,1},{1,0},{2,3},{3,2},{4,5},{5,4},{6,7},{7,6},{8,9},{9,8},{10,11... | collective-permute-start | bytes 1474568 | tf_op jit(solution)/shard_map/ppermute | solution.py:306
  67.5 2.6 %collective-permute-start.8 = (bf16[640,384]{1,0:T(8,128)(2,1)S(1)}, bf16[640,384]{1,0:T(8,128)(2,1)S(1)}, u32[]{:S(2)}, u32[]{:S(2)}) collective-permute-start(bf16[640,384]{1,0:T(8,128)(2,1)S(1)} %collective-permute-done.3.d0), channel_id=1, source_target_pairs={{0,1},{1,0},{2,3},{3,2},{4,5},{5,4},{6,7},{7,6},{8,9},{9,8},{10,11... | collective-permute-start | bytes 1474568 | tf_op jit(solution)/shard_map/ppermute | solution.py:306
  73.6 3.8 %collective-permute-start.9 = (bf16[640,384]{1,0:T(8,128)(2,1)S(1)}, bf16[640,384]{1,0:T(8,128)(2,1)S(1)}, u32[]{:S(2)}, u32[]{:S(2)}) collective-permute-start(bf16[640,384]{1,0:T(8,128)(2,1)S(1)} %get-tuple-element.53), channel_id=1, source_target_pairs={{0,1},{1,0},{2,3},{3,2},{4,5},{5,4},{6,7},{7,6},{8,9},{9,8},{10,11... | collective-permute-start | bytes 1474568 | tf_op jit(solution)/shard_map/ppermute | solution.py:306
  77.5 9.7 %collective-permute-start.10 = (bf16[3,640,384]{2,1,0:T(8,128)(2,1)S(1)}, bf16[3,640,384]{2,1,0:T(8,128)(2,1)S(1)}, u32[]{:S(2)}, u32[]{:S(2)}) collective-permute-start(bf16[3,640,384]{2,1,0:T(8,128)(2,1)S(1)} %get-tuple-element.57), channel_id=1, source_target_pairs={{0,1},{1,0},{2,3},{3,2},{4,5},{5,4},{6,7},{7,6},{8,9},{9,8},{10,11... | collective-permute-start | bytes 4423688 | tf_op jit(solution)/shard_map/ppermute | solution.py:306
  77.9 9.2 %collective-permute-start.11 = (bf16[320,384]{1,0:T(8,128)(2,1)S(1)}, bf16[320,384]{1,0:T(8,128)(2,1)S(1)}, u32[]{:S(2)}, u32[]{:S(2)}) collective-permute-start(bf16[320,384]{1,0:T(8,128)(2,1)S(1)} %get-tuple-element.58), channel_id=1, source_target_pairs={{0,2},{2,4},{4,6},{6,0},{1,3},{3,5},{5,7},{7,1},{8,10},{10,12},{12... | collective-permute-start | bytes 737288 | tf_op jit(solution)/shard_map/ppermute | solution.py:303
  78.5 8.6 %collective-permute-start.12 = (bf16[320,384]{1,0:T(8,128)(2,1)S(1)}, bf16[320,384]{1,0:T(8,128)(2,1)S(1)}, u32[]{:S(2)}, u32[]{:S(2)}) collective-permute-start(bf16[320,384]{1,0:T(8,128)(2,1)S(1)} %get-tuple-element.59), channel_id=1, source_target_pairs={{0,6},{2,0},{4,2},{6,4},{1,7},{3,1},{5,3},{7,5},{8,14},{10,8},{12,... | collective-permute-start | bytes 737288 | tf_op jit(solution)/shard_map/ppermute | solution.py:303
  87.5 13.7 %collective-permute-start.13 = (bf16[640,384]{1,0:T(8,128)(2,1)S(1)}, bf16[640,384]{1,0:T(8,128)(2,1)S(1)}, u32[]{:S(2)}, u32[]{:S(2)}) collective-permute-start(bf16[640,384]{1,0:T(8,128)(2,1)S(1)} %get-tuple-element.61), channel_id=1, source_target_pairs={{0,2},{2,4},{4,6},{6,0},{1,3},{3,5},{5,7},{7,1},{8,10},{10,12},{12... | collective-permute-start | bytes 1474568 | tf_op jit(solution)/shard_map/ppermute | solution.py:303
  87.8 13.4 %collective-permute-start.14 = (bf16[640,384]{1,0:T(8,128)(2,1)S(1)}, bf16[640,384]{1,0:T(8,128)(2,1)S(1)}, u32[]{:S(2)}, u32[]{:S(2)}) collective-permute-start(bf16[640,384]{1,0:T(8,128)(2,1)S(1)} %get-tuple-element.62), channel_id=1, source_target_pairs={{0,6},{2,0},{4,2},{6,4},{1,7},{3,1},{5,3},{7,5},{8,14},{10,8},{12,... | collective-permute-start | bytes 1474568 | tf_op jit(solution)/shard_map/ppermute | solution.py:303
  90.8 14.3 %all-to-all-start.2 = ((bf16[16,128,128]{2,1,0:T(8,128)(2,1)}), bf16[16,128,128]{2,1,0:T(8,128)(2,1)S(1)}, u32[]{:S(2)}, u32[]{:S(2)}) async-start(bf16[16,128,128]{2,1,0:T(8,128)(2,1)} %shard_map.158.refs_9_), calls=%async_computation.2 | async-start | bytes 1048576 | tf_op jit(solution)/shard_map/all_to_all | solution.py:347
  105.1 13.5 %all-to-all-start.3 = ((bf16[16,40,384]{2,1,0:T(8,128)(2,1)}), bf16[16,40,384]{2,1,0:T(8,128)(2,1)S(1)}, u32[]{:S(2)}, u32[]{:S(2)}) async-start(bf16[16,40,384]{2,1,0:T(8,128)(2,1)} %bitcast.6), calls=%async_computation.3 | async-start | bytes 983040 | tf_op jit(solution)/shard_map/all_to_all | solution.py:405

commit v6 on v5

--- a/solution.py
+++ b/solution.py
@@ -15,7 +15,8 @@
 CTX = 16
 CAP = 40
 ROWS = CTX * CAP
-CUT = ROWS // 2
+PART = ROWS // 2
+CUT = PART // 2
 FEAT = 384
 HID = 640
 MARKS = 16
@@ -210,61 +211,73 @@
 
 ORDER = ((0, 0), (0, 1), (-1, 0), (-1, 1), (1, 0), (1, 1), (2, 0), (2, 1))
 ALL = len(ORDER) * FEAT
-EARLY = 6
 OUT_ORDER = (2, -1, 1, 0)
 
 
-def forward_kernel(from_left, from_right, x_ref, d_ref, sems):
-    pairs = ((from_left.at[:, pl.ds(0, FEAT)], x_ref), (from_right.at[:, pl.ds(FEAT, FEAT)], d_ref))
+def split_kernel(rows, first, second, sems):
+    pairs = [(rows.at[pl.ds(i * PART, PART), :], out) for i, out in enumerate((first, second))]
     for copy in fetch(pairs, sems):
         copy.wait()
 
 
-def expert_early_kernel(place, *refs):
-    chunks, (wg, wu, wd) = refs[:EARLY], refs[EARLY : EARLY + 3]
-    (pre, hid, cat, down_late), (xs, ds, down_w, sems) = refs[-8:-4], refs[-4:]
-    stages = ([], [], [], [])
+def lay_out(chunks, xs, ds):
+    moves = []
+    for i, chunk in enumerate(chunks):
+        side = pl.ds(i * FEAT, FEAT)
+        moves.append(((chunk.at[:, pl.ds(FEAT, FEAT)], ds.at[:, side]), (chunk.at[:, pl.ds(0, FEAT)], xs.at[:, side])))
+    return moves
+
+
+def middle(gate, up, hid, mid_ref):
+    s = 1.0 / (1.0 + jnp.exp(-gate))
+    mid_ref[:, :HID] = (hid * up * s * (1.0 + gate * (1.0 - s))).astype(BF)
+    mid_ref[:, HID:] = (hid * gate * s).astype(BF)
+
+
+def expert_first_kernel(place, *refs):
+    chunks, (wg, wu, wd) = refs[:8], refs[8:11]
+    (mid_ref, far_ref, cat, down), (xs, ds, sems) = refs[-7:-3], refs[-3:]
+    stages = ([], [], [])
+    moves = lay_out(chunks, xs, ds)
     for i, (offset, sibling) in enumerate(ORDER):
         block = feature_block(place, offset, sibling)
         side = pl.ds(i * FEAT, FEAT)
-        late = i >= EARLY
-        if not late:
-            stages[0].append((wd.at[0, :, pl.ds(block, FEAT)], down_w.at[:, side]))
-            stages[0].append((chunks[i].at[:, pl.ds(FEAT, FEAT)], ds.at[:, side]))
-            stages[1].append((chunks[i].at[:, pl.ds(0, FEAT)], xs.at[:, side]))
-        else:
-            stages[3].append((wd.at[0, :, pl.ds(block, FEAT)], down_late.at[:, pl.ds((i - EARLY) * FEAT, FEAT)]))
-        stages[3 if late else 1].append((wg.at[0, pl.ds(block, FEAT), :], cat.at[side, pl.ds(0, HID)]))
-        stages[3 if late else 2].append((wu.at[0, pl.ds(block, FEAT), :], cat.at[side, pl.ds(HID, HID)]))
-    copies = fetch(stages[0] + stages[1] + stages[2] + stages[3], sems)
+        stages[0].extend([(wd.at[0, :, pl.ds(block, FEAT)], down.at[:, side]), moves[i][0]])
+        stages[1].extend([(wg.at[0, pl.ds(block, FEAT), :], cat.at[side, pl.ds(0, HID)]), moves[i][1]])
+        stages[2].append((wu.at[0, pl.ds(block, FEAT), :], cat.at[side, pl.ds(HID, HID)]))
+    copies = fetch(stages[0] + stages[1] + stages[2], sems)
 
     def ready(n):
         for _ in range(n):
             copies.pop(0).wait()
 
     ready(len(stages[0]))
-    hid[...] = mm(ds[...], down_w[...], NT)
+    hid = mm(ds[...], down[...], NT)
     ready(len(stages[1]))
-    pre[:, :HID] = mm(xs[...], cat[: EARLY * FEAT, :HID])
+    gate = mm(xs[...], cat[:, :HID])
     ready(len(stages[2]))
-    pre[:, HID:] = mm(xs[...], cat[: EARLY * FEAT, HID:])
-    ready(len(stages[3]))
+    up = mm(xs[...], cat[:, HID:])
+    middle(gate, up, hid, mid_ref)
+    far_ref[...] = out_block(mid_ref, cat, OUT_ORDER[0], 1).astype(BF)
+
+
+def expert_second_kernel(*refs):
+    chunks, (cat, down, mid_ref, far_ref, xs, ds, sems) = refs[:8], refs[8:]
+    moves = lay_out(chunks, xs, ds)
+    copies = fetch([m[0] for m in moves] + [m[1] for m in moves], sems)
+    for copy in copies[:8]:
+        copy.wait()
+    hid = mm(ds[...], down[...], NT)
+    for copy in copies[8:]:
+        copy.wait()
+    both = mm(xs[...], cat[...])
+    middle(both[:, :HID], both[:, HID:], hid, mid_ref)
+    far_ref[...] = out_block(mid_ref, cat, OUT_ORDER[0], 1).astype(BF)
 
 
 def out_block(mid_ref, cat, offset, sibling):
     at = ORDER.index((offset, sibling)) * FEAT
     return mm(mid_ref[...], cat[at : at + FEAT, :], NT)
-
-
-def expert_mid_kernel(pre, hid_ref, x0, d0, x1, d1, cat, down_late, mid_ref, far_ref):
-    late = slice(EARLY * FEAT, None)
-    hid = hid_ref[...] + mm(jnp.concatenate([d0[...], d1[...]], axis=1), down_late[...], NT)
-    both = pre[...] + mm(jnp.concatenate([x0[...], x1[...]], axis=1), cat[late, :])
-    gate, up = both[:, :HID], both[:, HID:]
-    s = 1.0 / (1.0 + jnp.exp(-gate))
-    mid_ref[:, :HID] = (hid * up * s * (1.0 + gate * (1.0 - s))).astype(BF)
-    mid_ref[:, HID:] = (hid * gate * s).astype(BF)
-    far_ref[...] = out_block(mid_ref, cat, OUT_ORDER[0], 1).astype(BF)
 
 
 def expert_out_kernel(mid_ref, cat, far_ref, rest_ref):
@@ -273,22 +286,27 @@
         rest_ref[i] = out_block(mid_ref, cat, offset, 1).astype(BF)
 
 
-def expert_rest_kernel(mid_ref, cat, rest_ref):
-    for i, offset in enumerate(OUT_ORDER[1:]):
-        rest_ref[i] = out_block(mid_ref, cat, offset, 0)
-
-
 def far_kernel(mine, away, right_ref, left_ref):
     right_ref[...] = (mine[:CUT] + away[:CUT].astype(F32)).astype(BF)
     left_ref[...] = (mine[CUT:] + away[CUT:].astype(F32)).astype(BF)
 
 
-def near_kernel(mine, away, via_right, via_left, left_ref, right_ref, here_ref):
-    left_ref[:CUT] = (mine[0, :CUT] + away[0, :CUT].astype(F32)).astype(BF)
-    left_ref[CUT:] = (mine[0, CUT:] + away[0, CUT:].astype(F32) + via_left[...].astype(F32)).astype(BF)
-    right_ref[:CUT] = (mine[1, :CUT] + away[1, :CUT].astype(F32) + via_right[...].astype(F32)).astype(BF)
-    right_ref[CUT:] = (mine[1, CUT:] + away[1, CUT:].astype(F32)).astype(BF)
-    here_ref[...] = mine[2] + away[2].astype(F32)
+def near_kernel(mid_ref, cat, away, via_right, via_left, left_ref, right_ref):
+    left, right = [out_block(mid_ref, cat, offset, 0) + away[i].astype(F32) for i, offset in enumerate(OUT_ORDER[1:3])]
+    left_ref[:CUT] = left[:CUT].astype(BF)
+    left_ref[CUT:] = (left[CUT:] + via_left[...].astype(F32)).astype(BF)
+    right_ref[:CUT] = (right[:CUT] + via_right[...].astype(F32)).astype(BF)
+    right_ref[CUT:] = right[CUT:].astype(BF)
+
+
+def here_kernel(mid_ref, cat, away, here_ref):
+    here_ref[...] = out_block(mid_ref, cat, OUT_ORDER[3], 0) + away[2].astype(F32)
+
+
+def sum_kernel(here0, left0, right0, here1, left1, right1, out_ref):
+    for i, (here, left, right) in enumerate(((here0, left0, right0), (here1, left1, right1))):
+        total = here[...] + left[...].astype(F32) + right[...].astype(F32)
+        out_ref[i * PART : (i + 1) * PART] = total.astype(BF)
 
 
 def local(
@@ -297,7 +315,8 @@
     S = jax.ShapeDtypeStruct
     place = jnp.stack([lax.axis_index("x"), lax.axis_index("core")]).astype(I32)
     smem = pl.BlockSpec(memory_space=pltpu.SMEM)
-    block = S((ROWS, FEAT), BF)
+    block = S((PART, FEAT), BF)
+    tie = lax.optimization_barrier
 
     def ring(value, way):
         return lax.ppermute(value, "x", way)
@@ -315,7 +334,15 @@
         limit=6,
     )(in_hbm(expert_ids.T), in_hbm(moe_input), in_hbm(moe_cotangent))
     own = lax.all_to_all(rows.reshape(CTX, CAP, 2 * FEAT), "ctx", 0, 0, tiled=True).reshape(ROWS, 2 * FEAT)
-    from_left, from_right = ring(own, RIGHT), ring(own, LEFT)
+    halves = call(
+        split_kernel,
+        (S((PART, 2 * FEAT), BF),) * 2,
+        [anywhere()],
+        [pltpu.SemaphoreType.DMA((2,))],
+        size=2 * MIB,
+        limit=4,
+    )(own)
+    left0, right0 = ring(halves[0], RIGHT), ring(halves[0], LEFT)
 
     branch = [in_hbm(a) for a in (log_decay, doc_ids.reshape(1, TOK), queries, keys, values, out_grad)]
     held = [pltpu.VMEM((HEADS, TOK), F32), pltpu.VMEM((1, TOK), I32)] + [pltpu.VMEM((TOK, HEADS * HD), BF)] * 4
@@ -330,20 +357,90 @@
         limit=8,
     )(*branch, own)
     arrived = lax.all_to_all(message, "ctx", 0, 0, tiled=True)
-    from_left, from_right, arrived = lax.optimization_barrier((from_left, from_right, arrived))
-
-    x_far, d_far = call(
-        forward_kernel,
-        (block, block),
-        [anywhere()] * 2,
-        [pltpu.SemaphoreType.DMA((2,))],
-        size=2 * MIB,
-        limit=4,
-    )(from_left, from_right)
-    x_far, d_far = ring(x_far, RIGHT), ring(d_far, LEFT)
-    early = [c for a in (own, from_left, from_right) for c in (a, swap(a))]
+    left0, right0, message, own1 = tie((left0, right0, message, halves[1]))
+    far0, right1 = ring(left0, RIGHT), ring(own1, LEFT)
+    early0 = [c for a in (halves[0], left0, right0) for c in (a, swap(a))]
+    far0, right1, arrived, own1 = tie((far0, right1, arrived, own1))
+    left1, far1 = ring(own1, RIGHT), ring(right1, LEFT)
 
     scanned = call(scan_kernel, S((CTX, HD, HD), BF), [vmem()], flops=MIB, size=MIB, limit=4)(arrived)
+    wide = S((PART, 2 * HID), BF)
+    side = [pltpu.VMEM((PART, ALL), BF)] * 2
+    mid0, away0, cat, down = call(
+        expert_first_kernel,
+        (wide, block, S((ALL, 2 * HID), BF), S((HID, ALL), BF)),
+        [smem] + [anywhere()] * 12,
+        side + [pltpu.SemaphoreType.DMA((5 * len(ORDER),))],
+        flops=7 * PART * HID * ALL,
+        size=24 * MIB,
+        limit=28,
+    )(place, *early0, far0, swap(far0), *[in_hbm(w) for w in (w_gate, w_up, w_down)], scanned)
+
+    def out_sums(mid, away_far):
+        mine_far, rest = call(
+            expert_out_kernel,
+            (S((PART, FEAT), F32), S((RINGX - 1, PART, FEAT), BF)),
+            [vmem()] * 2,
+            flops=4 * PART * HID * RINGX * FEAT,
+            size=6 * MIB,
+            limit=14,
+        )(mid, cat)
+        part = S((CUT, FEAT), BF)
+        return call(far_kernel, (part, part), [vmem()] * 2, size=2 * MIB, flops=MIB, limit=6)(mine_far, swap(away_far)), rest
+
+    def near_sums(mid, rest, via):
+        return call(
+            near_kernel,
+            (block, block),
+            [vmem()] * 5,
+            flops=2 * PART * HID * RINGX * FEAT,
+            size=8 * MIB,
+            limit=14,
+        )(mid, cat, rest, *via)
+
+    def here_sum(mid, rest):
+        return call(
+            here_kernel,
+            S((PART, FEAT), F32),
+            [vmem()] * 3,
+            flops=PART * HID * RINGX * FEAT,
+            size=6 * MIB,
+            limit=14,
+        )(mid, cat, rest)
+
+    left1, far1, away0 = tie((left1, far1, away0))
+    ends0, rest0 = out_sums(mid0, away0)
+    own1_s = swap(own1)
+    ends0, rest0, own1 = tie((ends0, rest0, own1))
+    via0 = ring(ends0[0], RIGHT), ring(ends0[1], LEFT)
+    rest0 = swap(rest0)
+    mid1, away1 = call(
+        expert_second_kernel,
+        (wide, block),
+        [anywhere()] * 8 + [vmem()] * 2,
+        side + [pltpu.SemaphoreType.DMA((16,))],
+        flops=7 * PART * HID * ALL,
+        size=20 * MIB,
+        limit=28,
+    )(own1, own1_s, *[c for a in (left1, right1, far1) for c in (a, swap(a))], cat, down)
+    via0, rest0, mid0, mid1 = tie((via0, rest0, mid0, mid1))
+    near0 = near_sums(mid0, rest0, via0)
+    near0, mid0, mid1 = tie((near0, mid0, mid1))
+    here0 = here_sum(mid0, rest0)
+    mid1, here0 = tie((mid1, here0))
+    ends1, rest1 = out_sums(mid1, away1)
+    ends1, rest1, mid1 = tie((ends1, rest1, mid1))
+    via1 = ring(ends1[0], RIGHT), ring(ends1[1], LEFT)
+    pieces0 = here0, ring(near0[1], RIGHT), ring(near0[0], LEFT)
+    via1, pieces0 = tie((via1, pieces0))
+    rest1 = swap(rest1)
+    near1 = near_sums(mid1, rest1, via1)
+    near1, mid1 = tie((near1, mid1))
+    here1 = here_sum(mid1, rest1)
+    here1, scanned = tie((here1, scanned))
+    pieces = *pieces0, here1, ring(near1[1], RIGHT), ring(near1[0], LEFT)
+    summed = call(sum_kernel, S((ROWS, FEAT), BF), [vmem()] * 6, size=4 * MIB, flops=MIB, limit=12)(*pieces)
+
     carried = lax.all_to_all(scanned, "ctx", 0, 0, tiled=True)
     grads = call(
         attention_kernel,
@@ -355,53 +452,6 @@
         limit=12,
     )(*branch, carried)
 
-    n = EARLY * FEAT
-    pre, hid, cat, down_late = call(
-        expert_early_kernel,
-        (S((ROWS, 2 * HID), F32), S((ROWS, HID), F32), S((ALL, 2 * HID), BF), S((HID, ALL - n), BF)),
-        [smem] + [anywhere()] * (EARLY + 4),
-        [pltpu.VMEM((ROWS, n), BF)] * 2 + [pltpu.VMEM((HID, n), BF), pltpu.SemaphoreType.DMA((36,))],
-        flops=6 * ROWS * HID * n,
-        size=24 * MIB,
-        limit=28,
-    )(place, *early, *[in_hbm(w) for w in (w_gate, w_up, w_down)], scanned)
-    x_far, d_far, pre = lax.optimization_barrier((x_far, d_far, pre))
-    rest = (RINGX - 1, ROWS, FEAT)
-    mid, away_far = call(
-        expert_mid_kernel,
-        (S((ROWS, 2 * HID), BF), block),
-        [vmem()] * 8,
-        flops=8 * ROWS * HID * 2 * FEAT,
-        size=12 * MIB,
-        limit=32,
-    )(pre, hid, x_far, d_far, swap(x_far), swap(d_far), cat, down_late)
-    away_far = swap(away_far)
-    mine_far, away_rest = call(
-        expert_out_kernel,
-        (S((ROWS, FEAT), F32), S(rest, BF)),
-        [vmem()] * 2,
-        flops=4 * ROWS * HID * RINGX * FEAT,
-        size=8 * MIB,
-        limit=18,
-    )(mid, cat)
-
-    half = S((CUT, FEAT), BF)
-    to_right, to_left = call(far_kernel, (half, half), [vmem()] * 2, size=2 * MIB, flops=MIB, limit=8)(mine_far, away_far)
-    mid, away_rest, to_right, to_left = lax.optimization_barrier((mid, away_rest, to_right, to_left))
-    away_rest = swap(away_rest)
-    mine_rest = call(
-        expert_rest_kernel,
-        S(rest, F32),
-        [vmem()] * 2,
-        flops=3 * ROWS * HID * RINGX * FEAT,
-        size=8 * MIB,
-        limit=18,
-    )(mid, cat)
-    via_right, via_left = ring(to_right, RIGHT), ring(to_left, LEFT)
-    to_left, to_right, here = call(
-        near_kernel, (block, block, S((ROWS, FEAT), F32)), [vmem()] * 4, size=5 * MIB, flops=MIB, limit=16
-    )(mine_rest, away_rest, via_right, via_left)
-    summed = (here + ring(to_right, RIGHT).astype(F32) + ring(to_left, LEFT).astype(F32)).astype(BF)
     back = lax.all_to_all(summed.reshape(CTX, CAP, FEAT), "ctx", 0, 0, tiled=True)
     grad_moe = call(
         combine_kernel,

time: 121 us -> 133 us (1.099)
  starting transfers between devices: 25.9 us -> 39.3 us
  waiting for transfers between devices: 32.1 us -> 27.2 us
  Pallas kernels: 36.4 us -> 40.4 us
    ppermute x8 -> x14, starting transfers between devices: 13.1 us -> 22.8 us  [ring(): return lax.ppermute(value, 'x', way)]
    all_to_all x1, waiting for transfers between devices: 10.7 us -> 4.81 us  [local(): arrived = lax.all_to_all(message, 'ctx', 0, 0, tiled=True)]
    pallas_call x7 -> x12, Pallas kernels: 22.4 us -> 26.4 us  [the longest x1 10.8 us: local(): call(expert_first_kernel, (wide, block, S((ALL, 2 * HID), BF), S((HID, AL...]
    ppermute x8 -> x14, waiting for transfers between devices: 12.1 us -> 15.9 us  [ring(): return lax.ppermute(value, 'x', way)]
    ppermute x7 -> x12, waiting for transfers between devices: 2.07 us -> 0.03 us  [swap(): return lax.ppermute(value, 'core', SWAP)]
    all_to_all x1, starting transfers between devices: 3.57 us -> 5.07 us  [local(): carried = lax.all_to_all(scanned, 'ctx', 0, 0, tiled=True)]
    ppermute x7 -> x12, starting transfers between devices: 1.85 us -> 2.84 us  [swap(): return lax.ppermute(value, 'core', SWAP)]
  transfers between devices with their start and end apart: 18 -> 29, of which waited for: 8 -> 7; matrix products, arithmetic and copies ran while one was open for 1% -> 0% of each run, Pallas kernels for 24% -> 26%
where the time goes in v6:
time: 133 us; the launch traced here: 132 us
  Pallas kernels  40.4 us (30%)
  starting transfers between devices  39.3 us (30%)
  waiting for transfers between devices  27.2 us (20%)
  blocking collectives  24.4 us (18%)
    all_to_all x1, blocking collectives, local(): lax.all_to_all(rows.reshape(CTX, CAP, 2 * FEAT), 'ctx', 0, 0, tiled=True)  24.4 us
    ppermute x14, starting transfers between devices, ring(): return lax.ppermute(value, 'x', way)  22.8 us
    ppermute x14, waiting for transfers between devices, ring(): return lax.ppermute(value, 'x', way)  15.9 us
    pallas_call x1, Pallas kernels, local(): call(expert_first_kernel, (wide, block, S((ALL, 2 * HID), BF), S((HID, AL...  10.8 us
    pallas_call x1, Pallas kernels, local(): call(expert_second_kernel, (wide, block), [anywhere()] * 8 + [vmem()] * 2...  6.89 us
    pallas_call x1, Pallas kernels, local(): call(attention_kernel, (S((TOK, HEADS * HD), BF),) * 3, [anywhere()] * 6...  5.4 us
    all_to_all x1, starting transfers between devices, local(): carried = lax.all_to_all(scanned, 'ctx', 0, 0, tiled=True)  5.07 us
    all_to_all x1, starting transfers between devices, local(): lax.all_to_all(summed.reshape(CTX, CAP, FEAT), 'ctx', 0, 0, tiled=True)  4.97 us
  transfers between devices with their start and end apart: 29, of which 7 were waited for; matrix products, arithmetic and copies ran while one was open for 0% of the time, Pallas kernels for 26%

profile of v6, /device:TPU:0, one launch (start us, length us, event | category | flops | bytes accessed | tf_op | source)
XLA Modules:
  0.0 132.4 jit_solution(17317086710037616498)
XLA Ops:
  0.6 1.7 %shard_map.156 = (bf16[640,768]{1,0:T(8,128)(2,1)S(1)}, s32[2,256]{1,0:T(2,128)}) custom-call(s32[2,256]{1,0:T(2,128)} %bitcast.15, bf16[256,384]{1,0:T(8,128)(2,1)} %x_hbm.1, bf16[256,384]{1,0:T(8,128)(2,1)} %d_hbm.1), custom_call_target="tpu_custom_call" | custom-call | flops 251658240 | bytes 2097152 | tf_op jit(solution)/shard_map/pallas_call | solution.py:327
  2.4 24.4 %all_to_all.20 = bf16[16,40,768]{2,1,0:T(8,128)(2,1)S(1)} all-to-all(bf16[16,40,768]{2,1,0:T(8,128)(2,1)S(1)} %bitcast.11), channel_id=1, replica_groups=mesh['ctx'=16,'x'=4,'core'=2] {'ctx'}, dimensions={0} | all-to-all | bytes 1966080 | tf_op jit(solution)/shard_map/all_to_all | solution.py:336
  26.7 0.6 shard_map.157
  27.4 1.6 %collective-permute-start.1 = (bf16[320,768]{1,0:T(8,128)(2,1)S(1)}, bf16[320,768]{1,0:T(8,128)(2,1)S(1)}, u32[]{:S(2)}, u32[]{:S(2)}) collective-permute-start(bf16[320,768]{1,0:T(8,128)(2,1)S(1)} %get-tuple-element.69.refs_0_), channel_id=1, source_target_pairs={{0,2},{2,4},{4,6},{6,0},{1,3},{3,5},{5,7},{7,1},{8,10},{10,12},{12... | collective-permute-start | bytes 1474568 | tf_op jit(solution)/shard_map/ppermute | solution.py:322
  28.9 1.7 %collective-permute-start.2 = (bf16[320,768]{1,0:T(8,128)(2,1)S(1)}, bf16[320,768]{1,0:T(8,128)(2,1)S(1)}, u32[]{:S(2)}, u32[]{:S(2)}) collective-permute-start(bf16[320,768]{1,0:T(8,128)(2,1)S(1)} %get-tuple-element.69.refs_0_), channel_id=1, source_target_pairs={{0,6},{2,0},{4,2},{6,4},{1,7},{3,1},{5,3},{7,5},{8,14},{10,8},{12,... | collective-permute-start | bytes 1474568 | tf_op jit(solution)/shard_map/ppermute | solution.py:322
  30.7 3.9 %shard_map.158 = bf16[16,144,128]{2,1,0:T(8,128)(2,1)} custom-call(f32[8,256]{1,0:T(8,128)} %refs_0_.3, s32[1,256]{1,0:T(1,128)} %bitcast.13, bf16[256,1024]{1,0:T(8,128)(2,1)} %refs_2_.3, bf16[256,1024]{1,0:T(8,128)(2,1)} %refs_3_.3, bf16[256,1024]{1,0:T(8,128)(2,1)} %refs_4_.3, bf16[256,1024]{1,0:T(8,128)(2,1)} %refs_5_.3, bf16[640,768]{1,0:T(8,128)(2,1)S(1)} %bitcast.10), custom_call_target="tpu_custom_call" | custom-call | flops 134217728 | bytes 3145728 | tf_op jit(solution)/shard_map/pallas_call | solution.py:350
  34.6 3.6 %all-to-all-start.1 = ((bf16[16,144,128]{2,1,0:T(8,128)(2,1)}), bf16[16,144,128]{2,1,0:T(8,128)(2,1)S(1)}, u32[]{:S(2)}, u32[]{:S(2)}) async-start(bf16[16,144,128]{2,1,0:T(8,128)(2,1)} %shard_map.158), calls=%async_computation.1 | async-start | bytes 1179648 | tf_op jit(solution)/shard_map/all_to_all | solution.py:359
  38.2 2.3 %collective-permute-done.1.refs_2_ = bf16[320,768]{1,0:T(8,128)(2,1)S(1)} collective-permute-done((bf16[320,768]{1,0:T(8,128)(2,1)S(1)}, bf16[320,768]{1,0:T(8,128)(2,1)S(1)}, u32[]{:S(2)}, u32[]{:S(2)}) %collective-permute-start.1) | collective-permute-done | bytes 491552 | tf_op jit(solution)/shard_map/ppermute | solution.py:322
  40.5 1.5 %collective-permute-start.5 = (bf16[320,768]{1,0:T(8,128)(2,1)S(1)}, bf16[320,768]{1,0:T(8,128)(2,1)S(1)}, u32[]{:S(2)}, u32[]{:S(2)}) collective-permute-start(bf16[320,768]{1,0:T(8,128)(2,1)S(1)} %collective-permute-done.1.refs_2_), channel_id=1, source_target_pairs={{0,2},{2,4},{4,6},{6,0},{1,3},{3,5},{5,7},{7,1},{8,10},{10,12},{12... | collective-permute-start | bytes 1474568 | tf_op jit(solution)/shard_map/ppermute | solution.py:322
  42.0 1.7 %collective-permute-start.6 = (bf16[320,768]{1,0:T(8,128)(2,1)S(1)}, bf16[320,768]{1,0:T(8,128)(2,1)S(1)}, u32[]{:S(2)}, u32[]{:S(2)}) collective-permute-start(bf16[320,768]{1,0:T(8,128)(2,1)S(1)} %get-tuple-element.89.refs_0_), channel_id=1, source_target_pairs={{0,6},{2,0},{4,2},{6,4},{1,7},{3,1},{5,3},{7,5},{8,14},{10,8},{12,... | collective-permute-start | bytes 1474568 | tf_op jit(solution)/shard_map/ppermute | solution.py:322
  43.7 0.5 collective-permute-start.3
  44.2 4.8 %all-to-all-done.1.in_ref = bf16[16,144,128]{2,1,0:T(8,128)(2,1)S(1)} async-done(((bf16[16,144,128]{2,1,0:T(8,128)(2,1)}), bf16[16,144,128]{2,1,0:T(8,128)(2,1)S(1)}, u32[]{:S(2)}, u32[]{:S(2)}) %all-to-all-start.1) | async-done | bytes 589856 | tf_op jit(solution)/shard_map/all_to_all | solution.py:359
  49.1 3.5 %collective-permute-done.5.refs_6_ = bf16[320,768]{1,0:T(8,128)(2,1)S(1)} collective-permute-done((bf16[320,768]{1,0:T(8,128)(2,1)S(1)}, bf16[320,768]{1,0:T(8,128)(2,1)S(1)}, u32[]{:S(2)}, u32[]{:S(2)}) %collective-permute-start.5) | collective-permute-done | bytes 491552 | tf_op jit(solution)/shard_map/ppermute | solution.py:322
  52.6 0.9 collective-permute-start.8
  53.5 2.3 %collective-permute-start.9 = (bf16[320,768]{1,0:T(8,128)(2,1)S(1)}, bf16[320,768]{1,0:T(8,128)(2,1)S(1)}, u32[]{:S(2)}, u32[]{:S(2)}) collective-permute-start(bf16[320,768]{1,0:T(8,128)(2,1)S(1)} %collective-permute-done.6.refs_4_), channel_id=1, source_target_pairs={{0,6},{2,0},{4,2},{6,4},{1,7},{3,1},{5,3},{7,5},{8,14},{10,8},{12,... | collective-permute-start | bytes 1474568 | tf_op jit(solution)/shard_map/ppermute | solution.py:322
  55.9 0.1 pad_add_fusion.place
  55.9 1.0 shard_map.159.refs_11_
  56.9 10.8 %shard_map.160 = (bf16[320,1280]{1,0:T(8,128)(2,1)S(1)}, bf16[320,384]{1,0:T(8,128)(2,1)S(1)}, bf16[3072,1280]{1,0:T(8,128)(2,1)S(1)}, bf16[640,3072]{1,0:T(8,128)(2,1)S(1)}) custom-call(s32[2]{0:T(128)S(1)} %pad_add_fusion.place, bf16[320,768]{1,0:T(8,128)(2,1)S(1)} %get-tuple-element.69.refs_0_, bf16[320,768]{1,0:T(8,128)(2,1)} %collective-permute-done.refs_1_, ...), custom_call_target="tpu_custom_call" | custom-call | flops 4404019200 | bytes 25165824 | tf_op jit(solution)/shard_map/pallas_call | solution.py:369
  67.7 0.1 collective-permute-start.10
  67.8 0.5 collective-permute-start.14
  68.3 0.3 collective-permute-start.16
  68.6 0.2 collective-permute-start.15
  68.8 0.3 collective-permute-start.17
  69.1 1.9 %shard_map.161 = (f32[320,384]{1,0:T(8,128)S(1)}, bf16[3,320,384]{2,1,0:T(8,128)(2,1)S(1)}) custom-call(bf16[320,1280]{1,0:T(8,128)(2,1)S(1)} %get-tuple-element.102.mid_ref, bf16[3072,1280]{1,0:T(8,128)(2,1)S(1)} %get-tuple-element.77.cat.refs_8_), custom_call_target="tpu_custom_call" | custom-call | flops 1258291200 | bytes 6291456 | tf_op jit(solution)/shard_map/pallas_call | solution.py:380
  71.0 0.3 collective-permute-start.13
  71.4 0.8 collective-permute-start.11
  72.2 2.4 %collective-permute-start.12 = (bf16[160,384]{1,0:T(8,128)(2,1)S(1)}, bf16[160,384]{1,0:T(8,128)(2,1)S(1)}, u32[]{:S(2)}, u32[]{:S(2)}) collective-permute-start(bf16[160,384]{1,0:T(8,128)(2,1)S(1)} %get-tuple-element.87), channel_id=1, source_target_pairs={{0,6},{2,0},{4,2},{6,4},{1,7},{3,1},{5,3},{7,5},{8,14},{10,8},{12,... | collective-permute-start | bytes 368648 | tf_op jit(solution)/shard_map/ppermute | solution.py:322
  74.6 6.9 %shard_map.163 = (bf16[320,1280]{1,0:T(8,128)(2,1)S(1)}, bf16[320,384]{1,0:T(8,128)(2,1)S(1)}) custom-call(bf16[320,768]{1,0:T(8,128)(2,1)S(1)} %get-tuple-element.89.refs_0_, bf16[320,768]{1,0:T(8,128)(2,1)S(1)} %collective-permute-done.14.refs_1_, bf16[320,768]{1,0:T(8,128)(2,1)S(1)} %collective-permute-done.8.refs_2_, ...), custom_call_target="tpu_custom_call" | custom-call | flops 4404019200 | bytes 20971520 | tf_op jit(solution)/shard_map/pallas_call | solution.py:417
  81.5 0.1 collective-permute-start.18
  81.6 1.0 shard_map.164
  82.7 0.6 shard_map.165.here0
  83.3 1.9 %shard_map.166 = (f32[320,384]{1,0:T(8,128)S(1)}, bf16[3,320,384]{2,1,0:T(8,128)(2,1)S(1)}) custom-call(bf16[320,1280]{1,0:T(8,128)(2,1)S(1)} %get-tuple-element.120.mid_ref, bf16[3072,1280]{1,0:T(8,128)(2,1)S(1)} %get-tuple-element.77.cat.refs_8_), custom_call_target="tpu_custom_call" | custom-call | flops 1258291200 | bytes 6291456 | tf_op jit(solution)/shard_map/pallas_call | solution.py:380
  85.2 0.6 collective-permute-start.19
  85.8 3.2 %collective-permute-start.23 = (bf16[320,384]{1,0:T(8,128)(2,1)S(1)}, bf16[320,384]{1,0:T(8,128)(2,1)S(1)}, u32[]{:S(2)}, u32[]{:S(2)}) collective-permute-start(bf16[320,384]{1,0:T(8,128)(2,1)S(1)} %get-tuple-element.115), channel_id=1, source_target_pairs={{0,6},{2,0},{4,2},{6,4},{1,7},{3,1},{5,3},{7,5},{8,14},{10,8},{12,... | collective-permute-start | bytes 737288 | tf_op jit(solution)/shard_map/ppermute | solution.py:322
  89.0 3.2 %collective-permute-start.21 = (bf16[160,384]{1,0:T(8,128)(2,1)S(1)}, bf16[160,384]{1,0:T(8,128)(2,1)S(1)}, u32[]{:S(2)}, u32[]{:S(2)}) collective-permute-start(bf16[160,384]{1,0:T(8,128)(2,1)S(1)} %get-tuple-element.112), channel_id=1, source_target_pairs={{0,6},{2,0},{4,2},{6,4},{1,7},{3,1},{5,3},{7,5},{8,14},{10,8},{12,... | collective-permute-start | bytes 368648 | tf_op jit(solution)/shard_map/ppermute | solution.py:322
  92.2 5.3 %collective-permute-done.20.via_right = bf16[160,384]{1,0:T(8,128)(2,1)S(1)} collective-permute-done((bf16[160,384]{1,0:T(8,128)(2,1)S(1)}, bf16[160,384]{1,0:T(8,128)(2,1)S(1)}, u32[]{:S(2)}, u32[]{:S(2)}) %collective-permute-start.20) | collective-permute-done | bytes 122912 | tf_op jit(solution)/shard_map/ppermute | solution.py:322
  97.6 1.0 shard_map.168
  98.6 0.6 shard_map.169.here1
  99.2 5.1 %all-to-all-start.2 = ((bf16[16,128,128]{2,1,0:T(8,128)(2,1)}), bf16[16,128,128]{2,1,0:T(8,128)(2,1)S(1)}, u32[]{:S(2)}, u32[]{:S(2)}) async-start(bf16[16,128,128]{2,1,0:T(8,128)(2,1)} %shard_map.159.refs_11_), calls=%async_computation.2 | async-start | bytes 1048576 | tf_op jit(solution)/shard_map/all_to_all | solution.py:444
  104.3 0.1 collective-permute-start.24
  104.4 3.2 %collective-permute-start.25 = (bf16[320,384]{1,0:T(8,128)(2,1)S(1)}, bf16[320,384]{1,0:T(8,128)(2,1)S(1)}, u32[]{:S(2)}, u32[]{:S(2)}) collective-permute-start(bf16[320,384]{1,0:T(8,128)(2,1)S(1)} %get-tuple-element.130), channel_id=1, source_target_pairs={{0,6},{2,0},{4,2},{6,4},{1,7},{3,1},{5,3},{7,5},{8,14},{10,8},{12,... | collective-permute-start | bytes 737288 | tf_op jit(solution)/shard_map/ppermute | solution.py:322
  107.6 4.8 %collective-permute-done.24.left1 = bf16[320,384]{1,0:T(8,128)(2,1)S(1)} collective-permute-done((bf16[320,384]{1,0:T(8,128)(2,1)S(1)}, bf16[320,384]{1,0:T(8,128)(2,1)S(1)}, u32[]{:S(2)}, u32[]{:S(2)}) %collective-permute-start.24) | collective-permute-done | bytes 245792 | tf_op jit(solution)/shard_map/ppermute | solution.py:322
  112.4 0.9 shard_map.171
  113.3 1.9 %all-to-all-done.2.refs_6_ = bf16[16,128,128]{2,1,0:T(8,128)(2,1)S(1)} async-done(((bf16[16,128,128]{2,1,0:T(8,128)(2,1)}), bf16[16,128,128]{2,1,0:T(8,128)(2,1)S(1)}, u32[]{:S(2)}, u32[]{:S(2)}) %all-to-all-start.2) | async-done | bytes 524320 | tf_op jit(solution)/shard_map/all_to_all | solution.py:444
  115.2 5.0 %all-to-all-start.3 = ((bf16[16,40,384]{2,1,0:T(8,128)(2,1)}), bf16[16,40,384]{2,1,0:T(8,128)(2,1)S(1)}, u32[]{:S(2)}, u32[]{:S(2)}) async-start(bf16[16,40,384]{2,1,0:T(8,128)(2,1)} %bitcast.6), calls=%async_computation.3 | async-start | bytes 983040 | tf_op jit(solution)/shard_map/all_to_all | solution.py:455
  120.2 5.4 %shard_map.170 = (bf16[256,1024]{1,0:T(8,128)(2,1)}, bf16[256,1024]{1,0:T(8,128)(2,1)}, bf16[256,1024]{1,0:T(8,128)(2,1)}) custom-call(f32[8,256]{1,0:T(8,128)} %refs_0_.3, s32[1,256]{1,0:T(1,128)} %bitcast.14, bf16[256,1024]{1,0:T(8,128)(2,1)} %refs_2_.3, bf16[256,1024]{1,0:T(8,128)(2,1)} %refs_3_.3, bf16[256,1024]{1,0:T(8,128)(2,1)} %refs_4_.3, ...), custom_call_target="tpu_custom_call" | custom-call | flops 1073741824 | bytes 4194304 | tf_op jit(solution)/shard_map/pallas_call | solution.py:445
  125.6 4.6 %all-to-all-done.3 = bf16[16,40,384]{2,1,0:T(8,128)(2,1)S(1)} async-done(((bf16[16,40,384]{2,1,0:T(8,128)(2,1)}), bf16[16,40,384]{2,1,0:T(8,128)(2,1)S(1)}, u32[]{:S(2)}, u32[]{:S(2)}) %all-to-all-start.3) | async-done | bytes 491552 | tf_op jit(solution)/shard_map/all_to_all | solution.py:455
  130.2 2.0 %shard_map.172 = bf16[256,384]{1,0:T(8,128)(2,1)} custom-call(bf16[640,384]{1,0:T(8,128)(2,1)S(1)} %bitcast.12, s32[2,256]{1,0:T(2,128)} %get-tuple-element.131.slots_hbm, f32[2,256]{1,0:T(2,128)} %bitcast.16), custom_call_target="tpu_custom_call" | custom-call | flops 251658240 | bytes 1048576 | tf_op jit(solution)/shard_map/pallas_call | solution.py:456
  (29 shorter events, 0.2 us)
Async XLA Ops:
  27.4 13.1 %collective-permute-start.1 = (bf16[320,768]{1,0:T(8,128)(2,1)S(1)}, bf16[320,768]{1,0:T(8,128)(2,1)S(1)}, u32[]{:S(2)}, u32[]{:S(2)}) collective-permute-start(bf16[320,768]{1,0:T(8,128)(2,1)S(1)} %get-tuple-element.69.refs_0_), channel_id=1, source_target_pairs={{0,2},{2,4},{4,6},{6,0},{1,3},{3,5},{5,7},{7,1},{8,10},{10,12},{12... | collective-permute-start | bytes 1474568 | tf_op jit(solution)/shard_map/ppermute | solution.py:322
  28.9 11.5 %collective-permute-start.2 = (bf16[320,768]{1,0:T(8,128)(2,1)S(1)}, bf16[320,768]{1,0:T(8,128)(2,1)S(1)}, u32[]{:S(2)}, u32[]{:S(2)}) collective-permute-start(bf16[320,768]{1,0:T(8,128)(2,1)S(1)} %get-tuple-element.69.refs_0_), channel_id=1, source_target_pairs={{0,6},{2,0},{4,2},{6,4},{1,7},{3,1},{5,3},{7,5},{8,14},{10,8},{12,... | collective-permute-start | bytes 1474568 | tf_op jit(solution)/shard_map/ppermute | solution.py:322
  34.6 14.4 %all-to-all-start.1 = ((bf16[16,144,128]{2,1,0:T(8,128)(2,1)}), bf16[16,144,128]{2,1,0:T(8,128)(2,1)S(1)}, u32[]{:S(2)}, u32[]{:S(2)}) async-start(bf16[16,144,128]{2,1,0:T(8,128)(2,1)} %shard_map.158), calls=%async_computation.1 | async-start | bytes 1179648 | tf_op jit(solution)/shard_map/all_to_all | solution.py:359
  40.5 12.1 %collective-permute-start.5 = (bf16[320,768]{1,0:T(8,128)(2,1)S(1)}, bf16[320,768]{1,0:T(8,128)(2,1)S(1)}, u32[]{:S(2)}, u32[]{:S(2)}) collective-permute-start(bf16[320,768]{1,0:T(8,128)(2,1)S(1)} %collective-permute-done.1.refs_2_), channel_id=1, source_target_pairs={{0,2},{2,4},{4,6},{6,0},{1,3},{3,5},{5,7},{7,1},{8,10},{10,12},{12... | collective-permute-start | bytes 1474568 | tf_op jit(solution)/shard_map/ppermute | solution.py:322
  42.0 10.6 %collective-permute-start.6 = (bf16[320,768]{1,0:T(8,128)(2,1)S(1)}, bf16[320,768]{1,0:T(8,128)(2,1)S(1)}, u32[]{:S(2)}, u32[]{:S(2)}) collective-permute-start(bf16[320,768]{1,0:T(8,128)(2,1)S(1)} %get-tuple-element.89.refs_0_), channel_id=1, source_target_pairs={{0,6},{2,0},{4,2},{6,4},{1,7},{3,1},{5,3},{7,5},{8,14},{10,8},{12,... | collective-permute-start | bytes 1474568 | tf_op jit(solution)/shard_map/ppermute | solution.py:322
  43.7 9.8 %collective-permute-start = (bf16[320,768]{1,0:T(8,128)(2,1)S(1)}, bf16[320,768]{1,0:T(8,128)(2,1)}, u32[]{:S(2)}, u32[]{:S(2)}) collective-permute-start(bf16[320,768]{1,0:T(8,128)(2,1)S(1)} %get-tuple-element.69.refs_0_), channel_id=1, source_target_pairs={{0,1},{1,0},{2,3},{3,2},{4,5},{5,4},{6,7},{7,6},{8,9},{9,8},{10,11... | collective-permute-start | bytes 1474568 | tf_op jit(solution)/shard_map/ppermute | solution.py:325
  43.7 13.2 %collective-permute-start.3 = (bf16[320,768]{1,0:T(8,128)(2,1)S(1)}, bf16[320,768]{1,0:T(8,128)(2,1)}, u32[]{:S(2)}, u32[]{:S(2)}) collective-permute-start(bf16[320,768]{1,0:T(8,128)(2,1)S(1)} %collective-permute-done.1.refs_2_), channel_id=1, source_target_pairs={{0,1},{1,0},{2,3},{3,2},{4,5},{5,4},{6,7},{7,6},{8,9},{9,8},{10,11... | collective-permute-start | bytes 1474568 | tf_op jit(solution)/shard_map/ppermute | solution.py:325
  44.2 12.7 %collective-permute-start.4 = (bf16[320,768]{1,0:T(8,128)(2,1)S(1)}, bf16[320,768]{1,0:T(8,128)(2,1)}, u32[]{:S(2)}, u32[]{:S(2)}) collective-permute-start(bf16[320,768]{1,0:T(8,128)(2,1)S(1)} %collective-permute-done.2.refs_4_), channel_id=1, source_target_pairs={{0,1},{1,0},{2,3},{3,2},{4,5},{5,4},{6,7},{7,6},{8,9},{9,8},{10,11... | collective-permute-start | bytes 1474568 | tf_op jit(solution)/shard_map/ppermute | solution.py:325
  52.6 4.3 %collective-permute-start.7 = (bf16[320,768]{1,0:T(8,128)(2,1)S(1)}, bf16[320,768]{1,0:T(8,128)(2,1)}, u32[]{:S(2)}, u32[]{:S(2)}) collective-permute-start(bf16[320,768]{1,0:T(8,128)(2,1)S(1)} %collective-permute-done.5.refs_6_), channel_id=1, source_target_pairs={{0,1},{1,0},{2,3},{3,2},{4,5},{5,4},{6,7},{7,6},{8,9},{9,8},{10,11... | collective-permute-start | bytes 1474568 | tf_op jit(solution)/shard_map/ppermute | solution.py:325
  52.6 15.1 %collective-permute-start.8 = (bf16[320,768]{1,0:T(8,128)(2,1)S(1)}, bf16[320,768]{1,0:T(8,128)(2,1)S(1)}, u32[]{:S(2)}, u32[]{:S(2)}) collective-permute-start(bf16[320,768]{1,0:T(8,128)(2,1)S(1)} %get-tuple-element.89.refs_0_), channel_id=1, source_target_pairs={{0,2},{2,4},{4,6},{6,0},{1,3},{3,5},{5,7},{7,1},{8,10},{10,12},{12... | collective-permute-start | bytes 1474568 | tf_op jit(solution)/shard_map/ppermute | solution.py:322
  53.5 14.2 %collective-permute-start.9 = (bf16[320,768]{1,0:T(8,128)(2,1)S(1)}, bf16[320,768]{1,0:T(8,128)(2,1)S(1)}, u32[]{:S(2)}, u32[]{:S(2)}) collective-permute-start(bf16[320,768]{1,0:T(8,128)(2,1)S(1)} %collective-permute-done.6.refs_4_), channel_id=1, source_target_pairs={{0,6},{2,0},{4,2},{6,4},{1,7},{3,1},{5,3},{7,5},{8,14},{10,8},{12,... | collective-permute-start | bytes 1474568 | tf_op jit(solution)/shard_map/ppermute | solution.py:322
  67.7 3.2 %collective-permute-start.10 = (bf16[320,384]{1,0:T(8,128)(2,1)S(1)}, bf16[320,384]{1,0:T(8,128)(2,1)S(1)}, u32[]{:S(2)}, u32[]{:S(2)}) collective-permute-start(bf16[320,384]{1,0:T(8,128)(2,1)S(1)} %get-tuple-element.82), channel_id=1, source_target_pairs={{0,1},{1,0},{2,3},{3,2},{4,5},{5,4},{6,7},{7,6},{8,9},{9,8},{10,11... | collective-permute-start | bytes 737288 | tf_op jit(solution)/shard_map/ppermute | solution.py:325
  67.8 3.5 %collective-permute-start.14 = (bf16[320,768]{1,0:T(8,128)(2,1)S(1)}, bf16[320,768]{1,0:T(8,128)(2,1)S(1)}, u32[]{:S(2)}, u32[]{:S(2)}) collective-permute-start(bf16[320,768]{1,0:T(8,128)(2,1)S(1)} %get-tuple-element.89.refs_0_), channel_id=1, source_target_pairs={{0,1},{1,0},{2,3},{3,2},{4,5},{5,4},{6,7},{7,6},{8,9},{9,8},{10,11... | collective-permute-start | bytes 1474568 | tf_op jit(solution)/shard_map/ppermute | solution.py:325
  68.3 3.8 %collective-permute-start.16 = (bf16[320,768]{1,0:T(8,128)(2,1)S(1)}, bf16[320,768]{1,0:T(8,128)(2,1)S(1)}, u32[]{:S(2)}, u32[]{:S(2)}) collective-permute-start(bf16[320,768]{1,0:T(8,128)(2,1)S(1)} %collective-permute-done.6.refs_4_), channel_id=1, source_target_pairs={{0,1},{1,0},{2,3},{3,2},{4,5},{5,4},{6,7},{7,6},{8,9},{9,8},{10,11... | collective-permute-start | bytes 1474568 | tf_op jit(solution)/shard_map/ppermute | solution.py:325
  68.6 6.0 %collective-permute-start.15 = (bf16[320,768]{1,0:T(8,128)(2,1)S(1)}, bf16[320,768]{1,0:T(8,128)(2,1)S(1)}, u32[]{:S(2)}, u32[]{:S(2)}) collective-permute-start(bf16[320,768]{1,0:T(8,128)(2,1)S(1)} %collective-permute-done.8.refs_2_), channel_id=1, source_target_pairs={{0,1},{1,0},{2,3},{3,2},{4,5},{5,4},{6,7},{7,6},{8,9},{9,8},{10,11... | collective-permute-start | bytes 1474568 | tf_op jit(solution)/shard_map/ppermute | solution.py:325
  68.8 5.8 %collective-permute-start.17 = (bf16[320,768]{1,0:T(8,128)(2,1)S(1)}, bf16[320,768]{1,0:T(8,128)(2,1)S(1)}, u32[]{:S(2)}, u32[]{:S(2)}) collective-permute-start(bf16[320,768]{1,0:T(8,128)(2,1)S(1)} %collective-permute-done.9.refs_6_), channel_id=1, source_target_pairs={{0,1},{1,0},{2,3},{3,2},{4,5},{5,4},{6,7},{7,6},{8,9},{9,8},{10,11... | collective-permute-start | bytes 1474568 | tf_op jit(solution)/shard_map/ppermute | solution.py:325
  71.0 10.6 %collective-permute-start.13 = (bf16[3,320,384]{2,1,0:T(8,128)(2,1)S(1)}, bf16[3,320,384]{2,1,0:T(8,128)(2,1)S(1)}, u32[]{:S(2)}, u32[]{:S(2)}) collective-permute-start(bf16[3,320,384]{2,1,0:T(8,128)(2,1)S(1)} %get-tuple-element.88), channel_id=1, source_target_pairs={{0,1},{1,0},{2,3},{3,2},{4,5},{5,4},{6,7},{7,6},{8,9},{9,8},{10,11... | collective-permute-start | bytes 2211848 | tf_op jit(solution)/shard_map/ppermute | solution.py:325
  71.4 10.2 %collective-permute-start.11 = (bf16[160,384]{1,0:T(8,128)(2,1)S(1)}, bf16[160,384]{1,0:T(8,128)(2,1)S(1)}, u32[]{:S(2)}, u32[]{:S(2)}) collective-permute-start(bf16[160,384]{1,0:T(8,128)(2,1)S(1)} %get-tuple-element.86), channel_id=1, source_target_pairs={{0,2},{2,4},{4,6},{6,0},{1,3},{3,5},{5,7},{7,1},{8,10},{10,12},{12... | collective-permute-start | bytes 368648 | tf_op jit(solution)/shard_map/ppermute | solution.py:322
  72.2 9.5 %collective-permute-start.12 = (bf16[160,384]{1,0:T(8,128)(2,1)S(1)}, bf16[160,384]{1,0:T(8,128)(2,1)S(1)}, u32[]{:S(2)}, u32[]{:S(2)}) collective-permute-start(bf16[160,384]{1,0:T(8,128)(2,1)S(1)} %get-tuple-element.87), channel_id=1, source_target_pairs={{0,6},{2,0},{4,2},{6,4},{1,7},{3,1},{5,3},{7,5},{8,14},{10,8},{12,... | collective-permute-start | bytes 368648 | tf_op jit(solution)/shard_map/ppermute | solution.py:322
  81.5 3.6 %collective-permute-start.18 = (bf16[320,384]{1,0:T(8,128)(2,1)S(1)}, bf16[320,384]{1,0:T(8,128)(2,1)S(1)}, u32[]{:S(2)}, u32[]{:S(2)}) collective-permute-start(bf16[320,384]{1,0:T(8,128)(2,1)S(1)} %get-tuple-element.105), channel_id=1, source_target_pairs={{0,1},{1,0},{2,3},{3,2},{4,5},{5,4},{6,7},{7,6},{8,9},{9,8},{10,11... | collective-permute-start | bytes 737288 | tf_op jit(solution)/shard_map/ppermute | solution.py:325
  85.2 12.4 %collective-permute-start.19 = (bf16[3,320,384]{2,1,0:T(8,128)(2,1)S(1)}, bf16[3,320,384]{2,1,0:T(8,128)(2,1)S(1)}, u32[]{:S(2)}, u32[]{:S(2)}) collective-permute-start(bf16[3,320,384]{2,1,0:T(8,128)(2,1)S(1)} %get-tuple-element.110), channel_id=1, source_target_pairs={{0,1},{1,0},{2,3},{3,2},{4,5},{5,4},{6,7},{7,6},{8,9},{9,8},{10,11... | collective-permute-start | bytes 2211848 | tf_op jit(solution)/shard_map/ppermute | solution.py:325
  85.8 11.8 %collective-permute-start.22 = (bf16[320,384]{1,0:T(8,128)(2,1)S(1)}, bf16[320,384]{1,0:T(8,128)(2,1)S(1)}, u32[]{:S(2)}, u32[]{:S(2)}) collective-permute-start(bf16[320,384]{1,0:T(8,128)(2,1)S(1)} %get-tuple-element.114), channel_id=1, source_target_pairs={{0,2},{2,4},{4,6},{6,0},{1,3},{3,5},{5,7},{7,1},{8,10},{10,12},{12... | collective-permute-start | bytes 737288 | tf_op jit(solution)/shard_map/ppermute | solution.py:322
  85.8 11.8 %collective-permute-start.23 = (bf16[320,384]{1,0:T(8,128)(2,1)S(1)}, bf16[320,384]{1,0:T(8,128)(2,1)S(1)}, u32[]{:S(2)}, u32[]{:S(2)}) collective-permute-start(bf16[320,384]{1,0:T(8,128)(2,1)S(1)} %get-tuple-element.115), channel_id=1, source_target_pairs={{0,6},{2,0},{4,2},{6,4},{1,7},{3,1},{5,3},{7,5},{8,14},{10,8},{12,... | collective-permute-start | bytes 737288 | tf_op jit(solution)/shard_map/ppermute | solution.py:322
  89.0 8.5 %collective-permute-start.20 = (bf16[160,384]{1,0:T(8,128)(2,1)S(1)}, bf16[160,384]{1,0:T(8,128)(2,1)S(1)}, u32[]{:S(2)}, u32[]{:S(2)}) collective-permute-start(bf16[160,384]{1,0:T(8,128)(2,1)S(1)} %get-tuple-element.111), channel_id=1, source_target_pairs={{0,2},{2,4},{4,6},{6,0},{1,3},{3,5},{5,7},{7,1},{8,10},{10,12},{12... | collective-permute-start | bytes 368648 | tf_op jit(solution)/shard_map/ppermute | solution.py:322
  89.0 8.5 %collective-permute-start.21 = (bf16[160,384]{1,0:T(8,128)(2,1)S(1)}, bf16[160,384]{1,0:T(8,128)(2,1)S(1)}, u32[]{:S(2)}, u32[]{:S(2)}) collective-permute-start(bf16[160,384]{1,0:T(8,128)(2,1)S(1)} %get-tuple-element.112), channel_id=1, source_target_pairs={{0,6},{2,0},{4,2},{6,4},{1,7},{3,1},{5,3},{7,5},{8,14},{10,8},{12,... | collective-permute-start | bytes 368648 | tf_op jit(solution)/shard_map/ppermute | solution.py:322
  99.2 16.0 %all-to-all-start.2 = ((bf16[16,128,128]{2,1,0:T(8,128)(2,1)}), bf16[16,128,128]{2,1,0:T(8,128)(2,1)S(1)}, u32[]{:S(2)}, u32[]{:S(2)}) async-start(bf16[16,128,128]{2,1,0:T(8,128)(2,1)} %shard_map.159.refs_11_), calls=%async_computation.2 | async-start | bytes 1048576 | tf_op jit(solution)/shard_map/all_to_all | solution.py:444
  104.3 8.1 %collective-permute-start.24 = (bf16[320,384]{1,0:T(8,128)(2,1)S(1)}, bf16[320,384]{1,0:T(8,128)(2,1)S(1)}, u32[]{:S(2)}, u32[]{:S(2)}) collective-permute-start(bf16[320,384]{1,0:T(8,128)(2,1)S(1)} %get-tuple-element.129), channel_id=1, source_target_pairs={{0,2},{2,4},{4,6},{6,0},{1,3},{3,5},{5,7},{7,1},{8,10},{10,12},{12... | collective-permute-start | bytes 737288 | tf_op jit(solution)/shard_map/ppermute | solution.py:322
  104.4 8.0 %collective-permute-start.25 = (bf16[320,384]{1,0:T(8,128)(2,1)S(1)}, bf16[320,384]{1,0:T(8,128)(2,1)S(1)}, u32[]{:S(2)}, u32[]{:S(2)}) collective-permute-start(bf16[320,384]{1,0:T(8,128)(2,1)S(1)} %get-tuple-element.130), channel_id=1, source_target_pairs={{0,6},{2,0},{4,2},{6,4},{1,7},{3,1},{5,3},{7,5},{8,14},{10,8},{12,... | collective-permute-start | bytes 737288 | tf_op jit(solution)/shard_map/ppermute | solution.py:322
  115.2 14.9 %all-to-all-start.3 = ((bf16[16,40,384]{2,1,0:T(8,128)(2,1)}), bf16[16,40,384]{2,1,0:T(8,128)(2,1)S(1)}, u32[]{:S(2)}, u32[]{:S(2)}) async-start(bf16[16,40,384]{2,1,0:T(8,128)(2,1)} %bitcast.6), calls=%async_computation.3 | async-start | bytes 983040 | tf_op jit(solution)/shard_map/all_to_all | solution.py:455

commit v7 on v5

--- a/solution.py
+++ b/solution.py
@@ -210,7 +210,7 @@
 
 ORDER = ((0, 0), (0, 1), (-1, 0), (-1, 1), (1, 0), (1, 1), (2, 0), (2, 1))
 ALL = len(ORDER) * FEAT
-EARLY = 6
+OWN, EARLY = 2, 6
 OUT_ORDER = (2, -1, 1, 0)
 
 
@@ -220,35 +220,70 @@
         copy.wait()
 
 
-def expert_early_kernel(place, *refs):
-    chunks, (wg, wu, wd) = refs[:EARLY], refs[EARLY : EARLY + 3]
-    (pre, hid, cat, down_late), (xs, ds, down_w, sems) = refs[-8:-4], refs[-4:]
-    stages = ([], [], [], [])
-    for i, (offset, sibling) in enumerate(ORDER):
+def first_layer(place, blocks, chunks, weights, xs, ds, gate_up, down, sems, at=0):
+    wg, wu, wd = weights
+    stages = ([], [], [])
+    for i, (offset, sibling) in enumerate(blocks):
         block = feature_block(place, offset, sibling)
-        side = pl.ds(i * FEAT, FEAT)
-        late = i >= EARLY
-        if not late:
-            stages[0].append((wd.at[0, :, pl.ds(block, FEAT)], down_w.at[:, side]))
-            stages[0].append((chunks[i].at[:, pl.ds(FEAT, FEAT)], ds.at[:, side]))
-            stages[1].append((chunks[i].at[:, pl.ds(0, FEAT)], xs.at[:, side]))
-        else:
-            stages[3].append((wd.at[0, :, pl.ds(block, FEAT)], down_late.at[:, pl.ds((i - EARLY) * FEAT, FEAT)]))
-        stages[3 if late else 1].append((wg.at[0, pl.ds(block, FEAT), :], cat.at[side, pl.ds(0, HID)]))
-        stages[3 if late else 2].append((wu.at[0, pl.ds(block, FEAT), :], cat.at[side, pl.ds(HID, HID)]))
-    copies = fetch(stages[0] + stages[1] + stages[2] + stages[3], sems)
+        side, turned = pl.ds(i * FEAT, FEAT), pl.ds((at + i) * FEAT, FEAT)
+        stages[0].append((wd.at[0, :, pl.ds(block, FEAT)], down.at[:, side]))
+        stages[0].append((chunks[i].at[:, pl.ds(FEAT, FEAT)], ds.at[:, side]))
+        stages[1].append((wg.at[0, pl.ds(block, FEAT), :], gate_up.at[turned, pl.ds(0, HID)]))
+        stages[1].append((chunks[i].at[:, pl.ds(0, FEAT)], xs.at[:, side]))
+        stages[2].append((wu.at[0, pl.ds(block, FEAT), :], gate_up.at[turned, pl.ds(HID, HID)]))
+    return stages
+
+
+def expert_own_kernel(place, a0, a1, wg, wu, wd, pre_hbm, hid_hbm, xs, ds, gate_up, down, pre, hid, sems, out_sems):
+    stages = first_layer(place, ORDER[:OWN], (a0, a1), (wg, wu, wd), xs, ds, gate_up, down, sems)
+    copies = fetch(stages[0] + stages[1] + stages[2], sems)
 
     def ready(n):
         for _ in range(n):
             copies.pop(0).wait()
 
     ready(len(stages[0]))
-    hid[...] = mm(ds[...], down_w[...], NT)
+    hid[...] = mm(ds[...], down[...], NT)
+    leaving = [pltpu.make_async_copy(hid, hid_hbm, out_sems.at[0]), pltpu.make_async_copy(pre, pre_hbm, out_sems.at[1])]
+    leaving[0].start()
     ready(len(stages[1]))
-    pre[:, :HID] = mm(xs[...], cat[: EARLY * FEAT, :HID])
+    pre[:, :HID] = mm(xs[...], gate_up[:, :HID])
     ready(len(stages[2]))
-    pre[:, HID:] = mm(xs[...], cat[: EARLY * FEAT, HID:])
-    ready(len(stages[3]))
+    pre[:, HID:] = mm(xs[...], gate_up[:, HID:])
+    leaving[1].start()
+    for copy in leaving:
+        copy.wait()
+
+
+def expert_early_kernel(place, *refs):
+    chunks, (wg, wu, wd, pre_hbm, hid_hbm) = refs[:4], refs[4:9]
+    (pre, hid, cat, down_late), (xs, ds, down_w, sums, hids, sems) = refs[-10:-6], refs[-6:]
+    stages = first_layer(place, ORDER[OWN:EARLY], chunks, (wg, wu, wd), xs, ds, cat, down_w, sems, at=OWN)
+    stages[0].append((hid_hbm, hids))
+    stages[1].append((pre_hbm.at[:, pl.ds(0, HID)], sums.at[:, pl.ds(0, HID)]))
+    stages[2].append((pre_hbm.at[:, pl.ds(HID, HID)], sums.at[:, pl.ds(HID, HID)]))
+    rest = []
+    for i, (offset, sibling) in enumerate(ORDER):
+        block = feature_block(place, offset, sibling)
+        if i >= EARLY:
+            rest.append((wd.at[0, :, pl.ds(block, FEAT)], down_late.at[:, pl.ds((i - EARLY) * FEAT, FEAT)]))
+        if i >= EARLY or i < OWN:
+            rest.append((wg.at[0, pl.ds(block, FEAT), :], cat.at[pl.ds(i * FEAT, FEAT), pl.ds(0, HID)]))
+            rest.append((wu.at[0, pl.ds(block, FEAT), :], cat.at[pl.ds(i * FEAT, FEAT), pl.ds(HID, HID)]))
+    copies = fetch(stages[0] + stages[1] + stages[2] + rest, sems)
+
+    def ready(n):
+        for _ in range(n):
+            copies.pop(0).wait()
+
+    lines = slice(OWN * FEAT, EARLY * FEAT)
+    ready(len(stages[0]))
+    hid[...] = hids[...] + mm(ds[...], down_w[...], NT)
+    ready(len(stages[1]))
+    pre[:, :HID] = sums[:, :HID] + mm(xs[...], cat[lines, :HID])
+    ready(len(stages[2]))
+    pre[:, HID:] = sums[:, HID:] + mm(xs[...], cat[lines, HID:])
+    ready(len(rest))
 
 
 def out_block(mid_ref, cat, offset, sibling):
@@ -273,9 +308,13 @@
         rest_ref[i] = out_block(mid_ref, cat, offset, 1).astype(BF)
 
 
-def expert_rest_kernel(mid_ref, cat, rest_ref):
-    for i, offset in enumerate(OUT_ORDER[1:]):
-        rest_ref[i] = out_block(mid_ref, cat, offset, 0)
+def expert_rest_kernel(mid_ref, cat, away, left_ref, right_ref, left_sum, right_sum, here_ref):
+    left, right, here = [out_block(mid_ref, cat, offset, 0) + away[i].astype(F32) for i, offset in enumerate(OUT_ORDER[1:])]
+    left_ref[...] = left[:CUT].astype(BF)
+    left_sum[...] = left[CUT:]
+    right_sum[...] = right[:CUT]
+    right_ref[...] = right[CUT:].astype(BF)
+    here_ref[...] = here
 
 
 def far_kernel(mine, away, right_ref, left_ref):
@@ -283,12 +322,16 @@
     left_ref[...] = (mine[CUT:] + away[CUT:].astype(F32)).astype(BF)
 
 
-def near_kernel(mine, away, via_right, via_left, left_ref, right_ref, here_ref):
-    left_ref[:CUT] = (mine[0, :CUT] + away[0, :CUT].astype(F32)).astype(BF)
-    left_ref[CUT:] = (mine[0, CUT:] + away[0, CUT:].astype(F32) + via_left[...].astype(F32)).astype(BF)
-    right_ref[:CUT] = (mine[1, :CUT] + away[1, :CUT].astype(F32) + via_right[...].astype(F32)).astype(BF)
-    right_ref[CUT:] = (mine[1, CUT:] + away[1, CUT:].astype(F32)).astype(BF)
-    here_ref[...] = mine[2] + away[2].astype(F32)
+def near_kernel(left_sum, right_sum, via_left, via_right, left_ref, right_ref):
+    left_ref[...] = (left_sum[...] + via_left[...].astype(F32)).astype(BF)
+    right_ref[...] = (right_sum[...] + via_right[...].astype(F32)).astype(BF)
+
+
+def sum_kernel(here, from_right_a, from_right_b, from_left_a, from_left_b, out_ref):
+    top = here[:CUT] + from_right_a[...].astype(F32) + from_left_b[...].astype(F32)
+    out_ref[:CUT] = top.astype(BF)
+    low = here[CUT:] + from_right_b[...].astype(F32) + from_left_a[...].astype(F32)
+    out_ref[CUT:] = low.astype(BF)
 
 
 def local(
@@ -298,6 +341,7 @@
     place = jnp.stack([lax.axis_index("x"), lax.axis_index("core")]).astype(I32)
     smem = pl.BlockSpec(memory_space=pltpu.SMEM)
     block = S((ROWS, FEAT), BF)
+    tie = lax.optimization_barrier
 
     def ring(value, way):
         return lax.ppermute(value, "x", way)
@@ -330,7 +374,21 @@
         limit=8,
     )(*branch, own)
     arrived = lax.all_to_all(message, "ctx", 0, 0, tiled=True)
-    from_left, from_right, arrived = lax.optimization_barrier((from_left, from_right, arrived))
+    weights = [in_hbm(w) for w in (w_gate, w_up, w_down)]
+    own_s = swap(own)
+    n = OWN * FEAT
+    pre, hid = call(
+        expert_own_kernel,
+        (pltpu.HBM((ROWS, 2 * HID), F32), pltpu.HBM((ROWS, HID), F32)),
+        [smem] + [anywhere()] * 5,
+        [pltpu.VMEM((ROWS, n), BF)] * 2
+        + [pltpu.VMEM((n, 2 * HID), BF), pltpu.VMEM((HID, n), BF), pltpu.VMEM((ROWS, 2 * HID), F32), pltpu.VMEM((ROWS, HID), F32)]
+        + [pltpu.SemaphoreType.DMA((5 * OWN,)), pltpu.SemaphoreType.DMA((2,))],
+        flops=6 * ROWS * HID * n,
+        size=12 * MIB,
+        limit=20,
+    )(place, own, own_s, *weights)
+    from_left, from_right, arrived, pre = tie((from_left, from_right, arrived, pre))
 
     x_far, d_far = call(
         forward_kernel,
@@ -341,31 +399,22 @@
         limit=4,
     )(from_left, from_right)
     x_far, d_far = ring(x_far, RIGHT), ring(d_far, LEFT)
-    early = [c for a in (own, from_left, from_right) for c in (a, swap(a))]
+    early = [c for a in (from_left, from_right) for c in (a, swap(a))]
 
     scanned = call(scan_kernel, S((CTX, HD, HD), BF), [vmem()], flops=MIB, size=MIB, limit=4)(arrived)
-    carried = lax.all_to_all(scanned, "ctx", 0, 0, tiled=True)
-    grads = call(
-        attention_kernel,
-        (S((TOK, HEADS * HD), BF),) * 3,
-        [anywhere()] * 6 + [vmem()],
-        held,
-        flops=16 * HEADS * TOK * TOK * HD,
-        size=4 * MIB,
-        limit=12,
-    )(*branch, carried)
-
-    n = EARLY * FEAT
+    n = (EARLY - OWN) * FEAT
     pre, hid, cat, down_late = call(
         expert_early_kernel,
-        (S((ROWS, 2 * HID), F32), S((ROWS, HID), F32), S((ALL, 2 * HID), BF), S((HID, ALL - n), BF)),
-        [smem] + [anywhere()] * (EARLY + 4),
-        [pltpu.VMEM((ROWS, n), BF)] * 2 + [pltpu.VMEM((HID, n), BF), pltpu.SemaphoreType.DMA((36,))],
+        (S((ROWS, 2 * HID), F32), S((ROWS, HID), F32), S((ALL, 2 * HID), BF), S((HID, ALL - EARLY * FEAT), BF)),
+        [smem] + [anywhere()] * 10,
+        [pltpu.VMEM((ROWS, n), BF)] * 2
+        + [pltpu.VMEM((HID, n), BF), pltpu.VMEM((ROWS, 2 * HID), F32), pltpu.VMEM((ROWS, HID), F32)]
+        + [pltpu.SemaphoreType.DMA((34,))],
         flops=6 * ROWS * HID * n,
         size=24 * MIB,
-        limit=28,
-    )(place, *early, *[in_hbm(w) for w in (w_gate, w_up, w_down)], scanned)
-    x_far, d_far, pre = lax.optimization_barrier((x_far, d_far, pre))
+        limit=32,
+    )(place, *early, *weights, in_hbm(pre), in_hbm(hid), scanned)
+    x_far, d_far, pre = tie((x_far, d_far, pre))
     rest = (RINGX - 1, ROWS, FEAT)
     mid, away_far = call(
         expert_mid_kernel,
@@ -387,21 +436,35 @@
 
     half = S((CUT, FEAT), BF)
     to_right, to_left = call(far_kernel, (half, half), [vmem()] * 2, size=2 * MIB, flops=MIB, limit=8)(mine_far, away_far)
-    mid, away_rest, to_right, to_left = lax.optimization_barrier((mid, away_rest, to_right, to_left))
+    mid, away_rest, to_right, to_left = tie((mid, away_rest, to_right, to_left))
     away_rest = swap(away_rest)
-    mine_rest = call(
+    wide = S((CUT, FEAT), F32)
+    left_a, right_a, left_sum, right_sum, here = call(
         expert_rest_kernel,
-        S(rest, F32),
-        [vmem()] * 2,
+        (half, half, wide, wide, S((ROWS, FEAT), F32)),
+        [vmem()] * 3,
         flops=3 * ROWS * HID * RINGX * FEAT,
         size=8 * MIB,
-        limit=18,
-    )(mid, cat)
+        limit=20,
+    )(mid, cat, away_rest)
     via_right, via_left = ring(to_right, RIGHT), ring(to_left, LEFT)
-    to_left, to_right, here = call(
-        near_kernel, (block, block, S((ROWS, FEAT), F32)), [vmem()] * 4, size=5 * MIB, flops=MIB, limit=16
-    )(mine_rest, away_rest, via_right, via_left)
-    summed = (here + ring(to_right, RIGHT).astype(F32) + ring(to_left, LEFT).astype(F32)).astype(BF)
+    left_a, right_a = ring(left_a, LEFT), ring(right_a, RIGHT)
+    here, scanned = tie((here, scanned))
+    via_right, via_left, left_a, right_a = tie((via_right, via_left, left_a, right_a))
+    left_b, right_b = call(near_kernel, (half, half), [vmem()] * 4, limit=6)(left_sum, right_sum, via_left, via_right)
+    left_b, right_b = ring(left_b, LEFT), ring(right_b, RIGHT)
+    summed = call(sum_kernel, block, [vmem()] * 5, size=4 * MIB, flops=MIB, limit=8)(here, left_a, left_b, right_a, right_b)
+    carried = lax.all_to_all(scanned, "ctx", 0, 0, tiled=True)
+    grads = call(
+        attention_kernel,
+        (S((TOK, HEADS * HD), BF),) * 3,
+        [anywhere()] * 6 + [vmem()],
+        held,
+        flops=16 * HEADS * TOK * TOK * HD,
+        size=4 * MIB,
+        limit=12,
+    )(*branch, carried)
+
     back = lax.all_to_all(summed.reshape(CTX, CAP, FEAT), "ctx", 0, 0, tiled=True)
     grad_moe = call(
         combine_kernel,

time: 121 us -> 123 us (1.017)
  Pallas kernels: 36.4 us -> 40 us
  waiting for transfers between devices: 32.1 us -> 28.5 us
  starting transfers between devices: 25.9 us -> 27.9 us
    pallas_call x2 -> x4, Pallas kernels: 3.01 us -> 10.7 us  [the longest x1 6.98 us: local(): call(expert_own_kernel, (pltpu.HBM((ROWS, 2 * HID), F32), pltpu.HBM((ROWS...]
    all_to_all x1, waiting for transfers between devices: 10.7 us -> 5.52 us  [local(): arrived = lax.all_to_all(message, 'ctx', 0, 0, tiled=True)]
    ppermute x8 -> x10, waiting for transfers between devices: 12.1 us -> 16.4 us  [ring(): return lax.ppermute(value, 'x', way)]
    pallas_call x1, Pallas kernels: 12.1 us -> 8.12 us  [local(): call(expert_early_kernel, (S((ROWS, 2 * HID), F32), S((ROWS, HID), F32),...]
    all_to_all x1, waiting for transfers between devices: 2.96 us -> 0.01 us  [local(): carried = lax.all_to_all(scanned, 'ctx', 0, 0, tiled=True)]
    ppermute x8 -> x10, starting transfers between devices: 13.1 us -> 14.8 us  [ring(): return lax.ppermute(value, 'x', way)]
  transfers between devices with their start and end apart: 18 -> 20, of which waited for: 8 -> 10; matrix products, arithmetic and copies ran while one was open for 1% -> 0% of each run, Pallas kernels for 24% -> 26%
where the time goes in v7:
time: 123 us
  Pallas kernels  40 us (33%)
  waiting for transfers between devices  28.5 us (23%)
  starting transfers between devices  27.9 us (23%)
  blocking collectives  24.4 us (20%)
    all_to_all x1, blocking collectives, local(): lax.all_to_all(rows.reshape(CTX, CAP, 2 * FEAT), 'ctx', 0, 0, tiled=True)  24.4 us
    ppermute x10, waiting for transfers between devices, ring(): return lax.ppermute(value, 'x', way)  16.4 us
    ppermute x10, starting transfers between devices, ring(): return lax.ppermute(value, 'x', way)  14.8 us
    pallas_call x1, Pallas kernels, local(): call(expert_early_kernel, (S((ROWS, 2 * HID), F32), S((ROWS, HID), F32),...  8.12 us
    pallas_call x1, Pallas kernels, local(): call(expert_own_kernel, (pltpu.HBM((ROWS, 2 * HID), F32), pltpu.HBM((ROWS...  6.98 us
    all_to_all x1, waiting for transfers between devices, local(): arrived = lax.all_to_all(message, 'ctx', 0, 0, tiled=True)  5.52 us
    pallas_call x1, Pallas kernels, local(): call(attention_kernel, (S((TOK, HEADS * HD), BF),) * 3, [anywhere()] * 6...  5.4 us
    all_to_all x1, waiting for transfers between devices, local(): lax.all_to_all(summed.reshape(CTX, CAP, FEAT), 'ctx', 0, 0, tiled=True)  4.51 us
  transfers between devices with their start and end apart: 20, of which 10 were waited for; matrix products, arithmetic and copies ran while one was open for 0% of the time, Pallas kernels for 26%

profile of v7, /device:TPU:0, one launch (start us, length us, event | category | flops | bytes accessed | tf_op | source)
XLA Modules:
  0.0 122.7 jit_solution(16776210956806439259)
XLA Ops:
  0.6 1.7 %shard_map.156 = (bf16[640,768]{1,0:T(8,128)(2,1)S(1)}, s32[2,256]{1,0:T(2,128)}) custom-call(s32[2,256]{1,0:T(2,128)} %bitcast.18, bf16[256,384]{1,0:T(8,128)(2,1)} %x_hbm.1, bf16[256,384]{1,0:T(8,128)(2,1)} %d_hbm.1), custom_call_target="tpu_custom_call" | custom-call | flops 251658240 | bytes 2097152 | tf_op jit(solution)/shard_map/pallas_call | solution.py:352
  2.4 24.4 %all_to_all.20 = bf16[16,40,768]{2,1,0:T(8,128)(2,1)S(1)} all-to-all(bf16[16,40,768]{2,1,0:T(8,128)(2,1)S(1)} %bitcast.14), channel_id=1, replica_groups=mesh['ctx'=16,'x'=4,'core'=2] {'ctx'}, dimensions={0} | all-to-all | bytes 1966080 | tf_op jit(solution)/shard_map/all_to_all | solution.py:361
  26.7 0.0 collective-permute-start.2
  26.7 1.5 %collective-permute-start = (bf16[640,768]{1,0:T(8,128)(2,1)S(1)}, bf16[640,768]{1,0:T(8,128)(2,1)S(1)}, u32[]{:S(2)}, u32[]{:S(2)}) collective-permute-start(bf16[640,768]{1,0:T(8,128)(2,1)S(1)} %bitcast.10), channel_id=1, source_target_pairs={{0,2},{2,4},{4,6},{6,0},{1,3},{3,5},{5,7},{7,1},{8,10},{10,12},{12... | collective-permute-start | bytes 2949128 | tf_op jit(solution)/shard_map/ppermute | solution.py:347
  28.2 1.7 %collective-permute-start.1 = (bf16[640,768]{1,0:T(8,128)(2,1)S(1)}, bf16[640,768]{1,0:T(8,128)(2,1)S(1)}, u32[]{:S(2)}, u32[]{:S(2)}) collective-permute-start(bf16[640,768]{1,0:T(8,128)(2,1)S(1)} %bitcast.11), channel_id=1, source_target_pairs={{0,6},{2,0},{4,2},{6,4},{1,7},{3,1},{5,3},{7,5},{8,14},{10,8},{12,... | collective-permute-start | bytes 2949128 | tf_op jit(solution)/shard_map/ppermute | solution.py:347
  30.0 3.1 %shard_map.157 = bf16[16,144,128]{2,1,0:T(8,128)(2,1)S(1)} custom-call(f32[8,256]{1,0:T(8,128)} %refs_0_.3, s32[1,256]{1,0:T(1,128)} %bitcast.16, bf16[256,1024]{1,0:T(8,128)(2,1)} %refs_2_.3, bf16[256,1024]{1,0:T(8,128)(2,1)} %refs_3_.3, bf16[256,1024]{1,0:T(8,128)(2,1)} %refs_4_.5, bf16[256,1024]{1,0:T(8,128)(2,1)} %refs_5_.5, bf16[640,768]{1,0:T(8,128)(2,1)S(1)} %bitcast.12), custom_call_target="tpu_custom_call" | custom-call | flops 134217728 | bytes 3145728 | tf_op jit(solution)/shard_map/pallas_call | solution.py:367
  33.1 0.8 copy-done
  33.9 3.6 %all-to-all-start.1 = ((bf16[16,144,128]{2,1,0:T(8,128)(2,1)}), bf16[16,144,128]{2,1,0:T(8,128)(2,1)S(1)}, u32[]{:S(2)}, u32[]{:S(2)}) async-start(bf16[16,144,128]{2,1,0:T(8,128)(2,1)} %copy-done), calls=%async_computation.1 | async-start | bytes 1179648 | tf_op jit(solution)/shard_map/all_to_all | solution.py:376
  37.5 0.1 pad_add_fusion.place
  37.6 7.0 %shard_map.158 = (f32[640,1280]{1,0:T(8,128)}, f32[640,640]{1,0:T(8,128)}) custom-call(s32[2]{0:T(128)S(1)} %pad_add_fusion.place, bf16[640,768]{1,0:T(8,128)(2,1)S(1)} %bitcast.13, bf16[640,768]{1,0:T(8,128)(2,1)} %collective-permute-done.2.a1, bf16[1,3072,640]{2,1,0:T(8,128)(2,1)} %refs_4_.4, bf16[1,3072,640]{2,1,0:T(8,128)(2,1)} %refs_5_.4, ...), custom_call_target="tpu_custom_call" | custom-call | flops 1887436800 | bytes 12582912 | tf_op jit(solution)/shard_map/pallas_call | solution.py:380
  44.6 5.5 %all-to-all-done.1.in_ref = bf16[16,144,128]{2,1,0:T(8,128)(2,1)S(1)} async-done(((bf16[16,144,128]{2,1,0:T(8,128)(2,1)}), bf16[16,144,128]{2,1,0:T(8,128)(2,1)S(1)}, u32[]{:S(2)}, u32[]{:S(2)}) %all-to-all-start.1) | async-done | bytes 589856 | tf_op jit(solution)/shard_map/all_to_all | solution.py:376
  50.1 2.0 %collective-permute-done.from_left.refs_0_ = bf16[640,768]{1,0:T(8,128)(2,1)S(1)} collective-permute-done((bf16[640,768]{1,0:T(8,128)(2,1)S(1)}, bf16[640,768]{1,0:T(8,128)(2,1)S(1)}, u32[]{:S(2)}, u32[]{:S(2)}) %collective-permute-start) | collective-permute-done | bytes 983072 | tf_op jit(solution)/shard_map/ppermute | solution.py:347
  52.1 0.0 collective-permute-done.1.from_right.refs_2_
  52.1 0.5 collective-permute-start.6
  52.6 0.1 shard_map.159
  52.8 1.6 %collective-permute-start.3 = (bf16[640,384]{1,0:T(8,128)(2,1)S(1)}, bf16[640,384]{1,0:T(8,128)(2,1)S(1)}, u32[]{:S(2)}, u32[]{:S(2)}) collective-permute-start(bf16[640,384]{1,0:T(8,128)(2,1)S(1)} %get-tuple-element.51), channel_id=1, source_target_pairs={{0,2},{2,4},{4,6},{6,0},{1,3},{3,5},{5,7},{7,1},{8,10},{10,12},{12... | collective-permute-start | bytes 1474568 | tf_op jit(solution)/shard_map/ppermute | solution.py:347
  54.3 1.7 %collective-permute-start.4 = (bf16[640,384]{1,0:T(8,128)(2,1)S(1)}, bf16[640,384]{1,0:T(8,128)(2,1)S(1)}, u32[]{:S(2)}, u32[]{:S(2)}) collective-permute-start(bf16[640,384]{1,0:T(8,128)(2,1)S(1)} %get-tuple-element.52), channel_id=1, source_target_pairs={{0,6},{2,0},{4,2},{6,4},{1,7},{3,1},{5,3},{7,5},{8,14},{10,8},{12,... | collective-permute-start | bytes 1474568 | tf_op jit(solution)/shard_map/ppermute | solution.py:347
  56.1 1.0 shard_map.160.refs_9_
  57.0 8.1 %shard_map.161 = (f32[640,1280]{1,0:T(8,128)S(1)}, f32[640,640]{1,0:T(8,128)S(1)}, bf16[3072,1280]{1,0:T(8,128)(2,1)S(1)}, bf16[640,768]{1,0:T(8,128)(2,1)S(1)}) custom-call(s32[2]{0:T(128)S(1)} %pad_add_fusion.place, bf16[640,768]{1,0:T(8,128)(2,1)S(1)} %collective-permute-done.from_left.refs_0_, bf16[640,768]{1,0:T(8,128)(2,1)S(1)} %collective-permute-done.5.refs_1_, ...), custom_call_target="tpu_custom_call" | custom-call | flops 3774873600 | bytes 25165824 | tf_op jit(solution)/shard_map/pallas_call | solution.py:406
  65.2 2.0 %collective-permute-done.3.x0 = bf16[640,384]{1,0:T(8,128)(2,1)S(1)} collective-permute-done((bf16[640,384]{1,0:T(8,128)(2,1)S(1)}, bf16[640,384]{1,0:T(8,128)(2,1)S(1)}, u32[]{:S(2)}, u32[]{:S(2)}) %collective-permute-start.3) | collective-permute-done | bytes 491552 | tf_op jit(solution)/shard_map/ppermute | solution.py:347
  67.2 0.0 collective-permute-done.4.d0
  67.2 0.0 collective-permute-start.7
  67.2 0.5 collective-permute-start.8
  67.7 1.4 %collective-permute-done.7.x1 = bf16[640,384]{1,0:T(8,128)(2,1)S(1)} collective-permute-done((bf16[640,384]{1,0:T(8,128)(2,1)S(1)}, bf16[640,384]{1,0:T(8,128)(2,1)S(1)}, u32[]{:S(2)}, u32[]{:S(2)}) %collective-permute-start.7) | collective-permute-done | bytes 491552 | tf_op jit(solution)/shard_map/ppermute | solution.py:350
  69.0 0.7 collective-permute-done.8.d1
  69.7 3.4 %shard_map.162 = (bf16[640,1280]{1,0:T(8,128)(2,1)S(1)}, bf16[640,384]{1,0:T(8,128)(2,1)S(1)}) custom-call(f32[640,1280]{1,0:T(8,128)S(1)} %get-tuple-element.57.pre, f32[640,640]{1,0:T(8,128)S(1)} %get-tuple-element.58.hid_ref, bf16[640,384]{1,0:T(8,128)(2,1)S(1)} %collective-permute-done.3.x0, bf16[640,384]{1,0:T(8,128)(2,1)S(1)} %collective-permute-done.4.d0, ...), custom_call_target="tpu_custom_call" | custom-call | flops 2516582400 | bytes 12582912 | tf_op jit(solution)/shard_map/pallas_call | solution.py:419
  73.2 0.2 collective-permute-start.9
  73.4 3.5 %shard_map.163 = (f32[640,384]{1,0:T(8,128)S(1)}, bf16[3,640,384]{2,1,0:T(8,128)(2,1)S(1)}) custom-call(bf16[640,1280]{1,0:T(8,128)(2,1)S(1)} %get-tuple-element.69.mid_ref, bf16[3072,1280]{1,0:T(8,128)(2,1)S(1)} %get-tuple-element.61.cat), custom_call_target="tpu_custom_call" | custom-call | flops 2516582400 | bytes 8388608 | tf_op jit(solution)/shard_map/pallas_call | solution.py:428
  76.9 0.9 shard_map.164
  77.8 0.4 collective-permute-start.10
  78.2 1.2 collective-permute-start.11
  79.4 2.1 %collective-permute-start.12 = (bf16[320,384]{1,0:T(8,128)(2,1)}, bf16[320,384]{1,0:T(8,128)(2,1)S(1)}, u32[]{:S(2)}, u32[]{:S(2)}) collective-permute-start(bf16[320,384]{1,0:T(8,128)(2,1)} %get-tuple-element.78), channel_id=1, source_target_pairs={{0,6},{2,0},{4,2},{6,4},{1,7},{3,1},{5,3},{7,5},{8,14},{10,8},{12,... | collective-permute-start | bytes 737288 | tf_op jit(solution)/shard_map/ppermute | solution.py:347
  81.4 0.0 collective-permute-done.10.away
  81.4 2.7 %shard_map.165 = (bf16[320,384]{1,0:T(8,128)(2,1)}, bf16[320,384]{1,0:T(8,128)(2,1)}, f32[320,384]{1,0:T(8,128)S(1)}, f32[320,384]{1,0:T(8,128)S(1)}, f32[640,384]{1,0:T(8,128)S(1)}) custom-call(bf16[640,1280]{1,0:T(8,128)(2,1)S(1)} %get-tuple-element.69.mid_ref, bf16[3072,1280]{1,0:T(8,128)(2,1)S(1)} %get-tuple-element.61.cat, ...), custom_call_target="tpu_custom_call" | custom-call | flops 1887436800 | bytes 8388608 | tf_op jit(solution)/shard_map/pallas_call | solution.py:442
  84.1 3.0 %collective-permute-start.13 = (bf16[320,384]{1,0:T(8,128)(2,1)}, bf16[320,384]{1,0:T(8,128)(2,1)S(1)}, u32[]{:S(2)}, u32[]{:S(2)}) collective-permute-start(bf16[320,384]{1,0:T(8,128)(2,1)} %get-tuple-element.79), channel_id=1, source_target_pairs={{0,6},{2,0},{4,2},{6,4},{1,7},{3,1},{5,3},{7,5},{8,14},{10,8},{12,... | collective-permute-start | bytes 737288 | tf_op jit(solution)/shard_map/ppermute | solution.py:347
  87.1 3.6 %all-to-all-start.2 = ((bf16[16,128,128]{2,1,0:T(8,128)(2,1)}), bf16[16,128,128]{2,1,0:T(8,128)(2,1)S(1)}, u32[]{:S(2)}, u32[]{:S(2)}) async-start(bf16[16,128,128]{2,1,0:T(8,128)(2,1)} %shard_map.160.refs_9_), calls=%async_computation.2 | async-start | bytes 1048576 | tf_op jit(solution)/shard_map/all_to_all | solution.py:457
  90.7 2.4 %collective-permute-done.13.from_right_a = bf16[320,384]{1,0:T(8,128)(2,1)S(1)} collective-permute-done((bf16[320,384]{1,0:T(8,128)(2,1)}, bf16[320,384]{1,0:T(8,128)(2,1)S(1)}, u32[]{:S(2)}, u32[]{:S(2)}) %collective-permute-start.13) | collective-permute-done | bytes 245792 | tf_op jit(solution)/shard_map/ppermute | solution.py:347
  93.1 3.3 %collective-permute-done.14.from_left_a = bf16[320,384]{1,0:T(8,128)(2,1)S(1)} collective-permute-done((bf16[320,384]{1,0:T(8,128)(2,1)}, bf16[320,384]{1,0:T(8,128)(2,1)S(1)}, u32[]{:S(2)}, u32[]{:S(2)}) %collective-permute-start.14) | collective-permute-done | bytes 245792 | tf_op jit(solution)/shard_map/ppermute | solution.py:347
  96.4 0.1 shard_map.167
  96.5 0.4 collective-permute-start.15
  96.9 1.7 %collective-permute-start.16 = (bf16[320,384]{1,0:T(8,128)(2,1)S(1)}, bf16[320,384]{1,0:T(8,128)(2,1)S(1)}, u32[]{:S(2)}, u32[]{:S(2)}) collective-permute-start(bf16[320,384]{1,0:T(8,128)(2,1)S(1)} %get-tuple-element.88), channel_id=1, source_target_pairs={{0,2},{2,4},{4,6},{6,0},{1,3},{3,5},{5,7},{7,1},{8,10},{10,12},{12... | collective-permute-start | bytes 737288 | tf_op jit(solution)/shard_map/ppermute | solution.py:347
  98.6 5.1 %collective-permute-done.15.from_right_b = bf16[320,384]{1,0:T(8,128)(2,1)S(1)} collective-permute-done((bf16[320,384]{1,0:T(8,128)(2,1)S(1)}, bf16[320,384]{1,0:T(8,128)(2,1)S(1)}, u32[]{:S(2)}, u32[]{:S(2)}) %collective-permute-start.15) | collective-permute-done | bytes 245792 | tf_op jit(solution)/shard_map/ppermute | solution.py:347
  103.7 1.5 %collective-permute-done.16.from_left_b = bf16[320,384]{1,0:T(8,128)(2,1)S(1)} collective-permute-done((bf16[320,384]{1,0:T(8,128)(2,1)S(1)}, bf16[320,384]{1,0:T(8,128)(2,1)S(1)}, u32[]{:S(2)}, u32[]{:S(2)}) %collective-permute-start.16) | collective-permute-done | bytes 245792 | tf_op jit(solution)/shard_map/ppermute | solution.py:347
  105.2 0.9 shard_map.168
  106.2 4.3 %all-to-all-start.3 = ((bf16[16,40,384]{2,1,0:T(8,128)(2,1)}), bf16[16,40,384]{2,1,0:T(8,128)(2,1)S(1)}, u32[]{:S(2)}, u32[]{:S(2)}) async-start(bf16[16,40,384]{2,1,0:T(8,128)(2,1)} %bitcast.6), calls=%async_computation.3 | async-start | bytes 983040 | tf_op jit(solution)/shard_map/all_to_all | solution.py:468
  110.5 5.4 %shard_map.166 = (bf16[256,1024]{1,0:T(8,128)(2,1)}, bf16[256,1024]{1,0:T(8,128)(2,1)}, bf16[256,1024]{1,0:T(8,128)(2,1)}) custom-call(f32[8,256]{1,0:T(8,128)} %refs_0_.3, s32[1,256]{1,0:T(1,128)} %bitcast.17, bf16[256,1024]{1,0:T(8,128)(2,1)} %refs_2_.3, bf16[256,1024]{1,0:T(8,128)(2,1)} %refs_3_.3, bf16[256,1024]{1,0:T(8,128)(2,1)} %refs_4_.5, ...), custom_call_target="tpu_custom_call" | custom-call | flops 1073741824 | bytes 4194304 | tf_op jit(solution)/shard_map/pallas_call | solution.py:458
  115.9 4.5 %all-to-all-done.3 = bf16[16,40,384]{2,1,0:T(8,128)(2,1)S(1)} async-done(((bf16[16,40,384]{2,1,0:T(8,128)(2,1)}), bf16[16,40,384]{2,1,0:T(8,128)(2,1)S(1)}, u32[]{:S(2)}, u32[]{:S(2)}) %all-to-all-start.3) | async-done | bytes 491552 | tf_op jit(solution)/shard_map/all_to_all | solution.py:468
  120.4 2.0 %shard_map.169 = bf16[256,384]{1,0:T(8,128)(2,1)} custom-call(bf16[640,384]{1,0:T(8,128)(2,1)S(1)} %bitcast.15, s32[2,256]{1,0:T(2,128)} %get-tuple-element.89.slots_hbm, f32[2,256]{1,0:T(2,128)} %bitcast.19), custom_call_target="tpu_custom_call" | custom-call | flops 251658240 | bytes 1048576 | tf_op jit(solution)/shard_map/pallas_call | solution.py:469
  (10 shorter events, 0.0 us)
Async XLA Ops:
  26.7 10.8 %collective-permute-start.2 = (bf16[640,768]{1,0:T(8,128)(2,1)S(1)}, bf16[640,768]{1,0:T(8,128)(2,1)}, u32[]{:S(2)}, u32[]{:S(2)}) collective-permute-start(bf16[640,768]{1,0:T(8,128)(2,1)S(1)} %bitcast.9), channel_id=1, source_target_pairs={{0,1},{1,0},{2,3},{3,2},{4,5},{5,4},{6,7},{7,6},{8,9},{9,8},{10,11... | collective-permute-start | bytes 2949128 | tf_op jit(solution)/shard_map/ppermute | solution.py:350
  26.7 25.4 %collective-permute-start = (bf16[640,768]{1,0:T(8,128)(2,1)S(1)}, bf16[640,768]{1,0:T(8,128)(2,1)S(1)}, u32[]{:S(2)}, u32[]{:S(2)}) collective-permute-start(bf16[640,768]{1,0:T(8,128)(2,1)S(1)} %bitcast.10), channel_id=1, source_target_pairs={{0,2},{2,4},{4,6},{6,0},{1,3},{3,5},{5,7},{7,1},{8,10},{10,12},{12... | collective-permute-start | bytes 2949128 | tf_op jit(solution)/shard_map/ppermute | solution.py:347
  28.2 23.9 %collective-permute-start.1 = (bf16[640,768]{1,0:T(8,128)(2,1)S(1)}, bf16[640,768]{1,0:T(8,128)(2,1)S(1)}, u32[]{:S(2)}, u32[]{:S(2)}) collective-permute-start(bf16[640,768]{1,0:T(8,128)(2,1)S(1)} %bitcast.11), channel_id=1, source_target_pairs={{0,6},{2,0},{4,2},{6,4},{1,7},{3,1},{5,3},{7,5},{8,14},{10,8},{12,... | collective-permute-start | bytes 2949128 | tf_op jit(solution)/shard_map/ppermute | solution.py:347
  33.1 0.8 copy-start
  33.9 16.2 %all-to-all-start.1 = ((bf16[16,144,128]{2,1,0:T(8,128)(2,1)}), bf16[16,144,128]{2,1,0:T(8,128)(2,1)S(1)}, u32[]{:S(2)}, u32[]{:S(2)}) async-start(bf16[16,144,128]{2,1,0:T(8,128)(2,1)} %copy-done), calls=%async_computation.1 | async-start | bytes 1179648 | tf_op jit(solution)/shard_map/all_to_all | solution.py:376
  52.1 4.9 %collective-permute-start.5 = (bf16[640,768]{1,0:T(8,128)(2,1)S(1)}, bf16[640,768]{1,0:T(8,128)(2,1)S(1)}, u32[]{:S(2)}, u32[]{:S(2)}) collective-permute-start(bf16[640,768]{1,0:T(8,128)(2,1)S(1)} %collective-permute-done.from_left.refs_0_), channel_id=1, source_target_pairs={{0,1},{1,0},{2,3},{3,2},{4,5},{5,4},{6,7},{7,6},{8,9},{9,8},{10,11... | collective-permute-start | bytes 2949128 | tf_op jit(solution)/shard_map/ppermute | solution.py:350
  52.1 4.9 %collective-permute-start.6 = (bf16[640,768]{1,0:T(8,128)(2,1)S(1)}, bf16[640,768]{1,0:T(8,128)(2,1)S(1)}, u32[]{:S(2)}, u32[]{:S(2)}) collective-permute-start(bf16[640,768]{1,0:T(8,128)(2,1)S(1)} %collective-permute-done.1.from_right.refs_2_), channel_id=1, source_target_pairs={{0,1},{1,0},{2,3},{3,2},{4,5},{5,4},{6,7},{7,6},{8,9},{9,8},{10,11... | collective-permute-start | bytes 2949128 | tf_op jit(solution)/shard_map/ppermute | solution.py:350
  52.8 14.4 %collective-permute-start.3 = (bf16[640,384]{1,0:T(8,128)(2,1)S(1)}, bf16[640,384]{1,0:T(8,128)(2,1)S(1)}, u32[]{:S(2)}, u32[]{:S(2)}) collective-permute-start(bf16[640,384]{1,0:T(8,128)(2,1)S(1)} %get-tuple-element.51), channel_id=1, source_target_pairs={{0,2},{2,4},{4,6},{6,0},{1,3},{3,5},{5,7},{7,1},{8,10},{10,12},{12... | collective-permute-start | bytes 1474568 | tf_op jit(solution)/shard_map/ppermute | solution.py:347
  54.3 12.9 %collective-permute-start.4 = (bf16[640,384]{1,0:T(8,128)(2,1)S(1)}, bf16[640,384]{1,0:T(8,128)(2,1)S(1)}, u32[]{:S(2)}, u32[]{:S(2)}) collective-permute-start(bf16[640,384]{1,0:T(8,128)(2,1)S(1)} %get-tuple-element.52), channel_id=1, source_target_pairs={{0,6},{2,0},{4,2},{6,4},{1,7},{3,1},{5,3},{7,5},{8,14},{10,8},{12,... | collective-permute-start | bytes 1474568 | tf_op jit(solution)/shard_map/ppermute | solution.py:347
  67.2 1.9 %collective-permute-start.7 = (bf16[640,384]{1,0:T(8,128)(2,1)S(1)}, bf16[640,384]{1,0:T(8,128)(2,1)S(1)}, u32[]{:S(2)}, u32[]{:S(2)}) collective-permute-start(bf16[640,384]{1,0:T(8,128)(2,1)S(1)} %collective-permute-done.3.x0), channel_id=1, source_target_pairs={{0,1},{1,0},{2,3},{3,2},{4,5},{5,4},{6,7},{7,6},{8,9},{9,8},{10,11... | collective-permute-start | bytes 1474568 | tf_op jit(solution)/shard_map/ppermute | solution.py:350
  67.2 2.6 %collective-permute-start.8 = (bf16[640,384]{1,0:T(8,128)(2,1)S(1)}, bf16[640,384]{1,0:T(8,128)(2,1)S(1)}, u32[]{:S(2)}, u32[]{:S(2)}) collective-permute-start(bf16[640,384]{1,0:T(8,128)(2,1)S(1)} %collective-permute-done.4.d0), channel_id=1, source_target_pairs={{0,1},{1,0},{2,3},{3,2},{4,5},{5,4},{6,7},{7,6},{8,9},{9,8},{10,11... | collective-permute-start | bytes 1474568 | tf_op jit(solution)/shard_map/ppermute | solution.py:350
  73.2 3.8 %collective-permute-start.9 = (bf16[640,384]{1,0:T(8,128)(2,1)S(1)}, bf16[640,384]{1,0:T(8,128)(2,1)S(1)}, u32[]{:S(2)}, u32[]{:S(2)}) collective-permute-start(bf16[640,384]{1,0:T(8,128)(2,1)S(1)} %get-tuple-element.66), channel_id=1, source_target_pairs={{0,1},{1,0},{2,3},{3,2},{4,5},{5,4},{6,7},{7,6},{8,9},{9,8},{10,11... | collective-permute-start | bytes 1474568 | tf_op jit(solution)/shard_map/ppermute | solution.py:350
  77.8 3.6 %collective-permute-start.10 = (bf16[3,640,384]{2,1,0:T(8,128)(2,1)S(1)}, bf16[3,640,384]{2,1,0:T(8,128)(2,1)S(1)}, u32[]{:S(2)}, u32[]{:S(2)}) collective-permute-start(bf16[3,640,384]{2,1,0:T(8,128)(2,1)S(1)} %get-tuple-element.70), channel_id=1, source_target_pairs={{0,1},{1,0},{2,3},{3,2},{4,5},{5,4},{6,7},{7,6},{8,9},{9,8},{10,11... | collective-permute-start | bytes 4423688 | tf_op jit(solution)/shard_map/ppermute | solution.py:350
  78.2 12.5 %collective-permute-start.11 = (bf16[320,384]{1,0:T(8,128)(2,1)}, bf16[320,384]{1,0:T(8,128)(2,1)S(1)}, u32[]{:S(2)}, u32[]{:S(2)}) collective-permute-start(bf16[320,384]{1,0:T(8,128)(2,1)} %get-tuple-element.77), channel_id=1, source_target_pairs={{0,2},{2,4},{4,6},{6,0},{1,3},{3,5},{5,7},{7,1},{8,10},{10,12},{12... | collective-permute-start | bytes 737288 | tf_op jit(solution)/shard_map/ppermute | solution.py:347
  79.4 11.3 %collective-permute-start.12 = (bf16[320,384]{1,0:T(8,128)(2,1)}, bf16[320,384]{1,0:T(8,128)(2,1)S(1)}, u32[]{:S(2)}, u32[]{:S(2)}) collective-permute-start(bf16[320,384]{1,0:T(8,128)(2,1)} %get-tuple-element.78), channel_id=1, source_target_pairs={{0,6},{2,0},{4,2},{6,4},{1,7},{3,1},{5,3},{7,5},{8,14},{10,8},{12,... | collective-permute-start | bytes 737288 | tf_op jit(solution)/shard_map/ppermute | solution.py:347
  84.1 9.0 %collective-permute-start.13 = (bf16[320,384]{1,0:T(8,128)(2,1)}, bf16[320,384]{1,0:T(8,128)(2,1)S(1)}, u32[]{:S(2)}, u32[]{:S(2)}) collective-permute-start(bf16[320,384]{1,0:T(8,128)(2,1)} %get-tuple-element.79), channel_id=1, source_target_pairs={{0,6},{2,0},{4,2},{6,4},{1,7},{3,1},{5,3},{7,5},{8,14},{10,8},{12,... | collective-permute-start | bytes 737288 | tf_op jit(solution)/shard_map/ppermute | solution.py:347
  87.1 9.4 %collective-permute-start.14 = (bf16[320,384]{1,0:T(8,128)(2,1)}, bf16[320,384]{1,0:T(8,128)(2,1)S(1)}, u32[]{:S(2)}, u32[]{:S(2)}) collective-permute-start(bf16[320,384]{1,0:T(8,128)(2,1)} %get-tuple-element.80), channel_id=1, source_target_pairs={{0,2},{2,4},{4,6},{6,0},{1,3},{3,5},{5,7},{7,1},{8,10},{10,12},{12... | collective-permute-start | bytes 737288 | tf_op jit(solution)/shard_map/ppermute | solution.py:347
  87.1 19.1 %all-to-all-start.2 = ((bf16[16,128,128]{2,1,0:T(8,128)(2,1)}), bf16[16,128,128]{2,1,0:T(8,128)(2,1)S(1)}, u32[]{:S(2)}, u32[]{:S(2)}) async-start(bf16[16,128,128]{2,1,0:T(8,128)(2,1)} %shard_map.160.refs_9_), calls=%async_computation.2 | async-start | bytes 1048576 | tf_op jit(solution)/shard_map/all_to_all | solution.py:457
  96.5 7.2 %collective-permute-start.15 = (bf16[320,384]{1,0:T(8,128)(2,1)S(1)}, bf16[320,384]{1,0:T(8,128)(2,1)S(1)}, u32[]{:S(2)}, u32[]{:S(2)}) collective-permute-start(bf16[320,384]{1,0:T(8,128)(2,1)S(1)} %get-tuple-element.86), channel_id=1, source_target_pairs={{0,6},{2,0},{4,2},{6,4},{1,7},{3,1},{5,3},{7,5},{8,14},{10,8},{12,... | collective-permute-start | bytes 737288 | tf_op jit(solution)/shard_map/ppermute | solution.py:347
  96.9 8.3 %collective-permute-start.16 = (bf16[320,384]{1,0:T(8,128)(2,1)S(1)}, bf16[320,384]{1,0:T(8,128)(2,1)S(1)}, u32[]{:S(2)}, u32[]{:S(2)}) collective-permute-start(bf16[320,384]{1,0:T(8,128)(2,1)S(1)} %get-tuple-element.88), channel_id=1, source_target_pairs={{0,2},{2,4},{4,6},{6,0},{1,3},{3,5},{5,7},{7,1},{8,10},{10,12},{12... | collective-permute-start | bytes 737288 | tf_op jit(solution)/shard_map/ppermute | solution.py:347
  106.2 14.3 %all-to-all-start.3 = ((bf16[16,40,384]{2,1,0:T(8,128)(2,1)}), bf16[16,40,384]{2,1,0:T(8,128)(2,1)S(1)}, u32[]{:S(2)}, u32[]{:S(2)}) async-start(bf16[16,40,384]{2,1,0:T(8,128)(2,1)} %bitcast.6), calls=%async_computation.3 | async-start | bytes 983040 | tf_op jit(solution)/shard_map/all_to_all | solution.py:468

commit v8 on v7

--- a/solution.py
+++ b/solution.py
@@ -96,11 +96,13 @@
 def combine_kernel(rows_ref, slots_hbm, weights_hbm, out_ref, slots_ref, weights_ref, sems):
     for copy in fetch(((slots_hbm, slots_ref), (weights_hbm, weights_ref)), sems):
         copy.wait()
-    columns = jnp.concatenate([weights_ref[...], jnp.zeros((6, TOK), F32)], axis=0).T
+    lines = [weights_ref[...], slots_ref[...].astype(F32), jnp.zeros((4, TOK), F32)]
+    columns = jnp.concatenate(lines, axis=0).T
+    slot = lax.broadcasted_iota(I32, (TOK, ROWS), 1)
     total = jnp.zeros((TOK, FEAT), F32)
     for k in range(2):
-        pick = jnp.where(onehot(slots_ref[k : k + 1, :]), 1.0, 0.0).astype(BF)
-        total += columns[:, k : k + 1] * mm(pick, rows_ref[...], TN)
+        pick = jnp.where(slot == columns[:, 2 + k : 3 + k].astype(I32), 1.0, 0.0).astype(BF)
+        total += columns[:, k : k + 1] * mm(pick, rows_ref[...])
     out_ref[...] = total.astype(BF)
 
 
@@ -214,9 +216,8 @@
 OUT_ORDER = (2, -1, 1, 0)
 
 
-def forward_kernel(from_left, from_right, x_ref, d_ref, sems):
-    pairs = ((from_left.at[:, pl.ds(0, FEAT)], x_ref), (from_right.at[:, pl.ds(FEAT, FEAT)], d_ref))
-    for copy in fetch(pairs, sems):
+def split_kernel(rows, x_ref, d_ref, sems):
+    for copy in fetch(((rows.at[:, pl.ds(0, FEAT)], x_ref), (rows.at[:, pl.ds(FEAT, FEAT)], d_ref)), sems):
         copy.wait()
 
 
@@ -227,15 +228,15 @@
         block = feature_block(place, offset, sibling)
         side, turned = pl.ds(i * FEAT, FEAT), pl.ds((at + i) * FEAT, FEAT)
         stages[0].append((wd.at[0, :, pl.ds(block, FEAT)], down.at[:, side]))
-        stages[0].append((chunks[i].at[:, pl.ds(FEAT, FEAT)], ds.at[:, side]))
+        stages[0].append((chunks[i][1], ds.at[:, side]))
         stages[1].append((wg.at[0, pl.ds(block, FEAT), :], gate_up.at[turned, pl.ds(0, HID)]))
-        stages[1].append((chunks[i].at[:, pl.ds(0, FEAT)], xs.at[:, side]))
+        stages[1].append((chunks[i][0], xs.at[:, side]))
         stages[2].append((wu.at[0, pl.ds(block, FEAT), :], gate_up.at[turned, pl.ds(HID, HID)]))
     return stages
 
 
-def expert_own_kernel(place, a0, a1, wg, wu, wd, pre_hbm, hid_hbm, xs, ds, gate_up, down, pre, hid, sems, out_sems):
-    stages = first_layer(place, ORDER[:OWN], (a0, a1), (wg, wu, wd), xs, ds, gate_up, down, sems)
+def expert_own_kernel(place, x0, d0, x1, d1, wg, wu, wd, pre_hbm, hid_hbm, xs, ds, gate_up, down, pre, hid, sems, out_sems):
+    stages = first_layer(place, ORDER[:OWN], ((x0, d0), (x1, d1)), (wg, wu, wd), xs, ds, gate_up, down, sems)
     copies = fetch(stages[0] + stages[1] + stages[2], sems)
 
     def ready(n):
@@ -256,7 +257,7 @@
 
 
 def expert_early_kernel(place, *refs):
-    chunks, (wg, wu, wd, pre_hbm, hid_hbm) = refs[:4], refs[4:9]
+    chunks, (wg, wu, wd, pre_hbm, hid_hbm) = list(zip(refs[0:8:2], refs[1:8:2])), refs[8:13]
     (pre, hid, cat, down_late), (xs, ds, down_w, sums, hids, sems) = refs[-10:-6], refs[-6:]
     stages = first_layer(place, ORDER[OWN:EARLY], chunks, (wg, wu, wd), xs, ds, cat, down_w, sems, at=OWN)
     stages[0].append((hid_hbm, hids))
@@ -308,13 +309,9 @@
         rest_ref[i] = out_block(mid_ref, cat, offset, 1).astype(BF)
 
 
-def expert_rest_kernel(mid_ref, cat, away, left_ref, right_ref, left_sum, right_sum, here_ref):
-    left, right, here = [out_block(mid_ref, cat, offset, 0) + away[i].astype(F32) for i, offset in enumerate(OUT_ORDER[1:])]
-    left_ref[...] = left[:CUT].astype(BF)
-    left_sum[...] = left[CUT:]
-    right_sum[...] = right[:CUT]
-    right_ref[...] = right[CUT:].astype(BF)
-    here_ref[...] = here
+def expert_rest_kernel(mid_ref, cat, rest_ref):
+    for i, offset in enumerate(OUT_ORDER[1:]):
+        rest_ref[i] = out_block(mid_ref, cat, offset, 0)
 
 
 def far_kernel(mine, away, right_ref, left_ref):
@@ -322,16 +319,12 @@
     left_ref[...] = (mine[CUT:] + away[CUT:].astype(F32)).astype(BF)
 
 
-def near_kernel(left_sum, right_sum, via_left, via_right, left_ref, right_ref):
-    left_ref[...] = (left_sum[...] + via_left[...].astype(F32)).astype(BF)
-    right_ref[...] = (right_sum[...] + via_right[...].astype(F32)).astype(BF)
-
-
-def sum_kernel(here, from_right_a, from_right_b, from_left_a, from_left_b, out_ref):
-    top = here[:CUT] + from_right_a[...].astype(F32) + from_left_b[...].astype(F32)
-    out_ref[:CUT] = top.astype(BF)
-    low = here[CUT:] + from_right_b[...].astype(F32) + from_left_a[...].astype(F32)
-    out_ref[CUT:] = low.astype(BF)
+def near_kernel(mine, away, via_right, via_left, left_ref, right_ref, here_ref):
+    left_ref[:CUT] = (mine[0, :CUT] + away[0, :CUT].astype(F32)).astype(BF)
+    left_ref[CUT:] = (mine[0, CUT:] + away[0, CUT:].astype(F32) + via_left[...].astype(F32)).astype(BF)
+    right_ref[:CUT] = (mine[1, :CUT] + away[1, :CUT].astype(F32) + via_right[...].astype(F32)).astype(BF)
+    right_ref[CUT:] = (mine[1, CUT:] + away[1, CUT:].astype(F32)).astype(BF)
+    here_ref[...] = mine[2] + away[2].astype(F32)
 
 
 def local(
@@ -359,7 +352,10 @@
         limit=6,
     )(in_hbm(expert_ids.T), in_hbm(moe_input), in_hbm(moe_cotangent))
     own = lax.all_to_all(rows.reshape(CTX, CAP, 2 * FEAT), "ctx", 0, 0, tiled=True).reshape(ROWS, 2 * FEAT)
-    from_left, from_right = ring(own, RIGHT), ring(own, LEFT)
+    x_own, d_own = call(
+        split_kernel, (block, block), [anywhere()], [pltpu.SemaphoreType.DMA((2,))], size=2 * MIB, limit=4
+    )(own)
+    x_left, d_right = ring(x_own, RIGHT), ring(d_own, LEFT)
 
     branch = [in_hbm(a) for a in (log_decay, doc_ids.reshape(1, TOK), queries, keys, values, out_grad)]
     held = [pltpu.VMEM((HEADS, TOK), F32), pltpu.VMEM((1, TOK), I32)] + [pltpu.VMEM((TOK, HEADS * HD), BF)] * 4
@@ -373,40 +369,33 @@
         size=3 * MIB,
         limit=8,
     )(*branch, own)
+    d_next, x_next, message = tie((d_own, x_own, message))
+    d_left, x_right = ring(d_next, RIGHT), ring(x_next, LEFT)
     arrived = lax.all_to_all(message, "ctx", 0, 0, tiled=True)
     weights = [in_hbm(w) for w in (w_gate, w_up, w_down)]
-    own_s = swap(own)
     n = OWN * FEAT
     pre, hid = call(
         expert_own_kernel,
         (pltpu.HBM((ROWS, 2 * HID), F32), pltpu.HBM((ROWS, HID), F32)),
-        [smem] + [anywhere()] * 5,
+        [smem] + [anywhere()] * 7,
         [pltpu.VMEM((ROWS, n), BF)] * 2
         + [pltpu.VMEM((n, 2 * HID), BF), pltpu.VMEM((HID, n), BF), pltpu.VMEM((ROWS, 2 * HID), F32), pltpu.VMEM((ROWS, HID), F32)]
         + [pltpu.SemaphoreType.DMA((5 * OWN,)), pltpu.SemaphoreType.DMA((2,))],
         flops=6 * ROWS * HID * n,
         size=12 * MIB,
         limit=20,
-    )(place, own, own_s, *weights)
-    from_left, from_right, arrived, pre = tie((from_left, from_right, arrived, pre))
-
-    x_far, d_far = call(
-        forward_kernel,
-        (block, block),
-        [anywhere()] * 2,
-        [pltpu.SemaphoreType.DMA((2,))],
-        size=2 * MIB,
-        limit=4,
-    )(from_left, from_right)
-    x_far, d_far = ring(x_far, RIGHT), ring(d_far, LEFT)
-    early = [c for a in (from_left, from_right) for c in (a, swap(a))]
+    )(place, x_own, d_own, swap(x_own), swap(d_own), *weights)
+    x_left, d_right, pre = tie((x_left, d_right, pre))
+    x_far, d_far = ring(x_left, RIGHT), ring(d_right, LEFT)
+    d_left, x_right, arrived = tie((d_left, x_right, arrived))
+    early = [c for x, d in ((x_left, d_left), (x_right, d_right)) for c in (x, d, swap(x), swap(d))]
 
     scanned = call(scan_kernel, S((CTX, HD, HD), BF), [vmem()], flops=MIB, size=MIB, limit=4)(arrived)
     n = (EARLY - OWN) * FEAT
     pre, hid, cat, down_late = call(
         expert_early_kernel,
         (S((ROWS, 2 * HID), F32), S((ROWS, HID), F32), S((ALL, 2 * HID), BF), S((HID, ALL - EARLY * FEAT), BF)),
-        [smem] + [anywhere()] * 10,
+        [smem] + [anywhere()] * 14,
         [pltpu.VMEM((ROWS, n), BF)] * 2
         + [pltpu.VMEM((HID, n), BF), pltpu.VMEM((ROWS, 2 * HID), F32), pltpu.VMEM((ROWS, HID), F32)]
         + [pltpu.SemaphoreType.DMA((34,))],
@@ -438,22 +427,19 @@
     to_right, to_left = call(far_kernel, (half, half), [vmem()] * 2, size=2 * MIB, flops=MIB, limit=8)(mine_far, away_far)
     mid, away_rest, to_right, to_left = tie((mid, away_rest, to_right, to_left))
     away_rest = swap(away_rest)
-    wide = S((CUT, FEAT), F32)
-    left_a, right_a, left_sum, right_sum, here = call(
+    mine_rest = call(
         expert_rest_kernel,
-        (half, half, wide, wide, S((ROWS, FEAT), F32)),
-        [vmem()] * 3,
+        S(rest, F32),
+        [vmem()] * 2,
         flops=3 * ROWS * HID * RINGX * FEAT,
         size=8 * MIB,
-        limit=20,
-    )(mid, cat, away_rest)
+        limit=18,
+    )(mid, cat)
     via_right, via_left = ring(to_right, RIGHT), ring(to_left, LEFT)
-    left_a, right_a = ring(left_a, LEFT), ring(right_a, RIGHT)
-    here, scanned = tie((here, scanned))
-    via_right, via_left, left_a, right_a = tie((via_right, via_left, left_a, right_a))
-    left_b, right_b = call(near_kernel, (half, half), [vmem()] * 4, limit=6)(left_sum, right_sum, via_left, via_right)
-    left_b, right_b = ring(left_b, LEFT), ring(right_b, RIGHT)
-    summed = call(sum_kernel, block, [vmem()] * 5, size=4 * MIB, flops=MIB, limit=8)(here, left_a, left_b, right_a, right_b)
+    to_left, to_right, here = call(
+        near_kernel, (block, block, S((ROWS, FEAT), F32)), [vmem()] * 4, size=5 * MIB, flops=MIB, limit=16
+    )(mine_rest, away_rest, via_right, via_left)
+    summed = (here + ring(to_right, RIGHT).astype(F32) + ring(to_left, LEFT).astype(F32)).astype(BF)
     carried = lax.all_to_all(scanned, "ctx", 0, 0, tiled=True)
     grads = call(
         attention_kernel,

time: 123 us -> 126 us (1.024)
  starting transfers between devices: 27.9 us -> 33 us
  waiting for transfers between devices: 28.5 us -> 25.4 us
    all_to_all x1, waiting for transfers between devices: 0.01 us -> 5.77 us  [local(): carried = lax.all_to_all(scanned, 'ctx', 0, 0, tiled=True)]
    all_to_all x1, waiting for transfers between devices: 5.52 us -> 0.01 us  [local(): arrived = lax.all_to_all(message, 'ctx', 0, 0, tiled=True)]
    ppermute x10, waiting for transfers between devices: 16.4 us -> 13.1 us  [ring(): return lax.ppermute(value, 'x', way)]
    all_to_all x1, starting transfers between devices: 3.57 us -> 6.58 us  [local(): carried = lax.all_to_all(scanned, 'ctx', 0, 0, tiled=True)]
    ppermute x10, starting transfers between devices: 14.8 us -> 16.4 us  [ring(): return lax.ppermute(value, 'x', way)]
    ppermute x7 -> x10, starting transfers between devices: 1.61 us -> 2.86 us  [swap(): return lax.ppermute(value, 'core', SWAP)]
    pallas_call x4 -> x3, Pallas kernels: 3.86 us -> 4.08 us  [the longest x1 2.71 us: local(): call(expert_rest_kernel, S(rest, F32), [vmem()] * 2, flops=3 * ROWS * HID...]
  transfers between devices with their start and end apart: 20 -> 23, of which waited for: 10 -> 8; matrix products, arithmetic and copies ran while one was open for 0% -> 1% of each run, Pallas kernels for 26% -> 25%
where the time goes in v8:
time: 126 us; the launch traced here: 125 us
  Pallas kernels  40.7 us (32%)
  starting transfers between devices  33 us (26%)
  waiting for transfers between devices  25.4 us (20%)
  blocking collectives  24.4 us (19%)
    all_to_all x1, blocking collectives, local(): lax.all_to_all(rows.reshape(CTX, CAP, 2 * FEAT), 'ctx', 0, 0, tiled=True)  24.4 us
    ppermute x10, starting transfers between devices, ring(): return lax.ppermute(value, 'x', way)  16.4 us
    ppermute x10, waiting for transfers between devices, ring(): return lax.ppermute(value, 'x', way)  13.1 us
    pallas_call x1, Pallas kernels, local(): call(expert_early_kernel, (S((ROWS, 2 * HID), F32), S((ROWS, HID), F32),...  8.13 us
    pallas_call x1, Pallas kernels, local(): call(expert_own_kernel, (pltpu.HBM((ROWS, 2 * HID), F32), pltpu.HBM((ROWS...  6.98 us
    all_to_all x1, starting transfers between devices, local(): carried = lax.all_to_all(scanned, 'ctx', 0, 0, tiled=True)  6.58 us
    all_to_all x1, waiting for transfers between devices, local(): carried = lax.all_to_all(scanned, 'ctx', 0, 0, tiled=True)  5.77 us
    pallas_call x1, Pallas kernels, local(): call(attention_kernel, (S((TOK, HEADS * HD), BF),) * 3, [anywhere()] * 6...  5.4 us
  transfers between devices with their start and end apart: 23, of which 8 were waited for; matrix products, arithmetic and copies ran while one was open for 1% of the time, Pallas kernels for 25%

profile of v8, /device:TPU:0, one launch (start us, length us, event | category | flops | bytes accessed | tf_op | source)
XLA Modules:
  0.0 125.4 jit_solution(16979008241195038590)
XLA Ops:
  0.6 1.7 %shard_map.156 = (bf16[640,768]{1,0:T(8,128)(2,1)S(1)}, s32[2,256]{1,0:T(2,128)}) custom-call(s32[2,256]{1,0:T(2,128)} %bitcast.15, bf16[256,384]{1,0:T(8,128)(2,1)} %x_hbm.1, bf16[256,384]{1,0:T(8,128)(2,1)} %d_hbm.1), custom_call_target="tpu_custom_call" | custom-call | flops 251658240 | bytes 2097152 | tf_op jit(solution)/shard_map/pallas_call | solution.py:345
  2.4 24.4 %all_to_all.20 = bf16[16,40,768]{2,1,0:T(8,128)(2,1)S(1)} all-to-all(bf16[16,40,768]{2,1,0:T(8,128)(2,1)S(1)} %bitcast.11), channel_id=1, replica_groups=mesh['ctx'=16,'x'=4,'core'=2] {'ctx'}, dimensions={0} | all-to-all | bytes 1966080 | tf_op jit(solution)/shard_map/all_to_all | solution.py:354
  26.7 1.1 shard_map.157
  27.8 0.1 collective-permute-start.4
  27.9 0.5 collective-permute-start.5
  28.4 1.5 %collective-permute-start.2 = (bf16[640,384]{1,0:T(8,128)(2,1)}, bf16[640,384]{1,0:T(8,128)(2,1)S(1)}, u32[]{:S(2)}, u32[]{:S(2)}) collective-permute-start(bf16[640,384]{1,0:T(8,128)(2,1)} %get-tuple-element.46.x0), channel_id=1, source_target_pairs={{0,2},{2,4},{4,6},{6,0},{1,3},{3,5},{5,7},{7,1},{8,10},{10,12},{12... | collective-permute-start | bytes 1474568 | tf_op jit(solution)/shard_map/ppermute | solution.py:340
  29.9 1.7 %collective-permute-start.3 = (bf16[640,384]{1,0:T(8,128)(2,1)}, bf16[640,384]{1,0:T(8,128)(2,1)S(1)}, u32[]{:S(2)}, u32[]{:S(2)}) collective-permute-start(bf16[640,384]{1,0:T(8,128)(2,1)} %get-tuple-element.45.d0), channel_id=1, source_target_pairs={{0,6},{2,0},{4,2},{6,4},{1,7},{3,1},{5,3},{7,5},{8,14},{10,8},{12,... | collective-permute-start | bytes 1474568 | tf_op jit(solution)/shard_map/ppermute | solution.py:340
  31.6 3.9 %shard_map.158 = bf16[16,144,128]{2,1,0:T(8,128)(2,1)} custom-call(f32[8,256]{1,0:T(8,128)} %refs_0_.3, s32[1,256]{1,0:T(1,128)} %bitcast.13, bf16[256,1024]{1,0:T(8,128)(2,1)} %refs_2_.3, bf16[256,1024]{1,0:T(8,128)(2,1)} %refs_3_.3, bf16[256,1024]{1,0:T(8,128)(2,1)} %refs_4_.3, bf16[256,1024]{1,0:T(8,128)(2,1)} %refs_5_.3, bf16[640,768]{1,0:T(8,128)(2,1)S(1)} %bitcast.10), custom_call_target="tpu_custom_call" | custom-call | flops 134217728 | bytes 3145728 | tf_op jit(solution)/shard_map/pallas_call | solution.py:363
  35.6 3.6 %all-to-all-start.1 = ((bf16[16,144,128]{2,1,0:T(8,128)(2,1)}), bf16[16,144,128]{2,1,0:T(8,128)(2,1)S(1)}, u32[]{:S(2)}, u32[]{:S(2)}) async-start(bf16[16,144,128]{2,1,0:T(8,128)(2,1)} %shard_map.158), calls=%async_computation.1 | async-start | bytes 1179648 | tf_op jit(solution)/shard_map/all_to_all | solution.py:374
  39.2 0.4 collective-permute-start
  39.5 0.0 collective-permute-done.4.x1
  39.5 3.0 %collective-permute-start.1 = (bf16[640,384]{1,0:T(8,128)(2,1)}, bf16[640,384]{1,0:T(8,128)(2,1)S(1)}, u32[]{:S(2)}, u32[]{:S(2)}) collective-permute-start(bf16[640,384]{1,0:T(8,128)(2,1)} %get-tuple-element.46.x0), channel_id=1, source_target_pairs={{0,6},{2,0},{4,2},{6,4},{1,7},{3,1},{5,3},{7,5},{8,14},{10,8},{12,... | collective-permute-start | bytes 1474568 | tf_op jit(solution)/shard_map/ppermute | solution.py:340
  42.5 0.1 pad_add_fusion.place
  42.6 7.0 %shard_map.161 = (f32[640,1280]{1,0:T(8,128)}, f32[640,640]{1,0:T(8,128)}) custom-call(s32[2]{0:T(128)S(1)} %pad_add_fusion.place, bf16[640,384]{1,0:T(8,128)(2,1)} %get-tuple-element.46.x0, bf16[640,384]{1,0:T(8,128)(2,1)} %get-tuple-element.45.d0, bf16[640,384]{1,0:T(8,128)(2,1)S(1)} %collective-permute-done.4.x1, ...), custom_call_target="tpu_custom_call" | custom-call | flops 1887436800 | bytes 12582912 | tf_op jit(solution)/shard_map/pallas_call | solution.py:377
  49.6 0.0 collective-permute-done.2.refs_0_
  49.6 0.1 collective-permute-start.11
  49.7 0.5 collective-permute-start.8
  50.2 3.4 %collective-permute-done.refs_1_ = bf16[640,384]{1,0:T(8,128)(2,1)S(1)} collective-permute-done((bf16[640,384]{1,0:T(8,128)(2,1)}, bf16[640,384]{1,0:T(8,128)(2,1)S(1)}, u32[]{:S(2)}, u32[]{:S(2)}) %collective-permute-start) | collective-permute-done | bytes 491552 | tf_op jit(solution)/shard_map/ppermute | solution.py:340
  53.6 0.0 collective-permute-done.1.refs_4_
  53.6 0.5 collective-permute-start.9
  54.1 1.5 %collective-permute-start.6 = (bf16[640,384]{1,0:T(8,128)(2,1)S(1)}, bf16[640,384]{1,0:T(8,128)(2,1)S(1)}, u32[]{:S(2)}, u32[]{:S(2)}) collective-permute-start(bf16[640,384]{1,0:T(8,128)(2,1)S(1)} %collective-permute-done.2.refs_0_), channel_id=1, source_target_pairs={{0,2},{2,4},{4,6},{6,0},{1,3},{3,5},{5,7},{7,1},{8,10},{10,12},{12... | collective-permute-start | bytes 1474568 | tf_op jit(solution)/shard_map/ppermute | solution.py:340
  55.6 1.7 %collective-permute-start.7 = (bf16[640,384]{1,0:T(8,128)(2,1)S(1)}, bf16[640,384]{1,0:T(8,128)(2,1)S(1)}, u32[]{:S(2)}, u32[]{:S(2)}) collective-permute-start(bf16[640,384]{1,0:T(8,128)(2,1)S(1)} %collective-permute-done.3.refs_5_), channel_id=1, source_target_pairs={{0,6},{2,0},{4,2},{6,4},{1,7},{3,1},{5,3},{7,5},{8,14},{10,8},{12,... | collective-permute-start | bytes 1474568 | tf_op jit(solution)/shard_map/ppermute | solution.py:340
  57.3 1.0 shard_map.159.refs_13_
  58.3 8.1 %shard_map.162 = (f32[640,1280]{1,0:T(8,128)S(1)}, f32[640,640]{1,0:T(8,128)S(1)}, bf16[3072,1280]{1,0:T(8,128)(2,1)S(1)}, bf16[640,768]{1,0:T(8,128)(2,1)S(1)}) custom-call(s32[2]{0:T(128)S(1)} %pad_add_fusion.place, bf16[640,384]{1,0:T(8,128)(2,1)S(1)} %collective-permute-done.2.refs_0_, bf16[640,384]{1,0:T(8,128)(2,1)S(1)} %collective-permute-done.refs_1_, ...), custom_call_target="tpu_custom_call" | custom-call | flops 3774873600 | bytes 25165824 | tf_op jit(solution)/shard_map/pallas_call | solution.py:395
  66.5 2.1 %collective-permute-done.6.x0 = bf16[640,384]{1,0:T(8,128)(2,1)S(1)} collective-permute-done((bf16[640,384]{1,0:T(8,128)(2,1)S(1)}, bf16[640,384]{1,0:T(8,128)(2,1)S(1)}, u32[]{:S(2)}, u32[]{:S(2)}) %collective-permute-start.6) | collective-permute-done | bytes 491552 | tf_op jit(solution)/shard_map/ppermute | solution.py:340
  68.5 0.5 collective-permute-start.13
  69.0 1.4 %collective-permute-done.12.x1 = bf16[640,384]{1,0:T(8,128)(2,1)S(1)} collective-permute-done((bf16[640,384]{1,0:T(8,128)(2,1)S(1)}, bf16[640,384]{1,0:T(8,128)(2,1)S(1)}, u32[]{:S(2)}, u32[]{:S(2)}) %collective-permute-start.12) | collective-permute-done | bytes 491552 | tf_op jit(solution)/shard_map/ppermute | solution.py:343
  70.4 0.7 collective-permute-done.13.d1
  71.1 3.7 %shard_map.163 = (bf16[640,1280]{1,0:T(8,128)(2,1)S(1)}, bf16[640,384]{1,0:T(8,128)(2,1)S(1)}) custom-call(f32[640,1280]{1,0:T(8,128)S(1)} %get-tuple-element.60.pre, f32[640,640]{1,0:T(8,128)S(1)} %get-tuple-element.61.hid_ref, bf16[640,384]{1,0:T(8,128)(2,1)S(1)} %collective-permute-done.6.x0, bf16[640,384]{1,0:T(8,128)(2,1)S(1)} %collective-permute-done.7.d0, ...), custom_call_target="tpu_custom_call" | custom-call | flops 2516582400 | bytes 12582912 | tf_op jit(solution)/shard_map/pallas_call | solution.py:408
  74.8 0.2 collective-permute-start.14
  75.0 3.5 %shard_map.164 = (f32[640,384]{1,0:T(8,128)S(1)}, bf16[3,640,384]{2,1,0:T(8,128)(2,1)S(1)}) custom-call(bf16[640,1280]{1,0:T(8,128)(2,1)S(1)} %get-tuple-element.72.mid_ref, bf16[3072,1280]{1,0:T(8,128)(2,1)S(1)} %get-tuple-element.64.cat), custom_call_target="tpu_custom_call" | custom-call | flops 2516582400 | bytes 8388608 | tf_op jit(solution)/shard_map/pallas_call | solution.py:417
  78.5 0.1 shard_map.165
  78.6 0.5 collective-permute-start.15
  79.1 1.1 collective-permute-start.16
  80.2 2.1 %collective-permute-start.17 = (bf16[320,384]{1,0:T(8,128)(2,1)S(1)}, bf16[320,384]{1,0:T(8,128)(2,1)S(1)}, u32[]{:S(2)}, u32[]{:S(2)}) collective-permute-start(bf16[320,384]{1,0:T(8,128)(2,1)S(1)} %get-tuple-element.75), channel_id=1, source_target_pairs={{0,6},{2,0},{4,2},{6,4},{1,7},{3,1},{5,3},{7,5},{8,14},{10,8},{12,... | collective-permute-start | bytes 737288 | tf_op jit(solution)/shard_map/ppermute | solution.py:340
  82.3 2.7 %shard_map.166.mine = f32[3,640,384]{2,1,0:T(8,128)S(1)} custom-call(bf16[640,1280]{1,0:T(8,128)(2,1)S(1)} %get-tuple-element.72.mid_ref, bf16[3072,1280]{1,0:T(8,128)(2,1)S(1)} %get-tuple-element.64.cat), custom_call_target="tpu_custom_call" | custom-call | flops 1887436800 | bytes 8388608 | tf_op jit(solution)/shard_map/pallas_call | solution.py:430
  85.0 3.4 %collective-permute-done.16.via_right = bf16[320,384]{1,0:T(8,128)(2,1)S(1)} collective-permute-done((bf16[320,384]{1,0:T(8,128)(2,1)S(1)}, bf16[320,384]{1,0:T(8,128)(2,1)S(1)}, u32[]{:S(2)}, u32[]{:S(2)}) %collective-permute-start.16) | collective-permute-done | bytes 245792 | tf_op jit(solution)/shard_map/ppermute | solution.py:340
  88.5 0.3 shard_map.167
  88.8 1.2 collective-permute-start.18
  90.0 2.1 %collective-permute-start.19 = (bf16[640,384]{1,0:T(8,128)(2,1)S(1)}, bf16[640,384]{1,0:T(8,128)(2,1)S(1)}, u32[]{:S(2)}, u32[]{:S(2)}) collective-permute-start(bf16[640,384]{1,0:T(8,128)(2,1)S(1)} %get-tuple-element.78), channel_id=1, source_target_pairs={{0,6},{2,0},{4,2},{6,4},{1,7},{3,1},{5,3},{7,5},{8,14},{10,8},{12,... | collective-permute-start | bytes 1474568 | tf_op jit(solution)/shard_map/ppermute | solution.py:340
  92.1 6.6 %all-to-all-start.2 = ((bf16[16,128,128]{2,1,0:T(8,128)(2,1)}), bf16[16,128,128]{2,1,0:T(8,128)(2,1)S(1)}, u32[]{:S(2)}, u32[]{:S(2)}) async-start(bf16[16,128,128]{2,1,0:T(8,128)(2,1)} %shard_map.159.refs_13_), calls=%async_computation.2 | async-start | bytes 1048576 | tf_op jit(solution)/shard_map/all_to_all | solution.py:443
  98.7 4.2 %collective-permute-done.18 = bf16[640,384]{1,0:T(8,128)(2,1)S(1)} collective-permute-done((bf16[640,384]{1,0:T(8,128)(2,1)S(1)}, bf16[640,384]{1,0:T(8,128)(2,1)S(1)}, u32[]{:S(2)}, u32[]{:S(2)}) %collective-permute-start.18) | collective-permute-done | bytes 491552 | tf_op jit(solution)/shard_map/ppermute | solution.py:340
  102.9 0.9 add_convert_fusion
  103.8 5.8 %all-to-all-done.2.refs_6_ = bf16[16,128,128]{2,1,0:T(8,128)(2,1)S(1)} async-done(((bf16[16,128,128]{2,1,0:T(8,128)(2,1)}), bf16[16,128,128]{2,1,0:T(8,128)(2,1)S(1)}, u32[]{:S(2)}, u32[]{:S(2)}) %all-to-all-start.2) | async-done | bytes 524320 | tf_op jit(solution)/shard_map/all_to_all | solution.py:443
  109.6 3.6 %all-to-all-start.3 = ((bf16[16,40,384]{2,1,0:T(8,128)(2,1)}), bf16[16,40,384]{2,1,0:T(8,128)(2,1)S(1)}, u32[]{:S(2)}, u32[]{:S(2)}) async-start(bf16[16,40,384]{2,1,0:T(8,128)(2,1)} %bitcast.6), calls=%async_computation.3 | async-start | bytes 983040 | tf_op jit(solution)/shard_map/all_to_all | solution.py:454
  113.2 5.4 %shard_map.160 = (bf16[256,1024]{1,0:T(8,128)(2,1)}, bf16[256,1024]{1,0:T(8,128)(2,1)}, bf16[256,1024]{1,0:T(8,128)(2,1)}) custom-call(f32[8,256]{1,0:T(8,128)} %refs_0_.3, s32[1,256]{1,0:T(1,128)} %bitcast.14, bf16[256,1024]{1,0:T(8,128)(2,1)} %refs_2_.3, bf16[256,1024]{1,0:T(8,128)(2,1)} %refs_3_.3, bf16[256,1024]{1,0:T(8,128)(2,1)} %refs_4_.3, ...), custom_call_target="tpu_custom_call" | custom-call | flops 1073741824 | bytes 4194304 | tf_op jit(solution)/shard_map/pallas_call | solution.py:444
  118.6 4.5 %all-to-all-done.3 = bf16[16,40,384]{2,1,0:T(8,128)(2,1)S(1)} async-done(((bf16[16,40,384]{2,1,0:T(8,128)(2,1)}), bf16[16,40,384]{2,1,0:T(8,128)(2,1)S(1)}, u32[]{:S(2)}, u32[]{:S(2)}) %all-to-all-start.3) | async-done | bytes 491552 | tf_op jit(solution)/shard_map/all_to_all | solution.py:454
  123.1 2.1 %shard_map.168 = bf16[256,384]{1,0:T(8,128)(2,1)} custom-call(bf16[640,384]{1,0:T(8,128)(2,1)S(1)} %bitcast.12, s32[2,256]{1,0:T(2,128)} %get-tuple-element.79.slots_hbm, f32[2,256]{1,0:T(2,128)} %bitcast.16), custom_call_target="tpu_custom_call" | custom-call | flops 251658240 | bytes 1048576 | tf_op jit(solution)/shard_map/pallas_call | solution.py:455
  (14 shorter events, 0.0 us)
Async XLA Ops:
  27.8 11.7 %collective-permute-start.4 = (bf16[640,384]{1,0:T(8,128)(2,1)}, bf16[640,384]{1,0:T(8,128)(2,1)S(1)}, u32[]{:S(2)}, u32[]{:S(2)}) collective-permute-start(bf16[640,384]{1,0:T(8,128)(2,1)} %get-tuple-element.46.x0), channel_id=1, source_target_pairs={{0,1},{1,0},{2,3},{3,2},{4,5},{5,4},{6,7},{7,6},{8,9},{9,8},{10,11... | collective-permute-start | bytes 1474568 | tf_op jit(solution)/shard_map/ppermute | solution.py:343
  27.9 14.7 %collective-permute-start.5 = (bf16[640,384]{1,0:T(8,128)(2,1)}, bf16[640,384]{1,0:T(8,128)(2,1)S(1)}, u32[]{:S(2)}, u32[]{:S(2)}) collective-permute-start(bf16[640,384]{1,0:T(8,128)(2,1)} %get-tuple-element.45.d0), channel_id=1, source_target_pairs={{0,1},{1,0},{2,3},{3,2},{4,5},{5,4},{6,7},{7,6},{8,9},{9,8},{10,11... | collective-permute-start | bytes 1474568 | tf_op jit(solution)/shard_map/ppermute | solution.py:343
  28.4 21.2 %collective-permute-start.2 = (bf16[640,384]{1,0:T(8,128)(2,1)}, bf16[640,384]{1,0:T(8,128)(2,1)S(1)}, u32[]{:S(2)}, u32[]{:S(2)}) collective-permute-start(bf16[640,384]{1,0:T(8,128)(2,1)} %get-tuple-element.46.x0), channel_id=1, source_target_pairs={{0,2},{2,4},{4,6},{6,0},{1,3},{3,5},{5,7},{7,1},{8,10},{10,12},{12... | collective-permute-start | bytes 1474568 | tf_op jit(solution)/shard_map/ppermute | solution.py:340
  29.9 19.7 %collective-permute-start.3 = (bf16[640,384]{1,0:T(8,128)(2,1)}, bf16[640,384]{1,0:T(8,128)(2,1)S(1)}, u32[]{:S(2)}, u32[]{:S(2)}) collective-permute-start(bf16[640,384]{1,0:T(8,128)(2,1)} %get-tuple-element.45.d0), channel_id=1, source_target_pairs={{0,6},{2,0},{4,2},{6,4},{1,7},{3,1},{5,3},{7,5},{8,14},{10,8},{12,... | collective-permute-start | bytes 1474568 | tf_op jit(solution)/shard_map/ppermute | solution.py:340
  35.6 18.0 %all-to-all-start.1 = ((bf16[16,144,128]{2,1,0:T(8,128)(2,1)}), bf16[16,144,128]{2,1,0:T(8,128)(2,1)S(1)}, u32[]{:S(2)}, u32[]{:S(2)}) async-start(bf16[16,144,128]{2,1,0:T(8,128)(2,1)} %shard_map.158), calls=%async_computation.1 | async-start | bytes 1179648 | tf_op jit(solution)/shard_map/all_to_all | solution.py:374
  39.2 14.4 %collective-permute-start = (bf16[640,384]{1,0:T(8,128)(2,1)}, bf16[640,384]{1,0:T(8,128)(2,1)S(1)}, u32[]{:S(2)}, u32[]{:S(2)}) collective-permute-start(bf16[640,384]{1,0:T(8,128)(2,1)} %get-tuple-element.45.d0), channel_id=1, source_target_pairs={{0,2},{2,4},{4,6},{6,0},{1,3},{3,5},{5,7},{7,1},{8,10},{10,12},{12... | collective-permute-start | bytes 1474568 | tf_op jit(solution)/shard_map/ppermute | solution.py:340
  39.5 14.0 %collective-permute-start.1 = (bf16[640,384]{1,0:T(8,128)(2,1)}, bf16[640,384]{1,0:T(8,128)(2,1)S(1)}, u32[]{:S(2)}, u32[]{:S(2)}) collective-permute-start(bf16[640,384]{1,0:T(8,128)(2,1)} %get-tuple-element.46.x0), channel_id=1, source_target_pairs={{0,6},{2,0},{4,2},{6,4},{1,7},{3,1},{5,3},{7,5},{8,14},{10,8},{12,... | collective-permute-start | bytes 1474568 | tf_op jit(solution)/shard_map/ppermute | solution.py:340
  49.6 6.0 %collective-permute-start.11 = (bf16[640,384]{1,0:T(8,128)(2,1)S(1)}, bf16[640,384]{1,0:T(8,128)(2,1)S(1)}, u32[]{:S(2)}, u32[]{:S(2)}) collective-permute-start(bf16[640,384]{1,0:T(8,128)(2,1)S(1)} %collective-permute-done.3.refs_5_), channel_id=1, source_target_pairs={{0,1},{1,0},{2,3},{3,2},{4,5},{5,4},{6,7},{7,6},{8,9},{9,8},{10,11... | collective-permute-start | bytes 1474568 | tf_op jit(solution)/shard_map/ppermute | solution.py:343
  49.7 8.6 %collective-permute-start.8 = (bf16[640,384]{1,0:T(8,128)(2,1)S(1)}, bf16[640,384]{1,0:T(8,128)(2,1)S(1)}, u32[]{:S(2)}, u32[]{:S(2)}) collective-permute-start(bf16[640,384]{1,0:T(8,128)(2,1)S(1)} %collective-permute-done.2.refs_0_), channel_id=1, source_target_pairs={{0,1},{1,0},{2,3},{3,2},{4,5},{5,4},{6,7},{7,6},{8,9},{9,8},{10,11... | collective-permute-start | bytes 1474568 | tf_op jit(solution)/shard_map/ppermute | solution.py:343
  53.6 4.7 %collective-permute-start.10 = (bf16[640,384]{1,0:T(8,128)(2,1)S(1)}, bf16[640,384]{1,0:T(8,128)(2,1)S(1)}, u32[]{:S(2)}, u32[]{:S(2)}) collective-permute-start(bf16[640,384]{1,0:T(8,128)(2,1)S(1)} %collective-permute-done.1.refs_4_), channel_id=1, source_target_pairs={{0,1},{1,0},{2,3},{3,2},{4,5},{5,4},{6,7},{7,6},{8,9},{9,8},{10,11... | collective-permute-start | bytes 1474568 | tf_op jit(solution)/shard_map/ppermute | solution.py:343
  53.6 4.7 %collective-permute-start.9 = (bf16[640,384]{1,0:T(8,128)(2,1)S(1)}, bf16[640,384]{1,0:T(8,128)(2,1)S(1)}, u32[]{:S(2)}, u32[]{:S(2)}) collective-permute-start(bf16[640,384]{1,0:T(8,128)(2,1)S(1)} %collective-permute-done.refs_1_), channel_id=1, source_target_pairs={{0,1},{1,0},{2,3},{3,2},{4,5},{5,4},{6,7},{7,6},{8,9},{9,8},{10,11... | collective-permute-start | bytes 1474568 | tf_op jit(solution)/shard_map/ppermute | solution.py:343
  54.1 14.4 %collective-permute-start.6 = (bf16[640,384]{1,0:T(8,128)(2,1)S(1)}, bf16[640,384]{1,0:T(8,128)(2,1)S(1)}, u32[]{:S(2)}, u32[]{:S(2)}) collective-permute-start(bf16[640,384]{1,0:T(8,128)(2,1)S(1)} %collective-permute-done.2.refs_0_), channel_id=1, source_target_pairs={{0,2},{2,4},{4,6},{6,0},{1,3},{3,5},{5,7},{7,1},{8,10},{10,12},{12... | collective-permute-start | bytes 1474568 | tf_op jit(solution)/shard_map/ppermute | solution.py:340
  55.6 12.9 %collective-permute-start.7 = (bf16[640,384]{1,0:T(8,128)(2,1)S(1)}, bf16[640,384]{1,0:T(8,128)(2,1)S(1)}, u32[]{:S(2)}, u32[]{:S(2)}) collective-permute-start(bf16[640,384]{1,0:T(8,128)(2,1)S(1)} %collective-permute-done.3.refs_5_), channel_id=1, source_target_pairs={{0,6},{2,0},{4,2},{6,4},{1,7},{3,1},{5,3},{7,5},{8,14},{10,8},{12,... | collective-permute-start | bytes 1474568 | tf_op jit(solution)/shard_map/ppermute | solution.py:340
  68.5 1.9 %collective-permute-start.12 = (bf16[640,384]{1,0:T(8,128)(2,1)S(1)}, bf16[640,384]{1,0:T(8,128)(2,1)S(1)}, u32[]{:S(2)}, u32[]{:S(2)}) collective-permute-start(bf16[640,384]{1,0:T(8,128)(2,1)S(1)} %collective-permute-done.6.x0), channel_id=1, source_target_pairs={{0,1},{1,0},{2,3},{3,2},{4,5},{5,4},{6,7},{7,6},{8,9},{9,8},{10,11... | collective-permute-start | bytes 1474568 | tf_op jit(solution)/shard_map/ppermute | solution.py:343
  68.5 2.6 %collective-permute-start.13 = (bf16[640,384]{1,0:T(8,128)(2,1)S(1)}, bf16[640,384]{1,0:T(8,128)(2,1)S(1)}, u32[]{:S(2)}, u32[]{:S(2)}) collective-permute-start(bf16[640,384]{1,0:T(8,128)(2,1)S(1)} %collective-permute-done.7.d0), channel_id=1, source_target_pairs={{0,1},{1,0},{2,3},{3,2},{4,5},{5,4},{6,7},{7,6},{8,9},{9,8},{10,11... | collective-permute-start | bytes 1474568 | tf_op jit(solution)/shard_map/ppermute | solution.py:343
  74.8 3.8 %collective-permute-start.14 = (bf16[640,384]{1,0:T(8,128)(2,1)S(1)}, bf16[640,384]{1,0:T(8,128)(2,1)S(1)}, u32[]{:S(2)}, u32[]{:S(2)}) collective-permute-start(bf16[640,384]{1,0:T(8,128)(2,1)S(1)} %get-tuple-element.69), channel_id=1, source_target_pairs={{0,1},{1,0},{2,3},{3,2},{4,5},{5,4},{6,7},{7,6},{8,9},{9,8},{10,11... | collective-permute-start | bytes 1474568 | tf_op jit(solution)/shard_map/ppermute | solution.py:343
  78.6 9.8 %collective-permute-start.15 = (bf16[3,640,384]{2,1,0:T(8,128)(2,1)S(1)}, bf16[3,640,384]{2,1,0:T(8,128)(2,1)S(1)}, u32[]{:S(2)}, u32[]{:S(2)}) collective-permute-start(bf16[3,640,384]{2,1,0:T(8,128)(2,1)S(1)} %get-tuple-element.73), channel_id=1, source_target_pairs={{0,1},{1,0},{2,3},{3,2},{4,5},{5,4},{6,7},{7,6},{8,9},{9,8},{10,11... | collective-permute-start | bytes 4423688 | tf_op jit(solution)/shard_map/ppermute | solution.py:343
  79.1 9.4 %collective-permute-start.16 = (bf16[320,384]{1,0:T(8,128)(2,1)S(1)}, bf16[320,384]{1,0:T(8,128)(2,1)S(1)}, u32[]{:S(2)}, u32[]{:S(2)}) collective-permute-start(bf16[320,384]{1,0:T(8,128)(2,1)S(1)} %get-tuple-element.74), channel_id=1, source_target_pairs={{0,2},{2,4},{4,6},{6,0},{1,3},{3,5},{5,7},{7,1},{8,10},{10,12},{12... | collective-permute-start | bytes 737288 | tf_op jit(solution)/shard_map/ppermute | solution.py:340
  80.2 8.3 %collective-permute-start.17 = (bf16[320,384]{1,0:T(8,128)(2,1)S(1)}, bf16[320,384]{1,0:T(8,128)(2,1)S(1)}, u32[]{:S(2)}, u32[]{:S(2)}) collective-permute-start(bf16[320,384]{1,0:T(8,128)(2,1)S(1)} %get-tuple-element.75), channel_id=1, source_target_pairs={{0,6},{2,0},{4,2},{6,4},{1,7},{3,1},{5,3},{7,5},{8,14},{10,8},{12,... | collective-permute-start | bytes 737288 | tf_op jit(solution)/shard_map/ppermute | solution.py:340
  88.8 14.1 %collective-permute-start.18 = (bf16[640,384]{1,0:T(8,128)(2,1)S(1)}, bf16[640,384]{1,0:T(8,128)(2,1)S(1)}, u32[]{:S(2)}, u32[]{:S(2)}) collective-permute-start(bf16[640,384]{1,0:T(8,128)(2,1)S(1)} %get-tuple-element.77), channel_id=1, source_target_pairs={{0,2},{2,4},{4,6},{6,0},{1,3},{3,5},{5,7},{7,1},{8,10},{10,12},{12... | collective-permute-start | bytes 1474568 | tf_op jit(solution)/shard_map/ppermute | solution.py:340
  90.0 12.9 %collective-permute-start.19 = (bf16[640,384]{1,0:T(8,128)(2,1)S(1)}, bf16[640,384]{1,0:T(8,128)(2,1)S(1)}, u32[]{:S(2)}, u32[]{:S(2)}) collective-permute-start(bf16[640,384]{1,0:T(8,128)(2,1)S(1)} %get-tuple-element.78), channel_id=1, source_target_pairs={{0,6},{2,0},{4,2},{6,4},{1,7},{3,1},{5,3},{7,5},{8,14},{10,8},{12,... | collective-permute-start | bytes 1474568 | tf_op jit(solution)/shard_map/ppermute | solution.py:340
  92.1 17.5 %all-to-all-start.2 = ((bf16[16,128,128]{2,1,0:T(8,128)(2,1)}), bf16[16,128,128]{2,1,0:T(8,128)(2,1)S(1)}, u32[]{:S(2)}, u32[]{:S(2)}) async-start(bf16[16,128,128]{2,1,0:T(8,128)(2,1)} %shard_map.159.refs_13_), calls=%async_computation.2 | async-start | bytes 1048576 | tf_op jit(solution)/shard_map/all_to_all | solution.py:443
  109.6 13.5 %all-to-all-start.3 = ((bf16[16,40,384]{2,1,0:T(8,128)(2,1)}), bf16[16,40,384]{2,1,0:T(8,128)(2,1)S(1)}, u32[]{:S(2)}, u32[]{:S(2)}) async-start(bf16[16,40,384]{2,1,0:T(8,128)(2,1)} %bitcast.6), calls=%async_computation.3 | async-start | bytes 983040 | tf_op jit(solution)/shard_map/all_to_all | solution.py:454

commit v9 on v7

--- a/solution.py
+++ b/solution.py
@@ -93,9 +93,7 @@
     leaving.wait()
 
 
-def combine_kernel(rows_ref, slots_hbm, weights_hbm, out_ref, slots_ref, weights_ref, sems):
-    for copy in fetch(((slots_hbm, slots_ref), (weights_hbm, weights_ref)), sems):
-        copy.wait()
+def combine_kernel(rows_ref, slots_ref, weights_ref, out_ref):
     columns = jnp.concatenate([weights_ref[...], jnp.zeros((6, TOK), F32)], axis=0).T
     total = jnp.zeros((TOK, FEAT), F32)
     for k in range(2):
@@ -308,13 +306,9 @@
         rest_ref[i] = out_block(mid_ref, cat, offset, 1).astype(BF)
 
 
-def expert_rest_kernel(mid_ref, cat, away, left_ref, right_ref, left_sum, right_sum, here_ref):
-    left, right, here = [out_block(mid_ref, cat, offset, 0) + away[i].astype(F32) for i, offset in enumerate(OUT_ORDER[1:])]
-    left_ref[...] = left[:CUT].astype(BF)
-    left_sum[...] = left[CUT:]
-    right_sum[...] = right[:CUT]
-    right_ref[...] = right[CUT:].astype(BF)
-    here_ref[...] = here
+def expert_rest_kernel(mid_ref, cat, rest_ref):
+    for i, offset in enumerate(OUT_ORDER[1:]):
+        rest_ref[i] = out_block(mid_ref, cat, offset, 0)
 
 
 def far_kernel(mine, away, right_ref, left_ref):
@@ -322,16 +316,12 @@
     left_ref[...] = (mine[CUT:] + away[CUT:].astype(F32)).astype(BF)
 
 
-def near_kernel(left_sum, right_sum, via_left, via_right, left_ref, right_ref):
-    left_ref[...] = (left_sum[...] + via_left[...].astype(F32)).astype(BF)
-    right_ref[...] = (right_sum[...] + via_right[...].astype(F32)).astype(BF)
-
-
-def sum_kernel(here, from_right_a, from_right_b, from_left_a, from_left_b, out_ref):
-    top = here[:CUT] + from_right_a[...].astype(F32) + from_left_b[...].astype(F32)
-    out_ref[:CUT] = top.astype(BF)
-    low = here[CUT:] + from_right_b[...].astype(F32) + from_left_a[...].astype(F32)
-    out_ref[CUT:] = low.astype(BF)
+def near_kernel(mine, away, via_right, via_left, left_ref, right_ref, here_ref):
+    left_ref[:CUT] = (mine[0, :CUT] + away[0, :CUT].astype(F32)).astype(BF)
+    left_ref[CUT:] = (mine[0, CUT:] + away[0, CUT:].astype(F32) + via_left[...].astype(F32)).astype(BF)
+    right_ref[:CUT] = (mine[1, :CUT] + away[1, :CUT].astype(F32) + via_right[...].astype(F32)).astype(BF)
+    right_ref[CUT:] = (mine[1, CUT:] + away[1, CUT:].astype(F32)).astype(BF)
+    here_ref[...] = mine[2] + away[2].astype(F32)
 
 
 def local(
@@ -438,22 +428,20 @@
     to_right, to_left = call(far_kernel, (half, half), [vmem()] * 2, size=2 * MIB, flops=MIB, limit=8)(mine_far, away_far)
     mid, away_rest, to_right, to_left = tie((mid, away_rest, to_right, to_left))
     away_rest = swap(away_rest)
-    wide = S((CUT, FEAT), F32)
-    left_a, right_a, left_sum, right_sum, here = call(
+    mine_rest = call(
         expert_rest_kernel,
-        (half, half, wide, wide, S((ROWS, FEAT), F32)),
-        [vmem()] * 3,
+        S(rest, F32),
+        [vmem()] * 2,
         flops=3 * ROWS * HID * RINGX * FEAT,
         size=8 * MIB,
-        limit=20,
-    )(mid, cat, away_rest)
+        limit=18,
+    )(mid, cat)
+    mine_rest, scanned = tie((mine_rest, scanned))
     via_right, via_left = ring(to_right, RIGHT), ring(to_left, LEFT)
-    left_a, right_a = ring(left_a, LEFT), ring(right_a, RIGHT)
-    here, scanned = tie((here, scanned))
-    via_right, via_left, left_a, right_a = tie((via_right, via_left, left_a, right_a))
-    left_b, right_b = call(near_kernel, (half, half), [vmem()] * 4, limit=6)(left_sum, right_sum, via_left, via_right)
-    left_b, right_b = ring(left_b, LEFT), ring(right_b, RIGHT)
-    summed = call(sum_kernel, block, [vmem()] * 5, size=4 * MIB, flops=MIB, limit=8)(here, left_a, left_b, right_a, right_b)
+    to_left, to_right, here = call(
+        near_kernel, (block, block, S((ROWS, FEAT), F32)), [vmem()] * 4, size=5 * MIB, flops=MIB, limit=16
+    )(mine_rest, away_rest, via_right, via_left)
+    summed = (here + ring(to_right, RIGHT).astype(F32) + ring(to_left, LEFT).astype(F32)).astype(BF)
     carried = lax.all_to_all(scanned, "ctx", 0, 0, tiled=True)
     grads = call(
         attention_kernel,
@@ -469,12 +457,11 @@
     grad_moe = call(
         combine_kernel,
         S((TOK, FEAT), BF),
-        [vmem()] + [anywhere()] * 2,
-        [pltpu.VMEM((2, TOK), I32), pltpu.VMEM((2, TOK), F32), pltpu.SemaphoreType.DMA((2,))],
+        [vmem()] * 3,
         flops=4 * ROWS * TOK * FEAT,
         size=MIB,
         limit=8,
-    )(back.reshape(ROWS, FEAT), in_hbm(slots), in_hbm(router_weights.T))
+    )(back.reshape(ROWS, FEAT), slots, router_weights.T)
     return (*grads, grad_moe)
 
 

time: 123 us -> 121 us (0.984)
  starting transfers between devices: 27.9 us -> 25.5 us
  Pallas kernels: 40 us -> 37.8 us
  waiting for transfers between devices: 28.5 us -> 30 us
    all_to_all x1, waiting for transfers between devices: 0.01 us -> 2.97 us  [local(): carried = lax.all_to_all(scanned, 'ctx', 0, 0, tiled=True)]
    ppermute x10 -> x8, starting transfers between devices: 14.8 us -> 13.1 us  [ring(): return lax.ppermute(value, 'x', way)]
    ppermute x10 -> x8, waiting for transfers between devices: 16.4 us -> 14.8 us  [ring(): return lax.ppermute(value, 'x', way)]
    pallas_call x4 -> x3, Pallas kernels: 5.77 us -> 4.34 us  [the longest x1 2.7 us: local(): call(expert_rest_kernel, S(rest, F32), [vmem()] * 2, flops=3 * ROWS * HID...]
  transfers between devices with their start and end apart: 20 -> 18, of which waited for: 10 -> 9; matrix products, arithmetic and copies ran while one was open for 0% -> 1% of each run, Pallas kernels for 26% -> 26%
where the time goes in v9:
time: 121 us; the launch traced here: 120 us
  Pallas kernels  37.8 us (31%)
  waiting for transfers between devices  30 us (25%)
  starting transfers between devices  25.5 us (21%)
  blocking collectives  24.4 us (20%)
    all_to_all x1, blocking collectives, local(): lax.all_to_all(rows.reshape(CTX, CAP, 2 * FEAT), 'ctx', 0, 0, tiled=True)  24.4 us
    ppermute x8, waiting for transfers between devices, ring(): return lax.ppermute(value, 'x', way)  14.8 us
    ppermute x8, starting transfers between devices, ring(): return lax.ppermute(value, 'x', way)  13.1 us
    pallas_call x1, Pallas kernels, local(): call(expert_early_kernel, (S((ROWS, 2 * HID), F32), S((ROWS, HID), F32),...  8.12 us
    pallas_call x1, Pallas kernels, local(): call(expert_own_kernel, (pltpu.HBM((ROWS, 2 * HID), F32), pltpu.HBM((ROWS...  6.97 us
    all_to_all x1, waiting for transfers between devices, local(): arrived = lax.all_to_all(message, 'ctx', 0, 0, tiled=True)  5.53 us
    pallas_call x1, Pallas kernels, local(): call(attention_kernel, (S((TOK, HEADS * HD), BF),) * 3, [anywhere()] * 6...  5.4 us
    all_to_all x1, waiting for transfers between devices, local(): lax.all_to_all(summed.reshape(CTX, CAP, FEAT), 'ctx', 0, 0, tiled=True)  4.62 us
  transfers between devices with their start and end apart: 18, of which 9 were waited for; matrix products, arithmetic and copies ran while one was open for 1% of the time, Pallas kernels for 26%

profile of v9, /device:TPU:0, one launch (start us, length us, event | category | flops | bytes accessed | tf_op | source)
XLA Modules:
  0.0 120.4 jit_solution(11821420656483573651)
XLA Ops:
  0.6 1.7 %shard_map.156 = (bf16[640,768]{1,0:T(8,128)(2,1)S(1)}, s32[2,256]{1,0:T(2,128)}) custom-call(s32[2,256]{1,0:T(2,128)} %bitcast.19, bf16[256,384]{1,0:T(8,128)(2,1)} %x_hbm.1, bf16[256,384]{1,0:T(8,128)(2,1)} %d_hbm.1), custom_call_target="tpu_custom_call" | custom-call | flops 251658240 | bytes 2097152 | tf_op jit(solution)/shard_map/pallas_call | solution.py:342
  2.4 24.4 %all_to_all.20 = bf16[16,40,768]{2,1,0:T(8,128)(2,1)S(1)} all-to-all(bf16[16,40,768]{2,1,0:T(8,128)(2,1)S(1)} %bitcast.14), channel_id=1, replica_groups=mesh['ctx'=16,'x'=4,'core'=2] {'ctx'}, dimensions={0} | all-to-all | bytes 1966080 | tf_op jit(solution)/shard_map/all_to_all | solution.py:351
  26.7 0.0 collective-permute-start.2
  26.7 1.5 %collective-permute-start = (bf16[640,768]{1,0:T(8,128)(2,1)S(1)}, bf16[640,768]{1,0:T(8,128)(2,1)S(1)}, u32[]{:S(2)}, u32[]{:S(2)}) collective-permute-start(bf16[640,768]{1,0:T(8,128)(2,1)S(1)} %bitcast.10), channel_id=1, source_target_pairs={{0,2},{2,4},{4,6},{6,0},{1,3},{3,5},{5,7},{7,1},{8,10},{10,12},{12... | collective-permute-start | bytes 2949128 | tf_op jit(solution)/shard_map/ppermute | solution.py:337
  28.2 1.7 %collective-permute-start.1 = (bf16[640,768]{1,0:T(8,128)(2,1)S(1)}, bf16[640,768]{1,0:T(8,128)(2,1)S(1)}, u32[]{:S(2)}, u32[]{:S(2)}) collective-permute-start(bf16[640,768]{1,0:T(8,128)(2,1)S(1)} %bitcast.11), channel_id=1, source_target_pairs={{0,6},{2,0},{4,2},{6,4},{1,7},{3,1},{5,3},{7,5},{8,14},{10,8},{12,... | collective-permute-start | bytes 2949128 | tf_op jit(solution)/shard_map/ppermute | solution.py:337
  30.0 3.1 %shard_map.157 = bf16[16,144,128]{2,1,0:T(8,128)(2,1)S(1)} custom-call(f32[8,256]{1,0:T(8,128)} %refs_0_.3, s32[1,256]{1,0:T(1,128)} %bitcast.17, bf16[256,1024]{1,0:T(8,128)(2,1)} %refs_2_.3, bf16[256,1024]{1,0:T(8,128)(2,1)} %refs_3_.3, bf16[256,1024]{1,0:T(8,128)(2,1)} %refs_4_.5, bf16[256,1024]{1,0:T(8,128)(2,1)} %refs_5_.5, bf16[640,768]{1,0:T(8,128)(2,1)S(1)} %bitcast.12), custom_call_target="tpu_custom_call" | custom-call | flops 134217728 | bytes 3145728 | tf_op jit(solution)/shard_map/pallas_call | solution.py:357
  33.1 0.8 copy-done
  33.9 3.6 %all-to-all-start.1 = ((bf16[16,144,128]{2,1,0:T(8,128)(2,1)}), bf16[16,144,128]{2,1,0:T(8,128)(2,1)S(1)}, u32[]{:S(2)}, u32[]{:S(2)}) async-start(bf16[16,144,128]{2,1,0:T(8,128)(2,1)} %copy-done), calls=%async_computation.1 | async-start | bytes 1179648 | tf_op jit(solution)/shard_map/all_to_all | solution.py:366
  37.5 0.1 pad_add_fusion.place
  37.6 0.0 collective-permute-done.2.a1
  37.6 7.0 %shard_map.158 = (f32[640,1280]{1,0:T(8,128)}, f32[640,640]{1,0:T(8,128)}) custom-call(s32[2]{0:T(128)S(1)} %pad_add_fusion.place, bf16[640,768]{1,0:T(8,128)(2,1)S(1)} %bitcast.13, bf16[640,768]{1,0:T(8,128)(2,1)} %collective-permute-done.2.a1, bf16[1,3072,640]{2,1,0:T(8,128)(2,1)} %refs_4_.4, bf16[1,3072,640]{2,1,0:T(8,128)(2,1)} %refs_5_.4, ...), custom_call_target="tpu_custom_call" | custom-call | flops 1887436800 | bytes 12582912 | tf_op jit(solution)/shard_map/pallas_call | solution.py:370
  44.6 5.5 %all-to-all-done.1.in_ref = bf16[16,144,128]{2,1,0:T(8,128)(2,1)S(1)} async-done(((bf16[16,144,128]{2,1,0:T(8,128)(2,1)}), bf16[16,144,128]{2,1,0:T(8,128)(2,1)S(1)}, u32[]{:S(2)}, u32[]{:S(2)}) %all-to-all-start.1) | async-done | bytes 589856 | tf_op jit(solution)/shard_map/all_to_all | solution.py:366
  50.1 2.0 %collective-permute-done.from_left.refs_0_ = bf16[640,768]{1,0:T(8,128)(2,1)S(1)} collective-permute-done((bf16[640,768]{1,0:T(8,128)(2,1)S(1)}, bf16[640,768]{1,0:T(8,128)(2,1)S(1)}, u32[]{:S(2)}, u32[]{:S(2)}) %collective-permute-start) | collective-permute-done | bytes 983072 | tf_op jit(solution)/shard_map/ppermute | solution.py:337
  52.1 0.0 collective-permute-done.1.from_right.refs_2_
  52.1 0.0 collective-permute-start.5
  52.1 0.5 collective-permute-start.6
  52.6 0.1 shard_map.159
  52.8 1.6 %collective-permute-start.3 = (bf16[640,384]{1,0:T(8,128)(2,1)S(1)}, bf16[640,384]{1,0:T(8,128)(2,1)S(1)}, u32[]{:S(2)}, u32[]{:S(2)}) collective-permute-start(bf16[640,384]{1,0:T(8,128)(2,1)S(1)} %get-tuple-element.43), channel_id=1, source_target_pairs={{0,2},{2,4},{4,6},{6,0},{1,3},{3,5},{5,7},{7,1},{8,10},{10,12},{12... | collective-permute-start | bytes 1474568 | tf_op jit(solution)/shard_map/ppermute | solution.py:337
  54.3 1.7 %collective-permute-start.4 = (bf16[640,384]{1,0:T(8,128)(2,1)S(1)}, bf16[640,384]{1,0:T(8,128)(2,1)S(1)}, u32[]{:S(2)}, u32[]{:S(2)}) collective-permute-start(bf16[640,384]{1,0:T(8,128)(2,1)S(1)} %get-tuple-element.44), channel_id=1, source_target_pairs={{0,6},{2,0},{4,2},{6,4},{1,7},{3,1},{5,3},{7,5},{8,14},{10,8},{12,... | collective-permute-start | bytes 1474568 | tf_op jit(solution)/shard_map/ppermute | solution.py:337
  56.1 1.0 shard_map.160.refs_9_
  57.0 0.0 collective-permute-done.5.refs_1_
  57.0 8.1 %shard_map.161 = (f32[640,1280]{1,0:T(8,128)S(1)}, f32[640,640]{1,0:T(8,128)S(1)}, bf16[3072,1280]{1,0:T(8,128)(2,1)S(1)}, bf16[640,768]{1,0:T(8,128)(2,1)S(1)}) custom-call(s32[2]{0:T(128)S(1)} %pad_add_fusion.place, bf16[640,768]{1,0:T(8,128)(2,1)S(1)} %collective-permute-done.from_left.refs_0_, bf16[640,768]{1,0:T(8,128)(2,1)S(1)} %collective-permute-done.5.refs_1_, ...), custom_call_target="tpu_custom_call" | custom-call | flops 3774873600 | bytes 25165824 | tf_op jit(solution)/shard_map/pallas_call | solution.py:396
  65.2 2.0 %collective-permute-done.3.x0 = bf16[640,384]{1,0:T(8,128)(2,1)S(1)} collective-permute-done((bf16[640,384]{1,0:T(8,128)(2,1)S(1)}, bf16[640,384]{1,0:T(8,128)(2,1)S(1)}, u32[]{:S(2)}, u32[]{:S(2)}) %collective-permute-start.3) | collective-permute-done | bytes 491552 | tf_op jit(solution)/shard_map/ppermute | solution.py:337
  67.2 0.5 collective-permute-start.8
  67.7 1.4 %collective-permute-done.7.x1 = bf16[640,384]{1,0:T(8,128)(2,1)S(1)} collective-permute-done((bf16[640,384]{1,0:T(8,128)(2,1)S(1)}, bf16[640,384]{1,0:T(8,128)(2,1)S(1)}, u32[]{:S(2)}, u32[]{:S(2)}) %collective-permute-start.7) | collective-permute-done | bytes 491552 | tf_op jit(solution)/shard_map/ppermute | solution.py:340
  69.0 0.7 collective-permute-done.8.d1
  69.7 3.4 %shard_map.162 = (bf16[640,1280]{1,0:T(8,128)(2,1)S(1)}, bf16[640,384]{1,0:T(8,128)(2,1)S(1)}) custom-call(f32[640,1280]{1,0:T(8,128)S(1)} %get-tuple-element.49.pre, f32[640,640]{1,0:T(8,128)S(1)} %get-tuple-element.50.hid_ref, bf16[640,384]{1,0:T(8,128)(2,1)S(1)} %collective-permute-done.3.x0, bf16[640,384]{1,0:T(8,128)(2,1)S(1)} %collective-permute-done.4.d0, ...), custom_call_target="tpu_custom_call" | custom-call | flops 2516582400 | bytes 12582912 | tf_op jit(solution)/shard_map/pallas_call | solution.py:409
  73.2 0.2 collective-permute-start.9
  73.4 3.5 %shard_map.163 = (f32[640,384]{1,0:T(8,128)S(1)}, bf16[3,640,384]{2,1,0:T(8,128)(2,1)S(1)}) custom-call(bf16[640,1280]{1,0:T(8,128)(2,1)S(1)} %get-tuple-element.61.mid_ref, bf16[3072,1280]{1,0:T(8,128)(2,1)S(1)} %get-tuple-element.53.cat), custom_call_target="tpu_custom_call" | custom-call | flops 2516582400 | bytes 8388608 | tf_op jit(solution)/shard_map/pallas_call | solution.py:418
  76.9 0.0 collective-permute-done.9.away
  76.9 0.1 shard_map.164
  77.0 0.5 collective-permute-start.10
  77.5 1.2 collective-permute-start.11
  78.7 2.1 %collective-permute-start.12 = (bf16[320,384]{1,0:T(8,128)(2,1)S(1)}, bf16[320,384]{1,0:T(8,128)(2,1)S(1)}, u32[]{:S(2)}, u32[]{:S(2)}) collective-permute-start(bf16[320,384]{1,0:T(8,128)(2,1)S(1)} %get-tuple-element.69), channel_id=1, source_target_pairs={{0,6},{2,0},{4,2},{6,4},{1,7},{3,1},{5,3},{7,5},{8,14},{10,8},{12,... | collective-permute-start | bytes 737288 | tf_op jit(solution)/shard_map/ppermute | solution.py:337
  80.7 2.7 %shard_map.165.mine = f32[3,640,384]{2,1,0:T(8,128)S(1)} custom-call(bf16[640,1280]{1,0:T(8,128)(2,1)S(1)} %get-tuple-element.61.mid_ref, bf16[3072,1280]{1,0:T(8,128)(2,1)S(1)} %get-tuple-element.53.cat), custom_call_target="tpu_custom_call" | custom-call | flops 1887436800 | bytes 8388608 | tf_op jit(solution)/shard_map/pallas_call | solution.py:431
  83.4 3.5 %collective-permute-done.11.via_right = bf16[320,384]{1,0:T(8,128)(2,1)S(1)} collective-permute-done((bf16[320,384]{1,0:T(8,128)(2,1)S(1)}, bf16[320,384]{1,0:T(8,128)(2,1)S(1)}, u32[]{:S(2)}, u32[]{:S(2)}) %collective-permute-start.11) | collective-permute-done | bytes 245792 | tf_op jit(solution)/shard_map/ppermute | solution.py:337
  87.0 0.3 shard_map.167
  87.3 1.2 %collective-permute-start.13 = (bf16[640,384]{1,0:T(8,128)(2,1)S(1)}, bf16[640,384]{1,0:T(8,128)(2,1)S(1)}, u32[]{:S(2)}, u32[]{:S(2)}) collective-permute-start(bf16[640,384]{1,0:T(8,128)(2,1)S(1)} %get-tuple-element.71), channel_id=1, source_target_pairs={{0,2},{2,4},{4,6},{6,0},{1,3},{3,5},{5,7},{7,1},{8,10},{10,12},{12... | collective-permute-start | bytes 1474568 | tf_op jit(solution)/shard_map/ppermute | solution.py:337
  88.5 2.1 %collective-permute-start.14 = (bf16[640,384]{1,0:T(8,128)(2,1)S(1)}, bf16[640,384]{1,0:T(8,128)(2,1)S(1)}, u32[]{:S(2)}, u32[]{:S(2)}) collective-permute-start(bf16[640,384]{1,0:T(8,128)(2,1)S(1)} %get-tuple-element.72), channel_id=1, source_target_pairs={{0,6},{2,0},{4,2},{6,4},{1,7},{3,1},{5,3},{7,5},{8,14},{10,8},{12,... | collective-permute-start | bytes 1474568 | tf_op jit(solution)/shard_map/ppermute | solution.py:337
  90.6 3.6 %all-to-all-start.2 = ((bf16[16,128,128]{2,1,0:T(8,128)(2,1)}), bf16[16,128,128]{2,1,0:T(8,128)(2,1)S(1)}, u32[]{:S(2)}, u32[]{:S(2)}) async-start(bf16[16,128,128]{2,1,0:T(8,128)(2,1)} %shard_map.160.refs_9_), calls=%async_computation.2 | async-start | bytes 1048576 | tf_op jit(solution)/shard_map/all_to_all | solution.py:445
  94.2 7.3 %collective-permute-done.13 = bf16[640,384]{1,0:T(8,128)(2,1)S(1)} collective-permute-done((bf16[640,384]{1,0:T(8,128)(2,1)S(1)}, bf16[640,384]{1,0:T(8,128)(2,1)S(1)}, u32[]{:S(2)}, u32[]{:S(2)}) %collective-permute-start.13) | collective-permute-done | bytes 491552 | tf_op jit(solution)/shard_map/ppermute | solution.py:337
  101.5 0.0 collective-permute-done.14
  101.5 1.0 add_convert_fusion
  102.5 3.0 %all-to-all-done.2.refs_6_ = bf16[16,128,128]{2,1,0:T(8,128)(2,1)S(1)} async-done(((bf16[16,128,128]{2,1,0:T(8,128)(2,1)}), bf16[16,128,128]{2,1,0:T(8,128)(2,1)S(1)}, u32[]{:S(2)}, u32[]{:S(2)}) %all-to-all-start.2) | async-done | bytes 524320 | tf_op jit(solution)/shard_map/all_to_all | solution.py:445
  105.4 3.6 %all-to-all-start.3 = ((bf16[16,40,384]{2,1,0:T(8,128)(2,1)}), bf16[16,40,384]{2,1,0:T(8,128)(2,1)S(1)}, u32[]{:S(2)}, u32[]{:S(2)}) async-start(bf16[16,40,384]{2,1,0:T(8,128)(2,1)} %bitcast.6), calls=%async_computation.3 | async-start | bytes 983040 | tf_op jit(solution)/shard_map/all_to_all | solution.py:456
  109.0 5.4 %shard_map.166 = (bf16[256,1024]{1,0:T(8,128)(2,1)}, bf16[256,1024]{1,0:T(8,128)(2,1)}, bf16[256,1024]{1,0:T(8,128)(2,1)}) custom-call(f32[8,256]{1,0:T(8,128)} %refs_0_.3, s32[1,256]{1,0:T(1,128)} %bitcast.18, bf16[256,1024]{1,0:T(8,128)(2,1)} %refs_2_.3, bf16[256,1024]{1,0:T(8,128)(2,1)} %refs_3_.3, bf16[256,1024]{1,0:T(8,128)(2,1)} %refs_4_.5, ...), custom_call_target="tpu_custom_call" | custom-call | flops 1073741824 | bytes 4194304 | tf_op jit(solution)/shard_map/pallas_call | solution.py:446
  114.4 4.6 %all-to-all-done.3 = bf16[16,40,384]{2,1,0:T(8,128)(2,1)S(1)} async-done(((bf16[16,40,384]{2,1,0:T(8,128)(2,1)}), bf16[16,40,384]{2,1,0:T(8,128)(2,1)S(1)}, u32[]{:S(2)}, u32[]{:S(2)}) %all-to-all-start.3) | async-done | bytes 491552 | tf_op jit(solution)/shard_map/all_to_all | solution.py:456
  119.0 1.3 %shard_map.168 = bf16[256,384]{1,0:T(8,128)(2,1)} custom-call(bf16[640,384]{1,0:T(8,128)(2,1)S(1)} %bitcast.15, s32[2,256]{1,0:T(2,128)S(1)} %copy-done.2, f32[2,256]{1,0:T(2,128)S(1)} %bitcast.16), custom_call_target="tpu_custom_call" | custom-call | flops 251658240 | bytes 1048576 | tf_op jit(solution)/shard_map/pallas_call | solution.py:457
  (10 shorter events, 0.0 us)
Async XLA Ops:
  26.7 10.9 %collective-permute-start.2 = (bf16[640,768]{1,0:T(8,128)(2,1)S(1)}, bf16[640,768]{1,0:T(8,128)(2,1)}, u32[]{:S(2)}, u32[]{:S(2)}) collective-permute-start(bf16[640,768]{1,0:T(8,128)(2,1)S(1)} %bitcast.9), channel_id=1, source_target_pairs={{0,1},{1,0},{2,3},{3,2},{4,5},{5,4},{6,7},{7,6},{8,9},{9,8},{10,11... | collective-permute-start | bytes 2949128 | tf_op jit(solution)/shard_map/ppermute | solution.py:340
  26.7 25.4 %collective-permute-start = (bf16[640,768]{1,0:T(8,128)(2,1)S(1)}, bf16[640,768]{1,0:T(8,128)(2,1)S(1)}, u32[]{:S(2)}, u32[]{:S(2)}) collective-permute-start(bf16[640,768]{1,0:T(8,128)(2,1)S(1)} %bitcast.10), channel_id=1, source_target_pairs={{0,2},{2,4},{4,6},{6,0},{1,3},{3,5},{5,7},{7,1},{8,10},{10,12},{12... | collective-permute-start | bytes 2949128 | tf_op jit(solution)/shard_map/ppermute | solution.py:337
  28.2 23.9 %collective-permute-start.1 = (bf16[640,768]{1,0:T(8,128)(2,1)S(1)}, bf16[640,768]{1,0:T(8,128)(2,1)S(1)}, u32[]{:S(2)}, u32[]{:S(2)}) collective-permute-start(bf16[640,768]{1,0:T(8,128)(2,1)S(1)} %bitcast.11), channel_id=1, source_target_pairs={{0,6},{2,0},{4,2},{6,4},{1,7},{3,1},{5,3},{7,5},{8,14},{10,8},{12,... | collective-permute-start | bytes 2949128 | tf_op jit(solution)/shard_map/ppermute | solution.py:337
  33.1 0.8 copy-start
  33.9 16.2 %all-to-all-start.1 = ((bf16[16,144,128]{2,1,0:T(8,128)(2,1)}), bf16[16,144,128]{2,1,0:T(8,128)(2,1)S(1)}, u32[]{:S(2)}, u32[]{:S(2)}) async-start(bf16[16,144,128]{2,1,0:T(8,128)(2,1)} %copy-done), calls=%async_computation.1 | async-start | bytes 1179648 | tf_op jit(solution)/shard_map/all_to_all | solution.py:366
  52.1 4.9 %collective-permute-start.5 = (bf16[640,768]{1,0:T(8,128)(2,1)S(1)}, bf16[640,768]{1,0:T(8,128)(2,1)S(1)}, u32[]{:S(2)}, u32[]{:S(2)}) collective-permute-start(bf16[640,768]{1,0:T(8,128)(2,1)S(1)} %collective-permute-done.from_left.refs_0_), channel_id=1, source_target_pairs={{0,1},{1,0},{2,3},{3,2},{4,5},{5,4},{6,7},{7,6},{8,9},{9,8},{10,11... | collective-permute-start | bytes 2949128 | tf_op jit(solution)/shard_map/ppermute | solution.py:340
  52.1 4.9 %collective-permute-start.6 = (bf16[640,768]{1,0:T(8,128)(2,1)S(1)}, bf16[640,768]{1,0:T(8,128)(2,1)S(1)}, u32[]{:S(2)}, u32[]{:S(2)}) collective-permute-start(bf16[640,768]{1,0:T(8,128)(2,1)S(1)} %collective-permute-done.1.from_right.refs_2_), channel_id=1, source_target_pairs={{0,1},{1,0},{2,3},{3,2},{4,5},{5,4},{6,7},{7,6},{8,9},{9,8},{10,11... | collective-permute-start | bytes 2949128 | tf_op jit(solution)/shard_map/ppermute | solution.py:340
  52.8 14.4 %collective-permute-start.3 = (bf16[640,384]{1,0:T(8,128)(2,1)S(1)}, bf16[640,384]{1,0:T(8,128)(2,1)S(1)}, u32[]{:S(2)}, u32[]{:S(2)}) collective-permute-start(bf16[640,384]{1,0:T(8,128)(2,1)S(1)} %get-tuple-element.43), channel_id=1, source_target_pairs={{0,2},{2,4},{4,6},{6,0},{1,3},{3,5},{5,7},{7,1},{8,10},{10,12},{12... | collective-permute-start | bytes 1474568 | tf_op jit(solution)/shard_map/ppermute | solution.py:337
  54.3 12.9 %collective-permute-start.4 = (bf16[640,384]{1,0:T(8,128)(2,1)S(1)}, bf16[640,384]{1,0:T(8,128)(2,1)S(1)}, u32[]{:S(2)}, u32[]{:S(2)}) collective-permute-start(bf16[640,384]{1,0:T(8,128)(2,1)S(1)} %get-tuple-element.44), channel_id=1, source_target_pairs={{0,6},{2,0},{4,2},{6,4},{1,7},{3,1},{5,3},{7,5},{8,14},{10,8},{12,... | collective-permute-start | bytes 1474568 | tf_op jit(solution)/shard_map/ppermute | solution.py:337
  67.2 1.9 %collective-permute-start.7 = (bf16[640,384]{1,0:T(8,128)(2,1)S(1)}, bf16[640,384]{1,0:T(8,128)(2,1)S(1)}, u32[]{:S(2)}, u32[]{:S(2)}) collective-permute-start(bf16[640,384]{1,0:T(8,128)(2,1)S(1)} %collective-permute-done.3.x0), channel_id=1, source_target_pairs={{0,1},{1,0},{2,3},{3,2},{4,5},{5,4},{6,7},{7,6},{8,9},{9,8},{10,11... | collective-permute-start | bytes 1474568 | tf_op jit(solution)/shard_map/ppermute | solution.py:340
  67.2 2.6 %collective-permute-start.8 = (bf16[640,384]{1,0:T(8,128)(2,1)S(1)}, bf16[640,384]{1,0:T(8,128)(2,1)S(1)}, u32[]{:S(2)}, u32[]{:S(2)}) collective-permute-start(bf16[640,384]{1,0:T(8,128)(2,1)S(1)} %collective-permute-done.4.d0), channel_id=1, source_target_pairs={{0,1},{1,0},{2,3},{3,2},{4,5},{5,4},{6,7},{7,6},{8,9},{9,8},{10,11... | collective-permute-start | bytes 1474568 | tf_op jit(solution)/shard_map/ppermute | solution.py:340
  73.2 3.8 %collective-permute-start.9 = (bf16[640,384]{1,0:T(8,128)(2,1)S(1)}, bf16[640,384]{1,0:T(8,128)(2,1)S(1)}, u32[]{:S(2)}, u32[]{:S(2)}) collective-permute-start(bf16[640,384]{1,0:T(8,128)(2,1)S(1)} %get-tuple-element.58), channel_id=1, source_target_pairs={{0,1},{1,0},{2,3},{3,2},{4,5},{5,4},{6,7},{7,6},{8,9},{9,8},{10,11... | collective-permute-start | bytes 1474568 | tf_op jit(solution)/shard_map/ppermute | solution.py:340
  77.0 9.9 %collective-permute-start.10 = (bf16[3,640,384]{2,1,0:T(8,128)(2,1)S(1)}, bf16[3,640,384]{2,1,0:T(8,128)(2,1)S(1)}, u32[]{:S(2)}, u32[]{:S(2)}) collective-permute-start(bf16[3,640,384]{2,1,0:T(8,128)(2,1)S(1)} %get-tuple-element.67), channel_id=1, source_target_pairs={{0,1},{1,0},{2,3},{3,2},{4,5},{5,4},{6,7},{7,6},{8,9},{9,8},{10,11... | collective-permute-start | bytes 4423688 | tf_op jit(solution)/shard_map/ppermute | solution.py:340
  77.5 9.5 %collective-permute-start.11 = (bf16[320,384]{1,0:T(8,128)(2,1)S(1)}, bf16[320,384]{1,0:T(8,128)(2,1)S(1)}, u32[]{:S(2)}, u32[]{:S(2)}) collective-permute-start(bf16[320,384]{1,0:T(8,128)(2,1)S(1)} %get-tuple-element.68), channel_id=1, source_target_pairs={{0,2},{2,4},{4,6},{6,0},{1,3},{3,5},{5,7},{7,1},{8,10},{10,12},{12... | collective-permute-start | bytes 737288 | tf_op jit(solution)/shard_map/ppermute | solution.py:337
  78.7 8.3 %collective-permute-start.12 = (bf16[320,384]{1,0:T(8,128)(2,1)S(1)}, bf16[320,384]{1,0:T(8,128)(2,1)S(1)}, u32[]{:S(2)}, u32[]{:S(2)}) collective-permute-start(bf16[320,384]{1,0:T(8,128)(2,1)S(1)} %get-tuple-element.69), channel_id=1, source_target_pairs={{0,6},{2,0},{4,2},{6,4},{1,7},{3,1},{5,3},{7,5},{8,14},{10,8},{12,... | collective-permute-start | bytes 737288 | tf_op jit(solution)/shard_map/ppermute | solution.py:337
  87.3 14.2 %collective-permute-start.13 = (bf16[640,384]{1,0:T(8,128)(2,1)S(1)}, bf16[640,384]{1,0:T(8,128)(2,1)S(1)}, u32[]{:S(2)}, u32[]{:S(2)}) collective-permute-start(bf16[640,384]{1,0:T(8,128)(2,1)S(1)} %get-tuple-element.71), channel_id=1, source_target_pairs={{0,2},{2,4},{4,6},{6,0},{1,3},{3,5},{5,7},{7,1},{8,10},{10,12},{12... | collective-permute-start | bytes 1474568 | tf_op jit(solution)/shard_map/ppermute | solution.py:337
  88.5 13.0 %collective-permute-start.14 = (bf16[640,384]{1,0:T(8,128)(2,1)S(1)}, bf16[640,384]{1,0:T(8,128)(2,1)S(1)}, u32[]{:S(2)}, u32[]{:S(2)}) collective-permute-start(bf16[640,384]{1,0:T(8,128)(2,1)S(1)} %get-tuple-element.72), channel_id=1, source_target_pairs={{0,6},{2,0},{4,2},{6,4},{1,7},{3,1},{5,3},{7,5},{8,14},{10,8},{12,... | collective-permute-start | bytes 1474568 | tf_op jit(solution)/shard_map/ppermute | solution.py:337
  90.6 14.8 %all-to-all-start.2 = ((bf16[16,128,128]{2,1,0:T(8,128)(2,1)}), bf16[16,128,128]{2,1,0:T(8,128)(2,1)S(1)}, u32[]{:S(2)}, u32[]{:S(2)}) async-start(bf16[16,128,128]{2,1,0:T(8,128)(2,1)} %shard_map.160.refs_9_), calls=%async_computation.2 | async-start | bytes 1048576 | tf_op jit(solution)/shard_map/all_to_all | solution.py:445
  101.5 17.5 %copy-start.1 = (f32[256,2]{0,1:T(2,128)S(1)}, f32[256,2]{0,1:T(2,128)}, u32[]{:S(2)}) copy-start(f32[256,2]{0,1:T(2,128)} %param.21) | copy-start | bytes 6148
  101.5 17.5 %copy-start.2 = (s32[2,256]{1,0:T(2,128)S(1)}, s32[2,256]{1,0:T(2,128)}, u32[]{:S(2)}) copy-start(s32[2,256]{1,0:T(2,128)} %get-tuple-element.73.slots_ref) | copy-start | bytes 6148
  105.4 13.6 %all-to-all-start.3 = ((bf16[16,40,384]{2,1,0:T(8,128)(2,1)}), bf16[16,40,384]{2,1,0:T(8,128)(2,1)S(1)}, u32[]{:S(2)}, u32[]{:S(2)}) async-start(bf16[16,40,384]{2,1,0:T(8,128)(2,1)} %bitcast.6), calls=%async_computation.3 | async-start | bytes 983040 | tf_op jit(solution)/shard_map/all_to_all | solution.py:456

commit v10 on v9

--- a/solution.py
+++ b/solution.py
@@ -289,10 +289,14 @@
     return mm(mid_ref[...], cat[at : at + FEAT, :], NT)
 
 
-def expert_mid_kernel(pre, hid_ref, x0, d0, x1, d1, cat, down_late, mid_ref, far_ref):
-    late = slice(EARLY * FEAT, None)
-    hid = hid_ref[...] + mm(jnp.concatenate([d0[...], d1[...]], axis=1), down_late[...], NT)
-    both = pre[...] + mm(jnp.concatenate([x0[...], x1[...]], axis=1), cat[late, :])
+def expert_far_kernel(pre, hid, x, d, cat, down_late, pre_ref, hid_ref):
+    hid_ref[...] = hid[...] + mm(d[...], down_late[:, :FEAT], NT)
+    pre_ref[...] = pre[...] + mm(x[...], cat[EARLY * FEAT : (EARLY + 1) * FEAT, :])
+
+
+def expert_mid_kernel(pre, hid_ref, x, d, cat, down_late, mid_ref, far_ref):
+    hid = hid_ref[...] + mm(d[...], down_late[:, FEAT:], NT)
+    both = pre[...] + mm(x[...], cat[(EARLY + 1) * FEAT :, :])
     gate, up = both[:, :HID], both[:, HID:]
     s = 1.0 / (1.0 + jnp.exp(-gate))
     mid_ref[:, :HID] = (hid * up * s * (1.0 + gate * (1.0 - s))).astype(BF)
@@ -388,6 +392,7 @@
         size=2 * MIB,
         limit=4,
     )(from_left, from_right)
+    x_far, d_far, from_left, from_right = tie((x_far, d_far, from_left, from_right))
     x_far, d_far = ring(x_far, RIGHT), ring(d_far, LEFT)
     early = [c for a in (from_left, from_right) for c in (a, swap(a))]
 
@@ -406,14 +411,23 @@
     )(place, *early, *weights, in_hbm(pre), in_hbm(hid), scanned)
     x_far, d_far, pre = tie((x_far, d_far, pre))
     rest = (RINGX - 1, ROWS, FEAT)
+    x_swapped, d_swapped = swap(x_far), swap(d_far)
+    pre, hid = call(
+        expert_far_kernel,
+        (S((ROWS, 2 * HID), F32), S((ROWS, HID), F32)),
+        [vmem()] * 6,
+        flops=6 * ROWS * HID * FEAT,
+        size=10 * MIB,
+        limit=24,
+    )(pre, hid, x_far, d_far, cat, down_late)
     mid, away_far = call(
         expert_mid_kernel,
         (S((ROWS, 2 * HID), BF), block),
-        [vmem()] * 8,
+        [vmem()] * 6,
         flops=8 * ROWS * HID * 2 * FEAT,
         size=12 * MIB,
-        limit=32,
-    )(pre, hid, x_far, d_far, swap(x_far), swap(d_far), cat, down_late)
+        limit=30,
+    )(pre, hid, x_swapped, d_swapped, cat, down_late)
     away_far = swap(away_far)
     mine_far, away_rest = call(
         expert_out_kernel,

time: 121 us -> 122 us (level)
    ppermute x8, waiting for transfers between devices: 14.8 us -> 17 us  [ring(): return lax.ppermute(value, 'x', way)]
    ppermute x7, waiting for transfers between devices: 2.07 us -> 0.48 us  [swap(): return lax.ppermute(value, 'core', SWAP)]
    pallas_call x1 -> x2, Pallas kernels: 3.41 us -> 4.39 us  [the longest x1 2.82 us: local(): call(expert_mid_kernel, (S((ROWS, 2 * HID), BF), block), [vmem()] * 6, fl...]
  transfers between devices with their start and end apart: 18 -> 18, of which waited for: 9 -> 9; matrix products, arithmetic and copies ran while one was open for 1% -> 1% of each run, Pallas kernels for 26% -> 27%
where the time goes in v10:
time: 122 us
  Pallas kernels  38.8 us (32%)
  waiting for transfers between devices  30.8 us (25%)
  starting transfers between devices  25.1 us (21%)
  blocking collectives  24.4 us (20%)
    all_to_all x1, blocking collectives, local(): lax.all_to_all(rows.reshape(CTX, CAP, 2 * FEAT), 'ctx', 0, 0, tiled=True)  24.4 us
    ppermute x8, waiting for transfers between devices, ring(): return lax.ppermute(value, 'x', way)  17 us
    ppermute x8, starting transfers between devices, ring(): return lax.ppermute(value, 'x', way)  12.6 us
    pallas_call x1, Pallas kernels, local(): call(expert_early_kernel, (S((ROWS, 2 * HID), F32), S((ROWS, HID), F32),...  8.12 us
    pallas_call x1, Pallas kernels, local(): call(expert_own_kernel, (pltpu.HBM((ROWS, 2 * HID), F32), pltpu.HBM((ROWS...  6.98 us
    all_to_all x1, waiting for transfers between devices, local(): arrived = lax.all_to_all(message, 'ctx', 0, 0, tiled=True)  5.8 us
    pallas_call x1, Pallas kernels, local(): call(attention_kernel, (S((TOK, HEADS * HD), BF),) * 3, [anywhere()] * 6...  5.41 us
    all_to_all x1, waiting for transfers between devices, local(): lax.all_to_all(summed.reshape(CTX, CAP, FEAT), 'ctx', 0, 0, tiled=True)  4.47 us
  transfers between devices with their start and end apart: 18, of which 9 were waited for; matrix products, arithmetic and copies ran while one was open for 1% of the time, Pallas kernels for 27%

profile of v10, /device:TPU:0, one launch (start us, length us, event | category | flops | bytes accessed | tf_op | source)
XLA Modules:
  0.0 121.7 jit_solution(7653991474546686279)
XLA Ops:
  0.6 1.7 %shard_map.156 = (bf16[640,768]{1,0:T(8,128)(2,1)S(1)}, s32[2,256]{1,0:T(2,128)}) custom-call(s32[2,256]{1,0:T(2,128)} %bitcast.19, bf16[256,384]{1,0:T(8,128)(2,1)} %x_hbm.1, bf16[256,384]{1,0:T(8,128)(2,1)} %d_hbm.1), custom_call_target="tpu_custom_call" | custom-call | flops 251658240 | bytes 2097152 | tf_op jit(solution)/shard_map/pallas_call | solution.py:346
  2.4 24.4 %all_to_all.20 = bf16[16,40,768]{2,1,0:T(8,128)(2,1)S(1)} all-to-all(bf16[16,40,768]{2,1,0:T(8,128)(2,1)S(1)} %bitcast.14), channel_id=1, replica_groups=mesh['ctx'=16,'x'=4,'core'=2] {'ctx'}, dimensions={0} | all-to-all | bytes 1966080 | tf_op jit(solution)/shard_map/all_to_all | solution.py:355
  26.7 0.0 collective-permute-start.2
  26.7 2.8 %collective-permute-start.1 = (bf16[640,768]{1,0:T(8,128)(2,1)S(1)}, bf16[640,768]{1,0:T(8,128)(2,1)S(1)}, u32[]{:S(2)}, u32[]{:S(2)}) collective-permute-start(bf16[640,768]{1,0:T(8,128)(2,1)S(1)} %bitcast.10), channel_id=1, source_target_pairs={{0,6},{2,0},{4,2},{6,4},{1,7},{3,1},{5,3},{7,5},{8,14},{10,8},{12,... | collective-permute-start | bytes 2949128 | tf_op jit(solution)/shard_map/ppermute | solution.py:341
  29.5 3.1 %shard_map.157 = bf16[16,144,128]{2,1,0:T(8,128)(2,1)S(1)} custom-call(f32[8,256]{1,0:T(8,128)} %refs_0_.3, s32[1,256]{1,0:T(1,128)} %bitcast.17, bf16[256,1024]{1,0:T(8,128)(2,1)} %refs_2_.3, bf16[256,1024]{1,0:T(8,128)(2,1)} %refs_3_.3, bf16[256,1024]{1,0:T(8,128)(2,1)} %refs_4_.5, bf16[256,1024]{1,0:T(8,128)(2,1)} %refs_5_.5, bf16[640,768]{1,0:T(8,128)(2,1)S(1)} %bitcast.12), custom_call_target="tpu_custom_call" | custom-call | flops 134217728 | bytes 3145728 | tf_op jit(solution)/shard_map/pallas_call | solution.py:361
  32.6 0.8 copy-done
  33.4 3.6 %all-to-all-start.1 = ((bf16[16,144,128]{2,1,0:T(8,128)(2,1)}), bf16[16,144,128]{2,1,0:T(8,128)(2,1)S(1)}, u32[]{:S(2)}, u32[]{:S(2)}) async-start(bf16[16,144,128]{2,1,0:T(8,128)(2,1)} %copy-done), calls=%async_computation.1 | async-start | bytes 1179648 | tf_op jit(solution)/shard_map/all_to_all | solution.py:370
  37.0 0.1 pad_add_fusion.place
  37.1 0.0 collective-permute-done.2.a1
  37.1 7.0 %shard_map.158 = (f32[640,1280]{1,0:T(8,128)}, f32[640,640]{1,0:T(8,128)}) custom-call(s32[2]{0:T(128)S(1)} %pad_add_fusion.place, bf16[640,768]{1,0:T(8,128)(2,1)S(1)} %bitcast.13, bf16[640,768]{1,0:T(8,128)(2,1)} %collective-permute-done.2.a1, bf16[1,3072,640]{2,1,0:T(8,128)(2,1)} %refs_4_.4, bf16[1,3072,640]{2,1,0:T(8,128)(2,1)} %refs_5_.4, ...), custom_call_target="tpu_custom_call" | custom-call | flops 1887436800 | bytes 12582912 | tf_op jit(solution)/shard_map/pallas_call | solution.py:374
  44.1 5.8 %all-to-all-done.1.in_ref = bf16[16,144,128]{2,1,0:T(8,128)(2,1)S(1)} async-done(((bf16[16,144,128]{2,1,0:T(8,128)(2,1)}), bf16[16,144,128]{2,1,0:T(8,128)(2,1)S(1)}, u32[]{:S(2)}, u32[]{:S(2)}) %all-to-all-start.1) | async-done | bytes 589856 | tf_op jit(solution)/shard_map/all_to_all | solution.py:370
  49.9 1.3 %collective-permute-done.1.from_right.refs_2_ = bf16[640,768]{1,0:T(8,128)(2,1)S(1)} collective-permute-done((bf16[640,768]{1,0:T(8,128)(2,1)S(1)}, bf16[640,768]{1,0:T(8,128)(2,1)S(1)}, u32[]{:S(2)}, u32[]{:S(2)}) %collective-permute-start.1) | collective-permute-done | bytes 983072 | tf_op jit(solution)/shard_map/ppermute | solution.py:341
  51.2 3.4 %collective-permute-done.from_left.refs_0_ = bf16[640,768]{1,0:T(8,128)(2,1)S(1)} collective-permute-done((bf16[640,768]{1,0:T(8,128)(2,1)S(1)}, bf16[640,768]{1,0:T(8,128)(2,1)S(1)}, u32[]{:S(2)}, u32[]{:S(2)}) %collective-permute-start) | collective-permute-done | bytes 983072 | tf_op jit(solution)/shard_map/ppermute | solution.py:341
  54.6 0.1 shard_map.159
  54.7 0.1 collective-permute-start.5
  54.8 0.5 collective-permute-start.6
  55.3 3.2 %collective-permute-start.4 = (bf16[640,384]{1,0:T(8,128)(2,1)S(1)}, bf16[640,384]{1,0:T(8,128)(2,1)S(1)}, u32[]{:S(2)}, u32[]{:S(2)}) collective-permute-start(bf16[640,384]{1,0:T(8,128)(2,1)S(1)} %get-tuple-element.52), channel_id=1, source_target_pairs={{0,6},{2,0},{4,2},{6,4},{1,7},{3,1},{5,3},{7,5},{8,14},{10,8},{12,... | collective-permute-start | bytes 1474568 | tf_op jit(solution)/shard_map/ppermute | solution.py:341
  58.6 1.0 shard_map.160.refs_9_
  59.5 0.0 collective-permute-done.5.refs_1_
  59.5 0.0 collective-permute-done.6.refs_3_
  59.5 8.1 %shard_map.161 = (f32[640,1280]{1,0:T(8,128)S(1)}, f32[640,640]{1,0:T(8,128)S(1)}, bf16[3072,1280]{1,0:T(8,128)(2,1)S(1)}, bf16[640,768]{1,0:T(8,128)(2,1)S(1)}) custom-call(s32[2]{0:T(128)S(1)} %pad_add_fusion.place, bf16[640,768]{1,0:T(8,128)(2,1)S(1)} %collective-permute-done.from_left.refs_0_, bf16[640,768]{1,0:T(8,128)(2,1)S(1)} %collective-permute-done.5.refs_1_, ...), custom_call_target="tpu_custom_call" | custom-call | flops 3774873600 | bytes 25165824 | tf_op jit(solution)/shard_map/pallas_call | solution.py:401
  67.7 2.1 %collective-permute-done.3.x = bf16[640,384]{1,0:T(8,128)(2,1)S(1)} collective-permute-done((bf16[640,384]{1,0:T(8,128)(2,1)S(1)}, bf16[640,384]{1,0:T(8,128)(2,1)S(1)}, u32[]{:S(2)}, u32[]{:S(2)}) %collective-permute-start.3) | collective-permute-done | bytes 491552 | tf_op jit(solution)/shard_map/ppermute | solution.py:341
  69.7 0.0 collective-permute-done.4.d
  69.7 0.0 collective-permute-start.7
  69.8 0.5 collective-permute-start.8
  70.3 1.6 %shard_map.162 = (f32[640,1280]{1,0:T(8,128)S(1)}, f32[640,640]{1,0:T(8,128)S(1)}) custom-call(f32[640,1280]{1,0:T(8,128)S(1)} %get-tuple-element.59.pre, f32[640,640]{1,0:T(8,128)S(1)} %get-tuple-element.60.hid, bf16[640,384]{1,0:T(8,128)(2,1)S(1)} %collective-permute-done.3.x, bf16[640,384]{1,0:T(8,128)(2,1)S(1)} %collective-permute-done.4.d, ...), custom_call_target="tpu_custom_call" | custom-call | flops 943718400 | bytes 10485760 | tf_op jit(solution)/shard_map/pallas_call | solution.py:415
  71.9 0.5 collective-permute-done.8.d
  72.3 2.8 %shard_map.163 = (bf16[640,1280]{1,0:T(8,128)(2,1)S(1)}, bf16[640,384]{1,0:T(8,128)(2,1)S(1)}) custom-call(f32[640,1280]{1,0:T(8,128)S(1)} %get-tuple-element.65.pre, f32[640,640]{1,0:T(8,128)S(1)} %get-tuple-element.66.hid_ref, bf16[640,384]{1,0:T(8,128)(2,1)S(1)} %collective-permute-done.7.x, bf16[640,384]{1,0:T(8,128)(2,1)S(1)} %collective-permute-done.8.d, ...), custom_call_target="tpu_custom_call" | custom-call | flops 2516582400 | bytes 12582912 | tf_op jit(solution)/shard_map/pallas_call | solution.py:423
  75.1 0.2 collective-permute-start.9
  75.4 3.5 %shard_map.164 = (f32[640,384]{1,0:T(8,128)S(1)}, bf16[3,640,384]{2,1,0:T(8,128)(2,1)S(1)}) custom-call(bf16[640,1280]{1,0:T(8,128)(2,1)S(1)} %get-tuple-element.73.mid_ref, bf16[3072,1280]{1,0:T(8,128)(2,1)S(1)} %get-tuple-element.63.cat), custom_call_target="tpu_custom_call" | custom-call | flops 2516582400 | bytes 8388608 | tf_op jit(solution)/shard_map/pallas_call | solution.py:432
  78.9 0.0 collective-permute-done.9.away
  78.9 0.1 shard_map.165
  79.0 0.5 collective-permute-start.10
  79.5 0.0 collective-permute-start.11
  79.5 3.2 %collective-permute-start.12 = (bf16[320,384]{1,0:T(8,128)(2,1)S(1)}, bf16[320,384]{1,0:T(8,128)(2,1)S(1)}, u32[]{:S(2)}, u32[]{:S(2)}) collective-permute-start(bf16[320,384]{1,0:T(8,128)(2,1)S(1)} %get-tuple-element.81), channel_id=1, source_target_pairs={{0,6},{2,0},{4,2},{6,4},{1,7},{3,1},{5,3},{7,5},{8,14},{10,8},{12,... | collective-permute-start | bytes 737288 | tf_op jit(solution)/shard_map/ppermute | solution.py:341
  82.7 2.7 %shard_map.166.mine = f32[3,640,384]{2,1,0:T(8,128)S(1)} custom-call(bf16[640,1280]{1,0:T(8,128)(2,1)S(1)} %get-tuple-element.73.mid_ref, bf16[3072,1280]{1,0:T(8,128)(2,1)S(1)} %get-tuple-element.63.cat), custom_call_target="tpu_custom_call" | custom-call | flops 1887436800 | bytes 8388608 | tf_op jit(solution)/shard_map/pallas_call | solution.py:445
  85.4 3.3 %collective-permute-done.11.via_right = bf16[320,384]{1,0:T(8,128)(2,1)S(1)} collective-permute-done((bf16[320,384]{1,0:T(8,128)(2,1)S(1)}, bf16[320,384]{1,0:T(8,128)(2,1)S(1)}, u32[]{:S(2)}, u32[]{:S(2)}) %collective-permute-start.11) | collective-permute-done | bytes 245792 | tf_op jit(solution)/shard_map/ppermute | solution.py:341
  88.7 0.3 shard_map.168
  89.0 1.2 collective-permute-start.13
  90.2 2.1 %collective-permute-start.14 = (bf16[640,384]{1,0:T(8,128)(2,1)S(1)}, bf16[640,384]{1,0:T(8,128)(2,1)S(1)}, u32[]{:S(2)}, u32[]{:S(2)}) collective-permute-start(bf16[640,384]{1,0:T(8,128)(2,1)S(1)} %get-tuple-element.84), channel_id=1, source_target_pairs={{0,6},{2,0},{4,2},{6,4},{1,7},{3,1},{5,3},{7,5},{8,14},{10,8},{12,... | collective-permute-start | bytes 1474568 | tf_op jit(solution)/shard_map/ppermute | solution.py:341
  92.4 3.6 %all-to-all-start.2 = ((bf16[16,128,128]{2,1,0:T(8,128)(2,1)}), bf16[16,128,128]{2,1,0:T(8,128)(2,1)S(1)}, u32[]{:S(2)}, u32[]{:S(2)}) async-start(bf16[16,128,128]{2,1,0:T(8,128)(2,1)} %shard_map.160.refs_9_), calls=%async_computation.2 | async-start | bytes 1048576 | tf_op jit(solution)/shard_map/all_to_all | solution.py:459
  95.9 7.0 %collective-permute-done.13 = bf16[640,384]{1,0:T(8,128)(2,1)S(1)} collective-permute-done((bf16[640,384]{1,0:T(8,128)(2,1)S(1)}, bf16[640,384]{1,0:T(8,128)(2,1)S(1)}, u32[]{:S(2)}, u32[]{:S(2)}) %collective-permute-start.13) | collective-permute-done | bytes 491552 | tf_op jit(solution)/shard_map/ppermute | solution.py:341
  102.9 0.9 add_convert_fusion
  103.9 3.0 %all-to-all-done.2.refs_6_ = bf16[16,128,128]{2,1,0:T(8,128)(2,1)S(1)} async-done(((bf16[16,128,128]{2,1,0:T(8,128)(2,1)}), bf16[16,128,128]{2,1,0:T(8,128)(2,1)S(1)}, u32[]{:S(2)}, u32[]{:S(2)}) %all-to-all-start.2) | async-done | bytes 524320 | tf_op jit(solution)/shard_map/all_to_all | solution.py:459
  106.9 3.6 %all-to-all-start.3 = ((bf16[16,40,384]{2,1,0:T(8,128)(2,1)}), bf16[16,40,384]{2,1,0:T(8,128)(2,1)S(1)}, u32[]{:S(2)}, u32[]{:S(2)}) async-start(bf16[16,40,384]{2,1,0:T(8,128)(2,1)} %bitcast.6), calls=%async_computation.3 | async-start | bytes 983040 | tf_op jit(solution)/shard_map/all_to_all | solution.py:470
  110.4 5.4 %shard_map.167 = (bf16[256,1024]{1,0:T(8,128)(2,1)}, bf16[256,1024]{1,0:T(8,128)(2,1)}, bf16[256,1024]{1,0:T(8,128)(2,1)}) custom-call(f32[8,256]{1,0:T(8,128)} %refs_0_.3, s32[1,256]{1,0:T(1,128)} %bitcast.18, bf16[256,1024]{1,0:T(8,128)(2,1)} %refs_2_.3, bf16[256,1024]{1,0:T(8,128)(2,1)} %refs_3_.3, bf16[256,1024]{1,0:T(8,128)(2,1)} %refs_4_.5, ...), custom_call_target="tpu_custom_call" | custom-call | flops 1073741824 | bytes 4194304 | tf_op jit(solution)/shard_map/pallas_call | solution.py:460
  115.9 4.5 %all-to-all-done.3 = bf16[16,40,384]{2,1,0:T(8,128)(2,1)S(1)} async-done(((bf16[16,40,384]{2,1,0:T(8,128)(2,1)}), bf16[16,40,384]{2,1,0:T(8,128)(2,1)S(1)}, u32[]{:S(2)}, u32[]{:S(2)}) %all-to-all-start.3) | async-done | bytes 491552 | tf_op jit(solution)/shard_map/all_to_all | solution.py:470
  120.3 1.3 %shard_map.169 = bf16[256,384]{1,0:T(8,128)(2,1)} custom-call(bf16[640,384]{1,0:T(8,128)(2,1)S(1)} %bitcast.15, s32[2,256]{1,0:T(2,128)S(1)} %copy-done.2, f32[2,256]{1,0:T(2,128)S(1)} %bitcast.16), custom_call_target="tpu_custom_call" | custom-call | flops 251658240 | bytes 1048576 | tf_op jit(solution)/shard_map/pallas_call | solution.py:471
  (11 shorter events, 0.0 us)
Async XLA Ops:
  26.7 10.4 %collective-permute-start.2 = (bf16[640,768]{1,0:T(8,128)(2,1)S(1)}, bf16[640,768]{1,0:T(8,128)(2,1)}, u32[]{:S(2)}, u32[]{:S(2)}) collective-permute-start(bf16[640,768]{1,0:T(8,128)(2,1)S(1)} %bitcast.9), channel_id=1, source_target_pairs={{0,1},{1,0},{2,3},{3,2},{4,5},{5,4},{6,7},{7,6},{8,9},{9,8},{10,11... | collective-permute-start | bytes 2949128 | tf_op jit(solution)/shard_map/ppermute | solution.py:344
  26.7 24.4 %collective-permute-start.1 = (bf16[640,768]{1,0:T(8,128)(2,1)S(1)}, bf16[640,768]{1,0:T(8,128)(2,1)S(1)}, u32[]{:S(2)}, u32[]{:S(2)}) collective-permute-start(bf16[640,768]{1,0:T(8,128)(2,1)S(1)} %bitcast.10), channel_id=1, source_target_pairs={{0,6},{2,0},{4,2},{6,4},{1,7},{3,1},{5,3},{7,5},{8,14},{10,8},{12,... | collective-permute-start | bytes 2949128 | tf_op jit(solution)/shard_map/ppermute | solution.py:341
  29.5 25.1 %collective-permute-start = (bf16[640,768]{1,0:T(8,128)(2,1)S(1)}, bf16[640,768]{1,0:T(8,128)(2,1)S(1)}, u32[]{:S(2)}, u32[]{:S(2)}) collective-permute-start(bf16[640,768]{1,0:T(8,128)(2,1)S(1)} %bitcast.11), channel_id=1, source_target_pairs={{0,2},{2,4},{4,6},{6,0},{1,3},{3,5},{5,7},{7,1},{8,10},{10,12},{12... | collective-permute-start | bytes 2949128 | tf_op jit(solution)/shard_map/ppermute | solution.py:341
  32.6 0.8 copy-start
  33.4 16.5 %all-to-all-start.1 = ((bf16[16,144,128]{2,1,0:T(8,128)(2,1)}), bf16[16,144,128]{2,1,0:T(8,128)(2,1)S(1)}, u32[]{:S(2)}, u32[]{:S(2)}) async-start(bf16[16,144,128]{2,1,0:T(8,128)(2,1)} %copy-done), calls=%async_computation.1 | async-start | bytes 1179648 | tf_op jit(solution)/shard_map/all_to_all | solution.py:370
  54.7 4.8 %collective-permute-start.5 = (bf16[640,768]{1,0:T(8,128)(2,1)S(1)}, bf16[640,768]{1,0:T(8,128)(2,1)S(1)}, u32[]{:S(2)}, u32[]{:S(2)}) collective-permute-start(bf16[640,768]{1,0:T(8,128)(2,1)S(1)} %collective-permute-done.from_left.refs_0_), channel_id=1, source_target_pairs={{0,1},{1,0},{2,3},{3,2},{4,5},{5,4},{6,7},{7,6},{8,9},{9,8},{10,11... | collective-permute-start | bytes 2949128 | tf_op jit(solution)/shard_map/ppermute | solution.py:344
  54.8 4.7 %collective-permute-start.6 = (bf16[640,768]{1,0:T(8,128)(2,1)S(1)}, bf16[640,768]{1,0:T(8,128)(2,1)S(1)}, u32[]{:S(2)}, u32[]{:S(2)}) collective-permute-start(bf16[640,768]{1,0:T(8,128)(2,1)S(1)} %collective-permute-done.1.from_right.refs_2_), channel_id=1, source_target_pairs={{0,1},{1,0},{2,3},{3,2},{4,5},{5,4},{6,7},{7,6},{8,9},{9,8},{10,11... | collective-permute-start | bytes 2949128 | tf_op jit(solution)/shard_map/ppermute | solution.py:344
  55.3 14.4 %collective-permute-start.3 = (bf16[640,384]{1,0:T(8,128)(2,1)S(1)}, bf16[640,384]{1,0:T(8,128)(2,1)S(1)}, u32[]{:S(2)}, u32[]{:S(2)}) collective-permute-start(bf16[640,384]{1,0:T(8,128)(2,1)S(1)} %get-tuple-element.51), channel_id=1, source_target_pairs={{0,2},{2,4},{4,6},{6,0},{1,3},{3,5},{5,7},{7,1},{8,10},{10,12},{12... | collective-permute-start | bytes 1474568 | tf_op jit(solution)/shard_map/ppermute | solution.py:341
  55.3 14.4 %collective-permute-start.4 = (bf16[640,384]{1,0:T(8,128)(2,1)S(1)}, bf16[640,384]{1,0:T(8,128)(2,1)S(1)}, u32[]{:S(2)}, u32[]{:S(2)}) collective-permute-start(bf16[640,384]{1,0:T(8,128)(2,1)S(1)} %get-tuple-element.52), channel_id=1, source_target_pairs={{0,6},{2,0},{4,2},{6,4},{1,7},{3,1},{5,3},{7,5},{8,14},{10,8},{12,... | collective-permute-start | bytes 1474568 | tf_op jit(solution)/shard_map/ppermute | solution.py:341
  69.7 2.1 %collective-permute-start.7 = (bf16[640,384]{1,0:T(8,128)(2,1)S(1)}, bf16[640,384]{1,0:T(8,128)(2,1)S(1)}, u32[]{:S(2)}, u32[]{:S(2)}) collective-permute-start(bf16[640,384]{1,0:T(8,128)(2,1)S(1)} %collective-permute-done.3.x), channel_id=1, source_target_pairs={{0,1},{1,0},{2,3},{3,2},{4,5},{5,4},{6,7},{7,6},{8,9},{9,8},{10,11... | collective-permute-start | bytes 1474568 | tf_op jit(solution)/shard_map/ppermute | solution.py:344
  69.8 2.6 %collective-permute-start.8 = (bf16[640,384]{1,0:T(8,128)(2,1)S(1)}, bf16[640,384]{1,0:T(8,128)(2,1)S(1)}, u32[]{:S(2)}, u32[]{:S(2)}) collective-permute-start(bf16[640,384]{1,0:T(8,128)(2,1)S(1)} %collective-permute-done.4.d), channel_id=1, source_target_pairs={{0,1},{1,0},{2,3},{3,2},{4,5},{5,4},{6,7},{7,6},{8,9},{9,8},{10,11... | collective-permute-start | bytes 1474568 | tf_op jit(solution)/shard_map/ppermute | solution.py:344
  75.1 3.8 %collective-permute-start.9 = (bf16[640,384]{1,0:T(8,128)(2,1)S(1)}, bf16[640,384]{1,0:T(8,128)(2,1)S(1)}, u32[]{:S(2)}, u32[]{:S(2)}) collective-permute-start(bf16[640,384]{1,0:T(8,128)(2,1)S(1)} %get-tuple-element.70), channel_id=1, source_target_pairs={{0,1},{1,0},{2,3},{3,2},{4,5},{5,4},{6,7},{7,6},{8,9},{9,8},{10,11... | collective-permute-start | bytes 1474568 | tf_op jit(solution)/shard_map/ppermute | solution.py:344
  79.0 9.7 %collective-permute-start.10 = (bf16[3,640,384]{2,1,0:T(8,128)(2,1)S(1)}, bf16[3,640,384]{2,1,0:T(8,128)(2,1)S(1)}, u32[]{:S(2)}, u32[]{:S(2)}) collective-permute-start(bf16[3,640,384]{2,1,0:T(8,128)(2,1)S(1)} %get-tuple-element.79), channel_id=1, source_target_pairs={{0,1},{1,0},{2,3},{3,2},{4,5},{5,4},{6,7},{7,6},{8,9},{9,8},{10,11... | collective-permute-start | bytes 4423688 | tf_op jit(solution)/shard_map/ppermute | solution.py:344
  79.5 9.2 %collective-permute-start.11 = (bf16[320,384]{1,0:T(8,128)(2,1)S(1)}, bf16[320,384]{1,0:T(8,128)(2,1)S(1)}, u32[]{:S(2)}, u32[]{:S(2)}) collective-permute-start(bf16[320,384]{1,0:T(8,128)(2,1)S(1)} %get-tuple-element.80), channel_id=1, source_target_pairs={{0,2},{2,4},{4,6},{6,0},{1,3},{3,5},{5,7},{7,1},{8,10},{10,12},{12... | collective-permute-start | bytes 737288 | tf_op jit(solution)/shard_map/ppermute | solution.py:341
  79.5 9.2 %collective-permute-start.12 = (bf16[320,384]{1,0:T(8,128)(2,1)S(1)}, bf16[320,384]{1,0:T(8,128)(2,1)S(1)}, u32[]{:S(2)}, u32[]{:S(2)}) collective-permute-start(bf16[320,384]{1,0:T(8,128)(2,1)S(1)} %get-tuple-element.81), channel_id=1, source_target_pairs={{0,6},{2,0},{4,2},{6,4},{1,7},{3,1},{5,3},{7,5},{8,14},{10,8},{12,... | collective-permute-start | bytes 737288 | tf_op jit(solution)/shard_map/ppermute | solution.py:341
  89.0 13.9 %collective-permute-start.13 = (bf16[640,384]{1,0:T(8,128)(2,1)S(1)}, bf16[640,384]{1,0:T(8,128)(2,1)S(1)}, u32[]{:S(2)}, u32[]{:S(2)}) collective-permute-start(bf16[640,384]{1,0:T(8,128)(2,1)S(1)} %get-tuple-element.83), channel_id=1, source_target_pairs={{0,2},{2,4},{4,6},{6,0},{1,3},{3,5},{5,7},{7,1},{8,10},{10,12},{12... | collective-permute-start | bytes 1474568 | tf_op jit(solution)/shard_map/ppermute | solution.py:341
  90.2 12.7 %collective-permute-start.14 = (bf16[640,384]{1,0:T(8,128)(2,1)S(1)}, bf16[640,384]{1,0:T(8,128)(2,1)S(1)}, u32[]{:S(2)}, u32[]{:S(2)}) collective-permute-start(bf16[640,384]{1,0:T(8,128)(2,1)S(1)} %get-tuple-element.84), channel_id=1, source_target_pairs={{0,6},{2,0},{4,2},{6,4},{1,7},{3,1},{5,3},{7,5},{8,14},{10,8},{12,... | collective-permute-start | bytes 1474568 | tf_op jit(solution)/shard_map/ppermute | solution.py:341
  92.4 14.5 %all-to-all-start.2 = ((bf16[16,128,128]{2,1,0:T(8,128)(2,1)}), bf16[16,128,128]{2,1,0:T(8,128)(2,1)S(1)}, u32[]{:S(2)}, u32[]{:S(2)}) async-start(bf16[16,128,128]{2,1,0:T(8,128)(2,1)} %shard_map.160.refs_9_), calls=%async_computation.2 | async-start | bytes 1048576 | tf_op jit(solution)/shard_map/all_to_all | solution.py:459
  102.9 17.4 %copy-start.1 = (f32[256,2]{0,1:T(2,128)S(1)}, f32[256,2]{0,1:T(2,128)}, u32[]{:S(2)}) copy-start(f32[256,2]{0,1:T(2,128)} %param.21) | copy-start | bytes 6148
  102.9 17.4 %copy-start.2 = (s32[2,256]{1,0:T(2,128)S(1)}, s32[2,256]{1,0:T(2,128)}, u32[]{:S(2)}) copy-start(s32[2,256]{1,0:T(2,128)} %get-tuple-element.85.slots_ref) | copy-start | bytes 6148
  106.9 13.5 %all-to-all-start.3 = ((bf16[16,40,384]{2,1,0:T(8,128)(2,1)}), bf16[16,40,384]{2,1,0:T(8,128)(2,1)S(1)}, u32[]{:S(2)}, u32[]{:S(2)}) async-start(bf16[16,40,384]{2,1,0:T(8,128)(2,1)} %bitcast.6), calls=%async_computation.3 | async-start | bytes 983040 | tf_op jit(solution)/shard_map/all_to_all | solution.py:470

commit v11 on v10

--- a/solution.py
+++ b/solution.py
@@ -392,7 +392,6 @@
         size=2 * MIB,
         limit=4,
     )(from_left, from_right)
-    x_far, d_far, from_left, from_right = tie((x_far, d_far, from_left, from_right))
     x_far, d_far = ring(x_far, RIGHT), ring(d_far, LEFT)
     early = [c for a in (from_left, from_right) for c in (a, swap(a))]
 

time: 122 us -> 120 us (0.984)
  waiting for transfers between devices: 30.8 us -> 28.4 us
    ppermute x8, waiting for transfers between devices: 17 us -> 14.8 us  [ring(): return lax.ppermute(value, 'x', way)]
  transfers between devices with their start and end apart: 18 -> 18, of which waited for: 9 -> 8; matrix products, arithmetic and copies ran while one was open for 1% -> 1% of each run, Pallas kernels for 27% -> 27%
where the time goes in v11:
time: 120 us
  Pallas kernels  38.8 us (32%)
  waiting for transfers between devices  28.4 us (24%)
  starting transfers between devices  25.6 us (21%)
  blocking collectives  24.4 us (20%)
    all_to_all x1, blocking collectives, local(): lax.all_to_all(rows.reshape(CTX, CAP, 2 * FEAT), 'ctx', 0, 0, tiled=True)  24.4 us
    ppermute x8, waiting for transfers between devices, ring(): return lax.ppermute(value, 'x', way)  14.8 us
    ppermute x8, starting transfers between devices, ring(): return lax.ppermute(value, 'x', way)  13.1 us
    pallas_call x1, Pallas kernels, local(): call(expert_early_kernel, (S((ROWS, 2 * HID), F32), S((ROWS, HID), F32),...  8.12 us
    pallas_call x1, Pallas kernels, local(): call(expert_own_kernel, (pltpu.HBM((ROWS, 2 * HID), F32), pltpu.HBM((ROWS...  6.98 us
    all_to_all x1, waiting for transfers between devices, local(): arrived = lax.all_to_all(message, 'ctx', 0, 0, tiled=True)  5.52 us
    pallas_call x1, Pallas kernels, local(): call(attention_kernel, (S((TOK, HEADS * HD), BF),) * 3, [anywhere()] * 6...  5.4 us
    all_to_all x1, waiting for transfers between devices, local(): lax.all_to_all(summed.reshape(CTX, CAP, FEAT), 'ctx', 0, 0, tiled=True)  4.62 us
  transfers between devices with their start and end apart: 18, of which 8 were waited for; matrix products, arithmetic and copies ran while one was open for 1% of the time, Pallas kernels for 27%

profile of v11, /device:TPU:0, one launch (start us, length us, event | category | flops | bytes accessed | tf_op | source)
XLA Modules:
  0.0 119.8 jit_solution(2157894202489857796)
XLA Ops:
  0.6 1.7 %shard_map.156 = (bf16[640,768]{1,0:T(8,128)(2,1)S(1)}, s32[2,256]{1,0:T(2,128)}) custom-call(s32[2,256]{1,0:T(2,128)} %bitcast.19, bf16[256,384]{1,0:T(8,128)(2,1)} %x_hbm.1, bf16[256,384]{1,0:T(8,128)(2,1)} %d_hbm.1), custom_call_target="tpu_custom_call" | custom-call | flops 251658240 | bytes 2097152 | tf_op jit(solution)/shard_map/pallas_call | solution.py:346
  2.4 24.4 %all_to_all.20 = bf16[16,40,768]{2,1,0:T(8,128)(2,1)S(1)} all-to-all(bf16[16,40,768]{2,1,0:T(8,128)(2,1)S(1)} %bitcast.14), channel_id=1, replica_groups=mesh['ctx'=16,'x'=4,'core'=2] {'ctx'}, dimensions={0} | all-to-all | bytes 1966080 | tf_op jit(solution)/shard_map/all_to_all | solution.py:355
  26.7 1.5 %collective-permute-start = (bf16[640,768]{1,0:T(8,128)(2,1)S(1)}, bf16[640,768]{1,0:T(8,128)(2,1)S(1)}, u32[]{:S(2)}, u32[]{:S(2)}) collective-permute-start(bf16[640,768]{1,0:T(8,128)(2,1)S(1)} %bitcast.10), channel_id=1, source_target_pairs={{0,2},{2,4},{4,6},{6,0},{1,3},{3,5},{5,7},{7,1},{8,10},{10,12},{12... | collective-permute-start | bytes 2949128 | tf_op jit(solution)/shard_map/ppermute | solution.py:341
  28.2 1.7 %collective-permute-start.1 = (bf16[640,768]{1,0:T(8,128)(2,1)S(1)}, bf16[640,768]{1,0:T(8,128)(2,1)S(1)}, u32[]{:S(2)}, u32[]{:S(2)}) collective-permute-start(bf16[640,768]{1,0:T(8,128)(2,1)S(1)} %bitcast.11), channel_id=1, source_target_pairs={{0,6},{2,0},{4,2},{6,4},{1,7},{3,1},{5,3},{7,5},{8,14},{10,8},{12,... | collective-permute-start | bytes 2949128 | tf_op jit(solution)/shard_map/ppermute | solution.py:341
  30.0 3.1 %shard_map.157 = bf16[16,144,128]{2,1,0:T(8,128)(2,1)S(1)} custom-call(f32[8,256]{1,0:T(8,128)} %refs_0_.3, s32[1,256]{1,0:T(1,128)} %bitcast.17, bf16[256,1024]{1,0:T(8,128)(2,1)} %refs_2_.3, bf16[256,1024]{1,0:T(8,128)(2,1)} %refs_3_.3, bf16[256,1024]{1,0:T(8,128)(2,1)} %refs_4_.5, bf16[256,1024]{1,0:T(8,128)(2,1)} %refs_5_.5, bf16[640,768]{1,0:T(8,128)(2,1)S(1)} %bitcast.12), custom_call_target="tpu_custom_call" | custom-call | flops 134217728 | bytes 3145728 | tf_op jit(solution)/shard_map/pallas_call | solution.py:361
  33.1 0.8 copy-done
  33.9 3.6 %all-to-all-start.1 = ((bf16[16,144,128]{2,1,0:T(8,128)(2,1)}), bf16[16,144,128]{2,1,0:T(8,128)(2,1)S(1)}, u32[]{:S(2)}, u32[]{:S(2)}) async-start(bf16[16,144,128]{2,1,0:T(8,128)(2,1)} %copy-done), calls=%async_computation.1 | async-start | bytes 1179648 | tf_op jit(solution)/shard_map/all_to_all | solution.py:370
  37.5 0.1 pad_add_fusion.place
  37.6 0.0 collective-permute-done.2.a1
  37.6 7.0 %shard_map.158 = (f32[640,1280]{1,0:T(8,128)}, f32[640,640]{1,0:T(8,128)}) custom-call(s32[2]{0:T(128)S(1)} %pad_add_fusion.place, bf16[640,768]{1,0:T(8,128)(2,1)S(1)} %bitcast.13, bf16[640,768]{1,0:T(8,128)(2,1)} %collective-permute-done.2.a1, bf16[1,3072,640]{2,1,0:T(8,128)(2,1)} %refs_4_.4, bf16[1,3072,640]{2,1,0:T(8,128)(2,1)} %refs_5_.4, ...), custom_call_target="tpu_custom_call" | custom-call | flops 1887436800 | bytes 12582912 | tf_op jit(solution)/shard_map/pallas_call | solution.py:374
  44.6 5.5 %all-to-all-done.1.in_ref = bf16[16,144,128]{2,1,0:T(8,128)(2,1)S(1)} async-done(((bf16[16,144,128]{2,1,0:T(8,128)(2,1)}), bf16[16,144,128]{2,1,0:T(8,128)(2,1)S(1)}, u32[]{:S(2)}, u32[]{:S(2)}) %all-to-all-start.1) | async-done | bytes 589856 | tf_op jit(solution)/shard_map/all_to_all | solution.py:370
  50.1 2.0 %collective-permute-done.from_left.refs_0_ = bf16[640,768]{1,0:T(8,128)(2,1)S(1)} collective-permute-done((bf16[640,768]{1,0:T(8,128)(2,1)S(1)}, bf16[640,768]{1,0:T(8,128)(2,1)S(1)}, u32[]{:S(2)}, u32[]{:S(2)}) %collective-permute-start) | collective-permute-done | bytes 983072 | tf_op jit(solution)/shard_map/ppermute | solution.py:341
  52.1 0.0 collective-permute-done.1.from_right.refs_2_
  52.1 0.0 collective-permute-start.5
  52.1 0.5 collective-permute-start.6
  52.6 0.1 shard_map.159
  52.8 1.6 %collective-permute-start.3 = (bf16[640,384]{1,0:T(8,128)(2,1)S(1)}, bf16[640,384]{1,0:T(8,128)(2,1)S(1)}, u32[]{:S(2)}, u32[]{:S(2)}) collective-permute-start(bf16[640,384]{1,0:T(8,128)(2,1)S(1)} %get-tuple-element.45), channel_id=1, source_target_pairs={{0,2},{2,4},{4,6},{6,0},{1,3},{3,5},{5,7},{7,1},{8,10},{10,12},{12... | collective-permute-start | bytes 1474568 | tf_op jit(solution)/shard_map/ppermute | solution.py:341
  54.3 1.7 %collective-permute-start.4 = (bf16[640,384]{1,0:T(8,128)(2,1)S(1)}, bf16[640,384]{1,0:T(8,128)(2,1)S(1)}, u32[]{:S(2)}, u32[]{:S(2)}) collective-permute-start(bf16[640,384]{1,0:T(8,128)(2,1)S(1)} %get-tuple-element.46), channel_id=1, source_target_pairs={{0,6},{2,0},{4,2},{6,4},{1,7},{3,1},{5,3},{7,5},{8,14},{10,8},{12,... | collective-permute-start | bytes 1474568 | tf_op jit(solution)/shard_map/ppermute | solution.py:341
  56.1 1.0 shard_map.160.refs_9_
  57.0 0.0 collective-permute-done.5.refs_1_
  57.0 8.1 %shard_map.161 = (f32[640,1280]{1,0:T(8,128)S(1)}, f32[640,640]{1,0:T(8,128)S(1)}, bf16[3072,1280]{1,0:T(8,128)(2,1)S(1)}, bf16[640,768]{1,0:T(8,128)(2,1)S(1)}) custom-call(s32[2]{0:T(128)S(1)} %pad_add_fusion.place, bf16[640,768]{1,0:T(8,128)(2,1)S(1)} %collective-permute-done.from_left.refs_0_, bf16[640,768]{1,0:T(8,128)(2,1)S(1)} %collective-permute-done.5.refs_1_, ...), custom_call_target="tpu_custom_call" | custom-call | flops 3774873600 | bytes 25165824 | tf_op jit(solution)/shard_map/pallas_call | solution.py:400
  65.2 2.0 %collective-permute-done.3.x = bf16[640,384]{1,0:T(8,128)(2,1)S(1)} collective-permute-done((bf16[640,384]{1,0:T(8,128)(2,1)S(1)}, bf16[640,384]{1,0:T(8,128)(2,1)S(1)}, u32[]{:S(2)}, u32[]{:S(2)}) %collective-permute-start.3) | collective-permute-done | bytes 491552 | tf_op jit(solution)/shard_map/ppermute | solution.py:341
  67.2 0.5 collective-permute-start.8
  67.7 1.6 %shard_map.162 = (f32[640,1280]{1,0:T(8,128)S(1)}, f32[640,640]{1,0:T(8,128)S(1)}) custom-call(f32[640,1280]{1,0:T(8,128)S(1)} %get-tuple-element.51.pre, f32[640,640]{1,0:T(8,128)S(1)} %get-tuple-element.52.hid, bf16[640,384]{1,0:T(8,128)(2,1)S(1)} %collective-permute-done.3.x, bf16[640,384]{1,0:T(8,128)(2,1)S(1)} %collective-permute-done.4.d, ...), custom_call_target="tpu_custom_call" | custom-call | flops 943718400 | bytes 10485760 | tf_op jit(solution)/shard_map/pallas_call | solution.py:414
  69.3 0.0 collective-permute-done.7.x
  69.3 0.5 collective-permute-done.8.d
  69.7 2.8 %shard_map.163 = (bf16[640,1280]{1,0:T(8,128)(2,1)S(1)}, bf16[640,384]{1,0:T(8,128)(2,1)S(1)}) custom-call(f32[640,1280]{1,0:T(8,128)S(1)} %get-tuple-element.57.pre, f32[640,640]{1,0:T(8,128)S(1)} %get-tuple-element.58.hid_ref, bf16[640,384]{1,0:T(8,128)(2,1)S(1)} %collective-permute-done.7.x, bf16[640,384]{1,0:T(8,128)(2,1)S(1)} %collective-permute-done.8.d, ...), custom_call_target="tpu_custom_call" | custom-call | flops 2516582400 | bytes 12582912 | tf_op jit(solution)/shard_map/pallas_call | solution.py:422
  72.6 0.2 collective-permute-start.9
  72.8 3.5 %shard_map.164 = (f32[640,384]{1,0:T(8,128)S(1)}, bf16[3,640,384]{2,1,0:T(8,128)(2,1)S(1)}) custom-call(bf16[640,1280]{1,0:T(8,128)(2,1)S(1)} %get-tuple-element.65.mid_ref, bf16[3072,1280]{1,0:T(8,128)(2,1)S(1)} %get-tuple-element.55.cat), custom_call_target="tpu_custom_call" | custom-call | flops 2516582400 | bytes 8388608 | tf_op jit(solution)/shard_map/pallas_call | solution.py:431
  76.3 0.0 collective-permute-done.9.away
  76.3 0.1 shard_map.165
  76.4 0.5 collective-permute-start.10
  76.9 1.2 collective-permute-start.11
  78.1 2.1 %collective-permute-start.12 = (bf16[320,384]{1,0:T(8,128)(2,1)S(1)}, bf16[320,384]{1,0:T(8,128)(2,1)S(1)}, u32[]{:S(2)}, u32[]{:S(2)}) collective-permute-start(bf16[320,384]{1,0:T(8,128)(2,1)S(1)} %get-tuple-element.73), channel_id=1, source_target_pairs={{0,6},{2,0},{4,2},{6,4},{1,7},{3,1},{5,3},{7,5},{8,14},{10,8},{12,... | collective-permute-start | bytes 737288 | tf_op jit(solution)/shard_map/ppermute | solution.py:341
  80.1 2.7 %shard_map.166.mine = f32[3,640,384]{2,1,0:T(8,128)S(1)} custom-call(bf16[640,1280]{1,0:T(8,128)(2,1)S(1)} %get-tuple-element.65.mid_ref, bf16[3072,1280]{1,0:T(8,128)(2,1)S(1)} %get-tuple-element.55.cat), custom_call_target="tpu_custom_call" | custom-call | flops 1887436800 | bytes 8388608 | tf_op jit(solution)/shard_map/pallas_call | solution.py:444
  82.8 3.5 %collective-permute-done.11.via_right = bf16[320,384]{1,0:T(8,128)(2,1)S(1)} collective-permute-done((bf16[320,384]{1,0:T(8,128)(2,1)S(1)}, bf16[320,384]{1,0:T(8,128)(2,1)S(1)}, u32[]{:S(2)}, u32[]{:S(2)}) %collective-permute-start.11) | collective-permute-done | bytes 245792 | tf_op jit(solution)/shard_map/ppermute | solution.py:341
  86.4 0.0 collective-permute-done.12.via_left
  86.4 0.3 shard_map.168
  86.7 1.2 %collective-permute-start.13 = (bf16[640,384]{1,0:T(8,128)(2,1)S(1)}, bf16[640,384]{1,0:T(8,128)(2,1)S(1)}, u32[]{:S(2)}, u32[]{:S(2)}) collective-permute-start(bf16[640,384]{1,0:T(8,128)(2,1)S(1)} %get-tuple-element.75), channel_id=1, source_target_pairs={{0,2},{2,4},{4,6},{6,0},{1,3},{3,5},{5,7},{7,1},{8,10},{10,12},{12... | collective-permute-start | bytes 1474568 | tf_op jit(solution)/shard_map/ppermute | solution.py:341
  87.9 2.1 %collective-permute-start.14 = (bf16[640,384]{1,0:T(8,128)(2,1)S(1)}, bf16[640,384]{1,0:T(8,128)(2,1)S(1)}, u32[]{:S(2)}, u32[]{:S(2)}) collective-permute-start(bf16[640,384]{1,0:T(8,128)(2,1)S(1)} %get-tuple-element.76), channel_id=1, source_target_pairs={{0,6},{2,0},{4,2},{6,4},{1,7},{3,1},{5,3},{7,5},{8,14},{10,8},{12,... | collective-permute-start | bytes 1474568 | tf_op jit(solution)/shard_map/ppermute | solution.py:341
  90.0 3.6 %all-to-all-start.2 = ((bf16[16,128,128]{2,1,0:T(8,128)(2,1)}), bf16[16,128,128]{2,1,0:T(8,128)(2,1)S(1)}, u32[]{:S(2)}, u32[]{:S(2)}) async-start(bf16[16,128,128]{2,1,0:T(8,128)(2,1)} %shard_map.160.refs_9_), calls=%async_computation.2 | async-start | bytes 1048576 | tf_op jit(solution)/shard_map/all_to_all | solution.py:458
  93.6 7.3 %collective-permute-done.13 = bf16[640,384]{1,0:T(8,128)(2,1)S(1)} collective-permute-done((bf16[640,384]{1,0:T(8,128)(2,1)S(1)}, bf16[640,384]{1,0:T(8,128)(2,1)S(1)}, u32[]{:S(2)}, u32[]{:S(2)}) %collective-permute-start.13) | collective-permute-done | bytes 491552 | tf_op jit(solution)/shard_map/ppermute | solution.py:341
  100.9 0.9 add_convert_fusion
  101.8 3.0 %all-to-all-done.2.refs_6_ = bf16[16,128,128]{2,1,0:T(8,128)(2,1)S(1)} async-done(((bf16[16,128,128]{2,1,0:T(8,128)(2,1)}), bf16[16,128,128]{2,1,0:T(8,128)(2,1)S(1)}, u32[]{:S(2)}, u32[]{:S(2)}) %all-to-all-start.2) | async-done | bytes 524320 | tf_op jit(solution)/shard_map/all_to_all | solution.py:458
  104.8 3.6 %all-to-all-start.3 = ((bf16[16,40,384]{2,1,0:T(8,128)(2,1)}), bf16[16,40,384]{2,1,0:T(8,128)(2,1)S(1)}, u32[]{:S(2)}, u32[]{:S(2)}) async-start(bf16[16,40,384]{2,1,0:T(8,128)(2,1)} %bitcast.6), calls=%async_computation.3 | async-start | bytes 983040 | tf_op jit(solution)/shard_map/all_to_all | solution.py:469
  108.4 5.4 %shard_map.167 = (bf16[256,1024]{1,0:T(8,128)(2,1)}, bf16[256,1024]{1,0:T(8,128)(2,1)}, bf16[256,1024]{1,0:T(8,128)(2,1)}) custom-call(f32[8,256]{1,0:T(8,128)} %refs_0_.3, s32[1,256]{1,0:T(1,128)} %bitcast.18, bf16[256,1024]{1,0:T(8,128)(2,1)} %refs_2_.3, bf16[256,1024]{1,0:T(8,128)(2,1)} %refs_3_.3, bf16[256,1024]{1,0:T(8,128)(2,1)} %refs_4_.5, ...), custom_call_target="tpu_custom_call" | custom-call | flops 1073741824 | bytes 4194304 | tf_op jit(solution)/shard_map/pallas_call | solution.py:459
  113.8 4.6 %all-to-all-done.3 = bf16[16,40,384]{2,1,0:T(8,128)(2,1)S(1)} async-done(((bf16[16,40,384]{2,1,0:T(8,128)(2,1)}), bf16[16,40,384]{2,1,0:T(8,128)(2,1)S(1)}, u32[]{:S(2)}, u32[]{:S(2)}) %all-to-all-start.3) | async-done | bytes 491552 | tf_op jit(solution)/shard_map/all_to_all | solution.py:469
  118.4 1.3 %shard_map.169 = bf16[256,384]{1,0:T(8,128)(2,1)} custom-call(bf16[640,384]{1,0:T(8,128)(2,1)S(1)} %bitcast.15, s32[2,256]{1,0:T(2,128)S(1)} %copy-done.2, f32[2,256]{1,0:T(2,128)S(1)} %bitcast.16), custom_call_target="tpu_custom_call" | custom-call | flops 251658240 | bytes 1048576 | tf_op jit(solution)/shard_map/pallas_call | solution.py:470
  (11 shorter events, 0.0 us)
Async XLA Ops:
  26.7 10.8 %collective-permute-start.2 = (bf16[640,768]{1,0:T(8,128)(2,1)S(1)}, bf16[640,768]{1,0:T(8,128)(2,1)}, u32[]{:S(2)}, u32[]{:S(2)}) collective-permute-start(bf16[640,768]{1,0:T(8,128)(2,1)S(1)} %bitcast.9), channel_id=1, source_target_pairs={{0,1},{1,0},{2,3},{3,2},{4,5},{5,4},{6,7},{7,6},{8,9},{9,8},{10,11... | collective-permute-start | bytes 2949128 | tf_op jit(solution)/shard_map/ppermute | solution.py:344
  26.7 25.4 %collective-permute-start = (bf16[640,768]{1,0:T(8,128)(2,1)S(1)}, bf16[640,768]{1,0:T(8,128)(2,1)S(1)}, u32[]{:S(2)}, u32[]{:S(2)}) collective-permute-start(bf16[640,768]{1,0:T(8,128)(2,1)S(1)} %bitcast.10), channel_id=1, source_target_pairs={{0,2},{2,4},{4,6},{6,0},{1,3},{3,5},{5,7},{7,1},{8,10},{10,12},{12... | collective-permute-start | bytes 2949128 | tf_op jit(solution)/shard_map/ppermute | solution.py:341
  28.2 23.9 %collective-permute-start.1 = (bf16[640,768]{1,0:T(8,128)(2,1)S(1)}, bf16[640,768]{1,0:T(8,128)(2,1)S(1)}, u32[]{:S(2)}, u32[]{:S(2)}) collective-permute-start(bf16[640,768]{1,0:T(8,128)(2,1)S(1)} %bitcast.11), channel_id=1, source_target_pairs={{0,6},{2,0},{4,2},{6,4},{1,7},{3,1},{5,3},{7,5},{8,14},{10,8},{12,... | collective-permute-start | bytes 2949128 | tf_op jit(solution)/shard_map/ppermute | solution.py:341
  33.1 0.8 copy-start
  33.9 16.2 %all-to-all-start.1 = ((bf16[16,144,128]{2,1,0:T(8,128)(2,1)}), bf16[16,144,128]{2,1,0:T(8,128)(2,1)S(1)}, u32[]{:S(2)}, u32[]{:S(2)}) async-start(bf16[16,144,128]{2,1,0:T(8,128)(2,1)} %copy-done), calls=%async_computation.1 | async-start | bytes 1179648 | tf_op jit(solution)/shard_map/all_to_all | solution.py:370
  52.1 4.9 %collective-permute-start.5 = (bf16[640,768]{1,0:T(8,128)(2,1)S(1)}, bf16[640,768]{1,0:T(8,128)(2,1)S(1)}, u32[]{:S(2)}, u32[]{:S(2)}) collective-permute-start(bf16[640,768]{1,0:T(8,128)(2,1)S(1)} %collective-permute-done.from_left.refs_0_), channel_id=1, source_target_pairs={{0,1},{1,0},{2,3},{3,2},{4,5},{5,4},{6,7},{7,6},{8,9},{9,8},{10,11... | collective-permute-start | bytes 2949128 | tf_op jit(solution)/shard_map/ppermute | solution.py:344
  52.1 4.9 %collective-permute-start.6 = (bf16[640,768]{1,0:T(8,128)(2,1)S(1)}, bf16[640,768]{1,0:T(8,128)(2,1)S(1)}, u32[]{:S(2)}, u32[]{:S(2)}) collective-permute-start(bf16[640,768]{1,0:T(8,128)(2,1)S(1)} %collective-permute-done.1.from_right.refs_2_), channel_id=1, source_target_pairs={{0,1},{1,0},{2,3},{3,2},{4,5},{5,4},{6,7},{7,6},{8,9},{9,8},{10,11... | collective-permute-start | bytes 2949128 | tf_op jit(solution)/shard_map/ppermute | solution.py:344
  52.8 14.4 %collective-permute-start.3 = (bf16[640,384]{1,0:T(8,128)(2,1)S(1)}, bf16[640,384]{1,0:T(8,128)(2,1)S(1)}, u32[]{:S(2)}, u32[]{:S(2)}) collective-permute-start(bf16[640,384]{1,0:T(8,128)(2,1)S(1)} %get-tuple-element.45), channel_id=1, source_target_pairs={{0,2},{2,4},{4,6},{6,0},{1,3},{3,5},{5,7},{7,1},{8,10},{10,12},{12... | collective-permute-start | bytes 1474568 | tf_op jit(solution)/shard_map/ppermute | solution.py:341
  54.3 12.9 %collective-permute-start.4 = (bf16[640,384]{1,0:T(8,128)(2,1)S(1)}, bf16[640,384]{1,0:T(8,128)(2,1)S(1)}, u32[]{:S(2)}, u32[]{:S(2)}) collective-permute-start(bf16[640,384]{1,0:T(8,128)(2,1)S(1)} %get-tuple-element.46), channel_id=1, source_target_pairs={{0,6},{2,0},{4,2},{6,4},{1,7},{3,1},{5,3},{7,5},{8,14},{10,8},{12,... | collective-permute-start | bytes 1474568 | tf_op jit(solution)/shard_map/ppermute | solution.py:341
  67.2 2.1 %collective-permute-start.7 = (bf16[640,384]{1,0:T(8,128)(2,1)S(1)}, bf16[640,384]{1,0:T(8,128)(2,1)S(1)}, u32[]{:S(2)}, u32[]{:S(2)}) collective-permute-start(bf16[640,384]{1,0:T(8,128)(2,1)S(1)} %collective-permute-done.3.x), channel_id=1, source_target_pairs={{0,1},{1,0},{2,3},{3,2},{4,5},{5,4},{6,7},{7,6},{8,9},{9,8},{10,11... | collective-permute-start | bytes 1474568 | tf_op jit(solution)/shard_map/ppermute | solution.py:344
  67.2 2.6 %collective-permute-start.8 = (bf16[640,384]{1,0:T(8,128)(2,1)S(1)}, bf16[640,384]{1,0:T(8,128)(2,1)S(1)}, u32[]{:S(2)}, u32[]{:S(2)}) collective-permute-start(bf16[640,384]{1,0:T(8,128)(2,1)S(1)} %collective-permute-done.4.d), channel_id=1, source_target_pairs={{0,1},{1,0},{2,3},{3,2},{4,5},{5,4},{6,7},{7,6},{8,9},{9,8},{10,11... | collective-permute-start | bytes 1474568 | tf_op jit(solution)/shard_map/ppermute | solution.py:344
  72.6 3.8 %collective-permute-start.9 = (bf16[640,384]{1,0:T(8,128)(2,1)S(1)}, bf16[640,384]{1,0:T(8,128)(2,1)S(1)}, u32[]{:S(2)}, u32[]{:S(2)}) collective-permute-start(bf16[640,384]{1,0:T(8,128)(2,1)S(1)} %get-tuple-element.62), channel_id=1, source_target_pairs={{0,1},{1,0},{2,3},{3,2},{4,5},{5,4},{6,7},{7,6},{8,9},{9,8},{10,11... | collective-permute-start | bytes 1474568 | tf_op jit(solution)/shard_map/ppermute | solution.py:344
  76.4 9.9 %collective-permute-start.10 = (bf16[3,640,384]{2,1,0:T(8,128)(2,1)S(1)}, bf16[3,640,384]{2,1,0:T(8,128)(2,1)S(1)}, u32[]{:S(2)}, u32[]{:S(2)}) collective-permute-start(bf16[3,640,384]{2,1,0:T(8,128)(2,1)S(1)} %get-tuple-element.71), channel_id=1, source_target_pairs={{0,1},{1,0},{2,3},{3,2},{4,5},{5,4},{6,7},{7,6},{8,9},{9,8},{10,11... | collective-permute-start | bytes 4423688 | tf_op jit(solution)/shard_map/ppermute | solution.py:344
  76.9 9.5 %collective-permute-start.11 = (bf16[320,384]{1,0:T(8,128)(2,1)S(1)}, bf16[320,384]{1,0:T(8,128)(2,1)S(1)}, u32[]{:S(2)}, u32[]{:S(2)}) collective-permute-start(bf16[320,384]{1,0:T(8,128)(2,1)S(1)} %get-tuple-element.72), channel_id=1, source_target_pairs={{0,2},{2,4},{4,6},{6,0},{1,3},{3,5},{5,7},{7,1},{8,10},{10,12},{12... | collective-permute-start | bytes 737288 | tf_op jit(solution)/shard_map/ppermute | solution.py:341
  78.1 8.3 %collective-permute-start.12 = (bf16[320,384]{1,0:T(8,128)(2,1)S(1)}, bf16[320,384]{1,0:T(8,128)(2,1)S(1)}, u32[]{:S(2)}, u32[]{:S(2)}) collective-permute-start(bf16[320,384]{1,0:T(8,128)(2,1)S(1)} %get-tuple-element.73), channel_id=1, source_target_pairs={{0,6},{2,0},{4,2},{6,4},{1,7},{3,1},{5,3},{7,5},{8,14},{10,8},{12,... | collective-permute-start | bytes 737288 | tf_op jit(solution)/shard_map/ppermute | solution.py:341
  86.7 14.2 %collective-permute-start.13 = (bf16[640,384]{1,0:T(8,128)(2,1)S(1)}, bf16[640,384]{1,0:T(8,128)(2,1)S(1)}, u32[]{:S(2)}, u32[]{:S(2)}) collective-permute-start(bf16[640,384]{1,0:T(8,128)(2,1)S(1)} %get-tuple-element.75), channel_id=1, source_target_pairs={{0,2},{2,4},{4,6},{6,0},{1,3},{3,5},{5,7},{7,1},{8,10},{10,12},{12... | collective-permute-start | bytes 1474568 | tf_op jit(solution)/shard_map/ppermute | solution.py:341
  87.9 13.0 %collective-permute-start.14 = (bf16[640,384]{1,0:T(8,128)(2,1)S(1)}, bf16[640,384]{1,0:T(8,128)(2,1)S(1)}, u32[]{:S(2)}, u32[]{:S(2)}) collective-permute-start(bf16[640,384]{1,0:T(8,128)(2,1)S(1)} %get-tuple-element.76), channel_id=1, source_target_pairs={{0,6},{2,0},{4,2},{6,4},{1,7},{3,1},{5,3},{7,5},{8,14},{10,8},{12,... | collective-permute-start | bytes 1474568 | tf_op jit(solution)/shard_map/ppermute | solution.py:341
  90.0 14.8 %all-to-all-start.2 = ((bf16[16,128,128]{2,1,0:T(8,128)(2,1)}), bf16[16,128,128]{2,1,0:T(8,128)(2,1)S(1)}, u32[]{:S(2)}, u32[]{:S(2)}) async-start(bf16[16,128,128]{2,1,0:T(8,128)(2,1)} %shard_map.160.refs_9_), calls=%async_computation.2 | async-start | bytes 1048576 | tf_op jit(solution)/shard_map/all_to_all | solution.py:458
  100.9 17.5 %copy-start.1 = (f32[256,2]{0,1:T(2,128)S(1)}, f32[256,2]{0,1:T(2,128)}, u32[]{:S(2)}) copy-start(f32[256,2]{0,1:T(2,128)} %param.21) | copy-start | bytes 6148
  100.9 17.5 %copy-start.2 = (s32[2,256]{1,0:T(2,128)S(1)}, s32[2,256]{1,0:T(2,128)}, u32[]{:S(2)}) copy-start(s32[2,256]{1,0:T(2,128)} %get-tuple-element.77.slots_ref) | copy-start | bytes 6148
  104.8 13.6 %all-to-all-start.3 = ((bf16[16,40,384]{2,1,0:T(8,128)(2,1)}), bf16[16,40,384]{2,1,0:T(8,128)(2,1)S(1)}, u32[]{:S(2)}, u32[]{:S(2)}) async-start(bf16[16,40,384]{2,1,0:T(8,128)(2,1)} %bitcast.6), calls=%async_computation.3 | async-start | bytes 983040 | tf_op jit(solution)/shard_map/all_to_all | solution.py:469
